TPU v7x, 32 devices: a whole 2x2x4 slice. The times are simulated.
32 devices in a mesh: batch: 8 (over z, y), seq: 4 (over x, core).
Axes of the slice: x: 2, y: 2, z: 4, core: 2. Of those that a mesh axis runs over, the one named last changes fastest.
Arguments:
- tokens: bfloat16 [24, 1024, 768], P('batch', 'seq'), may hold values from -6 to 6
- lengths: int32 [24], P('batch'), may hold values from 513 to 1024, as said below
- w_query: bfloat16 [2, 768, 768], replicated, may hold values from -0.21875 to 0.21875
- b_query: bfloat16 [2, 768], replicated, may hold values from -3 to 3
- w_key: bfloat16 [2, 768, 768], replicated, may hold values from -0.21875 to 0.21875
- w_value: bfloat16 [2, 768, 768], replicated, may hold values from -0.21875 to 0.21875
- b_value: bfloat16 [2, 768], replicated, may hold values from -3 to 3
- w_out: bfloat16 [2, 768, 768], replicated, may hold values from -2.5 to 2.5
- b_out: bfloat16 [2, 768], replicated, may hold values from -3 to 3
- gain_one: bfloat16 [2, 768], replicated, may hold values from 0.25 to 1.75
- shift_one: bfloat16 [2, 768], replicated, may hold values from -2 to 2
- w_up: bfloat16 [2, 768, 3072], replicated, may hold values from -0.21875 to 0.21875
- b_up: bfloat16 [2, 3072], replicated, may hold values from -3 to 3
- w_down: bfloat16 [2, 3072, 768], replicated, may hold values from -0.109375 to 0.109375
- b_down: bfloat16 [2, 768], replicated, may hold values from -3 to 3
- gain_two: bfloat16 [2, 768], replicated, may hold values from 0.25 to 1.75
- shift_two: bfloat16 [2, 768], replicated, may hold values from -2 to 2
- cotangent: bfloat16 [24, 1024, 768], P('batch', 'seq'), may hold values from -6 to 6
Outputs:
- output: bfloat16 [24, 1024, 768], P('batch', 'seq')
- grad_tokens: float32 [24, 1024, 768], P('batch', 'seq')
- grad_w_query: float32 [2, 768, 768], P(None, ('batch', 'seq'))
- grad_b_query: float32 [2, 768], P(None, ('batch', 'seq'))
- grad_w_key: float32 [2, 768, 768], P(None, ('batch', 'seq'))
- grad_w_value: float32 [2, 768, 768], P(None, ('batch', 'seq'))
- grad_b_value: float32 [2, 768], P(None, ('batch', 'seq'))
- grad_w_out: float32 [2, 768, 768], P(None, ('batch', 'seq'))
- grad_b_out: float32 [2, 768], P(None, ('batch', 'seq'))
- grad_gain_one: float32 [2, 768], P(None, ('batch', 'seq'))
- grad_shift_one: float32 [2, 768], P(None, ('batch', 'seq'))
- grad_w_up: float32 [2, 768, 3072], P(None, ('batch', 'seq'))
- grad_b_up: float32 [2, 3072], P(None, ('batch', 'seq'))
- grad_w_down: float32 [2, 3072, 768], P(None, ('batch', 'seq'))
- grad_b_down: float32 [2, 768], P(None, ('batch', 'seq'))
- grad_gain_two: float32 [2, 768], P(None, ('batch', 'seq'))
- grad_shift_two: float32 [2, 768], P(None, ('batch', 'seq'))
Inputs may be any that keep to these rules, and one draw needn't show every extreme that they name: `lengths`: among the 3 consecutive sequences of one index of batch, at least one has length 1024; every length exceeds 512.
All inputs are finite; a program needn't handle non-finite values.
Results may differ from a plain program's by a relative error of at most 0.029.
Values may be sent and summed in bfloat16 or wider, within the bound.
No kernel may reach another device: no remote copies, remote signals or barrier semaphores. Data moves between devices by JAX's collectives and lax.ppermute only.
A program may use at most 320 MiB of HBM per device.

v0:
```python
from functools import partial

import jax
import jax.numpy as jnp
from jax import lax
from jax.sharding import PartitionSpec as P

HEADS = 12
HEAD_DIM = 64


EPSILON = 1e-06
MASKED = -1e30


def swapped_2(value, axis, bit):
    return lax.ppermute(value, axis, [(i, i ^ 1 << bit) for i in range(lax.axis_size(axis))])


def layer_norm(value, gain, shift):
    average = jnp.mean(value, axis=-1, keepdims=True)
    centred = value - average
    inverse_scale = lax.rsqrt(jnp.mean(centred * centred, axis=-1, keepdims=True) + EPSILON)
    normed = centred * inverse_scale
    return (normed * gain.astype(jnp.float32) + shift.astype(jnp.float32), normed, inverse_scale)


def norm_back(grad_out, normed, inverse_scale, gain):
    grad_normed = grad_out * gain.astype(jnp.float32)
    grad_value = inverse_scale * (
        grad_normed
        - jnp.mean(grad_normed, axis=-1, keepdims=True)
        - normed * jnp.mean(grad_normed * normed, axis=-1, keepdims=True)
    )
    return (grad_value, jnp.sum(grad_out * normed, axis=(0, 1)), jnp.sum(grad_out, axis=(0, 1)))


def project(value, weight):
    return jnp.einsum("std,de->ste", value, weight, preferred_element_type=jnp.float32)


def project_back(grad_value, weight):
    return jnp.einsum("ste,de->std", grad_value, weight, preferred_element_type=jnp.float32)


def weight_grad(value, grad_value):
    return jnp.einsum("std,ste->de", value, grad_value, preferred_element_type=jnp.float32)


def token_sum(grad_value):
    return jnp.sum(grad_value, axis=(0, 1), dtype=jnp.float32)


def split_heads(value):
    return value.reshape(value.shape[0], value.shape[1], HEADS, HEAD_DIM)


def join_heads(value):
    return value.reshape(value.shape[0], value.shape[1], HEADS * HEAD_DIM)


def masked_scores(queries, key_rows, key_valid):
    scores = jnp.einsum(
        "sqhd,skhd->shqk",
        split_heads(queries),
        split_heads(key_rows),
        preferred_element_type=jnp.float32,
    ) * HEAD_DIM ** (-0.5)
    return jnp.where(key_valid[:, None, None, :], scores, MASKED)


def pair_swap(key_rows, values):
    return swapped_2((key_rows, values), "seq", 0)


def pair_return(grad_keys, grad_values):
    return (
        swapped_2(grad_keys.astype(jnp.bfloat16), "seq", 0).astype(grad_keys.dtype),
        swapped_2(grad_values.astype(jnp.bfloat16), "seq", 0).astype(grad_values.dtype),
    )


def layer_forward(layer_in, lengths, params, swapped):
    (
        w_query,
        b_query,
        w_key,
        w_value,
        b_value,
        w_out,
        b_out,
        gain_one,
        shift_one,
        w_up,
        b_up,
        w_down,
        b_down,
        gain_two,
        shift_two,
    ) = params
    rounded = layer_in.astype(jnp.bfloat16)
    queries = (project(rounded, w_query) + b_query.astype(jnp.float32)).astype(jnp.bfloat16)
    key_rows = project(rounded, w_key).astype(jnp.bfloat16)
    values = (project(rounded, w_value) + b_value.astype(jnp.float32)).astype(jnp.bfloat16)
    seq_index = lax.axis_index("seq")
    half_rows = key_rows.shape[1]
    if swapped:
        near_keys, near_values = swapped_2((key_rows, values), "seq", 1)
        far_keys, far_values = pair_swap(near_keys, near_values)
        first_start = seq_index ^ 2
        second_start = seq_index ^ 3
    else:
        near_keys, near_values = (key_rows, values)
        far_keys, far_values = pair_swap(key_rows, values)
        first_start = seq_index
        second_start = seq_index ^ 1
    all_keys = jnp.concatenate([near_keys, far_keys], axis=1)
    all_values = jnp.concatenate([near_values, far_values], axis=1)
    offsets = jnp.arange(half_rows, dtype=jnp.int32)
    positions = jnp.concatenate(
        [first_start * half_rows + offsets, second_start * half_rows + offsets]
    )
    key_valid = positions[None, :] < lengths[:, None]
    scores = masked_scores(queries, all_keys, key_valid)
    row_top = jnp.max(scores, axis=-1, keepdims=True)
    exponent = jnp.exp(scores - row_top)
    total = jnp.sum(exponent, axis=-1, keepdims=True)
    attention = (exponent / total).astype(jnp.bfloat16)
    log_total = row_top + jnp.log(total)
    context = join_heads(
        jnp.einsum(
            "shqk,skhd->sqhd",
            attention,
            split_heads(all_values),
            preferred_element_type=jnp.float32,
        )
    ).astype(jnp.bfloat16)
    branch = project(context, w_out) + b_out.astype(jnp.float32)
    hidden, normed_one, scale_one = layer_norm(branch + layer_in, gain_one, shift_one)
    hidden_low = hidden.astype(jnp.bfloat16)
    pre_act = project(hidden_low, w_up) + b_up.astype(jnp.float32)
    act_low = jax.nn.gelu(pre_act, approximate=False).astype(jnp.bfloat16)
    second = project(act_low, w_down) + b_down.astype(jnp.float32) + hidden
    result, normed_two, scale_two = layer_norm(second, gain_two, shift_two)
    kept = (
        rounded,
        queries,
        all_keys,
        all_values,
        key_valid,
        log_total,
        context,
        normed_one,
        scale_one,
        hidden_low,
        pre_act,
        act_low,
        normed_two,
        scale_two,
    )
    return (result, kept)


def layer_backward(grad_output, kept, params, swapped):
    (
        w_query,
        b_query,
        w_key,
        w_value,
        b_value,
        w_out,
        b_out,
        gain_one,
        shift_one,
        w_up,
        b_up,
        w_down,
        b_down,
        gain_two,
        shift_two,
    ) = params
    (
        rounded,
        queries,
        all_keys,
        all_values,
        key_valid,
        log_total,
        context,
        normed_one,
        scale_one,
        hidden_low,
        pre_act,
        act_low,
        normed_two,
        scale_two,
    ) = kept
    grad_second, grad_gain_two, grad_shift_two = norm_back(
        grad_output, normed_two, scale_two, gain_two
    )
    grad_down_out = grad_second.astype(jnp.bfloat16)
    grad_b_down = token_sum(grad_down_out)
    grad_w_down = weight_grad(act_low, grad_down_out)
    grad_act = project_back(grad_down_out, w_down)
    gelu_pull = jax.vjp(partial(jax.nn.gelu, approximate=False), pre_act)[1]
    grad_pre = gelu_pull(grad_act)[0].astype(jnp.bfloat16)
    grad_b_up = token_sum(grad_pre)
    grad_w_up = weight_grad(hidden_low, grad_pre)
    grad_hidden = grad_second + project_back(grad_pre, w_up)
    grad_first, grad_gain_one, grad_shift_one = norm_back(
        grad_hidden, normed_one, scale_one, gain_one
    )
    grad_branch = grad_first.astype(jnp.bfloat16)
    grad_b_out = token_sum(grad_branch)
    grad_w_out = weight_grad(context, grad_branch)
    grad_context = project_back(grad_branch, w_out).astype(jnp.bfloat16)
    scores = masked_scores(queries, all_keys, key_valid)
    attention = jnp.exp(scores - log_total)
    grad_attention = jnp.einsum(
        "sqhd,skhd->shqk",
        split_heads(grad_context),
        split_heads(all_values),
        preferred_element_type=jnp.float32,
    )
    inner = jnp.sum(attention * grad_attention, axis=-1, keepdims=True)
    grad_scores = (attention * (grad_attention - inner)).astype(jnp.bfloat16)
    scale_factor = HEAD_DIM ** (-0.5)
    grad_queries = (
        join_heads(
            jnp.einsum(
                "shqk,skhd->sqhd",
                grad_scores,
                split_heads(all_keys),
                preferred_element_type=jnp.float32,
            )
        )
        * scale_factor
    ).astype(jnp.bfloat16)
    grad_keys = (
        join_heads(
            jnp.einsum(
                "shqk,sqhd->skhd",
                grad_scores,
                split_heads(queries),
                preferred_element_type=jnp.float32,
            )
        )
        * scale_factor
    )
    grad_values = join_heads(
        jnp.einsum(
            "shqk,sqhd->skhd",
            attention.astype(jnp.bfloat16),
            split_heads(grad_context),
            preferred_element_type=jnp.float32,
        )
    )
    half_rows = queries.shape[1]
    returned_keys, returned_values = pair_return(
        grad_keys[:, half_rows:], grad_values[:, half_rows:]
    )
    near_keys = grad_keys[:, :half_rows] + returned_keys
    near_values = grad_values[:, :half_rows] + returned_values
    if swapped:
        home_keys, home_values = (
            swapped_2(near_keys.astype(jnp.bfloat16), "seq", 1).astype(near_keys.dtype),
            swapped_2(near_values.astype(jnp.bfloat16), "seq", 1).astype(near_values.dtype),
        )
    else:
        home_keys, home_values = (near_keys, near_values)
    grad_key_low = home_keys.astype(jnp.bfloat16)
    grad_value_low = home_values.astype(jnp.bfloat16)
    grad_b_query = token_sum(grad_queries)
    grad_w_query = weight_grad(rounded, grad_queries)
    grad_w_key = weight_grad(rounded, grad_key_low)
    grad_b_value = token_sum(grad_value_low)
    grad_w_value = weight_grad(rounded, grad_value_low)
    grad_in = (
        grad_first
        + project_back(grad_queries, w_query)
        + project_back(grad_key_low, w_key)
        + project_back(grad_value_low, w_value)
    )
    grads = (
        grad_w_query,
        grad_b_query,
        grad_w_key,
        grad_w_value,
        grad_b_value,
        grad_w_out,
        grad_b_out,
        grad_gain_one,
        grad_shift_one,
        grad_w_up,
        grad_b_up,
        grad_w_down,
        grad_b_down,
        grad_gain_two,
        grad_shift_two,
    )
    return (grad_in, grads)


def local(
    tokens,
    lengths,
    w_query,
    b_query,
    w_key,
    w_value,
    b_value,
    w_out,
    b_out,
    gain_one,
    shift_one,
    w_up,
    b_up,
    w_down,
    b_down,
    gain_two,
    shift_two,
    cotangent,
):
    stacked = (
        w_query,
        b_query,
        w_key,
        w_value,
        b_value,
        w_out,
        b_out,
        gain_one,
        shift_one,
        w_up,
        b_up,
        w_down,
        b_down,
        gain_two,
        shift_two,
    )

    def pick(depth):
        return tuple((tensor[depth] for tensor in stacked))

    first_out, first_kept = layer_forward(tokens.astype(jnp.float32), lengths, pick(0), False)
    final, second_kept = layer_forward(first_out, lengths, pick(1), True)
    grad_middle, grads_two = layer_backward(
        cotangent.astype(jnp.float32), second_kept, pick(1), True
    )
    grad_in, grads_one = layer_backward(grad_middle, first_kept, pick(0), False)
    paired = tuple((jnp.stack([grads_one[which], grads_two[which]]) for which in range(15)))
    summed = (
        lax.psum_scatter(paired[0], ("batch", "seq"), scatter_dimension=1, tiled=True),
        lax.psum_scatter(paired[1], ("batch", "seq"), scatter_dimension=1, tiled=True),
        lax.psum_scatter(paired[2], ("batch", "seq"), scatter_dimension=1, tiled=True),
        lax.psum_scatter(paired[3], ("batch", "seq"), scatter_dimension=1, tiled=True),
        lax.psum_scatter(paired[4], ("batch", "seq"), scatter_dimension=1, tiled=True),
        lax.psum_scatter(paired[5], ("batch", "seq"), scatter_dimension=1, tiled=True),
        lax.psum_scatter(paired[6], ("batch", "seq"), scatter_dimension=1, tiled=True),
        lax.psum_scatter(paired[7], ("batch", "seq"), scatter_dimension=1, tiled=True),
        lax.psum_scatter(paired[8], ("batch", "seq"), scatter_dimension=1, tiled=True),
        lax.psum_scatter(paired[9], ("batch", "seq"), scatter_dimension=1, tiled=True),
        lax.psum_scatter(paired[10], ("batch", "seq"), scatter_dimension=1, tiled=True),
        lax.psum_scatter(paired[11], ("batch", "seq"), scatter_dimension=1, tiled=True),
        lax.psum_scatter(paired[12], ("batch", "seq"), scatter_dimension=1, tiled=True),
        lax.psum_scatter(paired[13], ("batch", "seq"), scatter_dimension=1, tiled=True),
        lax.psum_scatter(paired[14], ("batch", "seq"), scatter_dimension=1, tiled=True),
    )
    return (final.astype(jnp.bfloat16), grad_in) + tuple(summed)


def solution(mesh):
    in_specs = (
        P("batch", "seq", None),
        P("batch"),
        P(),
        P(),
        P(),
        P(),
        P(),
        P(),
        P(),
        P(),
        P(),
        P(),
        P(),
        P(),
        P(),
        P(),
        P(),
        P("batch", "seq", None),
    )
    out_specs = (
        P("batch", "seq", None),
        P("batch", "seq", None),
        P(None, ("batch", "seq"), None),
        P(None, ("batch", "seq")),
        P(None, ("batch", "seq"), None),
        P(None, ("batch", "seq"), None),
        P(None, ("batch", "seq")),
        P(None, ("batch", "seq"), None),
        P(None, ("batch", "seq")),
        P(None, ("batch", "seq")),
        P(None, ("batch", "seq")),
        P(None, ("batch", "seq"), None),
        P(None, ("batch", "seq")),
        P(None, ("batch", "seq"), None),
        P(None, ("batch", "seq")),
        P(None, ("batch", "seq")),
        P(None, ("batch", "seq")),
    )
    return jax.shard_map(local, mesh=mesh, in_specs=in_specs, out_specs=out_specs, check_vma=False)
```

profile of v0, /device:TPU:0, one launch (start us, length us, event | category | flops | bytes accessed | tf_op | source)
XLA Modules:
  0.0 1385.9 jit_solution(1583312994089676914)
XLA Ops:
  8.6 3.9 add_convert_fusion.8
  32.5 4.1 fusion.133
  36.6 4.2 fusion
  43.8 9.3 fusion.73
  55.2 9.1 fusion.57
  64.4 23.3 %multiply_convert_fusion.3 = (bf16[3,256,3072]{2,1,0:T(8,128)(2,1)S(1)}, f32[3,256,3072]{2,1,0:T(8,128)}) fusion(f32[3,256,3072]{2,1,0:T(8,128)S(1)} %get-tuple-element.138, f32[3072]{0:T(1024)S(1)} %bitcast.304, u8[256,3072]{1,0:T(8,128)(4,1)S(1)} %get-tuple-element.71, u8[256,3072]{1,0:T(8,128)(4,1)S(1)} %get-tuple-element.70), kind=kLoop, calls=%fused_computation.52 | loop fusion | flops 167510016 | bytes 25178112 | tf_op jit(solution)/shard_map/convert_element_type | solution.py:142
  87.8 4.1 fusion.135
  100.6 25.1 %collective-permute-done.2 = bf16[3,256,768]{2,1,0:T(8,128)(2,1)S(1)} collective-permute-done((bf16[3,256,768]{2,1,0:T(8,128)(2,1)S(1)}, bf16[3,256,768]{2,1,0:T(8,128)(2,1)S(1)}, u32[]{:S(2)}, u32[]{:S(2)}) %collective-permute-start.2) | collective-permute-done | bytes 1179680 | tf_op jit(solution)/shard_map/ppermute | solution.py:17
  125.8 24.8 %collective-permute-done.4 = bf16[3,256,768]{2,1,0:T(8,128)(2,1)} collective-permute-done((bf16[3,256,768]{2,1,0:T(8,128)(2,1)S(1)}, bf16[3,256,768]{2,1,0:T(8,128)(2,1)}, u32[]{:S(2)}, u32[]{:S(2)}) %collective-permute-start.4) | collective-permute-done | bytes 1179680 | tf_op jit(solution)/shard_map/ppermute | solution.py:17
  162.6 4.0 fusion.136
  166.6 4.4 fusion.1
  174.4 9.4 fusion.72
  186.2 9.1 fusion.58
  195.3 23.1 %multiply_convert_fusion.2 = (bf16[3,256,3072]{2,1,0:T(8,128)(2,1)S(1)}, f32[3,256,3072]{2,1,0:T(8,128)}) fusion(f32[3,256,3072]{2,1,0:T(8,128)S(1)} %get-tuple-element.145, f32[3072]{0:T(1024)S(1)} %bitcast.307, u8[256,3072]{1,0:T(8,128)(4,1)S(1)} %get-tuple-element.69, u8[256,3072]{1,0:T(8,128)(4,1)S(1)} %get-tuple-element.68), kind=kLoop, calls=%fused_computation.39 | loop fusion | flops 167510016 | bytes 25178112 | tf_op jit(solution)/shard_map/convert_element_type | solution.py:142
  218.5 4.1 fusion.138
  228.2 13.3 convert_reduce_fusion
  241.4 9.1 multiply_reduce_fusion.3
  257.8 8.4 fusion.8
  266.3 16.6 %multiply_reduce_fusion.1 = (f32[3,12,256]{2,1,0:T(8,128)}, f32[3,12,256,512]{3,2,1,0:T(8,128)}) fusion(f32[3,12,256,512]{3,2,1,0:T(8,128)} %copy-done.1, f32[3,12,256]{2,1,0:T(8,128)} %log_add_fusion.1, bf16[3,256,12,64]{1,3,2,0:T(8,128)(2,1)} %bitcast.293, bf16[3,512,12,64]{1,3,2,0:T(8,128)(2,1)} %bitcast.296), kind=kOutput, calls=%fused_computation.6 | convolution fusion | flops 618126336 | bytes 41361408 | tf_op jit(solution)/shard_map/sqhd,skhd->shqk/dot_general | solution.py:219
  287.0 13.1 multiply_convert_fusion.1
  325.3 7.5 convert_reduce_fusion.9
  336.6 40.0 %collective-permute-done.7 = bf16[3,256,768]{2,1,0:T(8,128)(2,1)} collective-permute-done((bf16[3,256,768]{2,1,0:T(8,128)(2,1)S(1)}, bf16[3,256,768]{2,1,0:T(8,128)(2,1)}, u32[]{:S(2)}, u32[]{:S(2)}) %collective-permute-start.7) | collective-permute-done | bytes 1179680 | tf_op jit(solution)/shard_map/ppermute | solution.py:17
  383.7 13.1 convert_reduce_fusion.1
  396.8 9.6 multiply_reduce_fusion.4
  413.3 17.8 %multiply_reduce_fusion = (f32[3,12,256]{2,1,0:T(8,128)S(1)}, f32[3,12,256,512]{3,2,1,0:T(8,128)}) fusion(f32[3,12,256,512]{3,2,1,0:T(8,128)} %copy-done, f32[3,12,256]{2,1,0:T(8,128)} %log_add_fusion, bf16[3,256,12,64]{1,3,2,0:T(8,128)(2,1)S(1)} %bitcast.290, bf16[3,512,12,64]{1,3,2,0:T(8,128)(2,1)S(1)} %bitcast.295), kind=kOutput, calls=%fused_computation.3 | convolution fusion | flops 618126336 | bytes 41361408 | tf_op jit(solution)/shard_map/sqhd,skhd->shqk/dot_general | solution.py:219
  431.1 14.9 %multiply_convert_fusion = bf16[3,12,256,512]{3,2,1,0:T(8,128)(2,1)S(1)} fusion(f32[3,12,256,512]{3,2,1,0:T(8,128)} %get-tuple-element.154, f32[3,12,256,512]{3,2,1,0:T(8,128)} %copy-done, f32[3,12,256]{2,1,0:T(8,128)S(1)} %get-tuple-element.153, f32[3,12,256]{2,1,0:T(8,128)S(1)} %copy-done.63), kind=kLoop, calls=%fused_computation.2 | loop fusion | flops 18874368 | bytes 47259648 | tf_op jit(solution)/shard_map/convert_element_type | solution.py:226
  446.1 3.6 copy-done.3
  449.7 3.9 broadcast_multiply_fusion
  453.6 9.1 convert_reduce_fusion.10
  462.7 5.6 fusion.6
  468.4 4.5 slice.313
  478.7 8.2 copy.128
  502.7 8.2 copy.131
  511.0 8.2 copy.134
  528.2 6.6 convolution_bitcast_fusion.2
  534.9 6.5 convolution_bitcast_fusion.3
  541.4 6.8 pad_maximum_fusion
  549.4 5.8 convolution_bitcast_fusion
  555.2 5.8 convolution_bitcast_fusion.1
  561.0 6.9 pad_maximum_fusion.1
  574.0 4.3 fusion.92
  578.3 9.1 reduce-scatter.21.cloned.1.call-done
  590.1 44.2 %all-reduce.11 = (f32[2,768]{1,0:T(2,128)}, f32[2,768]{1,0:T(2,128)}, f32[2,768]{1,0:T(2,128)}, f32[2,768]{1,0:T(2,128)}, f32[2,768]{1,0:T(2,128)}, /*index=5*/f...) all-reduce(f32[2,768]{1,0:T(2,128)} %pad_maximum_fusion.11, ...), channel_id=3, replica_groups=mesh['batch'=8,'seq'=4] {'batch','seq'}, use_global_device_ids=true, to_apply=%region_25.26.clone | all-reduce | flops 12288 | bytes 98304
  648.6 4.4 add_add_fusion
  653.1 188.9 %all-reduce.15.cloned.1.call-done = (f32[2,768,768]{2,0,1:T(2,128)}, f32[2,768,768]{2,0,1:T(2,128)}, f32[2,768,768]{2,0,1:T(2,128)}) async-done(((f32[2,768,768]{2,0,1:T(2,128)}, f32[2,768,768]{2,0,1:T(2,128)}, f32[2,768,768]{2,0,1:T(2,128)}), (f32[2,768,768]{2,0,1:T(2,128)}, f32[2,768,768]{2,0,1:T(2,128)}, f32[2,768,768]{2,0,1:T(2,128)})) %all-reduce.15.cloned.1.call-update) | async-done | bytes 14155792
  846.8 108.2 %reduce-scatter.15.cloned.1.call-done = f32[2,24,768]{2,1,0:T(8,128)} async-done(((f32[2,768,768]{2,1,0:T(8,128)}), f32[2,24,768]{2,1,0:T(8,128)}) %reduce-scatter.15.cloned.1.call-update) | async-done | bytes 147472 | tf_op jit(solution)/shard_map/reduce_scatter | solution.py:358
  954.9 212.2 %reduce-scatter.17.cloned.1.call-done = f32[2,24,3072]{2,1,0:T(8,128)} async-done(((f32[2,768,3072]{2,1,0:T(8,128)}), f32[2,24,3072]{2,1,0:T(8,128)}) %reduce-scatter.17.cloned.1.call-update) | async-done | bytes 589840 | tf_op jit(solution)/shard_map/reduce_scatter | solution.py:362
  1167.1 212.0 %reduce-scatter.19.cloned.1.call-done = f32[2,96,768]{2,1,0:T(8,128)} async-done(((f32[2,3072,768]{2,1,0:T(8,128)}), f32[2,96,768]{2,1,0:T(8,128)}) %reduce-scatter.19.cloned.1.call-update) | async-done | bytes 589840 | tf_op jit(solution)/shard_map/reduce_scatter | solution.py:364
  (476 shorter events, 171.2 us)
Async XLA Ops:
  7.2 580.2 %reduce-scatter.21.cloned.1.call-start = ((), (), s32[]{:S(2)}) async-start(), calls=%async_computation.7 | async-start | bytes 1622016
  12.5 9.7 collective-permute-start
  15.1 11.3 collective-permute-start.1
  17.1 70.7 %copy-start.71 = (f32[768]{0:T(1024)}, f32[768]{0:T(1024)S(1)}, u32[]{:S(2)}) copy-start(f32[768]{0:T(1024)S(1)} %get-tuple-element.167) | copy-start | bytes 9220
  17.1 70.7 %copy-start.77 = (f32[768]{0:T(1024)}, f32[768]{0:T(1024)S(1)}, u32[]{:S(2)}) copy-start(f32[768]{0:T(1024)S(1)} %get-tuple-element.97) | copy-start | bytes 9220
  17.1 201.4 %copy-start.79 = (f32[768]{0:T(1024)}, f32[768]{0:T(1024)S(1)}, u32[]{:S(2)}) copy-start(f32[768]{0:T(1024)S(1)} %get-tuple-element.96) | copy-start | bytes 9220
  17.1 361.8 %copy-start.75 = (f32[768]{0:T(1024)}, f32[768]{0:T(1024)S(1)}, u32[]{:S(2)}) copy-start(f32[768]{0:T(1024)S(1)} %get-tuple-element.168) | copy-start | bytes 9220
  54.5 33.3 %copy-start.9 = (f32[3,256,768]{2,1,0:T(8,128)}, f32[3,256,768]{2,1,0:T(8,128)S(1)}, u32[]{:S(2)}) copy-start(f32[3,256,768]{2,1,0:T(8,128)S(1)} %get-tuple-element.137) | copy-start | bytes 7077892
  54.5 33.3 %copy-start.69 = (f32[3,256]{1,0:T(4,128)}, f32[3,256]{1,0:T(4,128)S(1)}, u32[]{:S(2)}) copy-start(f32[3,256]{1,0:T(4,128)S(1)} %broadcast_multiply_fusion.13) | copy-start | bytes 9220
  54.9 32.9 %copy-start.73 = (f32[3,256]{1,0:T(4,128)}, f32[3,256]{1,0:T(4,128)S(1)}, u32[]{:S(2)}) copy-start(f32[3,256]{1,0:T(4,128)S(1)} %add_rsqrt_fusion.3) | copy-start | bytes 9220
  55.2 32.6 %slice-start.7 = ((s8[9437184]{0:T(1024)(128)(4,1)}), s8[4194304]{0:T(1024)(128)(4,1)S(1)}, s32[]{:S(2)}) async-start(s8[9437184]{0:T(1024)(128)(4,1)} %bitcast.312), calls=%async_computation.16 | async-start | bytes 8388608
  55.2 32.6 %slice-start.8 = ((s8[9437184]{0:T(1024)(128)(4,1)}), s8[4194304]{0:T(1024)(128)(4,1)S(1)}, s32[]{:S(2)}) async-start(s8[9437184]{0:T(1024)(128)(4,1)} %bitcast.312), calls=%async_computation.17 | async-start | bytes 8388608
  92.0 91.8 %copy-start.81 = (f32[3,256]{1,0:T(4,128)}, f32[3,256]{1,0:T(4,128)S(1)}, u32[]{:S(2)}) copy-start(f32[3,256]{1,0:T(4,128)S(1)} %broadcast_multiply_fusion.12) | copy-start | bytes 9220
  93.3 57.2 %copy-start.51 = (bf16[3,256,768]{2,1,0:T(8,128)(2,1)}, bf16[3,256,768]{2,1,0:T(8,128)(2,1)S(1)}, u32[]{:S(2)}) copy-start(bf16[3,256,768]{2,1,0:T(8,128)(2,1)S(1)} %fusion.60) | copy-start | bytes 3538948
  96.0 54.6 %copy-start.124 = (f32[768]{0:T(1024)S(1)}, f32[768]{0:T(1024)}, u32[]{:S(2)}) copy-start(f32[768]{0:T(1024)} %get-tuple-element.100) | copy-start | bytes 9220
  96.0 54.6 %copy-start.137 = (bf16[2,768,768]{2,1,0:T(8,128)(2,1)S(1)}, bf16[2,768,768]{2,1,0:T(8,128)(2,1)}, u32[]{:S(2)}) copy-start(bf16[2,768,768]{2,1,0:T(8,128)(2,1)} %param.20) | copy-start | bytes 7077892
  96.0 29.8 %collective-permute-start.2 = (bf16[3,256,768]{2,1,0:T(8,128)(2,1)S(1)}, bf16[3,256,768]{2,1,0:T(8,128)(2,1)S(1)}, u32[]{:S(2)}, u32[]{:S(2)}) collective-permute-start(bf16[3,256,768]{2,1,0:T(8,128)(2,1)S(1)} %add_convert_fusion.6), channel_id=1, source_target_pairs={{0,2},{1,3},{2,0},{3,1},{4,6},{5,7},{6,4},{7,5},{8,10},{9,11},{10,... | collective-permute-start | bytes 3538952 | tf_op jit(solution)/shard_map/ppermute | solution.py:17
  100.1 50.5 %collective-permute-start.4 = (bf16[3,256,768]{2,1,0:T(8,128)(2,1)S(1)}, bf16[3,256,768]{2,1,0:T(8,128)(2,1)}, u32[]{:S(2)}, u32[]{:S(2)}) collective-permute-start(bf16[3,256,768]{2,1,0:T(8,128)(2,1)S(1)} %convolution_convert_fusion.2), channel_id=1, source_target_pairs={{0,2},{1,3},{2,0},{3,1},{4,6},{5,7},{6,4},{7,5},{8,10},{9,11},{10,... | collective-permute-start | bytes 3538952 | tf_op jit(solution)/shard_map/ppermute | solution.py:17
  125.7 25.9 %copy-start.62 = (bf16[3,256,768]{2,1,0:T(8,128)(2,1)}, bf16[3,256,768]{2,1,0:T(8,128)(2,1)S(1)}, u32[]{:S(2)}) copy-start(bf16[3,256,768]{2,1,0:T(8,128)(2,1)S(1)} %collective-permute-done.2) | copy-start | bytes 3538948
  125.7 26.6 %collective-permute-start.3 = (bf16[3,256,768]{2,1,0:T(8,128)(2,1)S(1)}, bf16[3,256,768]{2,1,0:T(8,128)(2,1)}, u32[]{:S(2)}, u32[]{:S(2)}) collective-permute-start(bf16[3,256,768]{2,1,0:T(8,128)(2,1)S(1)} %collective-permute-done.2), channel_id=1, source_target_pairs={{0,1},{1,0},{2,3},{3,2},{4,5},{5,4},{6,7},{7,6},{8,9},{9,8},{10,11... | collective-permute-start | bytes 3538952 | tf_op jit(solution)/shard_map/ppermute | solution.py:17
  150.5 6.1 collective-permute-start.5
  185.5 193.5 %copy-start.4 = (f32[3,256,768]{2,1,0:T(8,128)}, f32[3,256,768]{2,1,0:T(8,128)S(1)}, u32[]{:S(2)}) copy-start(f32[3,256,768]{2,1,0:T(8,128)S(1)} %get-tuple-element.144) | copy-start | bytes 7077892
  185.9 193.1 %copy-start.76 = (f32[3,256]{1,0:T(4,128)}, f32[3,256]{1,0:T(4,128)S(1)}, u32[]{:S(2)}) copy-start(f32[3,256]{1,0:T(4,128)S(1)} %add_rsqrt_fusion.1) | copy-start | bytes 9220
  186.2 32.3 %slice-start.10 = ((s8[9437184]{0:T(1024)(128)(4,1)}), s8[1048576]{0:T(1024)(128)(4,1)S(1)}, s32[]{:S(2)}) async-start(s8[9437184]{0:T(1024)(128)(4,1)} %bitcast.314), calls=%async_computation.19 | async-start | bytes 2097152
  186.2 32.3 %slice-start.11 = ((s8[9437184]{0:T(1024)(128)(4,1)}), s8[4194304]{0:T(1024)(128)(4,1)S(1)}, s32[]{:S(2)}) async-start(s8[9437184]{0:T(1024)(128)(4,1)} %bitcast.314), calls=%async_computation.20 | async-start | bytes 8388608
  286.5 33.9 %collective-permute-start.8 = (bf16[3,256,768]{2,1,0:T(8,128)(2,1)}, bf16[3,256,768]{2,1,0:T(8,128)(2,1)}, u32[]{:S(2)}, u32[]{:S(2)}) collective-permute-start(bf16[3,256,768]{2,1,0:T(8,128)(2,1)} %copy.183), channel_id=1, source_target_pairs={{0,1},{1,0},{2,3},{3,2},{4,5},{5,4},{6,7},{7,6},{8,9},{9,8},{10,11... | collective-permute-start | bytes 3538952 | tf_op jit(solution)/shard_map/ppermute | solution.py:17
  307.6 16.9 %collective-permute-start.6 = (bf16[3,256,768]{2,1,0:T(8,128)(2,1)}, bf16[3,256,768]{2,1,0:T(8,128)(2,1)S(1)}, u32[]{:S(2)}, u32[]{:S(2)}) collective-permute-start(bf16[3,256,768]{2,1,0:T(8,128)(2,1)} %copy.181), channel_id=1, source_target_pairs={{0,1},{1,0},{2,3},{3,2},{4,5},{5,4},{6,7},{7,6},{8,9},{9,8},{10,11... | collective-permute-start | bytes 3538952 | tf_op jit(solution)/shard_map/ppermute | solution.py:17
  322.7 56.2 %collective-permute-start.9 = (bf16[3,256,768]{2,1,0:T(8,128)(2,1)S(1)}, bf16[3,256,768]{2,1,0:T(8,128)(2,1)S(1)}, u32[]{:S(2)}, u32[]{:S(2)}) collective-permute-start(bf16[3,256,768]{2,1,0:T(8,128)(2,1)S(1)} %add_convert_fusion.2), channel_id=1, source_target_pairs={{0,2},{1,3},{2,0},{3,1},{4,6},{5,7},{6,4},{7,5},{8,10},{9,11},{10,... | collective-permute-start | bytes 3538952 | tf_op jit(solution)/shard_map/ppermute | solution.py:17
  324.9 51.6 %collective-permute-start.7 = (bf16[3,256,768]{2,1,0:T(8,128)(2,1)S(1)}, bf16[3,256,768]{2,1,0:T(8,128)(2,1)}, u32[]{:S(2)}, u32[]{:S(2)}) collective-permute-start(bf16[3,256,768]{2,1,0:T(8,128)(2,1)S(1)} %add_convert_fusion.3), channel_id=1, source_target_pairs={{0,2},{1,3},{2,0},{3,1},{4,6},{5,7},{6,4},{7,5},{8,10},{9,11},{10,... | collective-permute-start | bytes 3538952 | tf_op jit(solution)/shard_map/ppermute | solution.py:17
  334.0 42.5 %copy-start.67 = (bf16[2,768,768]{2,1,0:T(8,128)(2,1)S(1)}, bf16[2,768,768]{2,1,0:T(8,128)(2,1)}, u32[]{:S(2)}) copy-start(bf16[2,768,768]{2,1,0:T(8,128)(2,1)} %param.22) | copy-start | bytes 7077892
  334.0 45.0 %copy-start.43 = (bf16[2,768,768]{2,1,0:T(8,128)(2,1)S(1)}, bf16[2,768,768]{2,1,0:T(8,128)(2,1)}, u32[]{:S(2)}) copy-start(bf16[2,768,768]{2,1,0:T(8,128)(2,1)} %param.23) | copy-start | bytes 7077892
  336.5 42.5 %copy-start.8 = (f32[3,256,768]{2,1,0:T(8,128)S(1)}, f32[3,256,768]{2,1,0:T(8,128)}, u32[]{:S(2)}) copy-start(f32[3,256,768]{2,1,0:T(8,128)} %copy-done.6) | copy-start | bytes 7077892
  336.5 42.5 %copy-start.27 = (f32[3,256,768]{2,1,0:T(8,128)S(1)}, f32[3,256,768]{2,1,0:T(8,128)}, u32[]{:S(2)}) copy-start(f32[3,256,768]{2,1,0:T(8,128)} %copy-done.26) | copy-start | bytes 7077892
  336.5 42.5 %copy-start.82 = (f32[3,256]{1,0:T(4,128)S(1)}, f32[3,256]{1,0:T(4,128)}, u32[]{:S(2)}) copy-start(f32[3,256]{1,0:T(4,128)} %copy-done.81) | copy-start | bytes 9220
  336.5 42.5 %copy-start.84 = (f32[768]{0:T(1024)S(1)}, f32[768]{0:T(1024)}, u32[]{:S(2)}) copy-start(f32[768]{0:T(1024)} %get-tuple-element.169) | copy-start | bytes 9220
  336.5 42.5 %copy-start.87 = (f32[3,256]{1,0:T(4,128)S(1)}, f32[3,256]{1,0:T(4,128)}, u32[]{:S(2)}) copy-start(f32[3,256]{1,0:T(4,128)} %copy-done.85) | copy-start | bytes 9220
  336.6 42.5 %copy-start.98 = (f32[3,256]{1,0:T(4,128)S(1)}, f32[3,256]{1,0:T(4,128)}, u32[]{:S(2)}) copy-start(f32[3,256]{1,0:T(4,128)} %copy-done.97) | copy-start | bytes 9220
  431.1 31.6 %slice-start = ((s8[18874368]{0:T(1024)(128)(4,1)}), s8[4194304]{0:T(1024)(128)(4,1)S(1)}, s32[]{:S(2)}) async-start(s8[18874368]{0:T(1024)(128)(4,1)} %bitcast.269), calls=%async_computation.9 | async-start | bytes 8388608
  431.1 31.6 %slice-start.1 = ((s8[18874368]{0:T(1024)(128)(4,1)}), s8[4194304]{0:T(1024)(128)(4,1)S(1)}, s32[]{:S(2)}) async-start(s8[18874368]{0:T(1024)(128)(4,1)} %bitcast.269), calls=%async_computation.10 | async-start | bytes 8388608
  431.1 31.6 %slice-start.2 = ((s8[18874368]{0:T(1024)(128)(4,1)}), s8[4194304]{0:T(1024)(128)(4,1)S(1)}, s32[]{:S(2)}) async-start(s8[18874368]{0:T(1024)(128)(4,1)} %bitcast.269), calls=%async_computation.11 | async-start | bytes 8388608
  473.0 23.7 %collective-permute-start.10 = (bf16[3,256,768]{1,2,0:T(8,128)(2,1)}, bf16[3,256,768]{1,2,0:T(8,128)(2,1)S(1)}, u32[]{:S(2)}, u32[]{:S(2)}) collective-permute-start(bf16[3,256,768]{1,2,0:T(8,128)(2,1)} %slice.313), channel_id=1, source_target_pairs={{0,1},{1,0},{2,3},{3,2},{4,5},{5,4},{6,7},{7,6},{8,9},{9,8},{10,11... | collective-permute-start | bytes 3538952 | tf_op jit(solution)/shard_map/ppermute | solution.py:17
  474.1 18.3 %collective-permute-start.11 = (bf16[3,256,768]{1,2,0:T(8,128)(2,1)}, bf16[3,256,768]{1,2,0:T(8,128)(2,1)}, u32[]{:S(2)}, u32[]{:S(2)}) collective-permute-start(bf16[3,256,768]{1,2,0:T(8,128)(2,1)} %slice.312), channel_id=1, source_target_pairs={{0,1},{1,0},{2,3},{3,2},{4,5},{5,4},{6,7},{7,6},{8,9},{9,8},{10,11... | collective-permute-start | bytes 3538952 | tf_op jit(solution)/shard_map/ppermute | solution.py:17
  488.7 353.3 %all-reduce.15.cloned.1.call-start = ((), (), s32[]{:S(2)}) async-start(), calls=%async_computation.8 | async-start | bytes 28311552
  519.2 435.7 %reduce-scatter.15.cloned.1.call-start = ((), (), s32[]{:S(2)}) async-start(), calls=%async_computation.4 | async-start | bytes 4866048 | tf_op jit(solution)/shard_map/reduce_scatter | solution.py:358
  526.5 640.6 %reduce-scatter.17.cloned.1.call-start = ((), (), s32[]{:S(2)}) async-start(), calls=%async_computation.5 | async-start | bytes 19464192 | tf_op jit(solution)/shard_map/reduce_scatter | solution.py:362
  548.2 830.9 %reduce-scatter.19.cloned.1.call-start = ((), (), s32[]{:S(2)}) async-start(), calls=%async_computation.6 | async-start | bytes 19464192 | tf_op jit(solution)/shard_map/reduce_scatter | solution.py:364
  574.0 70.7 %copy-start.37 = (bf16[3,256,768]{1,2,0:T(8,128)(2,1)S(1)}, bf16[3,256,768]{1,2,0:T(8,128)(2,1)}, u32[]{:S(2)}) copy-start(bf16[3,256,768]{1,2,0:T(8,128)(2,1)} %copy-done.36) | copy-start | bytes 3538948
  574.0 74.0 %copy-start.44 = (bf16[2,768,768]{2,1,0:T(8,128)(2,1)S(1)}, bf16[2,768,768]{2,1,0:T(8,128)(2,1)}, u32[]{:S(2)}) copy-start(bf16[2,768,768]{2,1,0:T(8,128)(2,1)} %param.23) | copy-start | bytes 7077892
  (124 other events, 702.6 us)
Sparse Core Ops, SparseCore 0:
  488.8 98.5 reduce-scatter.20
  593.8 248.1 all-reduce.14
  848.0 106.8 reduce-scatter.14
  962.9 204.1 reduce-scatter.16
  1175.1 203.9 reduce-scatter.18
where the time goes:
time: 1400 us; the launch traced here: 1390 us
  waiting for transfers between devices  820 us (59%)
  matrix products  244 us (17%)
  other arithmetic  146 us (10%)
  local copies, waits for them, and re-layouts  107 us (8%)
  blocking collectives  44.2 us (3%)
  between operations  16 us (1%)
    reduce_scatter x1, waiting for transfers between devices, local(): lax.psum_scatter(paired[9], ('batch', 'seq'), scatter_dimension=1, tiled=...  212 us
    reduce_scatter x1, waiting for transfers between devices, local(): lax.psum_scatter(paired[11], ('batch', 'seq'), scatter_dimension=1, tiled...  212 us
    unnamed x7, waiting for transfers between devices  198 us
    reduce_scatter x1, waiting for transfers between devices, local(): lax.psum_scatter(paired[5], ('batch', 'seq'), scatter_dimension=1, tiled=...  108 us
    ppermute x12, waiting for transfers between devices, swapped_2(): lax.ppermute(value, axis, [(i, i ^ 1 << bit) for i in range(lax.axis_size...  89.9 us
    dot_general x12, matrix products, project_back(): jnp.einsum('ste,de->std', grad_value, weight, preferred_element_type=jnp....  68.1 us
    unnamed x330, local copies, waits for them, and re-layouts  53.7 us
    convert_element_type x2, other arithmetic, layer_forward(): act_low = jax.nn.gelu(pre_act, approximate=False).astype(jnp.bfloat16)  46.4 us
  transfers between devices with their start and end apart: 17, of which 8 were waited for; matrix products, arithmetic and copies ran while one was open for 14% of the time, Pallas kernels for 0%

commit v1 on v0

--- a/solution.py
+++ b/solution.py
@@ -348,25 +348,93 @@
         cotangent.astype(jnp.float32), second_kept, pick(1), True
     )
     grad_in, grads_one = layer_backward(grad_middle, first_kept, pick(0), False)
-    paired = tuple((jnp.stack([grads_one[which], grads_two[which]]) for which in range(15)))
-    summed = (
-        lax.psum_scatter(paired[0], ("batch", "seq"), scatter_dimension=1, tiled=True),
-        lax.psum_scatter(paired[1], ("batch", "seq"), scatter_dimension=1, tiled=True),
-        lax.psum_scatter(paired[2], ("batch", "seq"), scatter_dimension=1, tiled=True),
-        lax.psum_scatter(paired[3], ("batch", "seq"), scatter_dimension=1, tiled=True),
-        lax.psum_scatter(paired[4], ("batch", "seq"), scatter_dimension=1, tiled=True),
-        lax.psum_scatter(paired[5], ("batch", "seq"), scatter_dimension=1, tiled=True),
-        lax.psum_scatter(paired[6], ("batch", "seq"), scatter_dimension=1, tiled=True),
-        lax.psum_scatter(paired[7], ("batch", "seq"), scatter_dimension=1, tiled=True),
-        lax.psum_scatter(paired[8], ("batch", "seq"), scatter_dimension=1, tiled=True),
-        lax.psum_scatter(paired[9], ("batch", "seq"), scatter_dimension=1, tiled=True),
-        lax.psum_scatter(paired[10], ("batch", "seq"), scatter_dimension=1, tiled=True),
-        lax.psum_scatter(paired[11], ("batch", "seq"), scatter_dimension=1, tiled=True),
-        lax.psum_scatter(paired[12], ("batch", "seq"), scatter_dimension=1, tiled=True),
-        lax.psum_scatter(paired[13], ("batch", "seq"), scatter_dimension=1, tiled=True),
-        lax.psum_scatter(paired[14], ("batch", "seq"), scatter_dimension=1, tiled=True),
-    )
-    return (final.astype(jnp.bfloat16), grad_in) + tuple(summed)
+    outs = reduce_grads(grads_one, grads_two)
+    return (final.astype(jnp.bfloat16), grad_in) + outs
+
+
+MATRICES = (0, 2, 3, 5)
+VECTORS = (1, 4, 6, 7, 8, 12, 13, 14, 10)
+
+
+def digit_bits():
+    low = lax.axis_size("seq").bit_length() - 1
+    high = lax.axis_size("batch").bit_length() - 1
+    return [("seq", bit) for bit in range(low)] + [("batch", bit) for bit in range(high)]
+
+
+def digit_orders():
+    digits = digit_bits()
+    core, across, rest = digits[0], digits[1], digits[2:]
+    if len(rest) < 2:
+        return [[core, across] + rest]
+    near, far, late = rest[0], rest[1], rest[2:]
+    return [
+        [core, across, near, far] + late,
+        [core, near, far, across] + late,
+        [core, far, across, near] + late,
+    ]
+
+
+def shard_sum(value, order):
+    digits = digit_bits()
+    left = list(reversed(digits))
+    groups, _, rows, columns = value.shape
+    value = value.reshape((groups,) + (2,) * len(left) + (rows, columns))
+    wide = jnp.float32
+    for step, (axis, bit) in enumerate(order):
+        place = 1 + left.index((axis, bit))
+        left.remove((axis, bit))
+        mine = lax.axis_index(axis) >> bit & 1
+        sent = lax.dynamic_index_in_dim(value, 1 - mine, place, keepdims=False)
+        kept = lax.dynamic_index_in_dim(value, mine, place, keepdims=False)
+        got = swapped_2(sent, axis, bit)
+        value = kept.astype(wide) + got.astype(wide)
+        if step < len(order) - 1:
+            value = value.astype(got.dtype)
+    return value
+
+
+def matrix_sum(value):
+    orders = digit_orders()
+    width = value.shape[-1] // len(orders)
+    parts = [
+        shard_sum(value[..., which * width : (which + 1) * width], order)
+        for which, order in enumerate(orders)
+    ]
+    return jnp.concatenate(parts, axis=-1)
+
+
+def reduce_grads(*layers):
+    devices = lax.axis_size("batch") * lax.axis_size("seq")
+    sums = []
+    for grads in reversed(layers):
+        low = [grad.astype(jnp.bfloat16) for grad in grads]
+        down = matrix_sum(low[11].reshape(1, devices, -1, low[11].shape[1]))[0]
+        up = matrix_sum(low[9].reshape(1, devices, -1, low[9].shape[1]))[0]
+        four = jnp.stack([low[which] for which in MATRICES])
+        four = matrix_sum(four.reshape(4, devices, -1, four.shape[2]))
+        sums.append((down, up, four))
+    sums.reverse()
+    vectors = jnp.concatenate(
+        [grads[which].reshape(devices, -1) for grads in layers for which in VECTORS], axis=1
+    )
+    vectors = jnp.pad(vectors, ((0, 0), (0, -vectors.shape[1] % 1024)))
+    vectors = shard_sum(vectors.reshape(1, devices, 8, -1), digit_orders()[0]).reshape(-1)
+    outs = [None] * 15
+    for place, which in enumerate(MATRICES):
+        outs[which] = jnp.stack([one[2][place] for one in sums])
+    outs[9] = jnp.stack([one[1] for one in sums])
+    outs[11] = jnp.stack([one[0] for one in sums])
+    start = 0
+    pieces = {}
+    for depth, grads in enumerate(layers):
+        for which in VECTORS:
+            width = grads[which].shape[0] // devices
+            pieces[depth, which] = vectors[start : start + width]
+            start += width
+    for which in VECTORS:
+        outs[which] = jnp.stack([pieces[depth, which] for depth in range(len(layers))])
+    return tuple(outs)
 
 
 def solution(mesh):

time: 1400 us -> 841 us (0.60)
  waiting for transfers between devices: 820 us -> 194 us
  starting transfers between devices: 7.87 us -> 93.7 us
  blocking collectives: 44.2 us -> 0 us
  local copies, waits for them, and re-layouts: 107 us -> 135 us
    reduce_scatter x3 -> x0, waiting for transfers between devices: 532 us -> none  [the longest x1 212 us: local(): lax.psum_scatter(paired[9], ('batch', 'seq'), scatter_dimension=1, tiled=...]
    unnamed x7 -> x0, waiting for transfers between devices: 198 us -> none
    ppermute x12 -> x107, waiting for transfers between devices: 89.9 us -> 194 us  [swapped_2(): lax.ppermute(value, axis, [(i, i ^ 1 << bit) for i in range(lax.axis_size...]
    ppermute x12 -> x107, starting transfers between devices: 7.28 us -> 93.7 us  [swapped_2(): lax.ppermute(value, axis, [(i, i ^ 1 << bit) for i in range(lax.axis_size...]
    unnamed x1 -> x0, blocking collectives: 44.2 us -> none
    dynamic_slice x0 -> x30, local copies, waits for them, and re-layouts: none -> 30.6 us  [the longest x15 16.1 us: shard_sum(): sent = lax.dynamic_index_in_dim(value, 1 - mine, place, keepdims=False)]
    another operation x19 -> x2, local copies, waits for them, and re-layouts: 25.5 us -> 0.15 us  [reduce_grads(): jnp.stack([pieces[depth, which] for depth in range(len(layers))])]
    convert_element_type x0 -> x72, other arithmetic: none -> 24.7 us  [shard_sum(): value = value.astype(got.dtype)]
  transfers between devices with their start and end apart: 17 -> 107, of which waited for: 8 -> 56; matrix products, arithmetic and copies ran while one was open for 14% -> 22% of each run, Pallas kernels for 0% -> 0%
where the time goes in v1:
time: 841 us; the launch traced here: 831 us
  matrix products  244 us (29%)
  waiting for transfers between devices  194 us (23%)
  other arithmetic  159 us (19%)
  local copies, waits for them, and re-layouts  135 us (16%)
  starting transfers between devices  93.7 us (11%)
    ppermute x107, waiting for transfers between devices, swapped_2(): lax.ppermute(value, axis, [(i, i ^ 1 << bit) for i in range(lax.axis_size...  194 us
    ppermute x107, starting transfers between devices, swapped_2(): lax.ppermute(value, axis, [(i, i ^ 1 << bit) for i in range(lax.axis_size...  93.7 us
    dot_general x12, matrix products, project_back(): jnp.einsum('ste,de->std', grad_value, weight, preferred_element_type=jnp....  63.8 us
    dot_general x12, matrix products, project(): jnp.einsum('std,de->ste', value, weight, preferred_element_type=jnp.float32)  46.5 us
    convert_element_type x2, other arithmetic, layer_forward(): act_low = jax.nn.gelu(pre_act, approximate=False).astype(jnp.bfloat16)  46.1 us
    dot_general x12, matrix products, weight_grad(): jnp.einsum('std,ste->de', value, grad_value, preferred_element_type=jnp.f...  40.5 us
    unnamed x402, local copies, waits for them, and re-layouts  37.1 us
    dot_general x2, matrix products, layer_backward(): jnp.einsum('sqhd,skhd->shqk', split_heads(grad_context), split_heads(all_...  32.6 us
  transfers between devices with their start and end apart: 107, of which 56 were waited for; matrix products, arithmetic and copies ran while one was open for 22% of the time, Pallas kernels for 0%

profile of v1, /device:TPU:0, one launch (start us, length us, event | category | flops | bytes accessed | tf_op | source)
XLA Modules:
  0.0 831.0 jit_solution(17875497564307845156)
XLA Ops:
  25.5 4.0 pad_maximum_fusion.2
  29.6 4.3 copy.75
  37.2 4.2 fusion
  44.3 9.3 %fusion.89 = bf16[3,12,64,256]{3,2,1,0:T(8,128)(2,1)S(1)} fusion(bf16[3,512,12,64]{1,3,2,0:T(8,128)(2,1)S(1)} %bitcast.857, f32[3,12,256,512]{3,2,1,0:T(8,128)} %copy-done, f32[3,12,256]{2,1,0:T(8,128)S(1)} %fusion, f32[3,12,256]{2,1,0:T(8,128)S(1)} %get-tuple-element.146), kind=kOutput, calls=%fused_computation.211 | convolution fusion | flops 618725376 | bytes 22487040 | tf_op jit(solution)/shard_map/shqk,skhd->sqhd/dot_general | solution.py:131
  55.8 9.1 %fusion.55 = (u8[256,3072]{1,0:T(8,128)(4,1)S(1)}, u8[256,3072]{1,0:T(8,128)(4,1)S(1)}, f32[3,256,3072]{2,1,0:T(8,128)S(1)}) fusion(f32[3072]{0:T(1024)S(1)} %bitcast.914, bf16[2,768,3072]{2,1,0:T(8,128)(2,1)} %param.29, f32[3,256,768]{2,1,0:T(8,128)S(1)} %get-tuple-element.149, f32[768]{0:T(1024)S(1)} %copy-done.151, f32[768]{0:T(1024)S(1)} %get-tuple-element.177, ...), kind=kOutput, calls=%fused_computation.160 | convolution fusion | flops 3658285056 | bytes 18112512 | tf_op jit(solution)/shard_map/std,de->ste/dot_general | solution.py:39
  64.8 23.1 %multiply_convert_fusion.3 = (bf16[3,256,3072]{2,1,0:T(8,128)(2,1)S(1)}, f32[3,256,3072]{2,1,0:T(8,128)}) fusion(f32[3,256,3072]{2,1,0:T(8,128)S(1)} %get-tuple-element.150, f32[3072]{0:T(1024)S(1)} %bitcast.915, u8[256,3072]{1,0:T(8,128)(4,1)S(1)} %get-tuple-element.20, u8[256,3072]{1,0:T(8,128)(4,1)S(1)} %get-tuple-element.19), kind=kLoop, calls=%fused_computation.54 | loop fusion | flops 167510016 | bytes 25178112 | tf_op jit(solution)/shard_map/convert_element_type | solution.py:142
  88.0 8.1 fusion.223
  104.8 24.8 %collective-permute-done.4 = bf16[3,256,768]{2,1,0:T(8,128)(2,1)} collective-permute-done((bf16[3,256,768]{2,1,0:T(8,128)(2,1)S(1)}, bf16[3,256,768]{2,1,0:T(8,128)(2,1)}, u32[]{:S(2)}, u32[]{:S(2)}) %collective-permute-start.4) | collective-permute-done | bytes 1179680 | tf_op jit(solution)/shard_map/ppermute | solution.py:17
  129.6 24.7 %collective-permute-done.2 = bf16[3,256,768]{2,1,0:T(8,128)(2,1)} collective-permute-done((bf16[3,256,768]{2,1,0:T(8,128)(2,1)S(1)}, bf16[3,256,768]{2,1,0:T(8,128)(2,1)}, u32[]{:S(2)}, u32[]{:S(2)}) %collective-permute-start.2) | collective-permute-done | bytes 1179680 | tf_op jit(solution)/shard_map/ppermute | solution.py:17
  154.3 3.4 add_convert_fusion.7
  163.9 4.3 copy.81
  171.3 4.3 copy.79
  175.7 4.7 fusion.224
  180.4 4.2 fusion.1
  188.1 9.4 %fusion.88 = bf16[3,12,64,256]{3,2,1,0:T(8,128)(2,1)S(1)} fusion(bf16[3,512,12,64]{1,3,2,0:T(8,128)(2,1)S(1)} %bitcast.859, f32[3,12,256,512]{3,2,1,0:T(8,128)} %copy-done.1, f32[3,12,256]{2,1,0:T(8,128)S(1)} %fusion.1, f32[3,12,256]{2,1,0:T(8,128)S(1)} %get-tuple-element.153), kind=kOutput, calls=%fused_computation.210 | convolution fusion | flops 618725376 | bytes 22487040 | tf_op jit(solution)/shard_map/shqk,skhd->sqhd/dot_general | solution.py:131
  200.0 9.1 %fusion.56 = (u8[256,3072]{1,0:T(8,128)(4,1)S(1)}, u8[256,3072]{1,0:T(8,128)(4,1)S(1)}, f32[3,256,3072]{2,1,0:T(8,128)S(1)}) fusion(f32[3072]{0:T(1024)S(1)} %bitcast.917, bf16[2,768,3072]{2,1,0:T(8,128)(2,1)} %param.29, f32[3,256,768]{2,1,0:T(8,128)S(1)} %get-tuple-element.156, f32[768]{0:T(1024)S(1)} %copy-done.153, f32[768]{0:T(1024)S(1)} %get-tuple-element.178, ...), kind=kOutput, calls=%fused_computation.161 | convolution fusion | flops 3658285056 | bytes 18112512 | tf_op jit(solution)/shard_map/std,de->ste/dot_general | solution.py:39
  209.2 23.0 %multiply_convert_fusion.2 = (bf16[3,256,3072]{2,1,0:T(8,128)(2,1)S(1)}, f32[3,256,3072]{2,1,0:T(8,128)}) fusion(f32[3,256,3072]{2,1,0:T(8,128)S(1)} %get-tuple-element.157, f32[3072]{0:T(1024)S(1)} %bitcast.918, u8[256,3072]{1,0:T(8,128)(4,1)S(1)} %get-tuple-element.18, u8[256,3072]{1,0:T(8,128)(4,1)S(1)} %get-tuple-element.17), kind=kLoop, calls=%fused_computation.41 | loop fusion | flops 167510016 | bytes 25178112 | tf_op jit(solution)/shard_map/convert_element_type | solution.py:142
  232.2 4.1 fusion.226
  241.9 5.9 bitcast_convert_fusion
  247.7 12.7 %convert_reduce_fusion = (f32[3072]{0:T(1024)}, bf16[3,256,3072]{2,1,0:T(8,128)(2,1)}) fusion(f32[3,256,3072]{2,1,0:T(8,128)} %get-tuple-element.64, bf16[3,256,768]{2,1,0:T(8,128)(2,1)S(1)} %get-tuple-element.54, bf16[2,3072,768]{2,1,0:T(8,128)(2,1)} %param.31, f32[3,256,3072]{2,1,0:T(8,128)S(1)} %get-tuple-element.157, f32[3072]{0:T(1024)S(1)} %bitcast.919), kind=kOutput, calls=%fused_computation.35 | convolution fusion | flops 3663983616 | bytes 29515776 | tf_op jit(solution)/shard_map/ste,de->std/dot_general | solution.py:43
  260.4 9.3 %multiply_reduce_fusion.2 = (f32[768]{0:T(1024)}, f32[3,256]{1,0:T(4,128)S(1)}, f32[3,256]{1,0:T(4,128)S(1)}, f32[768]{0:T(1024)}, f32[3,256,768]{2,1,0:T(8,128)S(1)}) fusion(f32[3,256,768]{2,1,0:T(8,128)S(1)} %get-tuple-element.156, f32[3,256]{1,0:T(4,128)S(1)} %add_rsqrt_fusion.1, f32[3,256]{1,0:T(4,128)S(1)} %broadcast_multiply_fusion.11, ...), kind=kOutput, calls=%fused_computation.116 | convolution fusion | flops 3634492416 | bytes 17731584 | tf_op jit(solution)/shard_map/ste,de->std/dot_general | solution.py:43
  269.8 6.5 bitcast_convert_fusion.2
  280.6 9.8 %fusion.8 = f32[3,12,64,512]{3,2,1,0:T(8,128)} fusion(bf16[3,256,12,64]{1,3,2,0:T(8,128)(2,1)S(1)} %bitcast.853, f32[3,12,256,512]{3,2,1,0:T(8,128)} %copy-done.1, f32[3,12,256]{2,1,0:T(8,128)} %log_add_fusion.1), kind=kOutput, calls=%fused_computation.21 | convolution fusion | flops 613416960 | bytes 24809472 | tf_op jit(solution)/shard_map/shqk,sqhd->skhd/dot_general | solution.py:251
  290.4 16.3 %multiply_reduce_fusion.1 = (f32[3,12,256]{2,1,0:T(8,128)S(1)}, f32[3,12,256,512]{3,2,1,0:T(8,128)}) fusion(f32[3,12,256,512]{3,2,1,0:T(8,128)} %copy-done.1, f32[3,12,256]{2,1,0:T(8,128)S(1)} %copy-done.90, bf16[3,256,12,64]{1,3,2,0:T(8,128)(2,1)S(1)} %bitcast.854, bf16[3,512,12,64]{1,3,2,0:T(8,128)(2,1)S(1)} %bitcast.860), kind=kOutput, calls=%fused_computation.4 | convolution fusion | flops 618126336 | bytes 41361408 | tf_op jit(solution)/shard_map/sqhd,skhd->shqk/dot_general | solution.py:219
  306.7 13.5 %multiply_convert_fusion.1 = bf16[3,12,256,512]{3,2,1,0:T(8,128)(2,1)S(1)} fusion(f32[3,12,256,512]{3,2,1,0:T(8,128)} %get-tuple-element.162, f32[3,12,256,512]{3,2,1,0:T(8,128)} %copy-done.1, f32[3,12,256]{2,1,0:T(8,128)S(1)} %get-tuple-element.161, f32[3,12,256]{2,1,0:T(8,128)S(1)} %copy-done.90), kind=kLoop, calls=%fused_computation.3 | loop fusion | flops 18874368 | bytes 47259648 | tf_op jit(solution)/shard_map/convert_element_type | solution.py:226
  320.1 4.6 convert_reduce_fusion.6
  324.8 3.9 broadcast_multiply_fusion.1
  330.1 3.9 fusion.214
  389.2 4.6 collective-permute-done.103
  413.7 4.0 collective-permute-done.98
  436.3 36.9 %collective-permute-done.70 = bf16[1,2,24,1024]{3,2,1,0:T(8,128)(2,1)S(1)} collective-permute-done((bf16[1,2,24,1024]{3,2,1,0:T(8,128)(2,1)S(1)}, bf16[1,2,24,1024]{3,2,1,0:T(8,128)(2,1)S(1)}, u32[]{:S(2)}, u32[]{:S(2)}) %collective-permute-start.70) | collective-permute-done | bytes 98336 | tf_op jit(solution)/shard_map/ppermute | solution.py:17
  494.8 5.9 bitcast_convert_fusion.1
  500.7 12.5 %convert_reduce_fusion.1 = (f32[3072]{0:T(1024)}, bf16[3,256,3072]{2,1,0:T(8,128)(2,1)}) fusion(f32[3,256,3072]{2,1,0:T(8,128)} %get-tuple-element.66, bf16[3,256,768]{2,1,0:T(8,128)(2,1)S(1)} %get-tuple-element.58, bf16[2,3072,768]{2,1,0:T(8,128)(2,1)} %param.31, f32[3,256,3072]{2,1,0:T(8,128)S(1)} %bitcast.862, f32[3072]{0:T(1024)S(1)} %bitcast.916), kind=kOutput, calls=%fused_computation.36 | convolution fusion | flops 3663983616 | bytes 29515776 | tf_op jit(solution)/shard_map/ste,de->std/dot_general | solution.py:43
  513.2 9.3 %multiply_reduce_fusion.4 = (f32[768]{0:T(1024)}, f32[3,256]{1,0:T(4,128)S(1)}, f32[3,256]{1,0:T(4,128)S(1)}, f32[768]{0:T(1024)}, f32[3,256,768]{2,1,0:T(8,128)S(1)}) fusion(f32[3,256,768]{2,1,0:T(8,128)S(1)} %copy-done.10, f32[3,256]{1,0:T(4,128)S(1)} %copy-done.125, f32[3,256]{1,0:T(4,128)S(1)} %copy-done.113, f32[768]{0:T(1024)S(1)} %copy-done.121, ...), kind=kOutput, calls=%fused_computation.122 | convolution fusion | flops 3633902592 | bytes 18911232 | tf_op jit(solution)/shard_map/ste,de->std/dot_general | solution.py:43
  522.6 6.3 bitcast_convert_fusion.3
  536.3 9.7 %fusion.6 = f32[3,12,64,512]{3,2,1,0:T(8,128)} fusion(bf16[3,256,12,64]{1,3,2,0:T(8,128)(2,1)S(1)} %bitcast.855, f32[3,12,256,512]{3,2,1,0:T(8,128)} %copy-done, f32[3,12,256]{2,1,0:T(8,128)} %log_add_fusion), kind=kOutput, calls=%fused_computation.20 | convolution fusion | flops 613416960 | bytes 24809472 | tf_op jit(solution)/shard_map/shqk,sqhd->skhd/dot_general | solution.py:251
  546.0 16.3 %multiply_reduce_fusion = (f32[3,12,256]{2,1,0:T(8,128)S(1)}, f32[3,12,256,512]{3,2,1,0:T(8,128)}) fusion(f32[3,12,256,512]{3,2,1,0:T(8,128)} %copy-done, f32[3,12,256]{2,1,0:T(8,128)S(1)} %copy-done.89, bf16[3,256,12,64]{1,3,2,0:T(8,128)(2,1)S(1)} %bitcast.856, bf16[3,512,12,64]{1,3,2,0:T(8,128)(2,1)S(1)} %bitcast.858), kind=kOutput, calls=%fused_computation.1 | convolution fusion | flops 618126336 | bytes 41361408 | tf_op jit(solution)/shard_map/sqhd,skhd->shqk/dot_general | solution.py:219
  562.3 13.1 %multiply_convert_fusion = bf16[3,12,256,512]{3,2,1,0:T(8,128)(2,1)S(1)} fusion(f32[3,12,256,512]{3,2,1,0:T(8,128)} %get-tuple-element.166, f32[3,12,256,512]{3,2,1,0:T(8,128)} %copy-done, f32[3,12,256]{2,1,0:T(8,128)S(1)} %get-tuple-element.165, f32[3,12,256]{2,1,0:T(8,128)S(1)} %copy-done.89), kind=kLoop, calls=%fused_computation | loop fusion | flops 18874368 | bytes 47259648 | tf_op jit(solution)/shard_map/convert_element_type | solution.py:226
  575.4 4.0 convert_reduce_fusion.10
  635.8 4.3 fusion.108
  699.8 4.0 collective-permute-done.58
  706.1 3.7 collective-permute-done.43
  718.1 3.7 collective-permute-done.46
  730.9 3.6 collective-permute-done.84
  734.9 3.6 collective-permute-done.34
  741.0 4.2 collective-permute-done.89
  747.3 3.5 collective-permute-done.49
  803.6 5.2 collective-permute-done.18
  (948 shorter events, 403.7 us)
Async XLA Ops:
  3.6 16.3 %collective-permute-start.1 = (bf16[3,256,768]{2,1,0:T(8,128)(2,1)S(1)}, bf16[3,256,768]{2,1,0:T(8,128)(2,1)}, u32[]{:S(2)}, u32[]{:S(2)}) collective-permute-start(bf16[3,256,768]{2,1,0:T(8,128)(2,1)S(1)} %convolution_convert_fusion.3), channel_id=1, source_target_pairs={{0,1},{1,0},{2,3},{3,2},{4,5},{5,4},{6,7},{7,6},{8,9},{9,8},{10,11... | collective-permute-start | bytes 3538952 | tf_op jit(solution)/shard_map/ppermute | solution.py:17
  6.8 18.7 %collective-permute-start = (bf16[3,256,768]{2,1,0:T(8,128)(2,1)}, bf16[3,256,768]{2,1,0:T(8,128)(2,1)}, u32[]{:S(2)}, u32[]{:S(2)}) collective-permute-start(bf16[3,256,768]{2,1,0:T(8,128)(2,1)} %add_convert_fusion.10), channel_id=1, source_target_pairs={{0,1},{1,0},{2,3},{3,2},{4,5},{5,4},{6,7},{7,6},{8,9},{9,8},{10,11... | collective-permute-start | bytes 3538952 | tf_op jit(solution)/shard_map/ppermute | solution.py:17
  99.7 29.9 %collective-permute-start.4 = (bf16[3,256,768]{2,1,0:T(8,128)(2,1)S(1)}, bf16[3,256,768]{2,1,0:T(8,128)(2,1)}, u32[]{:S(2)}, u32[]{:S(2)}) collective-permute-start(bf16[3,256,768]{2,1,0:T(8,128)(2,1)S(1)} %convolution_convert_fusion.2), channel_id=1, source_target_pairs={{0,2},{1,3},{2,0},{3,1},{4,6},{5,7},{6,4},{7,5},{8,10},{9,11},{10,... | collective-permute-start | bytes 3538952 | tf_op jit(solution)/shard_map/ppermute | solution.py:17
  103.8 50.4 %collective-permute-start.2 = (bf16[3,256,768]{2,1,0:T(8,128)(2,1)S(1)}, bf16[3,256,768]{2,1,0:T(8,128)(2,1)}, u32[]{:S(2)}, u32[]{:S(2)}) collective-permute-start(bf16[3,256,768]{2,1,0:T(8,128)(2,1)S(1)} %add_convert_fusion.8), channel_id=1, source_target_pairs={{0,2},{1,3},{2,0},{3,1},{4,6},{5,7},{6,4},{7,5},{8,10},{9,11},{10,... | collective-permute-start | bytes 3538952 | tf_op jit(solution)/shard_map/ppermute | solution.py:17
  129.6 31.1 %collective-permute-start.5 = (bf16[3,256,768]{2,1,0:T(8,128)(2,1)}, bf16[3,256,768]{2,1,0:T(8,128)(2,1)}, u32[]{:S(2)}, u32[]{:S(2)}) collective-permute-start(bf16[3,256,768]{2,1,0:T(8,128)(2,1)} %collective-permute-done.4), channel_id=1, source_target_pairs={{0,1},{1,0},{2,3},{3,2},{4,5},{5,4},{6,7},{7,6},{8,9},{9,8},{10,11... | collective-permute-start | bytes 3538952 | tf_op jit(solution)/shard_map/ppermute | solution.py:17
  154.3 13.9 %collective-permute-start.3 = (bf16[3,256,768]{2,1,0:T(8,128)(2,1)}, bf16[3,256,768]{2,1,0:T(8,128)(2,1)}, u32[]{:S(2)}, u32[]{:S(2)}) collective-permute-start(bf16[3,256,768]{2,1,0:T(8,128)(2,1)} %collective-permute-done.2), channel_id=1, source_target_pairs={{0,1},{1,0},{2,3},{3,2},{4,5},{5,4},{6,7},{7,6},{8,9},{9,8},{10,11... | collective-permute-start | bytes 3538952 | tf_op jit(solution)/shard_map/ppermute | solution.py:17
  340.6 35.6 %collective-permute-start.102 = (bf16[1,2,2,2,2,96,256]{6,5,1,3,4,2,0:T(8,128)(2,1)}, bf16[1,2,2,2,2,96,256]{6,5,1,3,4,2,0:T(8,128)(2,1)}, u32[]{:S(2)}, u32[]{:S(2)}) collective-permute-start(bf16[1,2,2,2,2,96,256]{6,5,1,3,4,2,0:T(8,128)(2,1)} %bitcast.816), channel_id=1, source_target_pairs={{0,1},{1,0},{2,3},{3,2},{4,5},{5,4},{6,7},{7,6},{8,9},{9,8},{10,11... | collective-permute-start | bytes 2359304 | tf_op jit(solution)/shard_map/ppermute | solution.py:17
  341.1 37.0 %collective-permute-start.92 = (bf16[1,2,2,2,2,96,256]{6,5,1,2,3,4,0:T(8,128)(2,1)}, bf16[1,2,2,2,2,96,256]{6,5,1,2,3,4,0:T(8,128)(2,1)}, u32[]{:S(2)}, u32[]{:S(2)}) collective-permute-start(bf16[1,2,2,2,2,96,256]{6,5,1,2,3,4,0:T(8,128)(2,1)} %bitcast.818), channel_id=1, source_target_pairs={{0,1},{1,0},{2,3},{3,2},{4,5},{5,4},{6,7},{7,6},{8,9},{9,8},{10,11... | collective-permute-start | bytes 2359304 | tf_op jit(solution)/shard_map/ppermute | solution.py:17
  350.2 29.9 %collective-permute-start.72 = (bf16[1,2,2,2,2,24,1024]{6,5,1,3,4,2,0:T(8,128)(2,1)}, bf16[1,2,2,2,2,24,1024]{6,5,1,3,4,2,0:T(8,128)(2,1)}, u32[]{:S(2)}, u32[]{:S(2)}) collective-permute-start(bf16[1,2,2,2,2,24,1024]{6,5,1,3,4,2,0:T(8,128)(2,1)} %bitcast.821), channel_id=1, source_target_pairs={{0,1},{1,0},{2,3},{3,2},{4,5},{5,4},{6,7},{7,6},{8,9},{9,8},{10,11... | collective-permute-start | bytes 2359304 | tf_op jit(solution)/shard_map/ppermute | solution.py:17
  350.7 31.1 %collective-permute-start.62 = (bf16[1,2,2,2,2,24,1024]{6,5,1,2,3,4,0:T(8,128)(2,1)}, bf16[1,2,2,2,2,24,1024]{6,5,1,2,3,4,0:T(8,128)(2,1)}, u32[]{:S(2)}, u32[]{:S(2)}) collective-permute-start(bf16[1,2,2,2,2,24,1024]{6,5,1,2,3,4,0:T(8,128)(2,1)} %bitcast.823), channel_id=1, source_target_pairs={{0,1},{1,0},{2,3},{3,2},{4,5},{5,4},{6,7},{7,6},{8,9},{9,8},{10,11... | collective-permute-start | bytes 2359304 | tf_op jit(solution)/shard_map/ppermute | solution.py:17
  352.7 32.6 %collective-permute-start.67 = (bf16[1,2,2,2,2,24,1024]{6,5,1,4,2,3,0:T(8,128)(2,1)}, bf16[1,2,2,2,2,24,1024]{6,5,1,4,2,3,0:T(8,128)(2,1)}, u32[]{:S(2)}, u32[]{:S(2)}) collective-permute-start(bf16[1,2,2,2,2,24,1024]{6,5,1,4,2,3,0:T(8,128)(2,1)} %bitcast.822), channel_id=1, source_target_pairs={{0,1},{1,0},{2,3},{3,2},{4,5},{5,4},{6,7},{7,6},{8,9},{9,8},{10,11... | collective-permute-start | bytes 2359304 | tf_op jit(solution)/shard_map/ppermute | solution.py:17
  376.2 12.1 %collective-permute-start.97 = (bf16[1,2,2,2,2,96,256]{6,5,1,4,2,3,0:T(8,128)(2,1)}, bf16[1,2,2,2,2,96,256]{6,5,1,4,2,3,0:T(8,128)(2,1)S(1)}, u32[]{:S(2)}, u32[]{:S(2)}) collective-permute-start(bf16[1,2,2,2,2,96,256]{6,5,1,4,2,3,0:T(8,128)(2,1)} %bitcast.911), channel_id=1, source_target_pairs={{0,1},{1,0},{2,3},{3,2},{4,5},{5,4},{6,7},{7,6},{8,9},{9,8},{10,11... | collective-permute-start | bytes 2359304 | tf_op jit(solution)/shard_map/ppermute | solution.py:17
  378.1 32.7 %collective-permute-start.8 = (bf16[3,256,768]{2,1,0:T(8,128)(2,1)S(1)}, bf16[3,256,768]{2,1,0:T(8,128)(2,1)S(1)}, u32[]{:S(2)}, u32[]{:S(2)}) collective-permute-start(bf16[3,256,768]{2,1,0:T(8,128)(2,1)S(1)} %copy-done.81), channel_id=1, source_target_pairs={{0,1},{1,0},{2,3},{3,2},{4,5},{5,4},{6,7},{7,6},{8,9},{9,8},{10,11... | collective-permute-start | bytes 3538952 | tf_op jit(solution)/shard_map/ppermute | solution.py:17
  380.1 32.7 %collective-permute-start.6 = (bf16[3,256,768]{2,1,0:T(8,128)(2,1)S(1)}, bf16[3,256,768]{2,1,0:T(8,128)(2,1)S(1)}, u32[]{:S(2)}, u32[]{:S(2)}) collective-permute-start(bf16[3,256,768]{2,1,0:T(8,128)(2,1)S(1)} %copy-done.80), channel_id=1, source_target_pairs={{0,1},{1,0},{2,3},{3,2},{4,5},{5,4},{6,7},{7,6},{8,9},{9,8},{10,11... | collective-permute-start | bytes 3538952 | tf_op jit(solution)/shard_map/ppermute | solution.py:17
  381.8 12.0 %collective-permute-start.103 = (bf16[1,2,2,2,96,256]{5,4,1,2,3,0:T(8,128)(2,1)S(1)}, bf16[1,2,2,2,96,256]{5,4,1,2,3,0:T(8,128)(2,1)S(1)}, u32[]{:S(2)}, u32[]{:S(2)}) collective-permute-start(bf16[1,2,2,2,96,256]{5,4,1,2,3,0:T(8,128)(2,1)S(1)} %dynamic-slice_bitcast_fusion.3), channel_id=1, source_target_pairs={{0,8},{4,12},{8,0},{12,4},{16,24},{20,28},{24,16},{28,20},{1,9},{5... | collective-permute-start | bytes 1179656 | tf_op jit(solution)/shard_map/ppermute | solution.py:17
  385.3 11.9 %collective-permute-start.93 = (bf16[1,2,2,2,96,256]{5,4,1,2,3,0:T(8,128)(2,1)S(1)}, bf16[1,2,2,2,96,256]{5,4,1,2,3,0:T(8,128)(2,1)S(1)}, u32[]{:S(2)}, u32[]{:S(2)}) collective-permute-start(bf16[1,2,2,2,96,256]{5,4,1,2,3,0:T(8,128)(2,1)S(1)} %dynamic-slice_bitcast_fusion.5), channel_id=1, source_target_pairs={{0,2},{1,3},{2,0},{3,1},{4,6},{5,7},{6,4},{7,5},{8,10},{9,11},{10,... | collective-permute-start | bytes 1179656 | tf_op jit(solution)/shard_map/ppermute | solution.py:17
  388.3 13.5 %collective-permute-start.73 = (bf16[1,2,2,2,24,1024]{5,4,1,2,3,0:T(8,128)(2,1)S(1)}, bf16[1,2,2,2,24,1024]{5,4,1,2,3,0:T(8,128)(2,1)S(1)}, u32[]{:S(2)}, u32[]{:S(2)}) collective-permute-start(bf16[1,2,2,2,24,1024]{5,4,1,2,3,0:T(8,128)(2,1)S(1)} %dynamic-slice_bitcast_fusion.9), channel_id=1, source_target_pairs={{0,8},{4,12},{8,0},{12,4},{16,24},{20,28},{24,16},{28,20},{1,9},{5... | collective-permute-start | bytes 1179656 | tf_op jit(solution)/shard_map/ppermute | solution.py:17
  397.2 12.1 %collective-permute-start.68 = (bf16[1,2,2,2,24,1024]{5,4,1,3,2,0:T(8,128)(2,1)S(1)}, bf16[1,2,2,2,24,1024]{5,4,1,3,2,0:T(8,128)(2,1)S(1)}, u32[]{:S(2)}, u32[]{:S(2)}) collective-permute-start(bf16[1,2,2,2,24,1024]{5,4,1,3,2,0:T(8,128)(2,1)S(1)} %dynamic-slice_bitcast_fusion.10), channel_id=1, source_target_pairs={{0,4},{4,0},{8,12},{12,8},{16,20},{20,16},{24,28},{28,24},{1,5},{5... | collective-permute-start | bytes 1179656 | tf_op jit(solution)/shard_map/ppermute | solution.py:17
  401.8 15.9 %collective-permute-start.98 = (bf16[1,2,2,2,96,256]{5,4,1,3,2,0:T(8,128)(2,1)S(1)}, bf16[1,2,2,2,96,256]{5,4,1,3,2,0:T(8,128)(2,1)S(1)}, u32[]{:S(2)}, u32[]{:S(2)}) collective-permute-start(bf16[1,2,2,2,96,256]{5,4,1,3,2,0:T(8,128)(2,1)S(1)} %dynamic-slice_bitcast_fusion.4), channel_id=1, source_target_pairs={{0,4},{4,0},{8,12},{12,8},{16,20},{20,16},{24,28},{28,24},{1,5},{5... | collective-permute-start | bytes 1179656 | tf_op jit(solution)/shard_map/ppermute | solution.py:17
  404.9 13.0 %collective-permute-start.104 = (bf16[1,2,2,96,256]{4,3,1,2,0:T(8,128)(2,1)S(1)}, bf16[1,2,2,96,256]{4,3,1,2,0:T(8,128)(2,1)S(1)}, u32[]{:S(2)}, u32[]{:S(2)}) collective-permute-start(bf16[1,2,2,96,256]{4,3,1,2,0:T(8,128)(2,1)S(1)} %dynamic-slice_bitcast_fusion.21), channel_id=1, source_target_pairs={{0,2},{1,3},{2,0},{3,1},{4,6},{5,7},{6,4},{7,5},{8,10},{9,11},{10,... | collective-permute-start | bytes 589832 | tf_op jit(solution)/shard_map/ppermute | solution.py:17
  409.3 12.2 %collective-permute-start.94 = (bf16[1,2,2,96,256]{4,3,1,2,0:T(8,128)(2,1)S(1)}, bf16[1,2,2,96,256]{4,3,1,2,0:T(8,128)(2,1)S(1)}, u32[]{:S(2)}, u32[]{:S(2)}) collective-permute-start(bf16[1,2,2,96,256]{4,3,1,2,0:T(8,128)(2,1)S(1)} %dynamic-slice_bitcast_fusion.23), channel_id=1, source_target_pairs={{0,4},{4,0},{8,12},{12,8},{16,20},{20,16},{24,28},{28,24},{1,5},{5... | collective-permute-start | bytes 589832 | tf_op jit(solution)/shard_map/ppermute | solution.py:17
  410.9 12.2 %collective-permute-start.74 = (bf16[1,2,2,24,1024]{4,3,1,2,0:T(8,128)(2,1)S(1)}, bf16[1,2,2,24,1024]{4,3,1,2,0:T(8,128)(2,1)S(1)}, u32[]{:S(2)}, u32[]{:S(2)}) collective-permute-start(bf16[1,2,2,24,1024]{4,3,1,2,0:T(8,128)(2,1)S(1)} %dynamic-slice_bitcast_fusion.27), channel_id=1, source_target_pairs={{0,2},{1,3},{2,0},{3,1},{4,6},{5,7},{6,4},{7,5},{8,10},{9,11},{10,... | collective-permute-start | bytes 589832 | tf_op jit(solution)/shard_map/ppermute | solution.py:17
  421.5 67.0 %collective-permute-start.9 = (bf16[3,256,768]{2,1,0:T(8,128)(2,1)S(1)}, bf16[3,256,768]{2,1,0:T(8,128)(2,1)S(1)}, u32[]{:S(2)}, u32[]{:S(2)}) collective-permute-start(bf16[3,256,768]{2,1,0:T(8,128)(2,1)S(1)} %add_convert_fusion.4), channel_id=1, source_target_pairs={{0,2},{1,3},{2,0},{3,1},{4,6},{5,7},{6,4},{7,5},{8,10},{9,11},{10,... | collective-permute-start | bytes 3538952 | tf_op jit(solution)/shard_map/ppermute | solution.py:17
  423.0 64.3 %collective-permute-start.7 = (bf16[3,256,768]{2,1,0:T(8,128)(2,1)S(1)}, bf16[3,256,768]{2,1,0:T(8,128)(2,1)S(1)}, u32[]{:S(2)}, u32[]{:S(2)}) collective-permute-start(bf16[3,256,768]{2,1,0:T(8,128)(2,1)S(1)} %add_convert_fusion.5), channel_id=1, source_target_pairs={{0,2},{1,3},{2,0},{3,1},{4,6},{5,7},{6,4},{7,5},{8,10},{9,11},{10,... | collective-permute-start | bytes 3538952 | tf_op jit(solution)/shard_map/ppermute | solution.py:17
  430.1 43.1 %collective-permute-start.70 = (bf16[1,2,24,1024]{3,2,1,0:T(8,128)(2,1)S(1)}, bf16[1,2,24,1024]{3,2,1,0:T(8,128)(2,1)S(1)}, u32[]{:S(2)}, u32[]{:S(2)}) collective-permute-start(bf16[1,2,24,1024]{3,2,1,0:T(8,128)(2,1)S(1)} %dynamic-slice_bitcast_fusion.46), channel_id=1, source_target_pairs={{0,2},{1,3},{2,0},{3,1},{4,6},{5,7},{6,4},{7,5},{8,10},{9,11},{10,... | collective-permute-start | bytes 294920 | tf_op jit(solution)/shard_map/ppermute | solution.py:17
  431.6 44.3 %collective-permute-start.100 = (bf16[1,2,96,256]{3,2,1,0:T(8,128)(2,1)S(1)}, bf16[1,2,96,256]{3,2,1,0:T(8,128)(2,1)S(1)}, u32[]{:S(2)}, u32[]{:S(2)}) collective-permute-start(bf16[1,2,96,256]{3,2,1,0:T(8,128)(2,1)S(1)} %dynamic-slice_bitcast_fusion.40), channel_id=1, source_target_pairs={{0,2},{1,3},{2,0},{3,1},{4,6},{5,7},{6,4},{7,5},{8,10},{9,11},{10,... | collective-permute-start | bytes 294920 | tf_op jit(solution)/shard_map/ppermute | solution.py:17
  433.9 43.2 %collective-permute-start.106 = (bf16[1,96,256]{2,1,0:T(8,128)(2,1)S(1)}, bf16[1,96,256]{2,1,0:T(8,128)(2,1)S(1)}, u32[]{:S(2)}, u32[]{:S(2)}) collective-permute-start(bf16[1,96,256]{2,1,0:T(8,128)(2,1)S(1)} %dynamic-slice_bitcast_fusion.58), channel_id=1, source_target_pairs={{0,16},{4,20},{8,24},{12,28},{16,0},{20,4},{24,8},{28,12},{1,17},{... | collective-permute-start | bytes 147464 | tf_op jit(solution)/shard_map/ppermute | solution.py:17
  592.0 48.1 %collective-permute-start.37 = (bf16[4,2,2,2,2,24,256]{6,5,0,1,3,4,2:T(8,128)(2,1)}, bf16[4,2,2,2,2,24,256]{6,5,0,1,3,4,2:T(8,128)(2,1)}, u32[]{:S(2)}, u32[]{:S(2)}) collective-permute-start(bf16[4,2,2,2,2,24,256]{6,5,0,1,3,4,2:T(8,128)(2,1)} %bitcast.826), channel_id=1, source_target_pairs={{0,1},{1,0},{2,3},{3,2},{4,5},{5,4},{6,7},{7,6},{8,9},{9,8},{10,11... | collective-permute-start | bytes 2359304 | tf_op jit(solution)/shard_map/ppermute | solution.py:17
  592.0 50.9 %collective-permute-start.27 = (bf16[4,2,2,2,2,24,256]{6,5,0,1,2,3,4:T(8,128)(2,1)}, bf16[4,2,2,2,2,24,256]{6,5,0,1,2,3,4:T(8,128)(2,1)}, u32[]{:S(2)}, u32[]{:S(2)}) collective-permute-start(bf16[4,2,2,2,2,24,256]{6,5,0,1,2,3,4:T(8,128)(2,1)} %bitcast.828), channel_id=1, source_target_pairs={{0,1},{1,0},{2,3},{3,2},{4,5},{5,4},{6,7},{7,6},{8,9},{9,8},{10,11... | collective-permute-start | bytes 2359304 | tf_op jit(solution)/shard_map/ppermute | solution.py:17
  600.0 45.1 %collective-permute-start.82 = (bf16[1,2,2,2,2,96,256]{6,5,1,4,2,3,0:T(8,128)(2,1)}, bf16[1,2,2,2,2,96,256]{6,5,1,4,2,3,0:T(8,128)(2,1)}, u32[]{:S(2)}, u32[]{:S(2)}) collective-permute-start(bf16[1,2,2,2,2,96,256]{6,5,1,4,2,3,0:T(8,128)(2,1)} %bitcast.820), channel_id=1, source_target_pairs={{0,1},{1,0},{2,3},{3,2},{4,5},{5,4},{6,7},{7,6},{8,9},{9,8},{10,11... | collective-permute-start | bytes 2359304 | tf_op jit(solution)/shard_map/ppermute | solution.py:17
  600.1 47.7 %collective-permute-start.32 = (bf16[4,2,2,2,2,24,256]{6,5,0,1,4,2,3:T(8,128)(2,1)}, bf16[4,2,2,2,2,24,256]{6,5,0,1,4,2,3:T(8,128)(2,1)}, u32[]{:S(2)}, u32[]{:S(2)}) collective-permute-start(bf16[4,2,2,2,2,24,256]{6,5,0,1,4,2,3:T(8,128)(2,1)} %bitcast.827), channel_id=1, source_target_pairs={{0,1},{1,0},{2,3},{3,2},{4,5},{5,4},{6,7},{7,6},{8,9},{9,8},{10,11... | collective-permute-start | bytes 2359304 | tf_op jit(solution)/shard_map/ppermute | solution.py:17
  600.5 49.7 %collective-permute-start.77 = (bf16[1,2,2,2,2,96,256]{6,5,4,3,2,1,0:T(8,128)(2,1)}, bf16[1,2,2,2,2,96,256]{6,5,4,3,2,1,0:T(8,128)(2,1)}, u32[]{:S(2)}, u32[]{:S(2)}) collective-permute-start(bf16[1,2,2,2,2,96,256]{6,5,4,3,2,1,0:T(8,128)(2,1)} %dynamic-slice_bitcast_fusion), channel_id=1, source_target_pairs={{0,1},{1,0},{2,3},{3,2},{4,5},{5,4},{6,7},{7,6},{8,9},{9,8},{10,11... | collective-permute-start | bytes 2359304 | tf_op jit(solution)/shard_map/ppermute | solution.py:17
  640.1 12.7 %collective-permute-start.87 = (bf16[1,2,2,2,2,96,256]{6,5,1,3,4,2,0:T(8,128)(2,1)S(1)}, bf16[1,2,2,2,2,96,256]{6,5,1,3,4,2,0:T(8,128)(2,1)S(1)}, u32[]{:S(2)}, u32[]{:S(2)}) collective-permute-start(bf16[1,2,2,2,2,96,256]{6,5,1,3,4,2,0:T(8,128)(2,1)S(1)} %bitcast.908), channel_id=1, source_target_pairs={{0,1},{1,0},{2,3},{3,2},{4,5},{5,4},{6,7},{7,6},{8,9},{9,8},{10,11... | collective-permute-start | bytes 2359304 | tf_op jit(solution)/shard_map/ppermute | solution.py:17
  642.8 11.3 %collective-permute-start.52 = (bf16[1,2,2,2,2,24,1024]{6,5,1,4,2,3,0:T(8,128)(2,1)S(1)}, bf16[1,2,2,2,2,24,1024]{6,5,1,4,2,3,0:T(8,128)(2,1)S(1)}, u32[]{:S(2)}, u32[]{:S(2)}) collective-permute-start(bf16[1,2,2,2,2,24,1024]{6,5,1,4,2,3,0:T(8,128)(2,1)S(1)} %bitcast.910), channel_id=1, source_target_pairs={{0,1},{1,0},{2,3},{3,2},{4,5},{5,4},{6,7},{7,6},{8,9},{9,8},{10,11... | collective-permute-start | bytes 2359304 | tf_op jit(solution)/shard_map/ppermute | solution.py:17
  645.1 13.1 %collective-permute-start.47 = (bf16[1,2,2,2,2,24,1024]{6,5,4,3,2,1,0:T(8,128)(2,1)S(1)}, bf16[1,2,2,2,2,24,1024]{6,5,4,3,2,1,0:T(8,128)(2,1)S(1)}, u32[]{:S(2)}, u32[]{:S(2)}) collective-permute-start(bf16[1,2,2,2,2,24,1024]{6,5,4,3,2,1,0:T(8,128)(2,1)S(1)} %copy-done.86), channel_id=1, source_target_pairs={{0,1},{1,0},{2,3},{3,2},{4,5},{5,4},{6,7},{7,6},{8,9},{9,8},{10,11... | collective-permute-start | bytes 2359304 | tf_op jit(solution)/shard_map/ppermute | solution.py:17
  647.7 13.1 %collective-permute-start.57 = (bf16[1,2,2,2,2,24,1024]{6,5,1,3,4,2,0:T(8,128)(2,1)S(1)}, bf16[1,2,2,2,2,24,1024]{6,5,1,3,4,2,0:T(8,128)(2,1)S(1)}, u32[]{:S(2)}, u32[]{:S(2)}) collective-permute-start(bf16[1,2,2,2,2,24,1024]{6,5,1,3,4,2,0:T(8,128)(2,1)S(1)} %bitcast.909), channel_id=1, source_target_pairs={{0,1},{1,0},{2,3},{3,2},{4,5},{5,4},{6,7},{7,6},{8,9},{9,8},{10,11... | collective-permute-start | bytes 2359304 | tf_op jit(solution)/shard_map/ppermute | solution.py:17
  650.3 13.3 %collective-permute-start.11 = (bf16[3,256,768]{2,1,0:T(8,128)(2,1)S(1)}, bf16[3,256,768]{2,1,0:T(8,128)(2,1)S(1)}, u32[]{:S(2)}, u32[]{:S(2)}) collective-permute-start(bf16[3,256,768]{2,1,0:T(8,128)(2,1)S(1)} %copy-done.82), channel_id=1, source_target_pairs={{0,1},{1,0},{2,3},{3,2},{4,5},{5,4},{6,7},{7,6},{8,9},{9,8},{10,11... | collective-permute-start | bytes 3538952 | tf_op jit(solution)/shard_map/ppermute | solution.py:17
  652.8 19.0 %collective-permute-start.10 = (bf16[3,256,768]{2,1,0:T(8,128)(2,1)}, bf16[3,256,768]{2,1,0:T(8,128)(2,1)}, u32[]{:S(2)}, u32[]{:S(2)}) collective-permute-start(bf16[3,256,768]{2,1,0:T(8,128)(2,1)} %copy.173), channel_id=1, source_target_pairs={{0,1},{1,0},{2,3},{3,2},{4,5},{5,4},{6,7},{7,6},{8,9},{9,8},{10,11... | collective-permute-start | bytes 3538952 | tf_op jit(solution)/shard_map/ppermute | solution.py:17
  654.1 30.6 %collective-permute-start.38 = (bf16[4,2,2,2,24,256]{5,4,0,1,2,3:T(8,128)(2,1)}, bf16[4,2,2,2,24,256]{5,4,0,1,2,3:T(8,128)(2,1)}, u32[]{:S(2)}, u32[]{:S(2)}) collective-permute-start(bf16[4,2,2,2,24,256]{5,4,0,1,2,3:T(8,128)(2,1)} %dynamic-slice_bitcast_fusion.15), channel_id=1, source_target_pairs={{0,8},{4,12},{8,0},{12,4},{16,24},{20,28},{24,16},{28,20},{1,9},{5... | collective-permute-start | bytes 1179656 | tf_op jit(solution)/shard_map/ppermute | solution.py:17
  658.2 28.9 %collective-permute-start.28 = (bf16[4,2,2,2,24,256]{5,4,0,1,2,3:T(8,128)(2,1)}, bf16[4,2,2,2,24,256]{5,4,0,1,2,3:T(8,128)(2,1)}, u32[]{:S(2)}, u32[]{:S(2)}) collective-permute-start(bf16[4,2,2,2,24,256]{5,4,0,1,2,3:T(8,128)(2,1)} %dynamic-slice_bitcast_fusion.17), channel_id=1, source_target_pairs={{0,2},{1,3},{2,0},{3,1},{4,6},{5,7},{6,4},{7,5},{8,10},{9,11},{10,... | collective-permute-start | bytes 1179656 | tf_op jit(solution)/shard_map/ppermute | solution.py:17
  660.8 29.0 %collective-permute-start.83 = (bf16[1,2,2,2,96,256]{5,4,1,3,2,0:T(8,128)(2,1)}, bf16[1,2,2,2,96,256]{5,4,1,3,2,0:T(8,128)(2,1)}, u32[]{:S(2)}, u32[]{:S(2)}) collective-permute-start(bf16[1,2,2,2,96,256]{5,4,1,3,2,0:T(8,128)(2,1)} %dynamic-slice_bitcast_fusion.7), channel_id=1, source_target_pairs={{0,4},{4,0},{8,12},{12,8},{16,20},{20,16},{24,28},{28,24},{1,5},{5... | collective-permute-start | bytes 1179656 | tf_op jit(solution)/shard_map/ppermute | solution.py:17
  663.7 28.8 %collective-permute-start.33 = (bf16[4,2,2,2,24,256]{5,4,0,1,3,2:T(8,128)(2,1)}, bf16[4,2,2,2,24,256]{5,4,0,1,3,2:T(8,128)(2,1)}, u32[]{:S(2)}, u32[]{:S(2)}) collective-permute-start(bf16[4,2,2,2,24,256]{5,4,0,1,3,2:T(8,128)(2,1)} %dynamic-slice_bitcast_fusion.16), channel_id=1, source_target_pairs={{0,4},{4,0},{8,12},{12,8},{16,20},{20,16},{24,28},{28,24},{1,5},{5... | collective-permute-start | bytes 1179656 | tf_op jit(solution)/shard_map/ppermute | solution.py:17
  671.8 23.3 %collective-permute-start.78 = (bf16[1,2,2,2,96,256]{5,4,3,2,1,0:T(8,128)(2,1)S(1)}, bf16[1,2,2,2,96,256]{5,4,3,2,1,0:T(8,128)(2,1)S(1)}, u32[]{:S(2)}, u32[]{:S(2)}) collective-permute-start(bf16[1,2,2,2,96,256]{5,4,3,2,1,0:T(8,128)(2,1)S(1)} %copy-done.101), channel_id=1, source_target_pairs={{0,2},{1,3},{2,0},{3,1},{4,6},{5,7},{6,4},{7,5},{8,10},{9,11},{10,... | collective-permute-start | bytes 1179656 | tf_op jit(solution)/shard_map/ppermute | solution.py:17
  685.4 11.9 %collective-permute-start.88 = (bf16[1,2,2,2,96,256]{5,4,1,2,3,0:T(8,128)(2,1)S(1)}, bf16[1,2,2,2,96,256]{5,4,1,2,3,0:T(8,128)(2,1)S(1)}, u32[]{:S(2)}, u32[]{:S(2)}) collective-permute-start(bf16[1,2,2,2,96,256]{5,4,1,2,3,0:T(8,128)(2,1)S(1)} %copy-done.103), channel_id=1, source_target_pairs={{0,8},{4,12},{8,0},{12,4},{16,24},{20,28},{24,16},{28,20},{1,9},{5... | collective-permute-start | bytes 1179656 | tf_op jit(solution)/shard_map/ppermute | solution.py:17
  697.3 103.4 %collective-permute-start.17 = (bf16[4,2,2,2,2,24,256]{6,5,0,1,4,2,3:T(8,128)(2,1)S(1)}, bf16[4,2,2,2,2,24,256]{6,5,0,1,4,2,3:T(8,128)(2,1)S(1)}, u32[]{:S(2)}, u32[]{:S(2)}) collective-permute-start(bf16[4,2,2,2,2,24,256]{6,5,0,1,4,2,3:T(8,128)(2,1)S(1)} %bitcast.907), channel_id=1, source_target_pairs={{0,1},{1,0},{2,3},{3,2},{4,5},{5,4},{6,7},{7,6},{8,9},{9,8},{10,11... | collective-permute-start | bytes 2359304 | tf_op jit(solution)/shard_map/ppermute | solution.py:17
  697.4 104.3 %collective-permute-start.12 = (bf16[4,2,2,2,2,24,256]{6,5,4,3,2,1,0:T(8,128)(2,1)S(1)}, bf16[4,2,2,2,2,24,256]{6,5,4,3,2,1,0:T(8,128)(2,1)S(1)}, u32[]{:S(2)}, u32[]{:S(2)}) collective-permute-start(bf16[4,2,2,2,2,24,256]{6,5,4,3,2,1,0:T(8,128)(2,1)S(1)} %dynamic-slice_bitcast_fusion.2), channel_id=1, source_target_pairs={{0,1},{1,0},{2,3},{3,2},{4,5},{5,4},{6,7},{7,6},{8,9},{9,8},{10,11... | collective-permute-start | bytes 2359304 | tf_op jit(solution)/shard_map/ppermute | solution.py:17
  699.6 103.6 %collective-permute-start.22 = (bf16[4,2,2,2,2,24,256]{6,5,0,1,3,4,2:T(8,128)(2,1)S(1)}, bf16[4,2,2,2,2,24,256]{6,5,0,1,3,4,2:T(8,128)(2,1)S(1)}, u32[]{:S(2)}, u32[]{:S(2)}) collective-permute-start(bf16[4,2,2,2,2,24,256]{6,5,0,1,3,4,2:T(8,128)(2,1)S(1)} %bitcast.906), channel_id=1, source_target_pairs={{0,1},{1,0},{2,3},{3,2},{4,5},{5,4},{6,7},{7,6},{8,9},{9,8},{10,11... | collective-permute-start | bytes 2359304 | tf_op jit(solution)/shard_map/ppermute | solution.py:17
  703.8 24.8 %collective-permute-start.39 = (bf16[4,2,2,24,256]{4,3,0,1,2:T(8,128)(2,1)S(1)}, bf16[4,2,2,24,256]{4,3,0,1,2:T(8,128)(2,1)S(1)}, u32[]{:S(2)}, u32[]{:S(2)}) collective-permute-start(bf16[4,2,2,24,256]{4,3,0,1,2:T(8,128)(2,1)S(1)} %dynamic-slice_bitcast_fusion.33), channel_id=1, source_target_pairs={{0,2},{1,3},{2,0},{3,1},{4,6},{5,7},{6,4},{7,5},{8,10},{9,11},{10,... | collective-permute-start | bytes 589832 | tf_op jit(solution)/shard_map/ppermute | solution.py:17
  (255 other events, 2545.8 us)

commit v2 on v0

v2 whole, which is shorter than its diff:
```python
from functools import partial

import jax
import jax.numpy as jnp
from jax import lax
from jax.experimental import pallas as pl
from jax.experimental.pallas import tpu as pltpu
from jax.sharding import PartitionSpec as P

HEADS = 12
HEAD_DIM = 64


EPSILON = 1e-06
MASKED = -1e30


def swapped_2(value, axis, bit):
    return lax.ppermute(value, axis, [(i, i ^ 1 << bit) for i in range(lax.axis_size(axis))])


TOKENS_MINOR = (((1,), (1,)), ((), ()))
TOKENS_MAJOR = (((0,), (0,)), ((), ()))
ROOT_HALF = 0.7071067811865476
ROOT_TAU = 0.3989422804014327
VMEM_BYTES = 56 * 1024 * 1024
FF_PARTS = 4
FAST = jnp.float32
LOW = jnp.bfloat16


COST_SCALE = 10


def cost(microseconds):
    return pl.CostEstimate(flops=int(microseconds * COST_SCALE * 1.15e9), bytes_accessed=1, transcendentals=0)


def mm(left, right):
    return jnp.dot(left, right, preferred_element_type=FAST)


def mm_nt(left, right):
    return lax.dot_general(left, right, TOKENS_MINOR, preferred_element_type=FAST)


def mm_tn(left, right):
    return lax.dot_general(left, right, TOKENS_MAJOR, preferred_element_type=FAST)


def row_norm(value):
    average = jnp.mean(value, axis=-1, keepdims=True)
    centred = value - average
    inverse_scale = lax.rsqrt(jnp.mean(centred * centred, axis=-1, keepdims=True) + EPSILON)
    return centred * inverse_scale, inverse_scale


def gelu_and_slope(value):
    size = jnp.abs(value)
    near = 1.0 / (1.0 + (0.3275911 * ROOT_HALF) * size)
    bell = jnp.exp(value * value * -0.5)
    poly = near * (
        0.127414796
        + near * (-0.142248368 + near * (0.7107068705 + near * (-0.7265760135 + near * 0.5307027145)))
    )
    tail = poly * bell
    below = jnp.where(value >= 0, 1.0 - tail, tail)
    return value * below, below + value * (bell * ROOT_TAU)


VEC_ROWS = dict(b_query=0, b_value=1, b_out=2, gain_one=3, shift_one=4, b_down=5, gain_two=6, shift_two=7)
VEC_UP = 8


def forward_kernel(layer, swapped, facts, own, near, far, top, vecs, *refs):
    weights, refs = refs[:6], refs[6:]
    refs = refs[len(refs) - 25 :]
    outs, scratch = refs[:16], refs[16:]
    (
        o_sent, o_extra, o_low, o_q, o_k, o_v, o_lse, o_ctx, o_n1, o_r1, o_hid, o_act, o_slope, o_n2, o_r2, o_done,
    ) = outs
    o_top = o_near = o_extra
    w_q, w_k, w_v, w_o, w_up, w_down, mix, ctx, sems = scratch
    first = pl.program_id(0) == 0
    held = (w_q, w_k, w_v, w_o, w_up, w_down)
    copies = [
        pltpu.make_async_copy(weights[i].at[layer], held[i], sems.at[i]) for i in range(6)
    ]

    @pl.when(first)
    def _():
        for copy in copies:
            copy.start()

    def ready(*which):
        @pl.when(first)
        def _():
            for i in which:
                copies[i].wait()

    def vec(name):
        row = VEC_ROWS[name]
        return vecs[layer, row : row + 1, :]

    rows = own.shape[1]
    x = own[0]
    ready(0, 1, 2)
    queries = (mm(x, w_q[...]) + vec("b_query")).astype(LOW)
    o_q[0] = queries * jnp.asarray(HEAD_DIM**-0.5, LOW)
    for part, source in ((0, near), (1, far)):
        block = source[0]
        o_k[0, part * rows : (part + 1) * rows, :] = mm(block, w_k[...]).astype(LOW)
        o_v[0, part * rows : (part + 1) * rows, :] = (mm(block, w_v[...]) + vec("b_value")).astype(LOW)
    seq = facts[5] + pl.program_id(0)
    length = facts[seq]
    lane = lax.broadcasted_iota(jnp.int32, (1, 2 * rows), 1)
    place = jnp.where(lane < rows, facts[3] + lane, facts[4] + (lane - rows))
    bias = jnp.where(place < length, 0.0, MASKED).astype(FAST)
    lower = lax.broadcasted_iota(jnp.int32, (1, 128), 1) < HEAD_DIM
    column = lax.broadcasted_iota(jnp.int32, (1, 128), 1)
    logs = jnp.zeros((rows, 128), FAST)
    for pair in range(HEADS // 2):
        lanes = slice(pair * 128, pair * 128 + 128)
        q_pair, k_pair, v_pair = o_q[0, :, lanes], o_k[0, :, lanes], o_v[0, :, lanes]
        got = []
        for side in range(2):
            mask = lower if side == 0 else ~lower
            q_one = jnp.where(mask, q_pair, jnp.zeros_like(q_pair))
            scores = mm_nt(q_one, k_pair) + bias
            high = jnp.max(scores, axis=-1, keepdims=True)
            weight = jnp.exp(scores - high)
            total = jnp.sum(weight, axis=-1, keepdims=True)
            got.append(mm(weight.astype(LOW), v_pair) * (1.0 / total))
            logs = jnp.where(column == 2 * pair + side, high + jnp.log(total), logs)
        ctx[:, lanes] = jnp.where(lower, got[0], got[1]).astype(LOW)
    o_lse[0] = logs.T[:16, :]
    o_ctx[0] = ctx[...]
    ready(3)
    branch = mm(ctx[...], w_o[...]) + vec("b_out") + top[0].astype(FAST)
    n1, r1 = row_norm(branch)
    o_n1[0] = n1.astype(LOW)
    o_r1[0] = r1
    hidden = n1 * vec("gain_one") + vec("shift_one")
    hid = hidden.astype(LOW)
    o_hid[0] = hid
    mix[...] = hidden + vec("b_down")
    ready(4, 5)
    width = w_up.shape[1] // FF_PARTS
    for part in range(FF_PARTS):
        cols = slice(part * width, (part + 1) * width)
        pre = mm(hid, w_up[:, cols]) + vecs[layer, VEC_UP + part : VEC_UP + part + 1, :]
        act, slope = gelu_and_slope(pre)
        act = act.astype(LOW)
        o_act[0, :, cols] = act
        o_slope[0, :, cols] = slope.astype(LOW)
        mix[...] += mm(act, w_down[cols, :])
    n2, r2 = row_norm(mix[...])
    o_n2[0] = n2.astype(LOW)
    o_r2[0] = r2
    result = n2 * vec("gain_two") + vec("shift_two")
    if not swapped:
        o_top[0] = result
    low = result.astype(LOW)
    o_sent[0] = low
    if swapped:
        o_near[0] = near[0]
    o_low[0] = low
    o_done[...] = jnp.zeros_like(o_done)


KEPT = ("extra", "low", "q", "k", "v", "lse", "ctx", "n1", "r1", "hid", "act", "slope", "n2", "r2")


def forward_call(layer, swapped, start, count, facts, own, near, far, top, vecs, weights, kept, sizes):
    seqs, rows, wide, hidden = sizes

    def taken(source):
        array, offset = source
        return pl.BlockSpec((1,) + array.shape[1:], lambda i: (start - offset + i, 0, 0))

    shapes = dict(
        extra=((rows, wide), LOW if swapped else FAST), low=((rows, wide), LOW),
        q=((rows, wide), LOW), k=((2 * rows, wide), LOW), v=((2 * rows, wide), LOW), lse=((16, rows), FAST),
        ctx=((rows, wide), LOW), n1=((rows, wide), LOW), r1=((rows, 1), FAST), hid=((rows, wide), LOW),
        act=((rows, hidden), LOW), slope=((rows, hidden), LOW), n2=((rows, wide), LOW), r2=((rows, 1), FAST),
    )
    out_shape = [jax.ShapeDtypeStruct((count, rows, wide), LOW)] + [
        jax.ShapeDtypeStruct((seqs,) + shapes[name][0], shapes[name][1]) for name in KEPT
    ]
    out_specs = [pl.BlockSpec((1, rows, wide), lambda i: (i, 0, 0))] + [
        pl.BlockSpec((1,) + shapes[name][0], lambda i: (start + i, 0, 0)) for name in KEPT
    ]
    out_shape.append(jax.ShapeDtypeStruct((8, 128), FAST))
    out_specs.append(pl.BlockSpec((8, 128), lambda i: (0, 0)))
    any_spec = pl.BlockSpec(memory_space=pl.ANY)
    ins = [facts, own[0], near[0], far[0], top[0], vecs, *weights]
    in_specs = [
        pl.BlockSpec(memory_space=pltpu.SMEM), taken(own), taken(near), taken(far), taken(top),
        pl.BlockSpec(vecs.shape, lambda i: (0, 0, 0)),
    ] + [any_spec] * 6
    aliases = {}
    if kept is not None:
        for place, name in enumerate(KEPT):
            aliases[len(ins) + place] = 1 + place
        ins += [kept[name] for name in KEPT]
        in_specs += [any_spec] * len(KEPT)
    got = pl.pallas_call(
        partial(forward_kernel, layer, swapped),
        grid=(count,),
        in_specs=in_specs,
        out_specs=out_specs,
        out_shape=out_shape,
        input_output_aliases=aliases,
        scratch_shapes=[
            pltpu.VMEM((wide, wide), LOW), pltpu.VMEM((wide, wide), LOW), pltpu.VMEM((wide, wide), LOW),
            pltpu.VMEM((wide, wide), LOW), pltpu.VMEM((wide, hidden), LOW), pltpu.VMEM((hidden, wide), LOW),
            pltpu.VMEM((rows, wide), FAST), pltpu.VMEM((rows, wide), LOW), pltpu.SemaphoreType.DMA((6,)),
        ],
        compiler_params=pltpu.CompilerParams(vmem_limit_bytes=VMEM_BYTES),
        cost_estimate=cost(14 * count),
        name=f"layer_forward_{layer}",
    )(*ins)
    return got[0], dict(zip(KEPT, got[1:-1], strict=True)), got[-1]


def norm_back_rows(grad, normed, inverse_scale, gain):
    dn = grad * gain
    return inverse_scale * (
        dn - jnp.mean(dn, axis=-1, keepdims=True) - normed * jnp.mean(dn * normed, axis=-1, keepdims=True)
    )


def column_sum(value):
    return jnp.sum(value.astype(FAST), axis=0, keepdims=True)


def ff_back_kernel(layer, top_grad, n2, r2, slope, n1, r1, vecs, *refs):
    weights, refs = refs[:3], refs[3:]
    o_dy, o_df, o_dz1, o_da, o_dc, o_vec, w_down, w_up, w_o, mix, sems = refs
    first = pl.program_id(0) == 0
    held = (w_down, w_up, w_o)
    copies = [pltpu.make_async_copy(weights[i].at[layer], held[i], sems.at[i]) for i in range(3)]

    @pl.when(first)
    def _():
        for copy in copies:
            copy.start()
        o_vec[...] = jnp.zeros_like(o_vec)

    def ready(which):
        @pl.when(first)
        def _():
            copies[which].wait()

    def vec(name):
        row = VEC_ROWS[name]
        return vecs[layer, row : row + 1, :]

    def add(row, value):
        o_vec[row : row + 1, :] += value

    grad = top_grad[0].astype(FAST)
    normed = n2[0].astype(FAST)
    add(VEC_ROWS["gain_two"], column_sum(grad * normed))
    add(VEC_ROWS["shift_two"], column_sum(grad))
    dz2 = norm_back_rows(grad, normed, r2[0], vec("gain_two"))
    dy = dz2.astype(LOW)
    o_dy[0] = dy
    add(VEC_ROWS["b_down"], column_sum(dy))
    mix[...] = dz2
    ready(0)
    width = w_up.shape[1] // FF_PARTS
    for part in range(FF_PARTS):
        cols = slice(part * width, (part + 1) * width)
        if part == 0:
            ready(1)
        df = (mm_nt(dy, w_down[cols, :]) * slope[0, :, cols].astype(FAST)).astype(LOW)
        o_df[0, :, cols] = df
        add(VEC_UP + part, column_sum(df))
        mix[...] += mm_nt(df, w_up[:, cols])
    grad = mix[...]
    normed = n1[0].astype(FAST)
    add(VEC_ROWS["gain_one"], column_sum(grad * normed))
    add(VEC_ROWS["shift_one"], column_sum(grad))
    dz1 = norm_back_rows(grad, normed, r1[0], vec("gain_one"))
    o_dz1[0] = dz1
    da = dz1.astype(LOW)
    o_da[0] = da
    add(VEC_ROWS["b_out"], column_sum(da))
    ready(2)
    o_dc[0] = mm_nt(da, w_o[...]).astype(LOW)


def ff_back_call(layer, top_grad, kept, vecs, w_down, w_up, w_out):
    seqs, rows, wide = top_grad.shape
    hidden = w_up.shape[2]
    ins = [top_grad, kept["n2"], kept["r2"], kept["slope"], kept["n1"], kept["r1"], vecs, w_down, w_up, w_out]
    each = lambda shape: pl.BlockSpec((1,) + tuple(shape[1:]), lambda i: (i, 0, 0))
    any_spec = pl.BlockSpec(memory_space=pl.ANY)
    in_specs = [each(x.shape) for x in ins[:6]] + [pl.BlockSpec(vecs.shape, lambda i: (0, 0, 0))] + [any_spec] * 3
    out_shape = [
        jax.ShapeDtypeStruct((seqs, rows, wide), LOW), jax.ShapeDtypeStruct((seqs, rows, hidden), LOW),
        jax.ShapeDtypeStruct((seqs, rows, wide), FAST), jax.ShapeDtypeStruct((seqs, rows, wide), LOW),
        jax.ShapeDtypeStruct((seqs, rows, wide), LOW), jax.ShapeDtypeStruct((vecs.shape[1], wide), FAST),
    ]
    out_specs = [each(x.shape) for x in out_shape[:5]] + [pl.BlockSpec(out_shape[5].shape, lambda i: (0, 0))]
    return pl.pallas_call(
        partial(ff_back_kernel, layer),
        grid=(seqs,),
        in_specs=in_specs,
        out_specs=out_specs,
        out_shape=out_shape,
        scratch_shapes=[
            pltpu.VMEM((hidden, wide), LOW), pltpu.VMEM((wide, hidden), LOW), pltpu.VMEM((wide, wide), LOW),
            pltpu.VMEM((rows, wide), FAST), pltpu.SemaphoreType.DMA((3,)),
        ],
        compiler_params=pltpu.CompilerParams(vmem_limit_bytes=VMEM_BYTES),
        cost_estimate=cost(19),
        name=f"ff_back_{layer}",
    )(*ins)


def attention_back_kernel(split, facts, q, k, v, lse, dc, *refs):
    o_dq, o_near, o_far, o_vec, bias = refs[len(refs) - 5 :]
    rows, wide = q.shape[1], q.shape[2]

    @pl.when(pl.program_id(0) == 0)
    def _():
        o_vec[...] = jnp.zeros_like(o_vec)

    length = facts[facts[5] + pl.program_id(0)]
    key = lax.broadcasted_iota(jnp.int32, (2 * rows, rows), 0)
    place = jnp.where(key < rows, facts[3] + key, facts[4] + (key - rows))
    bias[...] = jnp.where(place < length, 0.0, MASKED).astype(FAST)
    lower = lax.broadcasted_iota(jnp.int32, (1, 128), 1) < HEAD_DIM
    for pair in range(HEADS // 2):
        lanes = slice(pair * 128, pair * 128 + 128)
        q_pair, k_pair, v_pair, dc_pair = q[0, :, lanes], k[0, :, lanes], v[0, :, lanes], dc[0, :, lanes]
        dk = dv = None
        dq = []
        for side in range(2):
            one = 2 * pair + side
            mask = lower if side == 0 else ~lower
            q_one = jnp.where(mask, q_pair, jnp.zeros_like(q_pair))
            dc_one = jnp.where(mask, dc_pair, jnp.zeros_like(dc_pair))
            weight = jnp.exp(mm_nt(k_pair, q_one) + bias[...] - lse[0, one : one + 1, :])
            product = weight * mm_nt(v_pair, dc_one)
            ds = (product - weight * jnp.sum(product, axis=0, keepdims=True)).astype(LOW)
            dv_one = mm(weight.astype(LOW), dc_one)
            dk_one = mm(ds, q_one)
            dv = dv_one if dv is None else dv + dv_one
            dk = dk_one if dk is None else dk + dk_one
            dq.append(mm_tn(ds, k_pair))
        dq_pair = (jnp.where(lower, dq[0], dq[1]) * HEAD_DIM**-0.5).astype(LOW)
        o_dq[0, :, lanes] = dq_pair
        o_vec[0:1, lanes] += column_sum(dq_pair)
        o_near[0, 0, :, lanes] = dk[:rows].astype(LOW)
        o_far[0, 0, :, lanes] = dk[rows:].astype(LOW)
        o_near[0, 1, :, lanes] = dv[:rows].astype(LOW)
        o_far[0, 1, :, lanes] = dv[rows:].astype(LOW)


def blocks(shape, start):
    rest = len(shape) - 1
    return pl.BlockSpec((1,) + tuple(shape[1:]), lambda i: (start + i,) + (0,) * rest)


def chained(ins, in_specs, earlier, places):
    aliases = {}
    if earlier is not None:
        for array, place in zip(earlier, places, strict=True):
            aliases[len(ins)] = place
            ins.append(array)
            in_specs.append(pl.BlockSpec(memory_space=pl.ANY))
    return aliases


def attention_back_call(layer, split, start, count, facts, kept, dc, earlier):
    seqs, rows, wide = dc.shape
    ins = [facts, kept["q"], kept["k"], kept["v"], kept["lse"], dc]
    in_specs = [pl.BlockSpec(memory_space=pltpu.SMEM)] + [blocks(x.shape, start) for x in ins[1:]]
    whole = jax.ShapeDtypeStruct((seqs, rows, wide), LOW)
    both = jax.ShapeDtypeStruct((seqs, 2, rows, wide), LOW)
    single = jax.ShapeDtypeStruct((count, 2, rows, wide), LOW)
    out_shape = [whole, both, single if split else both, jax.ShapeDtypeStruct((8, wide), FAST)]
    out_specs = [
        blocks(whole.shape, start), blocks(both.shape, start), blocks(both.shape, 0 if split else start),
        pl.BlockSpec((8, wide), lambda i: (0, 0)),
    ]
    places = (0, 1) if split else (0, 1, 2)
    aliases = chained(ins, in_specs, earlier and earlier[: len(places)], places)
    return pl.pallas_call(
        partial(attention_back_kernel, split),
        grid=(count,),
        in_specs=in_specs,
        out_specs=out_specs,
        out_shape=out_shape,
        input_output_aliases=aliases,
        scratch_shapes=[pltpu.VMEM((2 * rows, rows), FAST)],
        compiler_params=pltpu.CompilerParams(vmem_limit_bytes=VMEM_BYTES),
        cost_estimate=cost(8 * count),
        name=f"attention_back_{layer}",
    )(*ins)


def input_back_kernel(layer, split, dq, near, *refs):
    got, refs = (refs[0], refs[1:]) if split else (None, refs)
    dz1, *refs = refs
    weights, refs = refs[:3], refs[3:]
    if split:
        o_own, o_pair, o_sent, o_vec, w_q, w_k, w_v, sems = refs[len(refs) - 8 :]
    else:
        o_own, o_vec, w_q, w_k, w_v, sems = refs
    first = pl.program_id(0) == 0
    held = (w_q, w_k, w_v)
    copies = [pltpu.make_async_copy(weights[i].at[layer], held[i], sems.at[i]) for i in range(3)]

    @pl.when(first)
    def _():
        for copy in copies:
            copy.start()
        o_vec[...] = jnp.zeros_like(o_vec)

    if split:
        dk = (near[0, 0].astype(FAST) + got[0, 0].astype(FAST)).astype(LOW)
        dv = (near[0, 1].astype(FAST) + got[0, 1].astype(FAST)).astype(LOW)
        o_pair[0, 0] = dk
        o_pair[0, 1] = dv
    else:
        dk, dv = near[0, 0], near[0, 1]
    o_vec[0:1, :] += column_sum(dv)

    @pl.when(first)
    def _():
        for copy in copies:
            copy.wait()

    far = mm_nt(dk, w_k[...]) + mm_nt(dv, w_v[...])
    here = dz1[0] + mm_nt(dq[0], w_q[...])
    if split:
        o_sent[0] = far.astype(LOW)
        o_own[0] = here
    else:
        o_own[0] = here + far


def input_back_call(layer, split, start, count, dq, near, got, dz1, weights, earlier):
    seqs, rows, wide = dq.shape
    ins = [dq, near]
    in_specs = [blocks(dq.shape, start), blocks(near.shape, start)]
    if split:
        ins.append(got)
        in_specs.append(blocks(got.shape, 0))
    ins += [dz1, *weights]
    in_specs += [blocks(dz1.shape, start)] + [pl.BlockSpec(memory_space=pl.ANY)] * 3
    out_shape = [jax.ShapeDtypeStruct((seqs, rows, wide), FAST)]
    out_specs = [blocks(dz1.shape, start)]
    if split:
        out_shape += [
            jax.ShapeDtypeStruct((seqs, 2, rows, wide), LOW), jax.ShapeDtypeStruct((count, rows, wide), LOW)
        ]
        out_specs += [blocks(out_shape[1].shape, start), blocks(out_shape[2].shape, 0)]
    out_shape.append(jax.ShapeDtypeStruct((8, wide), FAST))
    out_specs.append(pl.BlockSpec((8, wide), lambda i: (0, 0)))
    aliases = chained(ins, in_specs, earlier and earlier[:2], (0, 1))
    return pl.pallas_call(
        partial(input_back_kernel, layer, split),
        grid=(count,),
        in_specs=in_specs,
        out_specs=out_specs,
        out_shape=out_shape,
        input_output_aliases=aliases,
        scratch_shapes=[pltpu.VMEM((wide, wide), LOW)] * 3 + [pltpu.SemaphoreType.DMA((3,))],
        compiler_params=pltpu.CompilerParams(vmem_limit_bytes=VMEM_BYTES),
        cost_estimate=cost(2 + 3 * count),
        name=f"input_back_{layer}",
    )(*ins)


def wgrad_kernel(count, place_ref, *refs):
    lefts, rights, (o_kept, o_sent, full) = refs[:count], refs[count : 2 * count], refs[2 * count :]
    mine = place_ref[0]
    pairs, rows = o_kept.shape[1], o_kept.shape[2]
    for i in range(count):
        full[...] = mm_tn(lefts[i][...], rights[i][...])
        for pair in range(pairs):
            first = pl.multiple_of((2 * pair + mine) * rows, 8)
            second = pl.multiple_of((2 * pair + 1 - mine) * rows, 8)
            o_kept[i, pair] = full[pl.ds(first, rows), :].astype(LOW)
            o_sent[i, pair] = full[pl.ds(second, rows), :].astype(LOW)


def wgrad_call(name, place, devices, lefts, rights, chunk):
    tokens, height = lefts[0].shape
    width = rights[0].shape[1]
    count = len(lefts)
    rows = height // devices
    steps = height // chunk
    shape = jax.ShapeDtypeStruct((count, devices // 2, rows, width), LOW)
    out_spec = pl.BlockSpec((count, devices // 2 // steps, rows, width), lambda i: (0, i, 0, 0))
    return pl.pallas_call(
        partial(wgrad_kernel, count),
        grid=(steps,),
        in_specs=[pl.BlockSpec(memory_space=pltpu.SMEM)]
        + [pl.BlockSpec((tokens, chunk), lambda i: (0, i))] * count
        + [pl.BlockSpec((tokens, width), lambda i: (0, 0))] * count,
        out_specs=[out_spec] * 2,
        out_shape=[shape] * 2,
        scratch_shapes=[pltpu.VMEM((chunk, width), FAST)],
        compiler_params=pltpu.CompilerParams(vmem_limit_bytes=VMEM_BYTES),
        cost_estimate=cost(3 + 2 * count * height * width / 1e6),
        name=f"wgrad_{name}",
    )(place, *lefts, *rights)


def step_kernel(plan, bits, *refs):
    count = len(plan)
    for i, (outer, inner, digit) in enumerate(plan):
        kept, got = refs[2 * i], refs[2 * i + 1]
        o_kept, o_sent = refs[2 * count + 2 * i], refs[2 * count + 2 * i + 1]
        mine = bits[digit]
        for group in range(kept.shape[0]):
            for a in range(outer):
                for out, side in ((o_kept, mine), (o_sent, 1 - mine)):
                    source = pl.ds((2 * a + side) * inner, inner)
                    total = kept[group, source].astype(FAST) + got[group, source].astype(FAST)
                    out[group, a * inner : (a + 1) * inner] = total.astype(LOW)


def step_call(values, gots, plan, bits):
    steps = 1 if any(value.shape[3] % 384 for value in values) else 3
    ins, in_specs, out_specs, out_shape, moved = [], [], [], [], 0
    for value, got in zip(values, gots, strict=True):
        groups, parts, rows, columns = value.shape
        whole = pl.BlockSpec((groups, parts, rows, columns // steps), lambda i: (0, 0, 0, i))
        half = pl.BlockSpec((groups, parts // 2, rows, columns // steps), lambda i: (0, 0, 0, i))
        ins += [value, got]
        in_specs += [whole] * 2
        out_specs += [half] * 2
        out_shape += [jax.ShapeDtypeStruct((groups, parts // 2, rows, columns), LOW)] * 2
        moved += 6 * value.size
    return pl.pallas_call(
        partial(step_kernel, plan),
        grid=(steps,),
        in_specs=[pl.BlockSpec(memory_space=pltpu.SMEM)] + in_specs,
        out_specs=out_specs,
        out_shape=out_shape,
        compiler_params=pltpu.CompilerParams(vmem_limit_bytes=VMEM_BYTES),
        cost_estimate=cost(1 + moved / 3e6),
        name="exchange_step",
    )(bits, *ins)


def local(
    tokens, lengths, w_query, b_query, w_key, w_value, b_value, w_out, b_out, gain_one, shift_one,
    w_up, b_up, w_down, b_down, gain_two, shift_two, cotangent,
):
    seqs, rows, wide = tokens.shape
    hidden = w_up.shape[2]
    sizes = (seqs, rows, wide, hidden)
    weights = (w_query, w_key, w_value, w_out, w_up, w_down)
    vecs = jnp.stack([b_query, b_value, b_out, gain_one, shift_one, b_down, gain_two, shift_two], axis=1)
    vecs = jnp.concatenate([vecs, b_up.reshape(2, FF_PARTS, wide)], axis=1).astype(FAST)
    seq_index = lax.axis_index("seq").astype(jnp.int32)

    def facts_of(first, second, start):
        tail = jnp.stack([first * rows, second * rows, jnp.int32(start)])
        return jnp.concatenate([lengths, tail]).astype(jnp.int32)

    devices = lax.axis_size("batch") * lax.axis_size("seq")
    flat = lambda value: value.reshape(seqs * rows, value.shape[-1])
    cuts = [(0, 2), (2, seqs - 2)]
    other = swapped_2(tokens, "seq", 0)
    kept_one, sent = None, []
    for start, count in cuts:
        facts = facts_of(seq_index, seq_index ^ 1, start)
        low, kept_one, done = forward_call(
            0, False, start, count, facts, (tokens, 0), (tokens, 0), (other, 0), (tokens, 0), vecs, weights, kept_one, sizes
        )
        sent.append((low, start))
    nears = [(swapped_2(low[i : i + 1], "seq", 1), start + i) for low, start in sent for i in range(low.shape[0])]
    kept_two = None
    groups = [[0], list(range(1, seqs))]
    for number, group in enumerate(groups):
        start, count = group[0], len(group)
        arrived = [nears[i][0] for i in group]
        if number:
            arrived = after(arrived, done)
        near = jnp.concatenate(arrived) if count > 1 else arrived[0]
        far = swapped_2(near, "seq", 0)
        facts = facts_of(seq_index ^ 2, seq_index ^ 3, start)
        _, kept_two, done = forward_call(
            1, True, start, count, facts, (kept_one["low"], 0), (near, start), (far, start),
            (kept_one["extra"], 0), vecs, weights, kept_two, sizes,
        )
    final = kept_two["low"]

    back_weights = (w_query, w_key, w_value)
    digits = digit_orders()
    down_order, late_order, four_order, last_orders = digits
    up_order = down_order
    bits = jnp.stack([lax.axis_index(axis) >> bit & 1 for axis, bit in digit_list()]).astype(jnp.int32)
    wgrad = partial(wgrad_call, place=bits, devices=devices)

    kept = kept_two
    dy, df, dz1, da, dc, vec_two = ff_back_call(1, cotangent, kept, vecs, w_down, w_up, w_out)
    down_two = Sum(wgrad("down", lefts=[flat(kept["act"])], rights=[flat(dy)], chunk=wide), down_order, bits)
    facts = [facts_of(seq_index ^ 2, seq_index ^ 3, start) for start, _ in cuts]
    dc = after(dc, down_two.out)
    att = attention_back_call(1, True, 0, 2, facts[0], kept, dc, None)
    att = join(att, down_two)
    vec_q = att[3]
    advance(down_two)
    got = swapped_2(att[2], "seq", 0)
    dc = after(dc, down_two.out, att[2])
    att = attention_back_call(1, True, 2, seqs - 2, facts[1], kept, dc, att)
    vec_q += att[3]
    att, got = after((att, got))
    got_late = swapped_2(att[2], "seq", 0)
    ends = input_back_call(1, True, 0, 2, att[0], att[1], got, dz1, back_weights, None)
    vec_v = ends[3]
    ends, got_late, df = after((ends, got_late, df))
    arrived = [swapped_2(ends[2], "seq", 1)]
    up_two = Sum(wgrad("up", lefts=[flat(kept["hid"])], rights=[flat(df)], chunk=wide // 2), up_order, bits)
    got_late, ends = after((got_late, ends), up_two.out)
    ends = input_back_call(1, True, 2, seqs - 2, att[0], att[1], got_late, dz1, back_weights, ends)
    vec_v += ends[3]
    ends, da = after((ends, da))
    arrived.append(swapped_2(ends[2], "seq", 1))
    rest_two = wgrad("rest", lefts=[flat(kept["ctx"]), flat(kept_one["low"])], rights=[flat(da), flat(att[0])], chunk=wide // 2)
    rest_two, pair = join((rest_two, ends[1]), up_two, down_two)
    rest_two = Sum(rest_two, four_order, bits)
    advance(up_two, down_two)
    pair = after(pair, up_two.out, down_two.out, rest_two.out)
    pairs_two = wgrad("pair", lefts=[flat(kept["extra"])] * 2, rights=[flat(pair[:, 0]), flat(pair[:, 1])], chunk=wide // 2)
    pairs_two, arrived = join((pairs_two, arrived), rest_two)
    pairs_two = Sum(pairs_two, four_order, bits)
    vec_two = (vec_two, vec_q, vec_v)
    advance(rest_two)
    arrived = after(arrived, pairs_two.out, rest_two.out)
    middle = ends[0] + jnp.concatenate(arrived).astype(FAST)

    kept = kept_one
    ff = ff_back_call(0, middle, kept, vecs, w_down, w_up, w_out)
    ff = join(ff, down_two, pairs_two, rest_two)
    dy, df, dz1, da, dc, vec_one = ff
    advance(down_two, pairs_two, rest_two)
    dy = after(dy, down_two.out, pairs_two.out, rest_two.out)
    down_one = wgrad("down", lefts=[flat(kept["act"])], rights=[flat(dy)], chunk=wide)
    down_one, df = join((down_one, df), up_two, down_two)
    down_one = Sum(down_one, down_order, bits)
    advance(up_two, down_two)
    df = after(df, down_one.out, up_two.out, down_two.out)
    up_one = wgrad("up", lefts=[flat(kept["hid"])], rights=[flat(df)], chunk=wide // 2)
    up_one, dc = join((up_one, dc), down_one, down_two)
    up_one = Sum(up_one, late_order, bits)
    advance(down_one)
    facts = [facts_of(seq_index, seq_index ^ 1, start) for start, _ in cuts]
    dc = after(dc, up_one.out, down_one.out)
    att = attention_back_call(0, False, 0, 2, facts[0], kept, dc, None)
    vec_q = att[3]
    att, dc = join((att, dc), up_one, up_two, pairs_two, rest_two)
    advance(up_one, up_two, pairs_two, rest_two)
    dc = after(dc, up_one.out, up_two.out, pairs_two.out, rest_two.out)
    att = attention_back_call(0, False, 2, seqs - 2, facts[1], kept, dc, att)
    vec_q += att[3]
    att, da = join((att, da), down_one, up_two, pairs_two, rest_two)
    advance(down_one, up_two, pairs_two, rest_two)
    got = swapped_2(att[2], "seq", 0)
    da = after(da, att[2], down_one.out)
    rest_one = wgrad("rest", lefts=[flat(kept["ctx"]), flat(tokens)], rights=[flat(da), flat(att[0])], chunk=wide // 2)
    rest_one, got, dz1 = after((rest_one, got, dz1))
    rest_one = Sum(rest_one, four_order, bits)
    pair = (att[1].astype(FAST) + got.astype(FAST)).astype(LOW)
    pair = after(pair, rest_one.out)
    pairs_one = wgrad("pair", lefts=[flat(tokens)] * 2, rights=[flat(pair[:, 0]), flat(pair[:, 1])], chunk=wide // 2)
    pairs_one, dz1 = join((pairs_one, dz1), rest_one, up_one)
    pairs_one = Sum(pairs_one, last_orders[0], bits)
    advance(rest_one, up_one)
    dz1 = after(dz1, pairs_one.out, rest_one.out, up_one.out)
    ends = input_back_call(0, False, 0, seqs, att[0], pair, None, dz1, back_weights, None)
    ends, vec_q = join((ends, vec_q), pairs_one, down_one)
    vec_one = (vec_one, vec_q, ends[1])
    pieces = pairs_one.split(last_orders)
    advance(down_one)
    vectors = both_sums([vec_one, vec_two])
    live = pieces + [rest_one, down_one, up_one, pairs_two, rest_two, down_two, up_two]
    while any(one.got is not None for one in live):
        advance(*live)
    pairs_one = jnp.concatenate([one.value for one in pieces], axis=-1)
    sums = [
        (down_one.value[0], up_one.value[0], rest_one.value, pairs_one),
        (down_two.value[0], up_two.value[0], rest_two.value, pairs_two.value),
    ]
    return (final, ends[0]) + gathered(sums, vectors, devices)


def after(value, *others):
    return lax.optimization_barrier((value, others))[0]


def digit_list():
    return [
        (axis, bit) for axis in ("seq", "batch") for bit in range(lax.axis_size(axis).bit_length() - 1)
    ]


def digit_orders():
    low = lax.axis_size("seq").bit_length() - 1
    high = lax.axis_size("batch").bit_length() - 1
    core, across = ("seq", 0), [("seq", bit) for bit in range(1, low)]
    near, far, late = [("batch", 0)], [("batch", 1)], [("batch", bit) for bit in range(2, high)]
    first = [core] + near + far + across + late
    second = [core] + far + near + across + late
    third = [core] + across + near + far + late
    return first, second, third, (third, [core] + near + far + across + late, [core] + far + across + near + late)


def join(values, *sums):
    live = [one for one in sums if one.got is not None]
    values, gots = lax.optimization_barrier((values, [one.got for one in live]))
    for one, got in zip(live, gots, strict=True):
        one.got = got
    return values


def advance(*sums):
    live = [one for one in sums if one.got is not None]
    if not live:
        return
    for one in live:
        if not one.order:
            one.value = (one.value.astype(FAST) + one.got.astype(FAST))[:, 0]
            one.got = None
    live = [one for one in live if one.got is not None]
    if not live:
        return
    plan, routes = [], []
    for one in live:
        axis, bit = digit = one.order.pop(0)
        above = one.digits.index(digit)
        one.digits.remove(digit)
        plan.append((1 << above, 1 << len(one.digits) - above, digit_list().index(digit)))
        routes.append((axis, bit))
    halves = step_call([one.value for one in live], [one.got for one in live], tuple(plan), live[0].bits)
    for i, one in enumerate(live):
        one.value, one.out = halves[2 * i], halves[2 * i + 1]
        one.got = swapped_2(one.out, *routes[i])


class Sum:
    def __init__(self, halves, order, bits):
        self.value, self.out = halves
        self.bits = bits
        self.digits = list(reversed(digit_list()))[:-1]
        self.order = list(order[1:])
        self.got = swapped_2(self.out, *order[0])

    def split(self, orders):
        value = (self.value.astype(FAST) + self.got.astype(FAST)).astype(LOW)
        pieces = []
        width = value.shape[-1] // len(orders)
        for i, order in enumerate(orders):
            axis, bit = digit = order[1]
            place = 1 + self.digits.index(digit)
            piece = object.__new__(Sum)
            piece.bits = self.bits
            piece.digits, piece.order = [one for one in self.digits if one != digit], list(order[2:])
            part = value[..., i * width : (i + 1) * width]
            part = part.reshape(part.shape[:1] + (2,) * len(self.digits) + part.shape[2:])
            shape = (part.shape[0], -1) + part.shape[-2:]
            mine = lax.axis_index(axis) >> bit & 1
            piece.out = lax.dynamic_index_in_dim(part, 1 - mine, place, keepdims=False).reshape(shape)
            piece.value = lax.dynamic_index_in_dim(part, mine, place, keepdims=False).reshape(shape)
            piece.got = swapped_2(piece.out, axis, bit)
            pieces.append(piece)
        return pieces


def both_sums(layers):
    value = []
    for vec, vec_q, vec_v in layers:
        value.append(jnp.concatenate([vec_q[:1], vec_v[:1], vec[2:]]))
    value = jnp.stack(value)
    for axis in ("seq", "batch"):
        for bit in range(lax.axis_size(axis).bit_length() - 1):
            value = value + swapped_2(value, axis, bit)
    return value


VECTORS = (1, 4, 6, 7, 8, 12, 13, 14)


def gathered(sums, vectors, devices):
    outs = [None] * 15
    outs[0] = jnp.stack([one[2][1] for one in sums])
    outs[2] = jnp.stack([one[3][0] for one in sums])
    outs[3] = jnp.stack([one[3][1] for one in sums])
    outs[5] = jnp.stack([one[2][0] for one in sums])
    outs[9] = jnp.stack([one[1] for one in sums])
    outs[11] = jnp.stack([one[0] for one in sums])
    mine = lax.axis_index("batch") * lax.axis_size("seq") + lax.axis_index("seq")
    width = vectors.shape[2] // devices
    small = lax.dynamic_slice_in_dim(vectors[:, :8], mine * width, width, axis=2)
    for place, which in enumerate(VECTORS):
        outs[which] = small[:, place]
    large = vectors[:, 8:].reshape(vectors.shape[0], -1)
    width = large.shape[1] // devices
    outs[10] = lax.dynamic_slice_in_dim(large, mine * width, width, axis=1)
    return tuple(outs)


def solution(mesh):
    in_specs = (
        P("batch", "seq", None),
        P("batch"),
        P(),
        P(),
        P(),
        P(),
        P(),
        P(),
        P(),
        P(),
        P(),
        P(),
        P(),
        P(),
        P(),
        P(),
        P(),
        P("batch", "seq", None),
    )
    out_specs = (
        P("batch", "seq", None),
        P("batch", "seq", None),
        P(None, ("batch", "seq"), None),
        P(None, ("batch", "seq")),
        P(None, ("batch", "seq"), None),
        P(None, ("batch", "seq"), None),
        P(None, ("batch", "seq")),
        P(None, ("batch", "seq"), None),
        P(None, ("batch", "seq")),
        P(None, ("batch", "seq")),
        P(None, ("batch", "seq")),
        P(None, ("batch", "seq"), None),
        P(None, ("batch", "seq")),
        P(None, ("batch", "seq"), None),
        P(None, ("batch", "seq")),
        P(None, ("batch", "seq")),
        P(None, ("batch", "seq")),
    )
    return jax.shard_map(local, mesh=mesh, in_specs=in_specs, out_specs=out_specs, check_vma=False)
```

time: 1400 us -> 494 us (0.35)
  waiting for transfers between devices: 820 us -> 53.2 us
  Pallas kernels: 0 us -> 313 us
  matrix products: 244 us -> 0 us
  other arithmetic: 146 us -> 17.9 us
  local copies, waits for them, and re-layouts: 107 us -> 30.6 us
  starting transfers between devices: 7.87 us -> 68.2 us
  blocking collectives: 44.2 us -> 0 us
  between operations: 16 us -> 1.93 us
    reduce_scatter x3 -> x0, waiting for transfers between devices: 532 us -> none  [the longest x1 212 us: local(): lax.psum_scatter(paired[9], ('batch', 'seq'), scatter_dimension=1, tiled=...]
    pallas_call x0 -> x34, Pallas kernels: none -> 313 us  [the longest x4 91.1 us: forward_call(): pl.pallas_call(partial(forward_kernel, layer, swapped), grid=(count,), in...]
    dot_general x48 -> x0, matrix products: 244 us -> none  [the longest x12 68.1 us: project_back(): jnp.einsum('ste,de->std', grad_value, weight, preferred_element_type=jnp....]
    unnamed x7 -> x0, waiting for transfers between devices: 198 us -> none
    convert_element_type x14 -> x3, other arithmetic: 82.3 us -> 2.75 us  [the longest x1 1.55 us: split(): value = (self.value.astype(FAST) + self.got.astype(FAST)).astype(LOW)]
    ppermute x12 -> x64, starting transfers between devices: 7.28 us -> 68.2 us  [swapped_2(): lax.ppermute(value, axis, [(i, i ^ 1 << bit) for i in range(lax.axis_size...]
    unnamed x1 -> x0, blocking collectives: 44.2 us -> none
    unnamed x330 -> x115, local copies, waits for them, and re-layouts: 53.7 us -> 12 us
  transfers between devices with their start and end apart: 17 -> 64, of which waited for: 8 -> 12; matrix products, arithmetic and copies ran while one was open for 14% -> 7% of each run, Pallas kernels for 0% -> 47%
where the time goes in v2:
time: 494 us; the launch traced here: 485 us
  Pallas kernels  313 us (63%)
  starting transfers between devices  68.2 us (14%)
  waiting for transfers between devices  53.2 us (11%)
  local copies, waits for them, and re-layouts  30.6 us (6%)
  other arithmetic  17.9 us (4%)
    pallas_call x4, Pallas kernels, forward_call(): pl.pallas_call(partial(forward_kernel, layer, swapped), grid=(count,), in...  91.1 us
    ppermute x64, starting transfers between devices, swapped_2(): lax.ppermute(value, axis, [(i, i ^ 1 << bit) for i in range(lax.axis_size...  68.2 us
    pallas_call x8, Pallas kernels, wgrad_call(): pl.pallas_call(partial(wgrad_kernel, count), grid=(steps,), in_specs=[pl....  55.8 us
    pallas_call x13, Pallas kernels, step_call(): pl.pallas_call(partial(step_kernel, plan), grid=(steps,), in_specs=[pl.Bl...  54.2 us
    ppermute x64, waiting for transfers between devices, swapped_2(): lax.ppermute(value, axis, [(i, i ^ 1 << bit) for i in range(lax.axis_size...  53.2 us
    pallas_call x4, Pallas kernels, attention_back_call(): pl.pallas_call(partial(attention_back_kernel, split), grid=(count,), in_s...  50.3 us
    pallas_call x2, Pallas kernels, ff_back_call(): pl.pallas_call(partial(ff_back_kernel, layer), grid=(seqs,), in_specs=in_...  39.2 us
    pallas_call x3, Pallas kernels, input_back_call(): pl.pallas_call(partial(input_back_kernel, layer, split), grid=(count,), i...  22 us
  transfers between devices with their start and end apart: 64, of which 12 were waited for; matrix products, arithmetic and copies ran while one was open for 7% of the time, Pallas kernels for 47%

profile of v2, /device:TPU:0, one launch (start us, length us, event | category | flops | bytes accessed | tf_op | source)
XLA Modules:
  0.0 484.7 jit_solution(10837395065071963063)
XLA Ops:
  11.0 28.7 %layer_forward_0.2 = (bf16[2,256,768]{2,1,0:T(8,128)(2,1)}, f32[3,256,768]{2,1,0:T(8,128)}, bf16[3,256,768]{2,1,0:T(8,128)(2,1)}, bf16[3,256,768]{2,1,0:T(8,128)...) custom-call(s32[6]{0:T(128)} %get-tuple-element.579.facts, ...), custom_call_target="tpu_custom_call" | custom-call | flops 321999994880 | bytes 1 | tf_op jit(solution)/shard_map/layer_forward_0/pallas_call | solution.py:207
  39.7 2.1 fusion.4
  41.8 2.5 collective-permute-start.4
  44.3 16.5 %layer_forward_0.3 = (bf16[1,256,768]{2,1,0:T(8,128)(2,1)}, f32[3,256,768]{2,1,0:T(8,128)}, bf16[3,256,768]{2,1,0:T(8,128)(2,1)}, bf16[3,256,768]{2,1,0:T(8,128)...) custom-call(s32[6]{0:T(128)} %pad_add_fusion.1.facts, ...), custom_call_target="tpu_custom_call", output_to_operand_aliasing={{1}: (12, {}), {2}: (13, {}), {3}: (14, {}), {4}: (15, {}),... | custom-call | flops 160999997440 | bytes 1 | tf_op jit(solution)/shard_map/layer_forward_0/pallas_call | solution.py:207
  60.9 2.0 collective-permute-start.1
  64.2 8.9 %collective-permute-done.2 = bf16[1,256,768]{2,1,0:T(8,128)(2,1)S(1)} collective-permute-done((bf16[1,256,768]{2,1,0:T(8,128)(2,1)}, bf16[1,256,768]{2,1,0:T(8,128)(2,1)S(1)}, u32[]{:S(2)}, u32[]{:S(2)}) %collective-permute-start.2) | collective-permute-done | bytes 393248 | tf_op jit(solution)/shard_map/ppermute | solution.py:19
  73.1 7.7 %collective-permute-done.1 = bf16[1,256,768]{2,1,0:T(8,128)(2,1)S(1)} collective-permute-done((bf16[1,256,768]{2,1,0:T(8,128)(2,1)S(1)}, bf16[1,256,768]{2,1,0:T(8,128)(2,1)S(1)}, u32[]{:S(2)}, u32[]{:S(2)}) %collective-permute-start.1) | collective-permute-done | bytes 393248 | tf_op jit(solution)/shard_map/ppermute | solution.py:19
  83.1 16.6 %layer_forward_1.2 = (bf16[1,256,768]{2,1,0:T(8,128)(2,1)}, bf16[3,256,768]{2,1,0:T(8,128)(2,1)}, bf16[3,256,768]{2,1,0:T(8,128)(2,1)}, bf16[3,256,768]{2,1,0:T(...) custom-call(s32[6]{0:T(128)} %get-tuple-element.612.facts, ...), custom_call_target="tpu_custom_call" | custom-call | flops 160999997440 | bytes 1 | tf_op jit(solution)/shard_map/layer_forward_1/pallas_call | solution.py:207
  99.7 29.3 %layer_forward_1.3 = (bf16[2,256,768]{2,1,0:T(8,128)(2,1)}, bf16[3,256,768]{2,1,0:T(8,128)(2,1)}, bf16[3,256,768]{2,1,0:T(8,128)(2,1)}, bf16[3,256,768]{2,1,0:T(...) custom-call(s32[6]{0:T(128)} %get-tuple-element.613.facts, ...), custom_call_target="tpu_custom_call", output_to_operand_aliasing={{1}: (12, {}), {2}: (13, {}), {3}: (14, {}), {4}: (15, {}),... | custom-call | flops 321999994880 | bytes 1 | tf_op jit(solution)/shard_map/layer_forward_1/pallas_call | solution.py:207
  129.1 19.8 %ff_back_1.1 = (bf16[3,256,768]{2,1,0:T(8,128)(2,1)}, bf16[3,256,3072]{2,1,0:T(8,128)(2,1)}, f32[3,256,768]{2,1,0:T(8,128)}, bf16[3,256,768]{2,1,0:T(8,128)(2,1)...) custom-call(bf16[3,256,768]{2,1,0:T(8,128)(2,1)} %top_grad.1, bf16[3,256,768]{2,1,0:T(8,128)(2,1)} %get-tuple-element.342.n2, ...), custom_call_target="tpu_custom_call" | custom-call | flops 218500005888 | bytes 1 | tf_op jit(solution)/shard_map/ff_back_1/pallas_call | solution.py:307
  148.8 8.2 %wgrad_down.2 = (bf16[1,16,96,768]{3,2,1,0:T(8,128)(2,1)}, bf16[1,16,96,768]{3,2,1,0:T(8,128)(2,1)}) custom-call(s32[5]{0:T(128)} %stack.110.place_ref.bits, bf16[768,3072]{1,0:T(8,128)(2,1)} %bitcast.143, bf16[768,768]{1,0:T(8,128)(2,1)} %bitcast.157), custom_call_target="tpu_custom_call" | custom-call | flops 88763809792 | bytes 1 | tf_op jit(solution)/shard_map/wgrad_down/pallas_call | solution.py:501
  157.5 15.9 %attention_back_1.2 = (bf16[3,256,768]{2,1,0:T(8,128)(2,1)}, bf16[3,2,256,768]{3,2,1,0:T(8,128)(2,1)}, bf16[2,2,256,768]{3,2,1,0:T(8,128)(2,1)}, f32[8,768]{1,0:T(8,128)}) custom-call(s32[6]{0:T(128)} %get-tuple-element.612.facts, bf16[3,256,768]{2,1,0:T(8,128)(2,1)} %get-tuple-element.338.q, bf16[3,512,768]{2,1,0:T(8,128)(2,1)} %get-tuple-element.339.k, ...), custom_call_target="tpu_custom_call" | custom-call | flops 184000004096 | bytes 1 | tf_op jit(solution)/shard_map/attention_back_1/pallas_call | solution.py:392
  174.0 5.2 %exchange_step.13 = (bf16[1,8,96,768]{3,2,1,0:T(8,128)(2,1)}, bf16[1,8,96,768]{3,2,1,0:T(8,128)(2,1)}) custom-call(s32[5]{0:T(128)} %stack.110.place_ref.bits, bf16[1,16,96,768]{3,2,1,0:T(8,128)(2,1)} %get-tuple-element.352.refs_0_, bf16[1,16,96,768]{3,2,1,0:T(8,128)(2,1)} %collective-permute-done.6.refs_1_), custom_call_target="tpu_custom_call" | custom-call | flops 38631903232 | bytes 1 | tf_op jit(solution)/shard_map/exchange_step/pallas_call | solution.py:542
  180.8 9.3 %attention_back_1.3 = (bf16[3,256,768]{2,1,0:T(8,128)(2,1)}, bf16[3,2,256,768]{3,2,1,0:T(8,128)(2,1)}, bf16[1,2,256,768]{3,2,1,0:T(8,128)(2,1)}, f32[8,768]{1,0:T(8,128)}) custom-call(s32[6]{0:T(128)} %get-tuple-element.614.facts, bf16[3,256,768]{2,1,0:T(8,128)(2,1)} %get-tuple-element.338.q, ...), custom_call_target="tpu_custom_call", output_to_operand_aliasing={{0}: (6, {}), {1}: (7, {})} | custom-call | flops 92000002048 | bytes 1 | tf_op jit(solution)/shard_map/attention_back_1/pallas_call | solution.py:392
  192.6 7.6 %input_back_1.2 = (f32[3,256,768]{2,1,0:T(8,128)}, bf16[3,2,256,768]{3,2,1,0:T(8,128)(2,1)}, bf16[2,256,768]{2,1,0:T(8,128)(2,1)}, f32[8,768]{1,0:T(8,128)}) custom-call(bf16[3,256,768]{2,1,0:T(8,128)(2,1)} %get-tuple-element.367.dq, bf16[3,2,256,768]{3,2,1,0:T(8,128)(2,1)} %get-tuple-element.368.near, bf16[2,2,256,768]{3,2,1,0:T(8,128)(2,1)} %copy-done.29, ...), custom_call_target="tpu_custom_call" | custom-call | flops 92000002048 | bytes 1 | tf_op jit(solution)/shard_map/input_back_1/pallas_call | solution.py:466
  200.3 8.7 %wgrad_up.2 = (bf16[1,16,24,3072]{3,2,1,0:T(8,128)(2,1)}, bf16[1,16,24,3072]{3,2,1,0:T(8,128)(2,1)}) custom-call(s32[5]{0:T(128)} %stack.110.place_ref.bits, bf16[768,768]{1,0:T(8,128)(2,1)} %bitcast.152, bf16[768,3072]{1,0:T(8,128)(2,1)} %bitcast.142), custom_call_target="tpu_custom_call" | custom-call | flops 88763809792 | bytes 1 | tf_op jit(solution)/shard_map/wgrad_up/pallas_call | solution.py:501
  209.7 5.8 %input_back_1.3 = (f32[3,256,768]{2,1,0:T(8,128)}, bf16[3,2,256,768]{3,2,1,0:T(8,128)(2,1)}, bf16[1,256,768]{2,1,0:T(8,128)(2,1)}, f32[8,768]{1,0:T(8,128)}) custom-call(bf16[3,256,768]{2,1,0:T(8,128)(2,1)} %get-tuple-element.367.dq, bf16[3,2,256,768]{3,2,1,0:T(8,128)(2,1)} %get-tuple-element.368.near, ...), custom_call_target="tpu_custom_call", output_to_operand_aliasing={{0}: (7, {}), {1}: (8, {})} | custom-call | flops 57500000256 | bytes 1 | tf_op jit(solution)/shard_map/input_back_1/pallas_call | solution.py:466
  217.1 5.6 %wgrad_rest.2 = (bf16[2,16,24,768]{3,2,1,0:T(8,128)(2,1)}, bf16[2,16,24,768]{3,2,1,0:T(8,128)(2,1)}) custom-call(s32[5]{0:T(128)} %stack.110.place_ref.bits, bf16[768,768]{1,0:T(8,128)(2,1)} %bitcast.151, bf16[768,768]{1,0:T(8,128)(2,1)} %bitcast.153, bf16[768,768]{1,0:T(8,128)(2,1)} %bitcast.146, bf16[768,768]{1,0:T(8,128)(2,1)} %bitcast.156), custom_call_target="tpu_custom_call" | custom-call | flops 61631905792 | bytes 1 | tf_op jit(solution)/shard_map/wgrad_rest/pallas_call | solution.py:501
  225.5 5.9 %exchange_step.14 = (bf16[1,8,24,3072]{3,2,1,0:T(8,128)(2,1)}, bf16[1,8,24,3072]{3,2,1,0:T(8,128)(2,1)}, bf16[1,4,96,768]{3,2,1,0:T(8,128)(2,1)}, bf16[1,4,96,768]{3,2,1,0:T(8,128)(2,1)}) custom-call(s32[5]{0:T(128)} %stack.110.place_ref.bits, bf16[1,16,24,3072]{3,2,1,0:T(8,128)(2,1)} %get-tuple-element.400.refs_0_, bf16[1,16,24,3072]{3,2,1,0:T(8,128)(2,1)} %copy-done.27, ...), custom_call_target="tpu_custom_call" | custom-call | flops 52197855232 | bytes 1 | tf_op jit(solution)/shard_map/exchange_step/pallas_call | solution.py:542
  235.1 5.5 %wgrad_pair.2 = (bf16[2,16,24,768]{3,2,1,0:T(8,128)(2,1)}, bf16[2,16,24,768]{3,2,1,0:T(8,128)(2,1)}) custom-call(s32[5]{0:T(128)} %stack.110.place_ref.bits, bf16[768,768]{1,0:T(8,128)(2,1)} %bitcast.149, bf16[768,768]{1,0:T(8,128)(2,1)} %bitcast.150, bf16[768,768]{1,0:T(8,128)(2,1)} %bitcast.110, bf16[768,768]{1,0:T(8,128)(2,1)} %bitcast.109), custom_call_target="tpu_custom_call" | custom-call | flops 61631905792 | bytes 1 | tf_op jit(solution)/shard_map/wgrad_pair/pallas_call | solution.py:501
  241.6 3.7 exchange_step.15
  245.9 2.9 convert_add_fusion.top_grad
  248.7 19.5 %ff_back_0.1 = (bf16[3,256,768]{2,1,0:T(8,128)(2,1)}, bf16[3,256,3072]{2,1,0:T(8,128)(2,1)}, f32[3,256,768]{2,1,0:T(8,128)}, bf16[3,256,768]{2,1,0:T(8,128)(2,1)...) custom-call(f32[3,256,768]{2,1,0:T(8,128)} %convert_add_fusion.top_grad, bf16[3,256,768]{2,1,0:T(8,128)(2,1)} %get-tuple-element.419.n2, ...), custom_call_target="tpu_custom_call" | custom-call | flops 218500005888 | bytes 1 | tf_op jit(solution)/shard_map/ff_back_0/pallas_call | solution.py:307
  268.3 4.5 exchange_step.16
  276.4 8.2 %wgrad_down.3 = (bf16[1,16,96,768]{3,2,1,0:T(8,128)(2,1)}, bf16[1,16,96,768]{3,2,1,0:T(8,128)(2,1)}) custom-call(s32[5]{0:T(128)} %stack.110.place_ref.bits, bf16[768,3072]{1,0:T(8,128)(2,1)} %bitcast.144, bf16[768,768]{1,0:T(8,128)(2,1)} %bitcast.148), custom_call_target="tpu_custom_call" | custom-call | flops 88763809792 | bytes 1 | tf_op jit(solution)/shard_map/wgrad_down/pallas_call | solution.py:501
  285.9 3.6 exchange_step.17
  289.5 2.6 collective-permute-start.20
  292.6 8.4 %wgrad_up.3 = (bf16[1,16,24,3072]{3,2,1,0:T(8,128)(2,1)}, bf16[1,16,24,3072]{3,2,1,0:T(8,128)(2,1)}) custom-call(s32[5]{0:T(128)} %stack.110.place_ref.bits, bf16[768,768]{1,0:T(8,128)(2,1)} %bitcast.155, bf16[768,3072]{1,0:T(8,128)(2,1)} %bitcast.141), custom_call_target="tpu_custom_call" | custom-call | flops 88763809792 | bytes 1 | tf_op jit(solution)/shard_map/wgrad_up/pallas_call | solution.py:501
  302.6 4.7 exchange_step.18
  307.8 15.9 %attention_back_0.2 = (bf16[3,256,768]{2,1,0:T(8,128)(2,1)}, bf16[3,2,256,768]{3,2,1,0:T(8,128)(2,1)}, bf16[3,2,256,768]{3,2,1,0:T(8,128)(2,1)}, f32[8,768]{1,0:T(8,128)}) custom-call(s32[6]{0:T(128)} %get-tuple-element.579.facts, bf16[3,256,768]{2,1,0:T(8,128)(2,1)} %get-tuple-element.332.q, bf16[3,512,768]{2,1,0:T(8,128)(2,1)} %get-tuple-element.333.k, ...), custom_call_target="tpu_custom_call" | custom-call | flops 184000004096 | bytes 1 | tf_op jit(solution)/shard_map/attention_back_0/pallas_call | solution.py:392
  324.5 6.1 %exchange_step.19 = (bf16[1,8,24,3072]{3,2,1,0:T(8,128)(2,1)}, bf16[1,8,24,3072]{3,2,1,0:T(8,128)(2,1)}, bf16[1,2,24,3072]{3,2,1,0:T(8,128)(2,1)}, bf16[1,2,24,3...) custom-call(s32[5]{0:T(128)} %stack.110.place_ref.bits, ...), custom_call_target="tpu_custom_call" | custom-call | flops 55589343232 | bytes 1 | tf_op jit(solution)/shard_map/exchange_step/pallas_call | solution.py:542
  335.8 9.3 %attention_back_0.3 = (bf16[3,256,768]{2,1,0:T(8,128)(2,1)}, bf16[3,2,256,768]{3,2,1,0:T(8,128)(2,1)}, bf16[3,2,256,768]{3,2,1,0:T(8,128)(2,1)}, f32[8,768]{1,0:T(8,128)}) custom-call(s32[6]{0:T(128)} %pad_add_fusion.1.facts, bf16[3,256,768]{2,1,0:T(8,128)(2,1)} %get-tuple-element.332.q, ...), custom_call_target="tpu_custom_call", output_to_operand_aliasing={{0}: (6, {}), {1}: (7, {}), {2}: (8, {})} | custom-call | flops 92000002048 | bytes 1 | tf_op jit(solution)/shard_map/attention_back_0/pallas_call | solution.py:392
  347.2 4.0 exchange_step.20
  353.7 5.7 %wgrad_rest.3 = (bf16[2,16,24,768]{3,2,1,0:T(8,128)(2,1)}, bf16[2,16,24,768]{3,2,1,0:T(8,128)(2,1)}) custom-call(s32[5]{0:T(128)} %stack.110.place_ref.bits, bf16[768,768]{1,0:T(8,128)(2,1)} %bitcast.154, bf16[768,768]{1,0:T(8,128)(2,1)} %bitcast.136, bf16[768,768]{1,0:T(8,128)(2,1)} %bitcast.145, bf16[768,768]{1,0:T(8,128)(2,1)} %bitcast.147), custom_call_target="tpu_custom_call" | custom-call | flops 61631905792 | bytes 1 | tf_op jit(solution)/shard_map/wgrad_rest/pallas_call | solution.py:501
  359.4 20.6 %collective-permute-done.51 = bf16[2,1,24,768]{3,2,1,0:T(8,128)(2,1)S(1)} collective-permute-done((bf16[2,1,24,768]{3,2,1,0:T(8,128)(2,1)}, bf16[2,1,24,768]{3,2,1,0:T(8,128)(2,1)S(1)}, u32[]{:S(2)}, u32[]{:S(2)}) %collective-permute-start.51) | collective-permute-done | bytes 73760 | tf_op jit(solution)/shard_map/ppermute | solution.py:19
  383.4 5.6 %wgrad_pair.3 = (bf16[2,16,24,768]{3,2,1,0:T(8,128)(2,1)}, bf16[2,16,24,768]{3,2,1,0:T(8,128)(2,1)}) custom-call(s32[5]{0:T(128)} %stack.110.place_ref.bits, bf16[768,768]{1,0:T(8,128)(2,1)} %bitcast.137, bf16[768,768]{1,0:T(8,128)(2,1)} %bitcast.138, bf16[768,768]{1,0:T(8,128)(2,1)} %bitcast.112, bf16[768,768]{1,0:T(8,128)(2,1)} %bitcast.111), custom_call_target="tpu_custom_call" | custom-call | flops 61631905792 | bytes 1 | tf_op jit(solution)/shard_map/wgrad_pair/pallas_call | solution.py:501
  390.0 4.5 exchange_step.21
  395.5 8.6 %input_back_0.1 = (f32[3,256,768]{2,1,0:T(8,128)}, f32[8,768]{1,0:T(8,128)}) custom-call(bf16[3,256,768]{2,1,0:T(8,128)(2,1)} %get-tuple-element.488.dq, bf16[3,2,256,768]{3,2,1,0:T(8,128)(2,1)} %copy-done, f32[3,256,768]{2,1,0:T(8,128)} %get-tuple-element.520.refs_0_, bf16[2,768,768]{2,1,0:T(8,128)(2,1)} %refs_1_.13, bf16[2,768,768]{2,1,0:T(8,128)(2,1)} %refs_2_.17, ...), custom_call_target="tpu_custom_call" | custom-call | flops 126500003840 | bytes 1 | tf_op jit(solution)/shard_map/input_back_0/pallas_call | solution.py:466
  404.2 3.4 exchange_step.22
  414.3 4.5 collective-permute-done.53
  426.1 3.3 collective-permute-start.62
  430.8 4.1 exchange_step.23
  434.9 3.3 collective-permute-start.60
  445.4 4.0 collective-permute-done.56
  454.9 2.6 exchange_step.24
  460.8 6.4 %collective-permute-start.48 = (bf16[2,2,24,256]{3,2,1,0:T(8,128)(2,1)}, bf16[2,2,24,256]{3,2,1,0:T(8,128)(2,1)S(1)}, u32[]{:S(2)}, u32[]{:S(2)}) collective-permute-start(bf16[2,2,24,256]{3,2,1,0:T(8,128)(2,1)} %get-tuple-element.549), channel_id=1, source_target_pairs={{0,4},{4,0},{8,12},{12,8},{16,20},{20,16},{24,28},{28,24},{1,5},{5... | collective-permute-start | bytes 147464 | tf_op jit(solution)/shard_map/ppermute | solution.py:19
  468.0 2.2 collective-permute-start.61
  471.0 1.9 exchange_step.25
  (293 shorter events, 97.0 us)
Async XLA Ops:
  0.7 9.3 %collective-permute-start = (bf16[3,256,768]{2,1,0:T(8,128)(2,1)}, bf16[3,256,768]{2,1,0:T(8,128)(2,1)S(1)}, u32[]{:S(2)}, u32[]{:S(2)}) collective-permute-start(bf16[3,256,768]{2,1,0:T(8,128)(2,1)} %top.3), channel_id=1, source_target_pairs={{0,1},{1,0},{2,3},{3,2},{4,5},{5,4},{6,7},{7,6},{8,9},{9,8},{10,11... | collective-permute-start | bytes 3538952 | tf_op jit(solution)/shard_map/ppermute | solution.py:19
  41.8 21.7 %collective-permute-start.4 = (bf16[1,256,768]{2,1,0:T(8,128)(2,1)}, bf16[1,256,768]{2,1,0:T(8,128)(2,1)}, u32[]{:S(2)}, u32[]{:S(2)}) collective-permute-start(bf16[1,256,768]{2,1,0:T(8,128)(2,1)} %get-tuple-element.588), channel_id=1, source_target_pairs={{0,2},{1,3},{2,0},{3,1},{4,6},{5,7},{6,4},{7,5},{8,10},{9,11},{10,... | collective-permute-start | bytes 1179656 | tf_op jit(solution)/shard_map/ppermute | solution.py:19
  60.8 12.2 %collective-permute-start.2 = (bf16[1,256,768]{2,1,0:T(8,128)(2,1)}, bf16[1,256,768]{2,1,0:T(8,128)(2,1)S(1)}, u32[]{:S(2)}, u32[]{:S(2)}) collective-permute-start(bf16[1,256,768]{2,1,0:T(8,128)(2,1)} %get-tuple-element.313), channel_id=1, source_target_pairs={{0,2},{1,3},{2,0},{3,1},{4,6},{5,7},{6,4},{7,5},{8,10},{9,11},{10,... | collective-permute-start | bytes 1179656 | tf_op jit(solution)/shard_map/ppermute | solution.py:19
  60.9 19.8 %collective-permute-start.1 = (bf16[1,256,768]{2,1,0:T(8,128)(2,1)S(1)}, bf16[1,256,768]{2,1,0:T(8,128)(2,1)S(1)}, u32[]{:S(2)}, u32[]{:S(2)}) collective-permute-start(bf16[1,256,768]{2,1,0:T(8,128)(2,1)S(1)} %copy-done.8), channel_id=1, source_target_pairs={{0,2},{1,3},{2,0},{3,1},{4,6},{5,7},{6,4},{7,5},{8,10},{9,11},{10,... | collective-permute-start | bytes 1179656 | tf_op jit(solution)/shard_map/ppermute | solution.py:19
  63.6 18.8 %collective-permute-start.5 = (bf16[1,256,768]{2,1,0:T(8,128)(2,1)}, bf16[1,256,768]{2,1,0:T(8,128)(2,1)S(1)}, u32[]{:S(2)}, u32[]{:S(2)}) collective-permute-start(bf16[1,256,768]{2,1,0:T(8,128)(2,1)} %collective-permute-done.4.near), channel_id=1, source_target_pairs={{0,1},{1,0},{2,3},{3,2},{4,5},{5,4},{6,7},{7,6},{8,9},{9,8},{10,11... | collective-permute-start | bytes 1179656 | tf_op jit(solution)/shard_map/ppermute | solution.py:19
  82.3 17.4 %collective-permute-start.3 = (bf16[2,256,768]{2,1,0:T(8,128)(2,1)}, bf16[2,256,768]{2,1,0:T(8,128)(2,1)}, u32[]{:S(2)}, u32[]{:S(2)}) collective-permute-start(bf16[2,256,768]{2,1,0:T(8,128)(2,1)} %constant_dynamic-update-slice_fusion.near), channel_id=1, source_target_pairs={{0,1},{1,0},{2,3},{3,2},{4,5},{5,4},{6,7},{7,6},{8,9},{9,8},{10,11... | collective-permute-start | bytes 2359304 | tf_op jit(solution)/shard_map/ppermute | solution.py:19
  157.0 17.0 %collective-permute-start.6 = (bf16[1,16,96,768]{3,2,1,0:T(8,128)(2,1)}, bf16[1,16,96,768]{3,2,1,0:T(8,128)(2,1)}, u32[]{:S(2)}, u32[]{:S(2)}) collective-permute-start(bf16[1,16,96,768]{3,2,1,0:T(8,128)(2,1)} %get-tuple-element.350), channel_id=1, source_target_pairs={{0,1},{1,0},{2,3},{3,2},{4,5},{5,4},{6,7},{7,6},{8,9},{9,8},{10,11... | collective-permute-start | bytes 7077896 | tf_op jit(solution)/shard_map/ppermute | solution.py:19
  174.0 17.4 %collective-permute-start.7 = (bf16[2,2,256,768]{3,2,1,0:T(8,128)(2,1)}, bf16[2,2,256,768]{3,2,1,0:T(8,128)(2,1)S(1)}, u32[]{:S(2)}, u32[]{:S(2)}) collective-permute-start(bf16[2,2,256,768]{3,2,1,0:T(8,128)(2,1)} %get-tuple-element.359), channel_id=1, source_target_pairs={{0,1},{1,0},{2,3},{3,2},{4,5},{5,4},{6,7},{7,6},{8,9},{9,8},{10,11... | collective-permute-start | bytes 4718600 | tf_op jit(solution)/shard_map/ppermute | solution.py:19
  179.2 44.9 %collective-permute-start.10 = (bf16[1,8,96,768]{3,2,1,0:T(8,128)(2,1)}, bf16[1,8,96,768]{3,2,1,0:T(8,128)(2,1)}, u32[]{:S(2)}, u32[]{:S(2)}) collective-permute-start(bf16[1,8,96,768]{3,2,1,0:T(8,128)(2,1)} %get-tuple-element.358), channel_id=1, source_target_pairs={{0,4},{4,0},{8,12},{12,8},{16,20},{20,16},{24,28},{28,24},{1,5},{5... | collective-permute-start | bytes 3538952 | tf_op jit(solution)/shard_map/ppermute | solution.py:19
  208.9 15.1 %collective-permute-start.9 = (bf16[1,16,24,3072]{3,2,1,0:T(8,128)(2,1)}, bf16[1,16,24,3072]{3,2,1,0:T(8,128)(2,1)S(1)}, u32[]{:S(2)}, u32[]{:S(2)}) collective-permute-start(bf16[1,16,24,3072]{3,2,1,0:T(8,128)(2,1)} %get-tuple-element.383), channel_id=1, source_target_pairs={{0,1},{1,0},{2,3},{3,2},{4,5},{5,4},{6,7},{7,6},{8,9},{9,8},{10,11... | collective-permute-start | bytes 7077896 | tf_op jit(solution)/shard_map/ppermute | solution.py:19
  209.2 31.4 %collective-permute-start.11 = (bf16[2,256,768]{2,1,0:T(8,128)(2,1)}, bf16[2,256,768]{2,1,0:T(8,128)(2,1)}, u32[]{:S(2)}, u32[]{:S(2)}) collective-permute-start(bf16[2,256,768]{2,1,0:T(8,128)(2,1)} %get-tuple-element.380), channel_id=1, source_target_pairs={{0,2},{1,3},{2,0},{3,1},{4,6},{5,7},{6,4},{7,5},{8,10},{9,11},{10,... | collective-permute-start | bytes 2359304 | tf_op jit(solution)/shard_map/ppermute | solution.py:19
  215.5 25.1 %collective-permute-start.12 = (bf16[1,256,768]{2,1,0:T(8,128)(2,1)}, bf16[1,256,768]{2,1,0:T(8,128)(2,1)}, u32[]{:S(2)}, u32[]{:S(2)}) collective-permute-start(bf16[1,256,768]{2,1,0:T(8,128)(2,1)} %get-tuple-element.410), channel_id=1, source_target_pairs={{0,2},{1,3},{2,0},{3,1},{4,6},{5,7},{6,4},{7,5},{8,10},{9,11},{10,... | collective-permute-start | bytes 1179656 | tf_op jit(solution)/shard_map/ppermute | solution.py:19
  224.1 16.5 %collective-permute-start.13 = (bf16[2,16,24,768]{3,2,1,0:T(8,128)(2,1)}, bf16[2,16,24,768]{3,2,1,0:T(8,128)(2,1)S(1)}, u32[]{:S(2)}, u32[]{:S(2)}) collective-permute-start(bf16[2,16,24,768]{3,2,1,0:T(8,128)(2,1)} %get-tuple-element.406), channel_id=1, source_target_pairs={{0,1},{1,0},{2,3},{3,2},{4,5},{5,4},{6,7},{7,6},{8,9},{9,8},{10,11... | collective-permute-start | bytes 3538952 | tf_op jit(solution)/shard_map/ppermute | solution.py:19
  231.4 36.8 %collective-permute-start.14 = (bf16[1,4,96,768]{3,2,1,0:T(8,128)(2,1)}, bf16[1,4,96,768]{3,2,1,0:T(8,128)(2,1)}, u32[]{:S(2)}, u32[]{:S(2)}) collective-permute-start(bf16[1,4,96,768]{3,2,1,0:T(8,128)(2,1)} %get-tuple-element.405), channel_id=1, source_target_pairs={{0,8},{4,12},{8,0},{12,4},{16,24},{20,28},{24,16},{28,20},{1,9},{5... | collective-permute-start | bytes 1769480 | tf_op jit(solution)/shard_map/ppermute | solution.py:19
  233.0 52.2 %collective-permute-start.17 = (bf16[1,8,24,3072]{3,2,1,0:T(8,128)(2,1)}, bf16[1,8,24,3072]{3,2,1,0:T(8,128)(2,1)}, u32[]{:S(2)}, u32[]{:S(2)}) collective-permute-start(bf16[1,8,24,3072]{3,2,1,0:T(8,128)(2,1)} %get-tuple-element.404), channel_id=1, source_target_pairs={{0,4},{4,0},{8,12},{12,8},{16,20},{20,16},{24,28},{28,24},{1,5},{5... | collective-permute-start | bytes 3538952 | tf_op jit(solution)/shard_map/ppermute | solution.py:19
  245.3 22.9 %collective-permute-start.16 = (bf16[2,8,24,768]{3,2,1,0:T(8,128)(2,1)}, bf16[2,8,24,768]{3,2,1,0:T(8,128)(2,1)}, u32[]{:S(2)}, u32[]{:S(2)}) collective-permute-start(bf16[2,8,24,768]{3,2,1,0:T(8,128)(2,1)} %get-tuple-element.416), channel_id=1, source_target_pairs={{0,2},{1,3},{2,0},{3,1},{4,6},{5,7},{6,4},{7,5},{8,10},{9,11},{10,... | collective-permute-start | bytes 1769480 | tf_op jit(solution)/shard_map/ppermute | solution.py:19
  245.8 22.4 %collective-permute-start.15 = (bf16[2,16,24,768]{3,2,1,0:T(8,128)(2,1)}, bf16[2,16,24,768]{3,2,1,0:T(8,128)(2,1)}, u32[]{:S(2)}, u32[]{:S(2)}) collective-permute-start(bf16[2,16,24,768]{3,2,1,0:T(8,128)(2,1)} %get-tuple-element.413), channel_id=1, source_target_pairs={{0,1},{1,0},{2,3},{3,2},{4,5},{5,4},{6,7},{7,6},{8,9},{9,8},{10,11... | collective-permute-start | bytes 3538952 | tf_op jit(solution)/shard_map/ppermute | solution.py:19
  272.7 12.4 %collective-permute-start.18 = (bf16[1,2,96,768]{3,2,1,0:T(8,128)(2,1)}, bf16[1,2,96,768]{3,2,1,0:T(8,128)(2,1)S(1)}, u32[]{:S(2)}, u32[]{:S(2)}) collective-permute-start(bf16[1,2,96,768]{3,2,1,0:T(8,128)(2,1)} %get-tuple-element.437), channel_id=1, source_target_pairs={{0,2},{1,3},{2,0},{3,1},{4,6},{5,7},{6,4},{7,5},{8,10},{9,11},{10,... | collective-permute-start | bytes 884744 | tf_op jit(solution)/shard_map/ppermute | solution.py:19
  274.3 50.1 %collective-permute-start.23 = (bf16[2,8,24,768]{3,2,1,0:T(8,128)(2,1)}, bf16[2,8,24,768]{3,2,1,0:T(8,128)(2,1)}, u32[]{:S(2)}, u32[]{:S(2)}) collective-permute-start(bf16[2,8,24,768]{3,2,1,0:T(8,128)(2,1)} %get-tuple-element.438), channel_id=1, source_target_pairs={{0,2},{1,3},{2,0},{3,1},{4,6},{5,7},{6,4},{7,5},{8,10},{9,11},{10,... | collective-permute-start | bytes 1769480 | tf_op jit(solution)/shard_map/ppermute | solution.py:19
  274.8 49.6 %collective-permute-start.24 = (bf16[2,4,24,768]{3,2,1,0:T(8,128)(2,1)}, bf16[2,4,24,768]{3,2,1,0:T(8,128)(2,1)}, u32[]{:S(2)}, u32[]{:S(2)}) collective-permute-start(bf16[2,4,24,768]{3,2,1,0:T(8,128)(2,1)} %get-tuple-element.439), channel_id=1, source_target_pairs={{0,4},{4,0},{8,12},{12,8},{16,20},{20,16},{24,28},{28,24},{1,5},{5... | collective-permute-start | bytes 884744 | tf_op jit(solution)/shard_map/ppermute | solution.py:19
  285.2 15.8 %collective-permute-start.19 = (bf16[1,16,96,768]{3,2,1,0:T(8,128)(2,1)}, bf16[1,16,96,768]{3,2,1,0:T(8,128)(2,1)S(1)}, u32[]{:S(2)}, u32[]{:S(2)}) collective-permute-start(bf16[1,16,96,768]{3,2,1,0:T(8,128)(2,1)} %get-tuple-element.445), channel_id=1, source_target_pairs={{0,1},{1,0},{2,3},{3,2},{4,5},{5,4},{6,7},{7,6},{8,9},{9,8},{10,11... | collective-permute-start | bytes 7077896 | tf_op jit(solution)/shard_map/ppermute | solution.py:19
  289.5 11.5 %collective-permute-start.20 = (bf16[1,1,96,768]{3,2,1,0:T(8,128)(2,1)}, bf16[1,1,96,768]{3,2,1,0:T(8,128)(2,1)S(1)}, u32[]{:S(2)}, u32[]{:S(2)}) collective-permute-start(bf16[1,1,96,768]{3,2,1,0:T(8,128)(2,1)} %get-tuple-element.451), channel_id=1, source_target_pairs={{0,16},{4,20},{8,24},{12,28},{16,0},{20,4},{24,8},{28,12},{1,17},{... | collective-permute-start | bytes 442376 | tf_op jit(solution)/shard_map/ppermute | solution.py:19
  292.1 32.3 %collective-permute-start.22 = (bf16[1,4,24,3072]{3,2,1,0:T(8,128)(2,1)}, bf16[1,4,24,3072]{3,2,1,0:T(8,128)(2,1)}, u32[]{:S(2)}, u32[]{:S(2)}) collective-permute-start(bf16[1,4,24,3072]{3,2,1,0:T(8,128)(2,1)} %get-tuple-element.450), channel_id=1, source_target_pairs={{0,8},{4,12},{8,0},{12,4},{16,24},{20,28},{24,16},{28,20},{1,9},{5... | collective-permute-start | bytes 1769480 | tf_op jit(solution)/shard_map/ppermute | solution.py:19
  301.1 23.4 %collective-permute-start.21 = (bf16[1,16,24,3072]{3,2,1,0:T(8,128)(2,1)}, bf16[1,16,24,3072]{3,2,1,0:T(8,128)(2,1)}, u32[]{:S(2)}, u32[]{:S(2)}) collective-permute-start(bf16[1,16,24,3072]{3,2,1,0:T(8,128)(2,1)} %get-tuple-element.457), channel_id=1, source_target_pairs={{0,1},{1,0},{2,3},{3,2},{4,5},{5,4},{6,7},{7,6},{8,9},{9,8},{10,11... | collective-permute-start | bytes 7077896 | tf_op jit(solution)/shard_map/ppermute | solution.py:19
  307.3 39.1 %collective-permute-start.25 = (bf16[1,8,96,768]{3,2,1,0:T(8,128)(2,1)}, bf16[1,8,96,768]{3,2,1,0:T(8,128)(2,1)}, u32[]{:S(2)}, u32[]{:S(2)}) collective-permute-start(bf16[1,8,96,768]{3,2,1,0:T(8,128)(2,1)} %get-tuple-element.460), channel_id=1, source_target_pairs={{0,4},{4,0},{8,12},{12,8},{16,20},{20,16},{24,28},{28,24},{1,5},{5... | collective-permute-start | bytes 3538952 | tf_op jit(solution)/shard_map/ppermute | solution.py:19
  330.6 15.7 %collective-permute-start.26 = (bf16[1,2,24,3072]{3,2,1,0:T(8,128)(2,1)}, bf16[1,2,24,3072]{3,2,1,0:T(8,128)(2,1)S(1)}, u32[]{:S(2)}, u32[]{:S(2)}) collective-permute-start(bf16[1,2,24,3072]{3,2,1,0:T(8,128)(2,1)} %get-tuple-element.476), channel_id=1, source_target_pairs={{0,2},{1,3},{2,0},{3,1},{4,6},{5,7},{6,4},{7,5},{8,10},{9,11},{10,... | collective-permute-start | bytes 884744 | tf_op jit(solution)/shard_map/ppermute | solution.py:19
  332.2 14.2 %collective-permute-start.27 = (bf16[2,4,24,768]{3,2,1,0:T(8,128)(2,1)}, bf16[2,4,24,768]{3,2,1,0:T(8,128)(2,1)S(1)}, u32[]{:S(2)}, u32[]{:S(2)}) collective-permute-start(bf16[2,4,24,768]{3,2,1,0:T(8,128)(2,1)} %get-tuple-element.477), channel_id=1, source_target_pairs={{0,4},{4,0},{8,12},{12,8},{16,20},{20,16},{24,28},{28,24},{1,5},{5... | collective-permute-start | bytes 884744 | tf_op jit(solution)/shard_map/ppermute | solution.py:19
  333.7 12.6 %collective-permute-start.28 = (bf16[2,2,24,768]{3,2,1,0:T(8,128)(2,1)}, bf16[2,2,24,768]{3,2,1,0:T(8,128)(2,1)S(1)}, u32[]{:S(2)}, u32[]{:S(2)}) collective-permute-start(bf16[2,2,24,768]{3,2,1,0:T(8,128)(2,1)} %get-tuple-element.478), channel_id=1, source_target_pairs={{0,8},{4,12},{8,0},{12,4},{16,24},{20,28},{24,16},{28,20},{1,9},{5... | collective-permute-start | bytes 442376 | tf_op jit(solution)/shard_map/ppermute | solution.py:19
  335.3 53.7 %collective-permute-start.31 = (bf16[1,8,24,3072]{3,2,1,0:T(8,128)(2,1)}, bf16[1,8,24,3072]{3,2,1,0:T(8,128)(2,1)}, u32[]{:S(2)}, u32[]{:S(2)}) collective-permute-start(bf16[1,8,24,3072]{3,2,1,0:T(8,128)(2,1)} %get-tuple-element.475), channel_id=1, source_target_pairs={{0,8},{4,12},{8,0},{12,4},{16,24},{20,28},{24,16},{28,20},{1,9},{5... | collective-permute-start | bytes 3538952 | tf_op jit(solution)/shard_map/ppermute | solution.py:19
  346.4 34.3 %collective-permute-start.29 = (bf16[3,2,256,768]{3,2,1,0:T(8,128)(2,1)}, bf16[3,2,256,768]{3,2,1,0:T(8,128)(2,1)S(1)}, u32[]{:S(2)}, u32[]{:S(2)}) collective-permute-start(bf16[3,2,256,768]{3,2,1,0:T(8,128)(2,1)} %get-tuple-element.492), channel_id=1, source_target_pairs={{0,1},{1,0},{2,3},{3,2},{4,5},{5,4},{6,7},{7,6},{8,9},{9,8},{10,11... | collective-permute-start | bytes 7077896 | tf_op jit(solution)/shard_map/ppermute | solution.py:19
  351.3 52.9 %collective-permute-start.33 = (bf16[1,4,96,768]{3,2,1,0:T(8,128)(2,1)}, bf16[1,4,96,768]{3,2,1,0:T(8,128)(2,1)}, u32[]{:S(2)}, u32[]{:S(2)}) collective-permute-start(bf16[1,4,96,768]{3,2,1,0:T(8,128)(2,1)} %get-tuple-element.501), channel_id=1, source_target_pairs={{0,8},{4,12},{8,0},{12,4},{16,24},{20,28},{24,16},{28,20},{1,9},{5... | collective-permute-start | bytes 1769480 | tf_op jit(solution)/shard_map/ppermute | solution.py:19
  352.9 68.3 %collective-permute-start.40 = (bf16[2,2,24,768]{3,2,1,0:T(8,128)(2,1)}, bf16[2,2,24,768]{3,2,1,0:T(8,128)(2,1)}, u32[]{:S(2)}, u32[]{:S(2)}) collective-permute-start(bf16[2,2,24,768]{3,2,1,0:T(8,128)(2,1)} %get-tuple-element.533), channel_id=1, source_target_pairs={{0,8},{4,12},{8,0},{12,4},{16,24},{20,28},{24,16},{28,20},{1,9},{5... | collective-permute-start | bytes 442376 | tf_op jit(solution)/shard_map/ppermute | solution.py:19
  353.4 26.6 %collective-permute-start.51 = (bf16[2,1,24,768]{3,2,1,0:T(8,128)(2,1)}, bf16[2,1,24,768]{3,2,1,0:T(8,128)(2,1)S(1)}, u32[]{:S(2)}, u32[]{:S(2)}) collective-permute-start(bf16[2,1,24,768]{3,2,1,0:T(8,128)(2,1)} %get-tuple-element.555), channel_id=1, source_target_pairs={{0,16},{4,20},{8,24},{12,28},{16,0},{20,4},{24,8},{28,12},{1,17},{... | collective-permute-start | bytes 221192 | tf_op jit(solution)/shard_map/ppermute | solution.py:19
  389.0 15.2 %collective-permute-start.32 = (bf16[2,16,24,768]{3,2,1,0:T(8,128)(2,1)}, bf16[2,16,24,768]{3,2,1,0:T(8,128)(2,1)}, u32[]{:S(2)}, u32[]{:S(2)}) collective-permute-start(bf16[2,16,24,768]{3,2,1,0:T(8,128)(2,1)} %get-tuple-element.513), channel_id=1, source_target_pairs={{0,1},{1,0},{2,3},{3,2},{4,5},{5,4},{6,7},{7,6},{8,9},{9,8},{10,11... | collective-permute-start | bytes 3538952 | tf_op jit(solution)/shard_map/ppermute | solution.py:19
  394.4 27.2 %collective-permute-start.37 = (bf16[2,8,24,768]{3,2,1,0:T(8,128)(2,1)}, bf16[2,8,24,768]{3,2,1,0:T(8,128)(2,1)}, u32[]{:S(2)}, u32[]{:S(2)}) collective-permute-start(bf16[2,8,24,768]{3,2,1,0:T(8,128)(2,1)} %get-tuple-element.518), channel_id=1, source_target_pairs={{0,2},{1,3},{2,0},{3,1},{4,6},{5,7},{6,4},{7,5},{8,10},{9,11},{10,... | collective-permute-start | bytes 1769480 | tf_op jit(solution)/shard_map/ppermute | solution.py:19
  395.0 31.1 %collective-permute-start.39 = (bf16[1,4,24,3072]{3,2,1,0:T(8,128)(2,1)}, bf16[1,4,24,3072]{3,2,1,0:T(8,128)(2,1)}, u32[]{:S(2)}, u32[]{:S(2)}) collective-permute-start(bf16[1,4,24,3072]{3,2,1,0:T(8,128)(2,1)} %get-tuple-element.519), channel_id=1, source_target_pairs={{0,4},{4,0},{8,12},{12,8},{16,20},{20,16},{24,28},{28,24},{1,5},{5... | collective-permute-start | bytes 1769480 | tf_op jit(solution)/shard_map/ppermute | solution.py:19
  407.6 22.4 %collective-permute-start.38 = (bf16[1,2,96,768]{3,2,1,0:T(8,128)(2,1)}, bf16[1,2,96,768]{3,2,1,0:T(8,128)(2,1)S(1)}, u32[]{:S(2)}, u32[]{:S(2)}) collective-permute-start(bf16[1,2,96,768]{3,2,1,0:T(8,128)(2,1)} %get-tuple-element.530), channel_id=1, source_target_pairs={{0,2},{1,3},{2,0},{3,1},{4,6},{5,7},{6,4},{7,5},{8,10},{9,11},{10,... | collective-permute-start | bytes 884744 | tf_op jit(solution)/shard_map/ppermute | solution.py:19
  426.1 12.2 %collective-permute-start.62 = (bf16[1,1,24,3072]{3,2,1,0:T(8,128)(2,1)S(1)}, bf16[1,1,24,3072]{3,2,1,0:T(8,128)(2,1)S(1)}, u32[]{:S(2)}, u32[]{:S(2)}) collective-permute-start(bf16[1,1,24,3072]{3,2,1,0:T(8,128)(2,1)S(1)} %copy-done.44), channel_id=1, source_target_pairs={{0,16},{4,20},{8,24},{12,28},{16,0},{20,4},{24,8},{28,12},{1,17},{... | collective-permute-start | bytes 442376 | tf_op jit(solution)/shard_map/ppermute | solution.py:19
  429.4 12.7 %collective-permute-start.55 = (f32[2,12,768]{2,1,0:T(8,128)S(1)}, f32[2,12,768]{2,1,0:T(8,128)S(1)}, u32[]{:S(2)}, u32[]{:S(2)}) collective-permute-start(f32[2,12,768]{2,1,0:T(8,128)S(1)} %add.112), channel_id=1, source_target_pairs={{0,8},{4,12},{8,0},{12,4},{16,24},{20,28},{24,16},{28,20},{1,9},{5... | collective-permute-start | bytes 221192 | tf_op jit(solution)/shard_map/ppermute | solution.py:19
  438.3 15.8 %collective-permute-start.44 = (bf16[2,4,24,768]{3,2,1,0:T(8,128)(2,1)}, bf16[2,4,24,768]{3,2,1,0:T(8,128)(2,1)S(1)}, u32[]{:S(2)}, u32[]{:S(2)}) collective-permute-start(bf16[2,4,24,768]{3,2,1,0:T(8,128)(2,1)} %get-tuple-element.541), channel_id=1, source_target_pairs={{0,4},{4,0},{8,12},{12,8},{16,20},{20,16},{24,28},{28,24},{1,5},{5... | collective-permute-start | bytes 884744 | tf_op jit(solution)/shard_map/ppermute | solution.py:19
  440.2 13.9 %collective-permute-start.45 = (bf16[1,2,24,3072]{3,2,1,0:T(8,128)(2,1)}, bf16[1,2,24,3072]{3,2,1,0:T(8,128)(2,1)S(1)}, u32[]{:S(2)}, u32[]{:S(2)}) collective-permute-start(bf16[1,2,24,3072]{3,2,1,0:T(8,128)(2,1)} %get-tuple-element.543), channel_id=1, source_target_pairs={{0,2},{1,3},{2,0},{3,1},{4,6},{5,7},{6,4},{7,5},{8,10},{9,11},{10,... | collective-permute-start | bytes 884744 | tf_op jit(solution)/shard_map/ppermute | solution.py:19
  441.7 10.3 %collective-permute-start.41 = (bf16[2,4,24,256]{3,2,1,0:T(8,128)(2,1)}, bf16[2,4,24,256]{3,2,1,0:T(8,128)(2,1)S(1)}, u32[]{:S(2)}, u32[]{:S(2)}) collective-permute-start(bf16[2,4,24,256]{3,2,1,0:T(8,128)(2,1)} %get-tuple-element.535), channel_id=1, source_target_pairs={{0,4},{4,0},{8,12},{12,8},{16,20},{20,16},{24,28},{28,24},{1,5},{5... | collective-permute-start | bytes 294920 | tf_op jit(solution)/shard_map/ppermute | solution.py:19
  442.1 11.2 %collective-permute-start.42 = (bf16[2,4,24,256]{3,2,1,0:T(8,128)(2,1)}, bf16[2,4,24,256]{3,2,1,0:T(8,128)(2,1)S(1)}, u32[]{:S(2)}, u32[]{:S(2)}) collective-permute-start(bf16[2,4,24,256]{3,2,1,0:T(8,128)(2,1)} %get-tuple-element.537), channel_id=1, source_target_pairs={{0,8},{4,12},{8,0},{12,4},{16,24},{20,28},{24,16},{28,20},{1,9},{5... | collective-permute-start | bytes 294920 | tf_op jit(solution)/shard_map/ppermute | solution.py:19
  457.5 12.8 %collective-permute-start.49 = (bf16[2,2,24,768]{3,2,1,0:T(8,128)(2,1)}, bf16[2,2,24,768]{3,2,1,0:T(8,128)(2,1)S(1)}, u32[]{:S(2)}, u32[]{:S(2)}) collective-permute-start(bf16[2,2,24,768]{3,2,1,0:T(8,128)(2,1)} %get-tuple-element.551), channel_id=1, source_target_pairs={{0,8},{4,12},{8,0},{12,4},{16,24},{20,28},{24,16},{28,20},{1,9},{5... | collective-permute-start | bytes 442376 | tf_op jit(solution)/shard_map/ppermute | solution.py:19
  459.2 11.1 %collective-permute-start.46 = (bf16[2,2,24,256]{3,2,1,0:T(8,128)(2,1)}, bf16[2,2,24,256]{3,2,1,0:T(8,128)(2,1)S(1)}, u32[]{:S(2)}, u32[]{:S(2)}) collective-permute-start(bf16[2,2,24,256]{3,2,1,0:T(8,128)(2,1)} %get-tuple-element.545), channel_id=1, source_target_pairs={{0,8},{4,12},{8,0},{12,4},{16,24},{20,28},{24,16},{28,20},{1,9},{5... | collective-permute-start | bytes 147464 | tf_op jit(solution)/shard_map/ppermute | solution.py:19
  459.7 10.6 %collective-permute-start.47 = (bf16[2,2,24,256]{3,2,1,0:T(8,128)(2,1)}, bf16[2,2,24,256]{3,2,1,0:T(8,128)(2,1)S(1)}, u32[]{:S(2)}, u32[]{:S(2)}) collective-permute-start(bf16[2,2,24,256]{3,2,1,0:T(8,128)(2,1)} %get-tuple-element.547), channel_id=1, source_target_pairs={{0,2},{1,3},{2,0},{3,1},{4,6},{5,7},{6,4},{7,5},{8,10},{9,11},{10,... | collective-permute-start | bytes 147464 | tf_op jit(solution)/shard_map/ppermute | solution.py:19
  460.8 9.5 %collective-permute-start.48 = (bf16[2,2,24,256]{3,2,1,0:T(8,128)(2,1)}, bf16[2,2,24,256]{3,2,1,0:T(8,128)(2,1)S(1)}, u32[]{:S(2)}, u32[]{:S(2)}) collective-permute-start(bf16[2,2,24,256]{3,2,1,0:T(8,128)(2,1)} %get-tuple-element.549), channel_id=1, source_target_pairs={{0,4},{4,0},{8,12},{12,8},{16,20},{20,16},{24,28},{28,24},{1,5},{5... | collective-permute-start | bytes 147464 | tf_op jit(solution)/shard_map/ppermute | solution.py:19
  468.0 10.8 %collective-permute-start.61 = (bf16[1,1,24,3072]{3,2,1,0:T(8,128)(2,1)S(1)}, bf16[1,1,24,3072]{3,2,1,0:T(8,128)(2,1)S(1)}, u32[]{:S(2)}, u32[]{:S(2)}) collective-permute-start(bf16[1,1,24,3072]{3,2,1,0:T(8,128)(2,1)S(1)} %copy-done.46), channel_id=1, source_target_pairs={{0,16},{4,20},{8,24},{12,28},{16,0},{20,4},{24,8},{28,12},{1,17},{... | collective-permute-start | bytes 442376 | tf_op jit(solution)/shard_map/ppermute | solution.py:19
  (73 other events, 453.7 us)

commit v3 on v2

--- a/solution.py
+++ b/solution.py
@@ -23,8 +23,9 @@
 TOKENS_MAJOR = (((0,), (0,)), ((), ()))
 ROOT_HALF = 0.7071067811865476
 ROOT_TAU = 0.3989422804014327
-VMEM_BYTES = 56 * 1024 * 1024
+VMEM_MIB = dict(forward=60, ff_back=32, attention_back=16, input_back=18, wgrad=16, step=20, lanes=24)
 FF_PARTS = 4
+FACTS_TAIL = 4
 FAST = jnp.float32
 LOW = jnp.bfloat16
 
@@ -46,6 +47,24 @@
 
 def mm_tn(left, right):
     return lax.dot_general(left, right, TOKENS_MAJOR, preferred_element_type=FAST)
+
+
+def vectors_kernel(*refs):
+    *ins, out = refs
+    for place, ref in enumerate(ins[:-1]):
+        out[:, place, :] = ref[...].astype(FAST)
+    wide = out.shape[2]
+    for part in range(FF_PARTS):
+        out[:, len(ins) - 1 + part, :] = ins[-1][:, part * wide : (part + 1) * wide].astype(FAST)
+
+
+def vectors_call(*vectors):
+    layers, wide = vectors[0].shape
+    return pl.pallas_call(
+        vectors_kernel,
+        out_shape=jax.ShapeDtypeStruct((layers, len(vectors) - 1 + FF_PARTS, wide), FAST),
+        name="vectors",
+    )(*vectors)
 
 
 def row_norm(value):
@@ -72,7 +91,7 @@
 VEC_UP = 8
 
 
-def forward_kernel(layer, swapped, facts, own, near, far, top, vecs, *refs):
+def forward_kernel(layer, swapped, start, facts, own, near, far, top, vecs, *refs):
     weights, refs = refs[:6], refs[6:]
     refs = refs[len(refs) - 25 :]
     outs, scratch = refs[:16], refs[16:]
@@ -111,10 +130,10 @@
         block = source[0]
         o_k[0, part * rows : (part + 1) * rows, :] = mm(block, w_k[...]).astype(LOW)
         o_v[0, part * rows : (part + 1) * rows, :] = (mm(block, w_v[...]) + vec("b_value")).astype(LOW)
-    seq = facts[5] + pl.program_id(0)
-    length = facts[seq]
+    spots = facts.shape[0] - FACTS_TAIL + 2 * layer
+    length = facts[start + pl.program_id(0)]
     lane = lax.broadcasted_iota(jnp.int32, (1, 2 * rows), 1)
-    place = jnp.where(lane < rows, facts[3] + lane, facts[4] + (lane - rows))
+    place = jnp.where(lane < rows, facts[spots] + lane, facts[spots + 1] + (lane - rows))
     bias = jnp.where(place < length, 0.0, MASKED).astype(FAST)
     lower = lax.broadcasted_iota(jnp.int32, (1, 128), 1) < HEAD_DIM
     column = lax.broadcasted_iota(jnp.int32, (1, 128), 1)
@@ -205,7 +224,7 @@
         ins += [kept[name] for name in KEPT]
         in_specs += [any_spec] * len(KEPT)
     got = pl.pallas_call(
-        partial(forward_kernel, layer, swapped),
+        partial(forward_kernel, layer, swapped, start),
         grid=(count,),
         in_specs=in_specs,
         out_specs=out_specs,
@@ -216,7 +235,7 @@
             pltpu.VMEM((wide, wide), LOW), pltpu.VMEM((wide, hidden), LOW), pltpu.VMEM((hidden, wide), LOW),
             pltpu.VMEM((rows, wide), FAST), pltpu.VMEM((rows, wide), LOW), pltpu.SemaphoreType.DMA((6,)),
         ],
-        compiler_params=pltpu.CompilerParams(vmem_limit_bytes=VMEM_BYTES),
+        compiler_params=pltpu.CompilerParams(vmem_limit_bytes=VMEM_MIB["forward"] << 20),
         cost_estimate=cost(14 * count),
         name=f"layer_forward_{layer}",
     )(*ins)
@@ -314,13 +333,13 @@
             pltpu.VMEM((hidden, wide), LOW), pltpu.VMEM((wide, hidden), LOW), pltpu.VMEM((wide, wide), LOW),
             pltpu.VMEM((rows, wide), FAST), pltpu.SemaphoreType.DMA((3,)),
         ],
-        compiler_params=pltpu.CompilerParams(vmem_limit_bytes=VMEM_BYTES),
+        compiler_params=pltpu.CompilerParams(vmem_limit_bytes=VMEM_MIB["ff_back"] << 20),
         cost_estimate=cost(19),
         name=f"ff_back_{layer}",
     )(*ins)
 
 
-def attention_back_kernel(split, facts, q, k, v, lse, dc, *refs):
+def attention_back_kernel(layer, start, facts, q, k, v, lse, dc, *refs):
     o_dq, o_near, o_far, o_vec, bias = refs[len(refs) - 5 :]
     rows, wide = q.shape[1], q.shape[2]
 
@@ -328,9 +347,10 @@
     def _():
         o_vec[...] = jnp.zeros_like(o_vec)
 
-    length = facts[facts[5] + pl.program_id(0)]
+    spots = facts.shape[0] - FACTS_TAIL + 2 * layer
+    length = facts[start + pl.program_id(0)]
     key = lax.broadcasted_iota(jnp.int32, (2 * rows, rows), 0)
-    place = jnp.where(key < rows, facts[3] + key, facts[4] + (key - rows))
+    place = jnp.where(key < rows, facts[spots] + key, facts[spots + 1] + (key - rows))
     bias[...] = jnp.where(place < length, 0.0, MASKED).astype(FAST)
     lower = lax.broadcasted_iota(jnp.int32, (1, 128), 1) < HEAD_DIM
     for pair in range(HEADS // 2):
@@ -390,14 +410,14 @@
     places = (0, 1) if split else (0, 1, 2)
     aliases = chained(ins, in_specs, earlier and earlier[: len(places)], places)
     return pl.pallas_call(
-        partial(attention_back_kernel, split),
+        partial(attention_back_kernel, layer, start),
         grid=(count,),
         in_specs=in_specs,
         out_specs=out_specs,
         out_shape=out_shape,
         input_output_aliases=aliases,
         scratch_shapes=[pltpu.VMEM((2 * rows, rows), FAST)],
-        compiler_params=pltpu.CompilerParams(vmem_limit_bytes=VMEM_BYTES),
+        compiler_params=pltpu.CompilerParams(vmem_limit_bytes=VMEM_MIB["attention_back"] << 20),
         cost_estimate=cost(8 * count),
         name=f"attention_back_{layer}",
     )(*ins)
@@ -471,23 +491,31 @@
         out_shape=out_shape,
         input_output_aliases=aliases,
         scratch_shapes=[pltpu.VMEM((wide, wide), LOW)] * 3 + [pltpu.SemaphoreType.DMA((3,))],
-        compiler_params=pltpu.CompilerParams(vmem_limit_bytes=VMEM_BYTES),
+        compiler_params=pltpu.CompilerParams(vmem_limit_bytes=VMEM_MIB["input_back"] << 20),
         cost_estimate=cost(2 + 3 * count),
         name=f"input_back_{layer}",
     )(*ins)
 
 
 def wgrad_kernel(count, place_ref, *refs):
-    lefts, rights, (o_kept, o_sent, full) = refs[:count], refs[count : 2 * count], refs[2 * count :]
-    mine = place_ref[0]
+    lefts, rights, (o_kept, o_sent) = refs[:count], refs[count : 2 * count], refs[2 * count :]
     pairs, rows = o_kept.shape[1], o_kept.shape[2]
-    for i in range(count):
-        full[...] = mm_tn(lefts[i][...], rights[i][...])
-        for pair in range(pairs):
-            first = pl.multiple_of((2 * pair + mine) * rows, 8)
-            second = pl.multiple_of((2 * pair + 1 - mine) * rows, 8)
-            o_kept[i, pair] = full[pl.ds(first, rows), :].astype(LOW)
-            o_sent[i, pair] = full[pl.ds(second, rows), :].astype(LOW)
+
+    def write(o_even, o_odd):
+        for i in range(count):
+            full = mm_tn(lefts[i][...], rights[i][...])
+            for pair in range(pairs):
+                start = 2 * pair * rows
+                o_even[i, pair] = full[start : start + rows].astype(LOW)
+                o_odd[i, pair] = full[start + rows : start + 2 * rows].astype(LOW)
+
+    @pl.when(place_ref[0] == 0)
+    def _():
+        write(o_kept, o_sent)
+
+    @pl.when(place_ref[0] == 1)
+    def _():
+        write(o_sent, o_kept)
 
 
 def wgrad_call(name, place, devices, lefts, rights, chunk):
@@ -506,8 +534,7 @@
         + [pl.BlockSpec((tokens, width), lambda i: (0, 0))] * count,
         out_specs=[out_spec] * 2,
         out_shape=[shape] * 2,
-        scratch_shapes=[pltpu.VMEM((chunk, width), FAST)],
-        compiler_params=pltpu.CompilerParams(vmem_limit_bytes=VMEM_BYTES),
+        compiler_params=pltpu.CompilerParams(vmem_limit_bytes=VMEM_MIB["wgrad"] << 20),
         cost_estimate=cost(3 + 2 * count * height * width / 1e6),
         name=f"wgrad_{name}",
     )(place, *lefts, *rights)
@@ -545,9 +572,57 @@
         in_specs=[pl.BlockSpec(memory_space=pltpu.SMEM)] + in_specs,
         out_specs=out_specs,
         out_shape=out_shape,
-        compiler_params=pltpu.CompilerParams(vmem_limit_bytes=VMEM_BYTES),
+        compiler_params=pltpu.CompilerParams(vmem_limit_bytes=VMEM_MIB["step"] << 20),
         cost_estimate=cost(1 + moved / 3e6),
         name="exchange_step",
+    )(bits, *ins)
+
+
+def lanes_kernel(plan, bits, *refs):
+    count = len(refs) // 2 - len(plan)
+    ins, outs = refs[: 2 * count], refs[2 * count :]
+    for lane, (outer, inner, digit) in enumerate(plan):
+        mine = bits[digit]
+        for out, side in ((outs[2 * lane], mine), (outs[2 * lane + 1], 1 - mine)):
+            groups, parts, rows, columns = out.shape
+            first = 0
+            for i in range(count):
+                kept, got = ins[2 * i], ins[2 * i + 1]
+                wide = kept.shape[3] // len(plan)
+                cols = slice(lane * wide, (lane + 1) * wide)
+                for group in range(kept.shape[0]):
+                    for part in range(parts):
+                        source = (2 * (part // inner) + side) * inner + part % inner
+                        total = kept[group, source, :, cols].astype(FAST) + got[group, source, :, cols].astype(FAST)
+                        if groups == 1:
+                            total = [total[:, at : at + columns] for at in range(0, wide, columns)]
+                            total = total[0] if len(total) == 1 else jnp.concatenate(total, axis=0)
+                            out[0, part, first : first + total.shape[0], :] = total.astype(LOW)
+                        else:
+                            out[first + group, part] = total.astype(LOW)
+                first += rows // count if groups == 1 else kept.shape[0]
+
+
+def lanes_call(values, gots, plan, bits, stacked):
+    lanes = len(plan)
+    parts = values[0].shape[1]
+    columns = min(value.shape[3] for value in values) // lanes
+    if stacked:
+        shape = (1, parts // 2, sum(v.shape[2] * (v.shape[3] // lanes // columns) for v in values), columns)
+    else:
+        shape = (sum(v.shape[0] for v in values), parts // 2, values[0].shape[2], columns)
+    whole = lambda v: pl.BlockSpec((v.shape[0], parts // 2) + v.shape[2:], lambda i: (0, i, 0, 0))
+    half = pl.BlockSpec((shape[0], parts // 4) + shape[2:], lambda i: (0, i, 0, 0))
+    ins = [array for pair in zip(values, gots, strict=True) for array in pair]
+    return pl.pallas_call(
+        partial(lanes_kernel, tuple((outer // 2, inner, digit) for outer, inner, digit in plan)),
+        grid=(2,),
+        in_specs=[pl.BlockSpec(memory_space=pltpu.SMEM)] + [whole(v) for v in ins],
+        out_specs=[half] * (2 * lanes),
+        out_shape=[jax.ShapeDtypeStruct(shape, LOW)] * (2 * lanes),
+        compiler_params=pltpu.CompilerParams(vmem_limit_bytes=VMEM_MIB["lanes"] << 20),
+        cost_estimate=cost(6),
+        name="exchange_lanes",
     )(bits, *ins)
 
 
@@ -559,144 +634,131 @@
     hidden = w_up.shape[2]
     sizes = (seqs, rows, wide, hidden)
     weights = (w_query, w_key, w_value, w_out, w_up, w_down)
-    vecs = jnp.stack([b_query, b_value, b_out, gain_one, shift_one, b_down, gain_two, shift_two], axis=1)
-    vecs = jnp.concatenate([vecs, b_up.reshape(2, FF_PARTS, wide)], axis=1).astype(FAST)
+    vecs = vectors_call(b_query, b_value, b_out, gain_one, shift_one, b_down, gain_two, shift_two, b_up)
+    devices = lax.axis_size("batch") * lax.axis_size("seq")
     seq_index = lax.axis_index("seq").astype(jnp.int32)
-
-    def facts_of(first, second, start):
-        tail = jnp.stack([first * rows, second * rows, jnp.int32(start)])
-        return jnp.concatenate([lengths, tail]).astype(jnp.int32)
-
-    devices = lax.axis_size("batch") * lax.axis_size("seq")
+    spots = [(seq_index ^ flip) * rows for flip in (0, 1, 2, 3)]
+    facts = jnp.concatenate([lengths, jnp.stack(spots)]).astype(jnp.int32)
+    bits = jnp.stack([lax.axis_index(axis) >> bit & 1 for axis, bit in digit_list()]).astype(jnp.int32)
     flat = lambda value: value.reshape(seqs * rows, value.shape[-1])
     cuts = [(0, 2), (2, seqs - 2)]
+
+    kept_one, kept_two, nears = None, None, []
     other = swapped_2(tokens, "seq", 0)
-    kept_one, sent = None, []
     for start, count in cuts:
-        facts = facts_of(seq_index, seq_index ^ 1, start)
-        low, kept_one, done = forward_call(
+        low, kept_one, _ = forward_call(
             0, False, start, count, facts, (tokens, 0), (tokens, 0), (other, 0), (tokens, 0), vecs, weights, kept_one, sizes
         )
-        sent.append((low, start))
-    nears = [(swapped_2(low[i : i + 1], "seq", 1), start + i) for low, start in sent for i in range(low.shape[0])]
-    kept_two = None
-    groups = [[0], list(range(1, seqs))]
-    for number, group in enumerate(groups):
-        start, count = group[0], len(group)
-        arrived = [nears[i][0] for i in group]
-        if number:
-            arrived = after(arrived, done)
-        near = jnp.concatenate(arrived) if count > 1 else arrived[0]
+        low, kept_one["r2"] = tie(low, kept_one["r2"])
+        nears.append(swapped_2(low, "seq", 1))
+    for near, (start, count) in zip(nears, cuts, strict=True):
+        if kept_two is not None:
+            near, kept_two["r2"] = tie(near, kept_two["r2"])
+        else:
+            near, kept_one["r2"] = tie(near, kept_one["r2"])
         far = swapped_2(near, "seq", 0)
-        facts = facts_of(seq_index ^ 2, seq_index ^ 3, start)
-        _, kept_two, done = forward_call(
+        _, kept_two, _ = forward_call(
             1, True, start, count, facts, (kept_one["low"], 0), (near, start), (far, start),
             (kept_one["extra"], 0), vecs, weights, kept_two, sizes,
         )
     final = kept_two["low"]
 
     back_weights = (w_query, w_key, w_value)
-    digits = digit_orders()
-    down_order, late_order, four_order, last_orders = digits
-    up_order = down_order
-    bits = jnp.stack([lax.axis_index(axis) >> bit & 1 for axis, bit in digit_list()]).astype(jnp.int32)
+    near_first, far_first, across_first = digit_orders()
     wgrad = partial(wgrad_call, place=bits, devices=devices)
+    half = wide // 2
 
     kept = kept_two
     dy, df, dz1, da, dc, vec_two = ff_back_call(1, cotangent, kept, vecs, w_down, w_up, w_out)
-    down_two = Sum(wgrad("down", lefts=[flat(kept["act"])], rights=[flat(dy)], chunk=wide), down_order, bits)
-    facts = [facts_of(seq_index ^ 2, seq_index ^ 3, start) for start, _ in cuts]
-    dc = after(dc, down_two.out)
-    att = attention_back_call(1, True, 0, 2, facts[0], kept, dc, None)
+    down_two = wgrad("down", lefts=[flat(kept["act"])], rights=[flat(dy)], chunk=wide)
+    down_two, dc = Sum.begin(down_two, near_first, bits, dc)
+    att = attention_back_call(1, True, 0, 2, facts, kept, dc, None)
     att = join(att, down_two)
     vec_q = att[3]
-    advance(down_two)
-    got = swapped_2(att[2], "seq", 0)
-    dc = after(dc, down_two.out, att[2])
-    att = attention_back_call(1, True, 2, seqs - 2, facts[1], kept, dc, att)
+    (dc, far) = advance((dc, att[2]), down_two)
+    got = swapped_2(far, "seq", 0)
+    att = attention_back_call(1, True, 2, seqs - 2, facts, kept, dc, att)
     vec_q += att[3]
-    att, got = after((att, got))
+    att, got, df = tie(att, got, df)
     got_late = swapped_2(att[2], "seq", 0)
     ends = input_back_call(1, True, 0, 2, att[0], att[1], got, dz1, back_weights, None)
     vec_v = ends[3]
-    ends, got_late, df = after((ends, got_late, df))
+    ends, df = tie(ends, df)
     arrived = [swapped_2(ends[2], "seq", 1)]
-    up_two = Sum(wgrad("up", lefts=[flat(kept["hid"])], rights=[flat(df)], chunk=wide // 2), up_order, bits)
-    got_late, ends = after((got_late, ends), up_two.out)
+    up_two = wgrad("up", lefts=[flat(kept["hid"])], rights=[flat(df)], chunk=half)
+    up_two, (got_late, dz1) = Sum.begin(up_two, near_first, bits, (got_late, dz1))
     ends = input_back_call(1, True, 2, seqs - 2, att[0], att[1], got_late, dz1, back_weights, ends)
     vec_v += ends[3]
-    ends, da = after((ends, da))
+    ends = tie(*ends)
     arrived.append(swapped_2(ends[2], "seq", 1))
-    rest_two = wgrad("rest", lefts=[flat(kept["ctx"]), flat(kept_one["low"])], rights=[flat(da), flat(att[0])], chunk=wide // 2)
-    rest_two, pair = join((rest_two, ends[1]), up_two, down_two)
-    rest_two = Sum(rest_two, four_order, bits)
-    advance(up_two, down_two)
-    pair = after(pair, up_two.out, down_two.out, rest_two.out)
-    pairs_two = wgrad("pair", lefts=[flat(kept["extra"])] * 2, rights=[flat(pair[:, 0]), flat(pair[:, 1])], chunk=wide // 2)
-    pairs_two, arrived = join((pairs_two, arrived), rest_two)
-    pairs_two = Sum(pairs_two, four_order, bits)
+    ends = join(ends, up_two, down_two)
+    pair = advance(ends[1], up_two, down_two)
+    near = kept["extra"]
+    four_two = wgrad(
+        "four",
+        lefts=[flat(kept["ctx"]), flat(kept_one["low"]), flat(near), flat(near)],
+        rights=[flat(da), flat(att[0]), flat(pair[:, 0]), flat(pair[:, 1])],
+        chunk=half,
+    )
+    four_two, arrived = Sum.begin(four_two, across_first, bits, arrived)
     vec_two = (vec_two, vec_q, vec_v)
-    advance(rest_two)
-    arrived = after(arrived, pairs_two.out, rest_two.out)
     middle = ends[0] + jnp.concatenate(arrived).astype(FAST)
 
     kept = kept_one
     ff = ff_back_call(0, middle, kept, vecs, w_down, w_up, w_out)
-    ff = join(ff, down_two, pairs_two, rest_two)
-    dy, df, dz1, da, dc, vec_one = ff
-    advance(down_two, pairs_two, rest_two)
-    dy = after(dy, down_two.out, pairs_two.out, rest_two.out)
+    dy, df, dz1, da, dc, vec_one = join(ff, down_two, four_two)
+    dy = advance(dy, down_two, four_two)
     down_one = wgrad("down", lefts=[flat(kept["act"])], rights=[flat(dy)], chunk=wide)
-    down_one, df = join((down_one, df), up_two, down_two)
-    down_one = Sum(down_one, down_order, bits)
-    advance(up_two, down_two)
-    df = after(df, down_one.out, up_two.out, down_two.out)
-    up_one = wgrad("up", lefts=[flat(kept["hid"])], rights=[flat(df)], chunk=wide // 2)
-    up_one, dc = join((up_one, dc), down_one, down_two)
-    up_one = Sum(up_one, late_order, bits)
-    advance(down_one)
-    facts = [facts_of(seq_index, seq_index ^ 1, start) for start, _ in cuts]
-    dc = after(dc, up_one.out, down_one.out)
-    att = attention_back_call(0, False, 0, 2, facts[0], kept, dc, None)
+    down_one, df = Sum.begin(down_one, near_first, bits, df)
+    up_one = wgrad("up", lefts=[flat(kept["hid"])], rights=[flat(df)], chunk=half)
+    up_one, dc = join((up_one, dc), down_one, down_two, up_two)
+    up_one, dc = Sum.begin(up_one, near_first, bits, dc)
+    dc = advance(dc, down_two, up_two)
+    att = attention_back_call(0, False, 0, 2, facts, kept, dc, None)
     vec_q = att[3]
-    att, dc = join((att, dc), up_one, up_two, pairs_two, rest_two)
-    advance(up_one, up_two, pairs_two, rest_two)
-    dc = after(dc, up_one.out, up_two.out, pairs_two.out, rest_two.out)
-    att = attention_back_call(0, False, 2, seqs - 2, facts[1], kept, dc, att)
+    att, dc = join((att, dc), up_one, up_two, four_two, down_two)
+    lanes_one, dc = lanes_of(dc, down_one, up_one, stacked=True)
+    dc = advance(dc, up_two, four_two)
+    att = attention_back_call(0, False, 2, seqs - 2, facts, kept, dc, att)
     vec_q += att[3]
-    att, da = join((att, da), down_one, up_two, pairs_two, rest_two)
-    advance(down_one, up_two, pairs_two, rest_two)
+    att, da, vec_q = join((att, da, vec_q), up_two)
     got = swapped_2(att[2], "seq", 0)
-    da = after(da, att[2], down_one.out)
-    rest_one = wgrad("rest", lefts=[flat(kept["ctx"]), flat(tokens)], rights=[flat(da), flat(att[0])], chunk=wide // 2)
-    rest_one, got, dz1 = after((rest_one, got, dz1))
-    rest_one = Sum(rest_one, four_order, bits)
+    rest_one = wgrad("rest", lefts=[flat(kept["ctx"]), flat(tokens)], rights=[flat(da), flat(att[0])], chunk=half)
+    rest_one, got = tie(rest_one, got)
+    rest_one, got = Sum.begin(rest_one, across_first, bits, got)
     pair = (att[1].astype(FAST) + got.astype(FAST)).astype(LOW)
-    pair = after(pair, rest_one.out)
-    pairs_one = wgrad("pair", lefts=[flat(tokens)] * 2, rights=[flat(pair[:, 0]), flat(pair[:, 1])], chunk=wide // 2)
-    pairs_one, dz1 = join((pairs_one, dz1), rest_one, up_one)
-    pairs_one = Sum(pairs_one, last_orders[0], bits)
-    advance(rest_one, up_one)
-    dz1 = after(dz1, pairs_one.out, rest_one.out, up_one.out)
+    vectors = Whole([(vec_one, vec_q, jnp.sum(pair[:, 1].astype(FAST), axis=(0, 1))[None]), vec_two])
+    pair = vectors.send(pair)
+    pairs_one = wgrad("pair", lefts=[flat(tokens)] * 2, rights=[flat(pair[:, 0]), flat(pair[:, 1])], chunk=half)
+    pairs_one, dz1 = Sum.begin(pairs_one, near_first, bits, dz1)
+    dz1 = join(dz1, *lanes_one, vectors)
+    dz1 = advance(dz1, *lanes_one)
+    dz1 = vectors.send(dz1)
     ends = input_back_call(0, False, 0, seqs, att[0], pair, None, dz1, back_weights, None)
-    ends, vec_q = join((ends, vec_q), pairs_one, down_one)
-    vec_one = (vec_one, vec_q, ends[1])
-    pieces = pairs_one.split(last_orders)
-    advance(down_one)
-    vectors = both_sums([vec_one, vec_two])
-    live = pieces + [rest_one, down_one, up_one, pairs_two, rest_two, down_two, up_two]
+    result = join(ends[0], rest_one, pairs_one, vectors)
+    last_one, result = lanes_of(result, rest_one, pairs_one, stacked=False)
+    result = vectors.send(result)
+    live = [*lanes_one, *last_one, four_two, up_two, down_two]
+    result = join(result, *lanes_one, four_two, up_two, down_two, vectors)
+    result = advance(result, *lanes_one, four_two, up_two, down_two)
     while any(one.got is not None for one in live):
-        advance(*live)
-    pairs_one = jnp.concatenate([one.value for one in pieces], axis=-1)
+        result = vectors.send(result)
+        result = join(result, *live, vectors)
+        result = advance(result, *live)
+    rows_down = hidden // devices
+    both = [one.value[0] for one in lanes_one]
+    down_part = jnp.concatenate([one[:rows_down] for one in both], axis=-1)
+    up_part = [one[rows_down:].reshape(FF_PARTS, -1, one.shape[-1]) for one in both]
+    up_part = jnp.concatenate([one[part] for one in up_part for part in range(FF_PARTS)], axis=-1)
     sums = [
-        (down_one.value[0], up_one.value[0], rest_one.value, pairs_one),
-        (down_two.value[0], up_two.value[0], rest_two.value, pairs_two.value),
+        (down_part, up_part, jnp.concatenate([one.value for one in last_one], axis=-1)),
+        (down_two.value[0], up_two.value[0], four_two.value),
     ]
-    return (final, ends[0]) + gathered(sums, vectors, devices)
-
-
-def after(value, *others):
-    return lax.optimization_barrier((value, others))[0]
+    return (final, result) + gathered(sums, vectors.value, devices)
+
+
+def tie(*values):
+    return lax.optimization_barrier(values)
 
 
 def digit_list():
@@ -710,10 +772,17 @@
     high = lax.axis_size("batch").bit_length() - 1
     core, across = ("seq", 0), [("seq", bit) for bit in range(1, low)]
     near, far, late = [("batch", 0)], [("batch", 1)], [("batch", bit) for bit in range(2, high)]
-    first = [core] + near + far + across + late
-    second = [core] + far + near + across + late
-    third = [core] + across + near + far + late
-    return first, second, third, (third, [core] + near + far + across + late, [core] + far + across + near + late)
+    return (
+        [core] + near + far + across + late,
+        [core] + far + near + across + late,
+        [core] + across + near + far + late,
+    )
+
+
+def lane_orders():
+    digits = digit_list()[1:]
+    across, near, far, late = digits[:1], digits[1:2], digits[2:3], digits[3:]
+    return across + near + far + late, near + far + across + late, far + across + near + late
 
 
 def join(values, *sums):
@@ -724,68 +793,73 @@
     return values
 
 
-def advance(*sums):
+def advance(hold, *sums):
+    for one in sums:
+        if one.got is not None and not one.order:
+            one.value = (one.value.astype(FAST) + one.got.astype(FAST))[:, 0]
+            one.got = None
     live = [one for one in sums if one.got is not None]
     if not live:
-        return
-    for one in live:
-        if not one.order:
-            one.value = (one.value.astype(FAST) + one.got.astype(FAST))[:, 0]
-            one.got = None
-    live = [one for one in live if one.got is not None]
-    if not live:
-        return
+        return hold
     plan, routes = [], []
     for one in live:
-        axis, bit = digit = one.order.pop(0)
+        digit = one.order.pop(0)
         above = one.digits.index(digit)
         one.digits.remove(digit)
         plan.append((1 << above, 1 << len(one.digits) - above, digit_list().index(digit)))
-        routes.append((axis, bit))
+        routes.append(digit)
     halves = step_call([one.value for one in live], [one.got for one in live], tuple(plan), live[0].bits)
-    for i, one in enumerate(live):
-        one.value, one.out = halves[2 * i], halves[2 * i + 1]
-        one.got = swapped_2(one.out, *routes[i])
+    outs, hold = tie(halves[1::2], hold)
+    for one, value, out, route in zip(live, halves[::2], outs, routes, strict=True):
+        one.value = value
+        one.got = swapped_2(out, *route)
+    return hold
+
+
+def lanes_of(hold, *sums, stacked):
+    digits = sums[0].digits
+    plan, lanes = [], []
+    for order in lane_orders():
+        above = digits.index(order[0])
+        plan.append((1 << above, 1 << len(digits) - 1 - above, digit_list().index(order[0])))
+    halves = lanes_call([one.value for one in sums], [one.got for one in sums], tuple(plan), sums[0].bits, stacked)
+    outs, hold = tie(halves[1::2], hold)
+    for value, out, order in zip(halves[::2], outs, lane_orders(), strict=True):
+        one = Sum()
+        one.value, one.bits, one.order = value, sums[0].bits, list(order[1:])
+        one.digits = [digit for digit in digits if digit != order[0]]
+        one.got = swapped_2(out, *order[0])
+        lanes.append(one)
+    return lanes, hold
 
 
 class Sum:
-    def __init__(self, halves, order, bits):
-        self.value, self.out = halves
-        self.bits = bits
-        self.digits = list(reversed(digit_list()))[:-1]
-        self.order = list(order[1:])
-        self.got = swapped_2(self.out, *order[0])
-
-    def split(self, orders):
-        value = (self.value.astype(FAST) + self.got.astype(FAST)).astype(LOW)
-        pieces = []
-        width = value.shape[-1] // len(orders)
-        for i, order in enumerate(orders):
-            axis, bit = digit = order[1]
-            place = 1 + self.digits.index(digit)
-            piece = object.__new__(Sum)
-            piece.bits = self.bits
-            piece.digits, piece.order = [one for one in self.digits if one != digit], list(order[2:])
-            part = value[..., i * width : (i + 1) * width]
-            part = part.reshape(part.shape[:1] + (2,) * len(self.digits) + part.shape[2:])
-            shape = (part.shape[0], -1) + part.shape[-2:]
-            mine = lax.axis_index(axis) >> bit & 1
-            piece.out = lax.dynamic_index_in_dim(part, 1 - mine, place, keepdims=False).reshape(shape)
-            piece.value = lax.dynamic_index_in_dim(part, mine, place, keepdims=False).reshape(shape)
-            piece.got = swapped_2(piece.out, axis, bit)
-            pieces.append(piece)
-        return pieces
-
-
-def both_sums(layers):
-    value = []
-    for vec, vec_q, vec_v in layers:
-        value.append(jnp.concatenate([vec_q[:1], vec_v[:1], vec[2:]]))
-    value = jnp.stack(value)
-    for axis in ("seq", "batch"):
-        for bit in range(lax.axis_size(axis).bit_length() - 1):
-            value = value + swapped_2(value, axis, bit)
-    return value
+    @classmethod
+    def begin(cls, halves, order, bits, hold):
+        one = cls()
+        (one.value, out), hold = tie(halves, hold)
+        one.bits = bits
+        one.digits = list(reversed(digit_list()))[:-1]
+        one.order = list(order[1:])
+        one.got = swapped_2(out, *order[0])
+        return one, hold
+
+
+class Whole:
+    def __init__(self, layers):
+        rows = [jnp.concatenate([vec_q[:1], vec_v[:1], vec[2:]]) for vec, vec_q, vec_v in layers]
+        self.value = jnp.stack(rows)
+        self.got = None
+        self.order = digit_list()
+
+    def send(self, hold):
+        if self.got is not None:
+            self.value = self.value + self.got
+            self.got = None
+        if self.order:
+            self.value, hold = tie(self.value, hold)
+            self.got = swapped_2(self.value, *self.order.pop(0))
+        return hold
 
 
 VECTORS = (1, 4, 6, 7, 8, 12, 13, 14)
@@ -793,10 +867,8 @@
 
 def gathered(sums, vectors, devices):
     outs = [None] * 15
-    outs[0] = jnp.stack([one[2][1] for one in sums])
-    outs[2] = jnp.stack([one[3][0] for one in sums])
-    outs[3] = jnp.stack([one[3][1] for one in sums])
-    outs[5] = jnp.stack([one[2][0] for one in sums])
+    for place, which in enumerate((5, 0, 2, 3)):
+        outs[which] = jnp.stack([one[2][place] for one in sums])
     outs[9] = jnp.stack([one[1] for one in sums])
     outs[11] = jnp.stack([one[0] for one in sums])
     mine = lax.axis_index("batch") * lax.axis_size("seq") + lax.axis_index("seq")

time: 494 us -> 422 us (0.85)
  Pallas kernels: 313 us -> 248 us
  waiting for transfers between devices: 53.2 us -> 65.5 us
  other arithmetic: 17.9 us -> 8.57 us
  starting transfers between devices: 68.2 us -> 59.8 us
    pallas_call x13 -> x10, Pallas kernels: 54.2 us -> 27.3 us  [step_call(): pl.pallas_call(partial(step_kernel, plan), grid=(steps,), in_specs=[pl.Bl...]
    pallas_call x8 -> x7, Pallas kernels: 55.8 us -> 36.3 us  [wgrad_call(): pl.pallas_call(partial(wgrad_kernel, count), grid=(steps,), in_specs=[pl....]
    unnamed x115 -> x177, local copies, waits for them, and re-layouts: 12 us -> 25.1 us
    ppermute x64 -> x58, waiting for transfers between devices: 53.2 us -> 65.5 us  [swapped_2(): lax.ppermute(value, axis, [(i, i ^ 1 << bit) for i in range(lax.axis_size...]
    pallas_call x3, Pallas kernels: 22 us -> 12.3 us  [input_back_call(): pl.pallas_call(partial(input_back_kernel, layer, split), grid=(count,), i...]
    ppermute x64 -> x58, starting transfers between devices: 68.2 us -> 59.8 us  [swapped_2(): lax.ppermute(value, axis, [(i, i ^ 1 << bit) for i in range(lax.axis_size...]
    pallas_call x2, Pallas kernels: 39.2 us -> 33.2 us  [ff_back_call(): pl.pallas_call(partial(ff_back_kernel, layer), grid=(seqs,), in_specs=in_...]
    another operation x8 -> x0, local copies, waits for them, and re-layouts: 5.51 us -> none  [local(): jnp.stack([b_query, b_value, b_out, gain_one, shift_one, b_down, gain_two...]
  transfers between devices with their start and end apart: 64 -> 58, of which waited for: 12 -> 25; matrix products, arithmetic and copies ran while one was open for 7% -> 2% of each run, Pallas kernels for 47% -> 40%
where the time goes in v3:
time: 422 us; the launch traced here: 414 us
  Pallas kernels  248 us (59%)
  waiting for transfers between devices  65.5 us (16%)
  starting transfers between devices  59.8 us (14%)
  local copies, waits for them, and re-layouts  29.4 us (7%)
  other arithmetic  8.57 us (2%)
    pallas_call x4, Pallas kernels, forward_call(): pl.pallas_call(partial(forward_kernel, layer, swapped, start), grid=(coun...  91.3 us
    ppermute x58, waiting for transfers between devices, swapped_2(): lax.ppermute(value, axis, [(i, i ^ 1 << bit) for i in range(lax.axis_size...  65.5 us
    ppermute x58, starting transfers between devices, swapped_2(): lax.ppermute(value, axis, [(i, i ^ 1 << bit) for i in range(lax.axis_size...  59.8 us
    pallas_call x4, Pallas kernels, attention_back_call(): pl.pallas_call(partial(attention_back_kernel, layer, start), grid=(count,...  41.5 us
    pallas_call x7, Pallas kernels, wgrad_call(): pl.pallas_call(partial(wgrad_kernel, count), grid=(steps,), in_specs=[pl....  36.3 us
    pallas_call x2, Pallas kernels, ff_back_call(): pl.pallas_call(partial(ff_back_kernel, layer), grid=(seqs,), in_specs=in_...  33.2 us
    pallas_call x10, Pallas kernels, step_call(): pl.pallas_call(partial(step_kernel, plan), grid=(steps,), in_specs=[pl.Bl...  27.3 us
    unnamed x177, local copies, waits for them, and re-layouts  25.1 us
  transfers between devices with their start and end apart: 58, of which 25 were waited for; matrix products, arithmetic and copies ran while one was open for 2% of the time, Pallas kernels for 40%

profile of v3, /device:TPU:0, one launch (start us, length us, event | category | flops | bytes accessed | tf_op | source)
XLA Modules:
  0.0 413.5 jit_solution(9869939107021662730)
XLA Ops:
  4.9 28.5 %layer_forward_0.2 = (bf16[2,256,768]{2,1,0:T(8,128)(2,1)}, f32[3,256,768]{2,1,0:T(8,128)}, bf16[3,256,768]{2,1,0:T(8,128)(2,1)}, bf16[3,256,768]{2,1,0:T(8,128)...) custom-call(s32[7]{0:T(128)} %concatenate.21.facts, ...), custom_call_target="tpu_custom_call" | custom-call | flops 321999994880 | bytes 1 | tf_op jit(solution)/shard_map/layer_forward_0/pallas_call | solution.py:226
  33.5 2.9 collective-permute-start.2
  36.3 16.3 %layer_forward_0.3 = (bf16[1,256,768]{2,1,0:T(8,128)(2,1)}, f32[3,256,768]{2,1,0:T(8,128)}, bf16[3,256,768]{2,1,0:T(8,128)(2,1)}, bf16[3,256,768]{2,1,0:T(8,128)...) custom-call(s32[7]{0:T(128)} %concatenate.21.facts, ...), custom_call_target="tpu_custom_call", output_to_operand_aliasing={{1}: (12, {}), {2}: (13, {}), {3}: (14, {}), {4}: (15, {}),... | custom-call | flops 160999997440 | bytes 1 | tf_op jit(solution)/shard_map/layer_forward_0/pallas_call | solution.py:226
  52.7 1.9 collective-permute-done.2.near
  58.0 29.8 %layer_forward_1.2 = (bf16[2,256,768]{2,1,0:T(8,128)(2,1)}, bf16[3,256,768]{2,1,0:T(8,128)(2,1)}, bf16[3,256,768]{2,1,0:T(8,128)(2,1)}, bf16[3,256,768]{2,1,0:T(...) custom-call(s32[7]{0:T(128)} %concatenate.21.facts, ...), custom_call_target="tpu_custom_call" | custom-call | flops 321999994880 | bytes 1 | tf_op jit(solution)/shard_map/layer_forward_1/pallas_call | solution.py:226
  90.5 16.6 %layer_forward_1.3 = (bf16[1,256,768]{2,1,0:T(8,128)(2,1)}, bf16[3,256,768]{2,1,0:T(8,128)(2,1)}, bf16[3,256,768]{2,1,0:T(8,128)(2,1)}, bf16[3,256,768]{2,1,0:T(...) custom-call(s32[7]{0:T(128)} %concatenate.21.facts, ...), custom_call_target="tpu_custom_call", output_to_operand_aliasing={{1}: (12, {}), {2}: (13, {}), {3}: (14, {}), {4}: (15, {}),... | custom-call | flops 160999997440 | bytes 1 | tf_op jit(solution)/shard_map/layer_forward_1/pallas_call | solution.py:226
  107.2 2.3 copy-done.45
  114.0 16.0 %ff_back_1.1 = (bf16[3,256,768]{2,1,0:T(8,128)(2,1)S(1)}, bf16[3,256,3072]{2,1,0:T(8,128)(2,1)S(1)}, f32[3,256,768]{2,1,0:T(8,128)S(1)}, bf16[3,256,768]{2,1,0:T...) custom-call(bf16[3,256,768]{2,1,0:T(8,128)(2,1)S(1)} %copy-done.14, ...), custom_call_target="tpu_custom_call" | custom-call | flops 218500005888 | bytes 1 | tf_op jit(solution)/shard_map/ff_back_1/pallas_call | solution.py:326
  130.1 6.3 %wgrad_down.2 = (bf16[1,16,96,768]{3,2,1,0:T(8,128)(2,1)S(1)}, bf16[1,16,96,768]{3,2,1,0:T(8,128)(2,1)}) custom-call(s32[5]{0:T(128)S(1)} %stack.72.place_ref.bits, bf16[768,3072]{1,0:T(8,128)(2,1)S(1)} %bitcast.135, bf16[768,768]{1,0:T(8,128)(2,1)S(1)} %bitcast.151), custom_call_target="tpu_custom_call" | custom-call | flops 88763809792 | bytes 1 | tf_op jit(solution)/shard_map/wgrad_down/pallas_call | solution.py:529
  136.6 13.7 %attention_back_1.2 = (bf16[3,256,768]{2,1,0:T(8,128)(2,1)S(1)}, bf16[3,2,256,768]{3,2,1,0:T(8,128)(2,1)S(1)}, bf16[2,2,256,768]{3,2,1,0:T(8,128)(2,1)S(1)}, f32[8,768]{1,0:T(8,128)S(1)}) custom-call(s32[7]{0:T(128)S(1)} %copy-done.4, bf16[3,256,768]{2,1,0:T(8,128)(2,1)S(1)} %copy-done.55, bf16[3,512,768]{2,1,0:T(8,128)(2,1)S(1)} %copy-done.39, ...), custom_call_target="tpu_custom_call" | custom-call | flops 184000004096 | bytes 1 | tf_op jit(solution)/shard_map/attention_back_1/pallas_call | solution.py:412
  150.9 4.9 %exchange_step.10 = (bf16[1,8,96,768]{3,2,1,0:T(8,128)(2,1)S(1)}, bf16[1,8,96,768]{3,2,1,0:T(8,128)(2,1)}) custom-call(s32[5]{0:T(128)S(1)} %stack.72.place_ref.bits, bf16[1,16,96,768]{3,2,1,0:T(8,128)(2,1)S(1)} %get-tuple-element.441.refs_0_, bf16[1,16,96,768]{3,2,1,0:T(8,128)(2,1)} %collective-permute-done.5.refs_1_), custom_call_target="tpu_custom_call" | custom-call | flops 38631903232 | bytes 1 | tf_op jit(solution)/shard_map/exchange_step/pallas_call | solution.py:569
  158.0 7.1 %attention_back_1.3 = (bf16[3,256,768]{2,1,0:T(8,128)(2,1)S(1)}, bf16[3,2,256,768]{3,2,1,0:T(8,128)(2,1)S(1)}, bf16[1,2,256,768]{3,2,1,0:T(8,128)(2,1)S(1)}, f32[8,768]{1,0:T(8,128)S(1)}) custom-call(s32[7]{0:T(128)S(1)} %copy-done.4, bf16[3,256,768]{2,1,0:T(8,128)(2,1)S(1)} %copy-done.55, ...), custom_call_target="tpu_custom_call", output_to_operand_aliasing={{0}: (6, {}), {1}: (7, {})} | custom-call | flops 92000002048 | bytes 1 | tf_op jit(solution)/shard_map/attention_back_1/pallas_call | solution.py:412
  165.2 4.3 %input_back_1.2 = (f32[3,256,768]{2,1,0:T(8,128)S(1)}, bf16[3,2,256,768]{3,2,1,0:T(8,128)(2,1)S(1)}, bf16[2,256,768]{2,1,0:T(8,128)(2,1)}, f32[8,768]{1,0:T(8,128)S(1)}) custom-call(bf16[3,256,768]{2,1,0:T(8,128)(2,1)S(1)} %get-tuple-element.460.dq, bf16[3,2,256,768]{3,2,1,0:T(8,128)(2,1)S(1)} %get-tuple-element.461.near, ...), custom_call_target="tpu_custom_call" | custom-call | flops 92000002048 | bytes 1 | tf_op jit(solution)/shard_map/input_back_1/pallas_call | solution.py:486
  171.1 4.8 %wgrad_up.2 = (bf16[1,16,24,3072]{3,2,1,0:T(8,128)(2,1)S(1)}, bf16[1,16,24,3072]{3,2,1,0:T(8,128)(2,1)S(1)}) custom-call(s32[5]{0:T(128)S(1)} %stack.72.place_ref.bits, bf16[768,768]{1,0:T(8,128)(2,1)S(1)} %bitcast.144, bf16[768,3072]{1,0:T(8,128)(2,1)S(1)} %bitcast.136), custom_call_target="tpu_custom_call" | custom-call | flops 88763809792 | bytes 1 | tf_op jit(solution)/shard_map/wgrad_up/pallas_call | solution.py:529
  176.1 2.4 input_back_1.3
  179.8 4.9 %collective-permute-done.9.refs_3_ = bf16[1,8,96,768]{3,2,1,0:T(8,128)(2,1)} collective-permute-done((bf16[1,8,96,768]{3,2,1,0:T(8,128)(2,1)}, bf16[1,8,96,768]{3,2,1,0:T(8,128)(2,1)}, u32[]{:S(2)}, u32[]{:S(2)}) %collective-permute-start.9) | collective-permute-done | bytes 1179680 | tf_op jit(solution)/shard_map/ppermute | solution.py:19
  184.6 4.2 %exchange_step.11 = (bf16[1,8,24,3072]{3,2,1,0:T(8,128)(2,1)S(1)}, bf16[1,8,24,3072]{3,2,1,0:T(8,128)(2,1)}, bf16[1,4,96,768]{3,2,1,0:T(8,128)(2,1)S(1)}, bf16[1,4,96,768]{3,2,1,0:T(8,128)(2,1)}) custom-call(s32[5]{0:T(128)S(1)} %stack.72.place_ref.bits, bf16[1,16,24,3072]{3,2,1,0:T(8,128)(2,1)S(1)} %get-tuple-element.473.refs_0_, ...), custom_call_target="tpu_custom_call" | custom-call | flops 52197855232 | bytes 1 | tf_op jit(solution)/shard_map/exchange_step/pallas_call | solution.py:569
  190.8 6.2 %wgrad_four.1 = (bf16[4,16,24,768]{3,2,1,0:T(8,128)(2,1)S(1)}, bf16[4,16,24,768]{3,2,1,0:T(8,128)(2,1)}) custom-call(s32[5]{0:T(128)S(1)} %stack.72.place_ref.bits, bf16[768,768]{1,0:T(8,128)(2,1)S(1)} %bitcast.143, bf16[768,768]{1,0:T(8,128)(2,1)S(1)} %bitcast.146, bf16[768,768]{1,0:T(8,128)(2,1)S(1)} %bitcast.141, bf16[768,768]{1,0:T(8,128)(2,1)S(1)} %bitcast.142, ...), custom_call_target="tpu_custom_call" | custom-call | flops 88763809792 | bytes 1 | tf_op jit(solution)/shard_map/wgrad_four/pallas_call | solution.py:529
  201.9 17.2 %ff_back_0.1 = (bf16[3,256,768]{2,1,0:T(8,128)(2,1)S(1)}, bf16[3,256,3072]{2,1,0:T(8,128)(2,1)S(1)}, f32[3,256,768]{2,1,0:T(8,128)S(1)}, bf16[3,256,768]{2,1,0:T...) custom-call(f32[3,256,768]{2,1,0:T(8,128)S(1)} %convert_add_fusion.top_grad, ...), custom_call_target="tpu_custom_call" | custom-call | flops 218500005888 | bytes 1 | tf_op jit(solution)/shard_map/ff_back_0/pallas_call | solution.py:326
  220.5 4.6 %exchange_step.12 = (bf16[1,2,96,768]{3,2,1,0:T(8,128)(2,1)S(1)}, bf16[1,2,96,768]{3,2,1,0:T(8,128)(2,1)S(1)}, bf16[4,8,24,768]{3,2,1,0:T(8,128)(2,1)S(1)}, bf16[4,8,24,768]{3,2,1,0:T(8,128)(2,1)}) custom-call(s32[5]{0:T(128)S(1)} %stack.72.place_ref.bits, bf16[1,4,96,768]{3,2,1,0:T(8,128)(2,1)S(1)} %get-tuple-element.489.refs_0_, ...), custom_call_target="tpu_custom_call" | custom-call | flops 45414879232 | bytes 1 | tf_op jit(solution)/shard_map/exchange_step/pallas_call | solution.py:569
  225.1 5.4 %wgrad_down.3 = (bf16[1,16,96,768]{3,2,1,0:T(8,128)(2,1)S(1)}, bf16[1,16,96,768]{3,2,1,0:T(8,128)(2,1)S(1)}) custom-call(s32[5]{0:T(128)S(1)} %stack.72.place_ref.bits, bf16[768,3072]{1,0:T(8,128)(2,1)S(1)} %bitcast.138, bf16[768,768]{1,0:T(8,128)(2,1)S(1)} %bitcast.149), custom_call_target="tpu_custom_call" | custom-call | flops 88763809792 | bytes 1 | tf_op jit(solution)/shard_map/wgrad_down/pallas_call | solution.py:529
  232.7 5.9 %wgrad_up.3 = (bf16[1,16,24,3072]{3,2,1,0:T(8,128)(2,1)S(1)}, bf16[1,16,24,3072]{3,2,1,0:T(8,128)(2,1)}) custom-call(s32[5]{0:T(128)S(1)} %stack.72.place_ref.bits, bf16[768,768]{1,0:T(8,128)(2,1)S(1)} %bitcast.148, bf16[768,3072]{1,0:T(8,128)(2,1)S(1)} %bitcast.137), custom_call_target="tpu_custom_call" | custom-call | flops 88763809792 | bytes 1 | tf_op jit(solution)/shard_map/wgrad_up/pallas_call | solution.py:529
  241.1 4.2 %exchange_step.13 = (bf16[1,1,96,768]{3,2,1,0:T(8,128)(2,1)S(1)}, bf16[1,1,96,768]{3,2,1,0:T(8,128)(2,1)}, bf16[1,4,24,3072]{3,2,1,0:T(8,128)(2,1)S(1)}, bf16[1,4,24,3072]{3,2,1,0:T(8,128)(2,1)}) custom-call(s32[5]{0:T(128)S(1)} %copy-done.2, bf16[1,2,96,768]{3,2,1,0:T(8,128)(2,1)S(1)} %get-tuple-element.544.refs_0_, ...), custom_call_target="tpu_custom_call" | custom-call | flops 28457439232 | bytes 1 | tf_op jit(solution)/shard_map/exchange_step/pallas_call | solution.py:569
  245.8 2.6 collective-permute-start.20
  248.4 13.7 %attention_back_0.2 = (bf16[3,256,768]{2,1,0:T(8,128)(2,1)S(1)}, bf16[3,2,256,768]{3,2,1,0:T(8,128)(2,1)S(1)}, bf16[3,2,256,768]{3,2,1,0:T(8,128)(2,1)S(1)}, f32[8,768]{1,0:T(8,128)S(1)}) custom-call(s32[7]{0:T(128)S(1)} %copy-done.4, bf16[3,256,768]{2,1,0:T(8,128)(2,1)S(1)} %copy-done.54, bf16[3,512,768]{2,1,0:T(8,128)(2,1)S(1)} %copy-done.37, ...), custom_call_target="tpu_custom_call" | custom-call | flops 184000004096 | bytes 1 | tf_op jit(solution)/shard_map/attention_back_0/pallas_call | solution.py:412
  262.1 3.3 collective-permute-done.19.refs_3_
  265.4 2.5 exchange_lanes.2
  267.9 3.6 exchange_step.14
  273.1 7.1 %attention_back_0.3 = (bf16[3,256,768]{2,1,0:T(8,128)(2,1)S(1)}, bf16[3,2,256,768]{3,2,1,0:T(8,128)(2,1)S(1)}, bf16[3,2,256,768]{3,2,1,0:T(8,128)(2,1)S(1)}, f32[8,768]{1,0:T(8,128)S(1)}) custom-call(s32[7]{0:T(128)S(1)} %copy-done.4, bf16[3,256,768]{2,1,0:T(8,128)(2,1)S(1)} %copy-done.54, ...), custom_call_target="tpu_custom_call", output_to_operand_aliasing={{0}: (6, {}), {1}: (7, {}), {2}: (8, {})} | custom-call | flops 92000002048 | bytes 1 | tf_op jit(solution)/shard_map/attention_back_0/pallas_call | solution.py:412
  284.6 3.9 wgrad_rest.1
  290.5 3.9 wgrad_pair.1
  294.4 4.8 %collective-permute-done.23.refs_1_ = bf16[1,8,192,256]{3,2,1,0:T(8,128)(2,1)S(1)} collective-permute-done((bf16[1,8,192,256]{3,2,1,0:T(8,128)(2,1)S(1)}, bf16[1,8,192,256]{3,2,1,0:T(8,128)(2,1)S(1)}, u32[]{:S(2)}, u32[]{:S(2)}) %collective-permute-start.23) | collective-permute-done | bytes 786464 | tf_op jit(solution)/shard_map/ppermute | solution.py:19
  299.2 2.2 collective-permute-done.24.refs_3_
  305.2 5.6 %input_back_0.1 = (f32[3,256,768]{2,1,0:T(8,128)}, f32[8,768]{1,0:T(8,128)}) custom-call(bf16[3,256,768]{2,1,0:T(8,128)(2,1)S(1)} %get-tuple-element.587.dq, bf16[3,2,256,768]{3,2,1,0:T(8,128)(2,1)S(1)} %add_convert_fusion.near, f32[3,256,768]{2,1,0:T(8,128)S(1)} %copy-done.53, bf16[2,768,768]{2,1,0:T(8,128)(2,1)S(1)} %copy-done.7, ...), custom_call_target="tpu_custom_call" | custom-call | flops 126500003840 | bytes 1 | tf_op jit(solution)/shard_map/input_back_0/pallas_call | solution.py:486
  315.4 2.1 exchange_lanes.3
  318.3 4.5 %collective-permute-done.30.refs_1_ = bf16[1,4,192,256]{3,2,1,0:T(8,128)(2,1)S(1)} collective-permute-done((bf16[1,4,192,256]{3,2,1,0:T(8,128)(2,1)S(1)}, bf16[1,4,192,256]{3,2,1,0:T(8,128)(2,1)S(1)}, u32[]{:S(2)}, u32[]{:S(2)}) %collective-permute-start.30) | collective-permute-done | bytes 393248 | tf_op jit(solution)/shard_map/ppermute | solution.py:19
  325.0 2.2 exchange_step.16
  329.1 2.1 collective-permute-start.42
  335.4 6.1 %collective-permute-done.43 = f32[2,12,768]{2,1,0:T(8,128)S(1)} collective-permute-done((f32[2,12,768]{2,1,0:T(8,128)S(1)}, f32[2,12,768]{2,1,0:T(8,128)S(1)}, u32[]{:S(2)}, u32[]{:S(2)}) %collective-permute-start.43) | collective-permute-done | bytes 73760 | tf_op jit(solution)/shard_map/ppermute | solution.py:19
  344.9 2.6 collective-permute-done.36.refs_3_
  349.6 5.8 %collective-permute-done.37.refs_5_ = bf16[1,2,192,256]{3,2,1,0:T(8,128)(2,1)} collective-permute-done((bf16[1,2,192,256]{3,2,1,0:T(8,128)(2,1)}, bf16[1,2,192,256]{3,2,1,0:T(8,128)(2,1)}, u32[]{:S(2)}, u32[]{:S(2)}) %collective-permute-start.37) | collective-permute-done | bytes 196640 | tf_op jit(solution)/shard_map/ppermute | solution.py:19
  355.4 3.3 collective-permute-done.41.refs_13_
  367.9 1.8 collective-permute-start.51
  375.9 3.7 collective-permute-done.51
  381.7 1.9 collective-permute-done.45
  384.7 8.0 %collective-permute-done.46 = bf16[1,1,192,256]{3,2,1,0:T(8,128)(2,1)S(1)} collective-permute-done((bf16[1,1,192,256]{3,2,1,0:T(8,128)(2,1)S(1)}, bf16[1,1,192,256]{3,2,1,0:T(8,128)(2,1)S(1)}, u32[]{:S(2)}, u32[]{:S(2)}) %collective-permute-start.46) | collective-permute-done | bytes 98336 | tf_op jit(solution)/shard_map/ppermute | solution.py:19
  400.5 3.1 collective-permute-start.55
  403.6 2.8 collective-permute-start.57
  (327 shorter events, 98.2 us)
Async XLA Ops:
  33.5 21.1 %collective-permute-start.2 = (bf16[2,256,768]{2,1,0:T(8,128)(2,1)}, bf16[2,256,768]{2,1,0:T(8,128)(2,1)}, u32[]{:S(2)}, u32[]{:S(2)}) collective-permute-start(bf16[2,256,768]{2,1,0:T(8,128)(2,1)} %get-tuple-element.404), channel_id=1, source_target_pairs={{0,2},{1,3},{2,0},{3,1},{4,6},{5,7},{6,4},{7,5},{8,10},{9,11},{10,... | collective-permute-start | bytes 2359304 | tf_op jit(solution)/shard_map/ppermute | solution.py:19
  54.6 33.2 %collective-permute-start.1 = (bf16[1,256,768]{2,1,0:T(8,128)(2,1)}, bf16[1,256,768]{2,1,0:T(8,128)(2,1)}, u32[]{:S(2)}, u32[]{:S(2)}) collective-permute-start(bf16[1,256,768]{2,1,0:T(8,128)(2,1)} %get-tuple-element.403), channel_id=1, source_target_pairs={{0,2},{1,3},{2,0},{3,1},{4,6},{5,7},{6,4},{7,5},{8,10},{9,11},{10,... | collective-permute-start | bytes 1179656 | tf_op jit(solution)/shard_map/ppermute | solution.py:19
  136.4 14.5 %collective-permute-start.5 = (bf16[1,16,96,768]{3,2,1,0:T(8,128)(2,1)}, bf16[1,16,96,768]{3,2,1,0:T(8,128)(2,1)}, u32[]{:S(2)}, u32[]{:S(2)}) collective-permute-start(bf16[1,16,96,768]{3,2,1,0:T(8,128)(2,1)} %get-tuple-element.447), channel_id=1, source_target_pairs={{0,1},{1,0},{2,3},{3,2},{4,5},{5,4},{6,7},{7,6},{8,9},{9,8},{10,11... | collective-permute-start | bytes 7077896 | tf_op jit(solution)/shard_map/ppermute | solution.py:19
  155.8 9.3 %collective-permute-start.6 = (bf16[2,2,256,768]{3,2,1,0:T(8,128)(2,1)S(1)}, bf16[2,2,256,768]{3,2,1,0:T(8,128)(2,1)S(1)}, u32[]{:S(2)}, u32[]{:S(2)}) collective-permute-start(bf16[2,2,256,768]{3,2,1,0:T(8,128)(2,1)S(1)} %get-tuple-element.458), channel_id=1, source_target_pairs={{0,1},{1,0},{2,3},{3,2},{4,5},{5,4},{6,7},{7,6},{8,9},{9,8},{10,11... | collective-permute-start | bytes 4718600 | tf_op jit(solution)/shard_map/ppermute | solution.py:19
  156.2 28.4 %collective-permute-start.9 = (bf16[1,8,96,768]{3,2,1,0:T(8,128)(2,1)}, bf16[1,8,96,768]{3,2,1,0:T(8,128)(2,1)}, u32[]{:S(2)}, u32[]{:S(2)}) collective-permute-start(bf16[1,8,96,768]{3,2,1,0:T(8,128)(2,1)} %get-tuple-element.485), channel_id=1, source_target_pairs={{0,4},{4,0},{8,12},{12,8},{16,20},{20,16},{24,28},{28,24},{1,5},{5... | collective-permute-start | bytes 3538952 | tf_op jit(solution)/shard_map/ppermute | solution.py:19
  169.5 27.5 %collective-permute-start.10 = (bf16[2,256,768]{2,1,0:T(8,128)(2,1)}, bf16[2,256,768]{2,1,0:T(8,128)(2,1)}, u32[]{:S(2)}, u32[]{:S(2)}) collective-permute-start(bf16[2,256,768]{2,1,0:T(8,128)(2,1)} %get-tuple-element.500), channel_id=1, source_target_pairs={{0,2},{1,3},{2,0},{3,1},{4,6},{5,7},{6,4},{7,5},{8,10},{9,11},{10,... | collective-permute-start | bytes 2359304 | tf_op jit(solution)/shard_map/ppermute | solution.py:19
  175.9 8.7 %collective-permute-start.8 = (bf16[1,16,24,3072]{3,2,1,0:T(8,128)(2,1)S(1)}, bf16[1,16,24,3072]{3,2,1,0:T(8,128)(2,1)S(1)}, u32[]{:S(2)}, u32[]{:S(2)}) collective-permute-start(bf16[1,16,24,3072]{3,2,1,0:T(8,128)(2,1)S(1)} %get-tuple-element.484), channel_id=1, source_target_pairs={{0,1},{1,0},{2,3},{3,2},{4,5},{5,4},{6,7},{7,6},{8,9},{9,8},{10,11... | collective-permute-start | bytes 7077896 | tf_op jit(solution)/shard_map/ppermute | solution.py:19
  178.5 19.6 %collective-permute-start.11 = (bf16[1,256,768]{2,1,0:T(8,128)(2,1)S(1)}, bf16[1,256,768]{2,1,0:T(8,128)(2,1)S(1)}, u32[]{:S(2)}, u32[]{:S(2)}) collective-permute-start(bf16[1,256,768]{2,1,0:T(8,128)(2,1)S(1)} %get-tuple-element.483), channel_id=1, source_target_pairs={{0,2},{1,3},{2,0},{3,1},{4,6},{5,7},{6,4},{7,5},{8,10},{9,11},{10,... | collective-permute-start | bytes 1179656 | tf_op jit(solution)/shard_map/ppermute | solution.py:19
  198.1 22.4 %collective-permute-start.13 = (bf16[4,16,24,768]{3,2,1,0:T(8,128)(2,1)}, bf16[4,16,24,768]{3,2,1,0:T(8,128)(2,1)}, u32[]{:S(2)}, u32[]{:S(2)}) collective-permute-start(bf16[4,16,24,768]{3,2,1,0:T(8,128)(2,1)} %get-tuple-element.515), channel_id=1, source_target_pairs={{0,1},{1,0},{2,3},{3,2},{4,5},{5,4},{6,7},{7,6},{8,9},{9,8},{10,11... | collective-permute-start | bytes 7077896 | tf_op jit(solution)/shard_map/ppermute | solution.py:19
  198.2 22.3 %collective-permute-start.12 = (bf16[1,4,96,768]{3,2,1,0:T(8,128)(2,1)}, bf16[1,4,96,768]{3,2,1,0:T(8,128)(2,1)}, u32[]{:S(2)}, u32[]{:S(2)}) collective-permute-start(bf16[1,4,96,768]{3,2,1,0:T(8,128)(2,1)} %get-tuple-element.514), channel_id=1, source_target_pairs={{0,8},{4,12},{8,0},{12,4},{16,24},{20,28},{24,16},{28,20},{1,9},{5... | collective-permute-start | bytes 1769480 | tf_op jit(solution)/shard_map/ppermute | solution.py:19
  199.8 39.4 %collective-permute-start.16 = (bf16[1,8,24,3072]{3,2,1,0:T(8,128)(2,1)}, bf16[1,8,24,3072]{3,2,1,0:T(8,128)(2,1)}, u32[]{:S(2)}, u32[]{:S(2)}) collective-permute-start(bf16[1,8,24,3072]{3,2,1,0:T(8,128)(2,1)} %get-tuple-element.534), channel_id=1, source_target_pairs={{0,4},{4,0},{8,12},{12,8},{16,20},{20,16},{24,28},{28,24},{1,5},{5... | collective-permute-start | bytes 3538952 | tf_op jit(solution)/shard_map/ppermute | solution.py:19
  230.5 10.0 %collective-permute-start.14 = (bf16[1,16,96,768]{3,2,1,0:T(8,128)(2,1)S(1)}, bf16[1,16,96,768]{3,2,1,0:T(8,128)(2,1)S(1)}, u32[]{:S(2)}, u32[]{:S(2)}) collective-permute-start(bf16[1,16,96,768]{3,2,1,0:T(8,128)(2,1)S(1)} %get-tuple-element.532), channel_id=1, source_target_pairs={{0,1},{1,0},{2,3},{3,2},{4,5},{5,4},{6,7},{7,6},{8,9},{9,8},{10,11... | collective-permute-start | bytes 7077896 | tf_op jit(solution)/shard_map/ppermute | solution.py:19
  230.6 9.9 %collective-permute-start.15 = (bf16[1,2,96,768]{3,2,1,0:T(8,128)(2,1)S(1)}, bf16[1,2,96,768]{3,2,1,0:T(8,128)(2,1)S(1)}, u32[]{:S(2)}, u32[]{:S(2)}) collective-permute-start(bf16[1,2,96,768]{3,2,1,0:T(8,128)(2,1)S(1)} %get-tuple-element.533), channel_id=1, source_target_pairs={{0,2},{1,3},{2,0},{3,1},{4,6},{5,7},{6,4},{7,5},{8,10},{9,11},{10,... | collective-permute-start | bytes 884744 | tf_op jit(solution)/shard_map/ppermute | solution.py:19
  232.1 33.3 %collective-permute-start.19 = (bf16[4,8,24,768]{3,2,1,0:T(8,128)(2,1)}, bf16[4,8,24,768]{3,2,1,0:T(8,128)(2,1)}, u32[]{:S(2)}, u32[]{:S(2)}) collective-permute-start(bf16[4,8,24,768]{3,2,1,0:T(8,128)(2,1)} %get-tuple-element.558), channel_id=1, source_target_pairs={{0,2},{1,3},{2,0},{3,1},{4,6},{5,7},{6,4},{7,5},{8,10},{9,11},{10,... | collective-permute-start | bytes 3538952 | tf_op jit(solution)/shard_map/ppermute | solution.py:19
  245.3 20.1 %collective-permute-start.17 = (bf16[1,16,24,3072]{3,2,1,0:T(8,128)(2,1)}, bf16[1,16,24,3072]{3,2,1,0:T(8,128)(2,1)}, u32[]{:S(2)}, u32[]{:S(2)}) collective-permute-start(bf16[1,16,24,3072]{3,2,1,0:T(8,128)(2,1)} %get-tuple-element.556), channel_id=1, source_target_pairs={{0,1},{1,0},{2,3},{3,2},{4,5},{5,4},{6,7},{7,6},{8,9},{9,8},{10,11... | collective-permute-start | bytes 7077896 | tf_op jit(solution)/shard_map/ppermute | solution.py:19
  245.3 20.1 %collective-permute-start.18 = (bf16[1,4,24,3072]{3,2,1,0:T(8,128)(2,1)}, bf16[1,4,24,3072]{3,2,1,0:T(8,128)(2,1)}, u32[]{:S(2)}, u32[]{:S(2)}) collective-permute-start(bf16[1,4,24,3072]{3,2,1,0:T(8,128)(2,1)} %get-tuple-element.557), channel_id=1, source_target_pairs={{0,8},{4,12},{8,0},{12,4},{16,24},{20,28},{24,16},{28,20},{1,9},{5... | collective-permute-start | bytes 1769480 | tf_op jit(solution)/shard_map/ppermute | solution.py:19
  245.8 19.6 %collective-permute-start.20 = (bf16[1,1,96,768]{3,2,1,0:T(8,128)(2,1)}, bf16[1,1,96,768]{3,2,1,0:T(8,128)(2,1)}, u32[]{:S(2)}, u32[]{:S(2)}) collective-permute-start(bf16[1,1,96,768]{3,2,1,0:T(8,128)(2,1)} %get-tuple-element.559), channel_id=1, source_target_pairs={{0,16},{4,20},{8,24},{12,28},{16,0},{20,4},{24,8},{28,12},{1,17},{... | collective-permute-start | bytes 442376 | tf_op jit(solution)/shard_map/ppermute | solution.py:19
  271.6 13.0 %collective-permute-start.21 = (bf16[1,2,24,3072]{3,2,1,0:T(8,128)(2,1)S(1)}, bf16[1,2,24,3072]{3,2,1,0:T(8,128)(2,1)S(1)}, u32[]{:S(2)}, u32[]{:S(2)}) collective-permute-start(bf16[1,2,24,3072]{3,2,1,0:T(8,128)(2,1)S(1)} %get-tuple-element.582), channel_id=1, source_target_pairs={{0,2},{1,3},{2,0},{3,1},{4,6},{5,7},{6,4},{7,5},{8,10},{9,11},{10,... | collective-permute-start | bytes 884744 | tf_op jit(solution)/shard_map/ppermute | solution.py:19
  280.2 18.9 %collective-permute-start.23 = (bf16[1,8,192,256]{3,2,1,0:T(8,128)(2,1)S(1)}, bf16[1,8,192,256]{3,2,1,0:T(8,128)(2,1)S(1)}, u32[]{:S(2)}, u32[]{:S(2)}) collective-permute-start(bf16[1,8,192,256]{3,2,1,0:T(8,128)(2,1)S(1)} %get-tuple-element.601), channel_id=1, source_target_pairs={{0,2},{1,3},{2,0},{3,1},{4,6},{5,7},{6,4},{7,5},{8,10},{9,11},{10,... | collective-permute-start | bytes 2359304 | tf_op jit(solution)/shard_map/ppermute | solution.py:19
  280.8 20.5 %collective-permute-start.24 = (bf16[1,8,192,256]{3,2,1,0:T(8,128)(2,1)S(1)}, bf16[1,8,192,256]{3,2,1,0:T(8,128)(2,1)S(1)}, u32[]{:S(2)}, u32[]{:S(2)}) collective-permute-start(bf16[1,8,192,256]{3,2,1,0:T(8,128)(2,1)S(1)} %get-tuple-element.602), channel_id=1, source_target_pairs={{0,4},{4,0},{8,12},{12,8},{16,20},{20,16},{24,28},{28,24},{1,5},{5... | collective-permute-start | bytes 2359304 | tf_op jit(solution)/shard_map/ppermute | solution.py:19
  282.2 19.1 %collective-permute-start.25 = (bf16[1,8,192,256]{3,2,1,0:T(8,128)(2,1)S(1)}, bf16[1,8,192,256]{3,2,1,0:T(8,128)(2,1)S(1)}, u32[]{:S(2)}, u32[]{:S(2)}) collective-permute-start(bf16[1,8,192,256]{3,2,1,0:T(8,128)(2,1)S(1)} %get-tuple-element.603), channel_id=1, source_target_pairs={{0,8},{4,12},{8,0},{12,4},{16,24},{20,28},{24,16},{28,20},{1,9},{5... | collective-permute-start | bytes 2359304 | tf_op jit(solution)/shard_map/ppermute | solution.py:19
  284.0 34.4 %collective-permute-start.33 = (bf16[4,4,24,768]{3,2,1,0:T(8,128)(2,1)}, bf16[4,4,24,768]{3,2,1,0:T(8,128)(2,1)}, u32[]{:S(2)}, u32[]{:S(2)}) collective-permute-start(bf16[4,4,24,768]{3,2,1,0:T(8,128)(2,1)} %get-tuple-element.636), channel_id=1, source_target_pairs={{0,4},{4,0},{8,12},{12,8},{16,20},{20,16},{24,28},{28,24},{1,5},{5... | collective-permute-start | bytes 1769480 | tf_op jit(solution)/shard_map/ppermute | solution.py:19
  290.3 11.1 %collective-permute-start.26 = (f32[2,12,768]{2,1,0:T(8,128)S(1)}, f32[2,12,768]{2,1,0:T(8,128)S(1)}, u32[]{:S(2)}, u32[]{:S(2)}) collective-permute-start(f32[2,12,768]{2,1,0:T(8,128)S(1)} %pad_maximum_fusion.7), channel_id=1, source_target_pairs={{0,1},{1,0},{2,3},{3,2},{4,5},{5,4},{6,7},{7,6},{8,9},{9,8},{10,11... | collective-permute-start | bytes 221192 | tf_op jit(solution)/shard_map/ppermute | solution.py:19
  299.2 14.8 %collective-permute-start.28 = (bf16[2,16,24,768]{3,2,1,0:T(8,128)(2,1)}, bf16[2,16,24,768]{3,2,1,0:T(8,128)(2,1)}, u32[]{:S(2)}, u32[]{:S(2)}) collective-permute-start(bf16[2,16,24,768]{3,2,1,0:T(8,128)(2,1)} %get-tuple-element.621), channel_id=1, source_target_pairs={{0,1},{1,0},{2,3},{3,2},{4,5},{5,4},{6,7},{7,6},{8,9},{9,8},{10,11... | collective-permute-start | bytes 3538952 | tf_op jit(solution)/shard_map/ppermute | solution.py:19
  301.3 14.1 %collective-permute-start.27 = (bf16[2,16,24,768]{3,2,1,0:T(8,128)(2,1)}, bf16[2,16,24,768]{3,2,1,0:T(8,128)(2,1)}, u32[]{:S(2)}, u32[]{:S(2)}) collective-permute-start(bf16[2,16,24,768]{3,2,1,0:T(8,128)(2,1)} %get-tuple-element.620), channel_id=1, source_target_pairs={{0,1},{1,0},{2,3},{3,2},{4,5},{5,4},{6,7},{7,6},{8,9},{9,8},{10,11... | collective-permute-start | bytes 3538952 | tf_op jit(solution)/shard_map/ppermute | solution.py:19
  302.5 9.7 %collective-permute-start.29 = (f32[2,12,768]{2,1,0:T(8,128)S(1)}, f32[2,12,768]{2,1,0:T(8,128)S(1)}, u32[]{:S(2)}, u32[]{:S(2)}) collective-permute-start(f32[2,12,768]{2,1,0:T(8,128)S(1)} %add.71), channel_id=1, source_target_pairs={{0,2},{1,3},{2,0},{3,1},{4,6},{5,7},{6,4},{7,5},{8,10},{9,11},{10,... | collective-permute-start | bytes 221192 | tf_op jit(solution)/shard_map/ppermute | solution.py:19
  310.8 12.0 %collective-permute-start.30 = (bf16[1,4,192,256]{3,2,1,0:T(8,128)(2,1)S(1)}, bf16[1,4,192,256]{3,2,1,0:T(8,128)(2,1)S(1)}, u32[]{:S(2)}, u32[]{:S(2)}) collective-permute-start(bf16[1,4,192,256]{3,2,1,0:T(8,128)(2,1)S(1)} %get-tuple-element.633), channel_id=1, source_target_pairs={{0,4},{4,0},{8,12},{12,8},{16,20},{20,16},{24,28},{28,24},{1,5},{5... | collective-permute-start | bytes 1179656 | tf_op jit(solution)/shard_map/ppermute | solution.py:19
  312.3 11.2 %collective-permute-start.31 = (bf16[1,4,192,256]{3,2,1,0:T(8,128)(2,1)S(1)}, bf16[1,4,192,256]{3,2,1,0:T(8,128)(2,1)S(1)}, u32[]{:S(2)}, u32[]{:S(2)}) collective-permute-start(bf16[1,4,192,256]{3,2,1,0:T(8,128)(2,1)S(1)} %get-tuple-element.634), channel_id=1, source_target_pairs={{0,8},{4,12},{8,0},{12,4},{16,24},{20,28},{24,16},{28,20},{1,9},{5... | collective-permute-start | bytes 1179656 | tf_op jit(solution)/shard_map/ppermute | solution.py:19
  314.0 11.0 %collective-permute-start.32 = (bf16[1,4,192,256]{3,2,1,0:T(8,128)(2,1)S(1)}, bf16[1,4,192,256]{3,2,1,0:T(8,128)(2,1)S(1)}, u32[]{:S(2)}, u32[]{:S(2)}) collective-permute-start(bf16[1,4,192,256]{3,2,1,0:T(8,128)(2,1)S(1)} %get-tuple-element.635), channel_id=1, source_target_pairs={{0,2},{1,3},{2,0},{3,1},{4,6},{5,7},{6,4},{7,5},{8,10},{9,11},{10,... | collective-permute-start | bytes 1179656 | tf_op jit(solution)/shard_map/ppermute | solution.py:19
  317.6 7.4 %collective-permute-start.34 = (f32[2,12,768]{2,1,0:T(8,128)S(1)}, f32[2,12,768]{2,1,0:T(8,128)S(1)}, u32[]{:S(2)}, u32[]{:S(2)}) collective-permute-start(f32[2,12,768]{2,1,0:T(8,128)S(1)} %add.72), channel_id=1, source_target_pairs={{0,4},{4,0},{8,12},{12,8},{16,20},{20,16},{24,28},{28,24},{1,5},{5... | collective-permute-start | bytes 221192 | tf_op jit(solution)/shard_map/ppermute | solution.py:19
  329.1 13.8 %collective-permute-start.42 = (bf16[1,1,24,3072]{3,2,1,0:T(8,128)(2,1)S(1)}, bf16[1,1,24,3072]{3,2,1,0:T(8,128)(2,1)S(1)}, u32[]{:S(2)}, u32[]{:S(2)}) collective-permute-start(bf16[1,1,24,3072]{3,2,1,0:T(8,128)(2,1)S(1)} %get-tuple-element.666), channel_id=1, source_target_pairs={{0,16},{4,20},{8,24},{12,28},{16,0},{20,4},{24,8},{28,12},{1,17},{... | collective-permute-start | bytes 442376 | tf_op jit(solution)/shard_map/ppermute | solution.py:19
  331.3 13.2 %collective-permute-start.35 = (bf16[1,2,192,256]{3,2,1,0:T(8,128)(2,1)S(1)}, bf16[1,2,192,256]{3,2,1,0:T(8,128)(2,1)S(1)}, u32[]{:S(2)}, u32[]{:S(2)}) collective-permute-start(bf16[1,2,192,256]{3,2,1,0:T(8,128)(2,1)S(1)} %get-tuple-element.659), channel_id=1, source_target_pairs={{0,8},{4,12},{8,0},{12,4},{16,24},{20,28},{24,16},{28,20},{1,9},{5... | collective-permute-start | bytes 589832 | tf_op jit(solution)/shard_map/ppermute | solution.py:19
  332.0 9.5 %collective-permute-start.43 = (f32[2,12,768]{2,1,0:T(8,128)S(1)}, f32[2,12,768]{2,1,0:T(8,128)S(1)}, u32[]{:S(2)}, u32[]{:S(2)}) collective-permute-start(f32[2,12,768]{2,1,0:T(8,128)S(1)} %add.73), channel_id=1, source_target_pairs={{0,8},{4,12},{8,0},{12,4},{16,24},{20,28},{24,16},{28,20},{1,9},{5... | collective-permute-start | bytes 221192 | tf_op jit(solution)/shard_map/ppermute | solution.py:19
  333.4 25.3 %collective-permute-start.38 = (bf16[4,8,24,256]{3,2,1,0:T(8,128)(2,1)S(1)}, bf16[4,8,24,256]{3,2,1,0:T(8,128)(2,1)S(1)}, u32[]{:S(2)}, u32[]{:S(2)}) collective-permute-start(bf16[4,8,24,256]{3,2,1,0:T(8,128)(2,1)S(1)} %get-tuple-element.662), channel_id=1, source_target_pairs={{0,2},{1,3},{2,0},{3,1},{4,6},{5,7},{6,4},{7,5},{8,10},{9,11},{10,... | collective-permute-start | bytes 1179656 | tf_op jit(solution)/shard_map/ppermute | solution.py:19
  334.9 12.6 %collective-permute-start.36 = (bf16[1,2,192,256]{3,2,1,0:T(8,128)(2,1)S(1)}, bf16[1,2,192,256]{3,2,1,0:T(8,128)(2,1)S(1)}, u32[]{:S(2)}, u32[]{:S(2)}) collective-permute-start(bf16[1,2,192,256]{3,2,1,0:T(8,128)(2,1)S(1)} %get-tuple-element.660), channel_id=1, source_target_pairs={{0,2},{1,3},{2,0},{3,1},{4,6},{5,7},{6,4},{7,5},{8,10},{9,11},{10,... | collective-permute-start | bytes 589832 | tf_op jit(solution)/shard_map/ppermute | solution.py:19
  341.5 17.2 %collective-permute-start.39 = (bf16[4,8,24,256]{3,2,1,0:T(8,128)(2,1)S(1)}, bf16[4,8,24,256]{3,2,1,0:T(8,128)(2,1)S(1)}, u32[]{:S(2)}, u32[]{:S(2)}) collective-permute-start(bf16[4,8,24,256]{3,2,1,0:T(8,128)(2,1)S(1)} %get-tuple-element.663), channel_id=1, source_target_pairs={{0,4},{4,0},{8,12},{12,8},{16,20},{20,16},{24,28},{28,24},{1,5},{5... | collective-permute-start | bytes 1179656 | tf_op jit(solution)/shard_map/ppermute | solution.py:19
  342.9 15.8 %collective-permute-start.40 = (bf16[4,8,24,256]{3,2,1,0:T(8,128)(2,1)S(1)}, bf16[4,8,24,256]{3,2,1,0:T(8,128)(2,1)S(1)}, u32[]{:S(2)}, u32[]{:S(2)}) collective-permute-start(bf16[4,8,24,256]{3,2,1,0:T(8,128)(2,1)S(1)} %get-tuple-element.664), channel_id=1, source_target_pairs={{0,8},{4,12},{8,0},{12,4},{16,24},{20,28},{24,16},{28,20},{1,9},{5... | collective-permute-start | bytes 1179656 | tf_op jit(solution)/shard_map/ppermute | solution.py:19
  344.5 14.2 %collective-permute-start.41 = (bf16[4,2,24,768]{3,2,1,0:T(8,128)(2,1)S(1)}, bf16[4,2,24,768]{3,2,1,0:T(8,128)(2,1)S(1)}, u32[]{:S(2)}, u32[]{:S(2)}) collective-permute-start(bf16[4,2,24,768]{3,2,1,0:T(8,128)(2,1)S(1)} %get-tuple-element.665), channel_id=1, source_target_pairs={{0,8},{4,12},{8,0},{12,4},{16,24},{20,28},{24,16},{28,20},{1,9},{5... | collective-permute-start | bytes 884744 | tf_op jit(solution)/shard_map/ppermute | solution.py:19
  348.2 7.2 %collective-permute-start.37 = (bf16[1,2,192,256]{3,2,1,0:T(8,128)(2,1)}, bf16[1,2,192,256]{3,2,1,0:T(8,128)(2,1)}, u32[]{:S(2)}, u32[]{:S(2)}) collective-permute-start(bf16[1,2,192,256]{3,2,1,0:T(8,128)(2,1)} %get-tuple-element.661), channel_id=1, source_target_pairs={{0,4},{4,0},{8,12},{12,8},{16,20},{20,16},{24,28},{28,24},{1,5},{5... | collective-permute-start | bytes 589832 | tf_op jit(solution)/shard_map/ppermute | solution.py:19
  367.9 11.7 %collective-permute-start.51 = (f32[2,12,768]{2,1,0:T(8,128)S(1)}, f32[2,12,768]{2,1,0:T(8,128)S(1)}, u32[]{:S(2)}, u32[]{:S(2)}) collective-permute-start(f32[2,12,768]{2,1,0:T(8,128)S(1)} %add.74), channel_id=1, source_target_pairs={{0,16},{4,20},{8,24},{12,28},{16,0},{20,4},{24,8},{28,12},{1,17},{... | collective-permute-start | bytes 221192 | tf_op jit(solution)/shard_map/ppermute | solution.py:19
  369.7 12.0 %collective-permute-start.44 = (bf16[1,1,192,256]{3,2,1,0:T(8,128)(2,1)S(1)}, bf16[1,1,192,256]{3,2,1,0:T(8,128)(2,1)S(1)}, u32[]{:S(2)}, u32[]{:S(2)}) collective-permute-start(bf16[1,1,192,256]{3,2,1,0:T(8,128)(2,1)S(1)} %get-tuple-element.693), channel_id=1, source_target_pairs={{0,16},{4,20},{8,24},{12,28},{16,0},{20,4},{24,8},{28,12},{1,17},{... | collective-permute-start | bytes 294920 | tf_op jit(solution)/shard_map/ppermute | solution.py:19
  370.9 12.7 %collective-permute-start.45 = (bf16[1,1,192,256]{3,2,1,0:T(8,128)(2,1)S(1)}, bf16[1,1,192,256]{3,2,1,0:T(8,128)(2,1)S(1)}, u32[]{:S(2)}, u32[]{:S(2)}) collective-permute-start(bf16[1,1,192,256]{3,2,1,0:T(8,128)(2,1)S(1)} %get-tuple-element.694), channel_id=1, source_target_pairs={{0,16},{4,20},{8,24},{12,28},{16,0},{20,4},{24,8},{28,12},{1,17},{... | collective-permute-start | bytes 294920 | tf_op jit(solution)/shard_map/ppermute | solution.py:19
  373.6 19.0 %collective-permute-start.47 = (bf16[4,4,24,256]{3,2,1,0:T(8,128)(2,1)S(1)}, bf16[4,4,24,256]{3,2,1,0:T(8,128)(2,1)S(1)}, u32[]{:S(2)}, u32[]{:S(2)}) collective-permute-start(bf16[4,4,24,256]{3,2,1,0:T(8,128)(2,1)S(1)} %get-tuple-element.696), channel_id=1, source_target_pairs={{0,4},{4,0},{8,12},{12,8},{16,20},{20,16},{24,28},{28,24},{1,5},{5... | collective-permute-start | bytes 589832 | tf_op jit(solution)/shard_map/ppermute | solution.py:19
  374.3 18.3 %collective-permute-start.48 = (bf16[4,4,24,256]{3,2,1,0:T(8,128)(2,1)S(1)}, bf16[4,4,24,256]{3,2,1,0:T(8,128)(2,1)S(1)}, u32[]{:S(2)}, u32[]{:S(2)}) collective-permute-start(bf16[4,4,24,256]{3,2,1,0:T(8,128)(2,1)S(1)} %get-tuple-element.697), channel_id=1, source_target_pairs={{0,8},{4,12},{8,0},{12,4},{16,24},{20,28},{24,16},{28,20},{1,9},{5... | collective-permute-start | bytes 589832 | tf_op jit(solution)/shard_map/ppermute | solution.py:19
  379.6 13.0 %collective-permute-start.49 = (bf16[4,4,24,256]{3,2,1,0:T(8,128)(2,1)S(1)}, bf16[4,4,24,256]{3,2,1,0:T(8,128)(2,1)S(1)}, u32[]{:S(2)}, u32[]{:S(2)}) collective-permute-start(bf16[4,4,24,256]{3,2,1,0:T(8,128)(2,1)S(1)} %get-tuple-element.698), channel_id=1, source_target_pairs={{0,2},{1,3},{2,0},{3,1},{4,6},{5,7},{6,4},{7,5},{8,10},{9,11},{10,... | collective-permute-start | bytes 589832 | tf_op jit(solution)/shard_map/ppermute | solution.py:19
  381.7 10.9 %collective-permute-start.50 = (bf16[4,1,24,768]{3,2,1,0:T(8,128)(2,1)S(1)}, bf16[4,1,24,768]{3,2,1,0:T(8,128)(2,1)S(1)}, u32[]{:S(2)}, u32[]{:S(2)}) collective-permute-start(bf16[4,1,24,768]{3,2,1,0:T(8,128)(2,1)S(1)} %get-tuple-element.699), channel_id=1, source_target_pairs={{0,16},{4,20},{8,24},{12,28},{16,0},{20,4},{24,8},{28,12},{1,17},{... | collective-permute-start | bytes 442376 | tf_op jit(solution)/shard_map/ppermute | solution.py:19
  383.6 9.1 %collective-permute-start.46 = (bf16[1,1,192,256]{3,2,1,0:T(8,128)(2,1)S(1)}, bf16[1,1,192,256]{3,2,1,0:T(8,128)(2,1)S(1)}, u32[]{:S(2)}, u32[]{:S(2)}) collective-permute-start(bf16[1,1,192,256]{3,2,1,0:T(8,128)(2,1)S(1)} %get-tuple-element.695), channel_id=1, source_target_pairs={{0,16},{4,20},{8,24},{12,28},{16,0},{20,4},{24,8},{28,12},{1,17},{... | collective-permute-start | bytes 294920 | tf_op jit(solution)/shard_map/ppermute | solution.py:19
  400.5 7.2 %collective-permute-start.55 = (bf16[4,1,24,256]{3,2,0,1:T(8,128)(2,1)S(1)}, bf16[4,1,24,256]{3,2,0,1:T(8,128)(2,1)S(1)}, u32[]{:S(2)}, u32[]{:S(2)}) collective-permute-start(bf16[4,1,24,256]{3,2,0,1:T(8,128)(2,1)S(1)} %bitcast.134), channel_id=1, source_target_pairs={{0,16},{4,20},{8,24},{12,28},{16,0},{20,4},{24,8},{28,12},{1,17},{... | collective-permute-start | bytes 147464 | tf_op jit(solution)/shard_map/ppermute | solution.py:19
  (94 other events, 650.6 us)

commit v4 on v3

--- a/solution.py
+++ b/solution.py
@@ -23,7 +23,7 @@
 TOKENS_MAJOR = (((0,), (0,)), ((), ()))
 ROOT_HALF = 0.7071067811865476
 ROOT_TAU = 0.3989422804014327
-VMEM_MIB = dict(forward=60, ff_back=32, attention_back=16, input_back=18, wgrad=16, step=20, lanes=24)
+VMEM_MIB = dict(forward=60, ff_back=32, attention_back=16, input_back=18, wgrad=16, step=20, lanes=24, finish=16)
 FF_PARTS = 4
 FACTS_TAIL = 4
 FAST = jnp.float32
@@ -370,10 +370,11 @@
             dk_one = mm(ds, q_one)
             dv = dv_one if dv is None else dv + dv_one
             dk = dk_one if dk is None else dk + dk_one
-            dq.append(mm_tn(ds, k_pair))
-        dq_pair = (jnp.where(lower, dq[0], dq[1]) * HEAD_DIM**-0.5).astype(LOW)
+            dq.append(mm_tn(k_pair, ds)[side * HEAD_DIM : (side + 1) * HEAD_DIM])
+        dq_pair = (jnp.concatenate(dq, axis=0).T * HEAD_DIM**-0.5).astype(LOW)
         o_dq[0, :, lanes] = dq_pair
         o_vec[0:1, lanes] += column_sum(dq_pair)
+        o_vec[1:2, lanes] += column_sum(dv)
         o_near[0, 0, :, lanes] = dk[:rows].astype(LOW)
         o_far[0, 0, :, lanes] = dk[rows:].astype(LOW)
         o_near[0, 1, :, lanes] = dv[:rows].astype(LOW)
@@ -428,9 +429,9 @@
     dz1, *refs = refs
     weights, refs = refs[:3], refs[3:]
     if split:
-        o_own, o_pair, o_sent, o_vec, w_q, w_k, w_v, sems = refs[len(refs) - 8 :]
+        o_own, o_pair, o_sent, w_q, w_k, w_v, sems = refs[len(refs) - 7 :]
     else:
-        o_own, o_vec, w_q, w_k, w_v, sems = refs
+        o_own, w_q, w_k, w_v, sems = refs[len(refs) - 5 :]
     first = pl.program_id(0) == 0
     held = (w_q, w_k, w_v)
     copies = [pltpu.make_async_copy(weights[i].at[layer], held[i], sems.at[i]) for i in range(3)]
@@ -439,7 +440,6 @@
     def _():
         for copy in copies:
             copy.start()
-        o_vec[...] = jnp.zeros_like(o_vec)
 
     if split:
         dk = (near[0, 0].astype(FAST) + got[0, 0].astype(FAST)).astype(LOW)
@@ -448,7 +448,6 @@
         o_pair[0, 1] = dv
     else:
         dk, dv = near[0, 0], near[0, 1]
-    o_vec[0:1, :] += column_sum(dv)
 
     @pl.when(first)
     def _():
@@ -480,9 +479,8 @@
             jax.ShapeDtypeStruct((seqs, 2, rows, wide), LOW), jax.ShapeDtypeStruct((count, rows, wide), LOW)
         ]
         out_specs += [blocks(out_shape[1].shape, start), blocks(out_shape[2].shape, 0)]
-    out_shape.append(jax.ShapeDtypeStruct((8, wide), FAST))
-    out_specs.append(pl.BlockSpec((8, wide), lambda i: (0, 0)))
-    aliases = chained(ins, in_specs, earlier and earlier[:2], (0, 1))
+    places = (0, 1) if split else (0,)
+    aliases = chained(ins, in_specs, earlier and earlier[: len(places)], places)
     return pl.pallas_call(
         partial(input_back_kernel, layer, split),
         grid=(count,),
@@ -626,6 +624,42 @@
     )(bits, *ins)
 
 
+def finish_kernel(lanes, *refs):
+    ins, (o_down, o_up, *o_four) = refs[: 4 * lanes + 6], refs[4 * lanes + 6 :]
+    total = lambda i, group: ins[2 * i][group, 0].astype(FAST) + ins[2 * i + 1][group, 0].astype(FAST)
+    rows_down, rows, wide = o_down.shape[1], o_up.shape[1], o_down.shape[2] // lanes
+    for lane in range(lanes):
+        both = total(lane, 0)
+        cols = slice(lane * wide, (lane + 1) * wide)
+        o_down[0, :, cols] = both[:rows_down]
+        for part in range(FF_PARTS):
+            at = (lane * FF_PARTS + part) * wide
+            first = rows_down + part * rows
+            o_up[0, :, at : at + wide] = both[first : first + rows]
+        for group, out in enumerate(o_four):
+            out[0, :, cols] = total(lanes + lane, group)
+    o_down[1] = total(2 * lanes, 0)
+    o_up[1] = total(2 * lanes + 1, 0)
+    for group, out in enumerate(o_four):
+        out[1] = total(2 * lanes + 2, group)
+
+
+def finish_call(both, four, down_two, up_two, four_two):
+    rows_down, wide = down_two.value.shape[2:]
+    rows, hidden = up_two.value.shape[2:]
+    sums = [*both, *four, down_two, up_two, four_two]
+    square = jax.ShapeDtypeStruct((2, rows, wide), FAST)
+    return pl.pallas_call(
+        partial(finish_kernel, len(both)),
+        out_shape=[
+            jax.ShapeDtypeStruct((2, rows_down, wide), FAST), jax.ShapeDtypeStruct((2, rows, hidden), FAST),
+            *[square] * four_two.value.shape[0],
+        ],
+        compiler_params=pltpu.CompilerParams(vmem_limit_bytes=VMEM_MIB["finish"] << 20),
+        name="finish",
+    )(*[array for one in sums for array in (one.value, one.got)])
+
+
 def local(
     tokens, lengths, w_query, b_query, w_key, w_value, b_value, w_out, b_out, gain_one, shift_one,
     w_up, b_up, w_down, b_down, gain_two, shift_two, cotangent,
@@ -682,13 +716,11 @@
     att, got, df = tie(att, got, df)
     got_late = swapped_2(att[2], "seq", 0)
     ends = input_back_call(1, True, 0, 2, att[0], att[1], got, dz1, back_weights, None)
-    vec_v = ends[3]
     ends, df = tie(ends, df)
     arrived = [swapped_2(ends[2], "seq", 1)]
     up_two = wgrad("up", lefts=[flat(kept["hid"])], rights=[flat(df)], chunk=half)
     up_two, (got_late, dz1) = Sum.begin(up_two, near_first, bits, (got_late, dz1))
     ends = input_back_call(1, True, 2, seqs - 2, att[0], att[1], got_late, dz1, back_weights, ends)
-    vec_v += ends[3]
     ends = tie(*ends)
     arrived.append(swapped_2(ends[2], "seq", 1))
     ends = join(ends, up_two, down_two)
@@ -701,7 +733,7 @@
         chunk=half,
     )
     four_two, arrived = Sum.begin(four_two, across_first, bits, arrived)
-    vec_two = (vec_two, vec_q, vec_v)
+    vec_two = (vec_two, vec_q)
     middle = ends[0] + jnp.concatenate(arrived).astype(FAST)
 
     kept = kept_one
@@ -714,46 +746,43 @@
     up_one, dc = join((up_one, dc), down_one, down_two, up_two)
     up_one, dc = Sum.begin(up_one, near_first, bits, dc)
     dc = advance(dc, down_two, up_two)
-    att = attention_back_call(0, False, 0, 2, facts, kept, dc, None)
+    att = attention_back_call(0, False, 0, 1, facts, kept, dc, None)
     vec_q = att[3]
-    att, dc = join((att, dc), up_one, up_two, four_two, down_two)
+    att, dc = join((att, dc), up_one, up_two, down_two)
     lanes_one, dc = lanes_of(dc, down_one, up_one, stacked=True)
-    dc = advance(dc, up_two, four_two)
-    att = attention_back_call(0, False, 2, seqs - 2, facts, kept, dc, att)
+    dc = advance(dc, up_two)
+    att = attention_back_call(0, False, 1, seqs - 1, facts, kept, dc, att)
     vec_q += att[3]
-    att, da, vec_q = join((att, da, vec_q), up_two)
-    got = swapped_2(att[2], "seq", 0)
+    early = [four_two, up_two, down_two]
+    att, da, vec_q = join((att, da, vec_q), *lanes_one, *early)
+    vectors = Whole([(vec_one, vec_q), vec_two])
+    far, da = advance((att[2], da), *lanes_one, *early)
+    far, da = vectors.send((far, da))
+    got = swapped_2(far, "seq", 0)
     rest_one = wgrad("rest", lefts=[flat(kept["ctx"]), flat(tokens)], rights=[flat(da), flat(att[0])], chunk=half)
-    rest_one, got = tie(rest_one, got)
+    rest_one, got = join((rest_one, got), vectors)
     rest_one, got = Sum.begin(rest_one, across_first, bits, got)
+    got = vectors.send(got)
     pair = (att[1].astype(FAST) + got.astype(FAST)).astype(LOW)
-    vectors = Whole([(vec_one, vec_q, jnp.sum(pair[:, 1].astype(FAST), axis=(0, 1))[None]), vec_two])
-    pair = vectors.send(pair)
     pairs_one = wgrad("pair", lefts=[flat(tokens)] * 2, rights=[flat(pair[:, 0]), flat(pair[:, 1])], chunk=half)
+    pairs_one, dz1 = join((pairs_one, dz1), *lanes_one, rest_one, vectors, *early)
     pairs_one, dz1 = Sum.begin(pairs_one, near_first, bits, dz1)
-    dz1 = join(dz1, *lanes_one, vectors)
-    dz1 = advance(dz1, *lanes_one)
+    dz1 = advance(dz1, *lanes_one, *early)
     dz1 = vectors.send(dz1)
-    ends = input_back_call(0, False, 0, seqs, att[0], pair, None, dz1, back_weights, None)
-    result = join(ends[0], rest_one, pairs_one, vectors)
-    last_one, result = lanes_of(result, rest_one, pairs_one, stacked=False)
-    result = vectors.send(result)
-    live = [*lanes_one, *last_one, four_two, up_two, down_two]
-    result = join(result, *lanes_one, four_two, up_two, down_two, vectors)
-    result = advance(result, *lanes_one, four_two, up_two, down_two)
-    while any(one.got is not None for one in live):
+    ends = input_back_call(0, False, 0, 2, att[0], pair, None, dz1, back_weights, None)
+    (dz1, ends) = join((dz1, ends), *lanes_one, pairs_one, vectors, *early)
+    last_one, dz1 = lanes_of(dz1, rest_one, pairs_one, stacked=False)
+    dz1 = advance(dz1, *lanes_one, *early)
+    dz1 = vectors.send(dz1)
+    ends = input_back_call(0, False, 2, seqs - 2, att[0], pair, None, dz1, back_weights, ends)
+    live = [*last_one, *lanes_one, *early]
+    result = join(ends[0], *live, vectors)
+    while any(one.order for one in live):
+        result = advance(result, *live)
         result = vectors.send(result)
         result = join(result, *live, vectors)
-        result = advance(result, *live)
-    rows_down = hidden // devices
-    both = [one.value[0] for one in lanes_one]
-    down_part = jnp.concatenate([one[:rows_down] for one in both], axis=-1)
-    up_part = [one[rows_down:].reshape(FF_PARTS, -1, one.shape[-1]) for one in both]
-    up_part = jnp.concatenate([one[part] for one in up_part for part in range(FF_PARTS)], axis=-1)
-    sums = [
-        (down_part, up_part, jnp.concatenate([one.value for one in last_one], axis=-1)),
-        (down_two.value[0], up_two.value[0], four_two.value),
-    ]
+    vectors.send(())
+    sums = finish_call(lanes_one, last_one, down_two, up_two, four_two)
     return (final, result) + gathered(sums, vectors.value, devices)
 
 
@@ -794,11 +823,7 @@
 
 
 def advance(hold, *sums):
-    for one in sums:
-        if one.got is not None and not one.order:
-            one.value = (one.value.astype(FAST) + one.got.astype(FAST))[:, 0]
-            one.got = None
-    live = [one for one in sums if one.got is not None]
+    live = [one for one in sums if one.order]
     if not live:
         return hold
     plan, routes = [], []
@@ -847,7 +872,7 @@
 
 class Whole:
     def __init__(self, layers):
-        rows = [jnp.concatenate([vec_q[:1], vec_v[:1], vec[2:]]) for vec, vec_q, vec_v in layers]
+        rows = [jnp.concatenate([vec_low[:2], vec[2:]]) for vec, vec_low in layers]
         self.value = jnp.stack(rows)
         self.got = None
         self.order = digit_list()
@@ -867,10 +892,8 @@
 
 def gathered(sums, vectors, devices):
     outs = [None] * 15
-    for place, which in enumerate((5, 0, 2, 3)):
-        outs[which] = jnp.stack([one[2][place] for one in sums])
-    outs[9] = jnp.stack([one[1] for one in sums])
-    outs[11] = jnp.stack([one[0] for one in sums])
+    for which, value in zip((11, 9, 5, 0, 2, 3), sums, strict=True):
+        outs[which] = value
     mine = lax.axis_index("batch") * lax.axis_size("seq") + lax.axis_index("seq")
     width = vectors.shape[2] // devices
     small = lax.dynamic_slice_in_dim(vectors[:, :8], mine * width, width, axis=2)

time: 422 us -> 401 us (0.950)
  local copies, waits for them, and re-layouts: 29.4 us -> 16.5 us
  other arithmetic: 8.57 us -> 2.77 us
  Pallas kernels: 248 us -> 243 us
    unnamed x177 -> x126, local copies, waits for them, and re-layouts: 25.1 us -> 12.9 us
    another operation x9 -> x0, other arithmetic: 5.39 us -> none  [the longest x4 2.68 us: gathered(): outs[which] = jnp.stack([one[2][place] for one in sums])]
    pallas_call x10 -> x11, Pallas kernels: 27.3 us -> 25.7 us  [step_call(): pl.pallas_call(partial(step_kernel, plan), grid=(steps,), in_specs=[pl.Bl...]
    pallas_call x3 -> x4, Pallas kernels: 12.3 us -> 12.9 us  [input_back_call(): pl.pallas_call(partial(input_back_kernel, layer, split), grid=(count,), i...]
  transfers between devices with their start and end apart: 58 -> 58, of which waited for: 25 -> 22; matrix products, arithmetic and copies ran while one was open for 2% -> 2% of each run, Pallas kernels for 40% -> 41%
where the time goes in v4:
time: 401 us; the launch traced here: 394 us
  Pallas kernels  243 us (61%)
  waiting for transfers between devices  65 us (16%)
  starting transfers between devices  63.8 us (16%)
  local copies, waits for them, and re-layouts  16.5 us (4%)
    pallas_call x4, Pallas kernels, forward_call(): pl.pallas_call(partial(forward_kernel, layer, swapped, start), grid=(coun...  91.3 us
    ppermute x58, waiting for transfers between devices, swapped_2(): lax.ppermute(value, axis, [(i, i ^ 1 << bit) for i in range(lax.axis_size...  65 us
    ppermute x58, starting transfers between devices, swapped_2(): lax.ppermute(value, axis, [(i, i ^ 1 << bit) for i in range(lax.axis_size...  63.8 us
    pallas_call x4, Pallas kernels, attention_back_call(): pl.pallas_call(partial(attention_back_kernel, layer, start), grid=(count,...  39.3 us
    pallas_call x7, Pallas kernels, wgrad_call(): pl.pallas_call(partial(wgrad_kernel, count), grid=(steps,), in_specs=[pl....  34.3 us
    pallas_call x2, Pallas kernels, ff_back_call(): pl.pallas_call(partial(ff_back_kernel, layer), grid=(seqs,), in_specs=in_...  33.1 us
    pallas_call x11, Pallas kernels, step_call(): pl.pallas_call(partial(step_kernel, plan), grid=(steps,), in_specs=[pl.Bl...  25.7 us
    unnamed x126, local copies, waits for them, and re-layouts  12.9 us
  transfers between devices with their start and end apart: 58, of which 22 were waited for; matrix products, arithmetic and copies ran while one was open for 2% of the time, Pallas kernels for 41%

profile of v4, /device:TPU:0, one launch (start us, length us, event | category | flops | bytes accessed | tf_op | source)
XLA Modules:
  0.0 393.6 jit_solution(18109605075888255551)
XLA Ops:
  4.9 28.5 %layer_forward_0.2 = (bf16[2,256,768]{2,1,0:T(8,128)(2,1)}, f32[3,256,768]{2,1,0:T(8,128)}, bf16[3,256,768]{2,1,0:T(8,128)(2,1)}, bf16[3,256,768]{2,1,0:T(8,128)...) custom-call(s32[7]{0:T(128)} %concatenate.12.facts, ...), custom_call_target="tpu_custom_call" | custom-call | flops 321999994880 | bytes 1 | tf_op jit(solution)/shard_map/layer_forward_0/pallas_call | solution.py:226
  33.5 2.9 collective-permute-start.2
  36.3 16.3 %layer_forward_0.3 = (bf16[1,256,768]{2,1,0:T(8,128)(2,1)}, f32[3,256,768]{2,1,0:T(8,128)}, bf16[3,256,768]{2,1,0:T(8,128)(2,1)}, bf16[3,256,768]{2,1,0:T(8,128)...) custom-call(s32[7]{0:T(128)} %concatenate.12.facts, ...), custom_call_target="tpu_custom_call", output_to_operand_aliasing={{1}: (12, {}), {2}: (13, {}), {3}: (14, {}), {4}: (15, {}),... | custom-call | flops 160999997440 | bytes 1 | tf_op jit(solution)/shard_map/layer_forward_0/pallas_call | solution.py:226
  57.9 29.8 %layer_forward_1.2 = (bf16[2,256,768]{2,1,0:T(8,128)(2,1)}, bf16[3,256,768]{2,1,0:T(8,128)(2,1)}, bf16[3,256,768]{2,1,0:T(8,128)(2,1)}, bf16[3,256,768]{2,1,0:T(...) custom-call(s32[7]{0:T(128)} %concatenate.12.facts, ...), custom_call_target="tpu_custom_call" | custom-call | flops 321999994880 | bytes 1 | tf_op jit(solution)/shard_map/layer_forward_1/pallas_call | solution.py:226
  90.5 16.6 %layer_forward_1.3 = (bf16[1,256,768]{2,1,0:T(8,128)(2,1)}, bf16[3,256,768]{2,1,0:T(8,128)(2,1)}, bf16[3,256,768]{2,1,0:T(8,128)(2,1)}, bf16[3,256,768]{2,1,0:T(...) custom-call(s32[7]{0:T(128)} %concatenate.12.facts, ...), custom_call_target="tpu_custom_call", output_to_operand_aliasing={{1}: (12, {}), {2}: (13, {}), {3}: (14, {}), {4}: (15, {}),... | custom-call | flops 160999997440 | bytes 1 | tf_op jit(solution)/shard_map/layer_forward_1/pallas_call | solution.py:226
  107.2 2.3 copy-done.36
  114.0 16.0 %ff_back_1.1 = (bf16[3,256,768]{2,1,0:T(8,128)(2,1)S(1)}, bf16[3,256,3072]{2,1,0:T(8,128)(2,1)S(1)}, f32[3,256,768]{2,1,0:T(8,128)S(1)}, bf16[3,256,768]{2,1,0:T...) custom-call(bf16[3,256,768]{2,1,0:T(8,128)(2,1)S(1)} %copy-done.17, ...), custom_call_target="tpu_custom_call" | custom-call | flops 218500005888 | bytes 1 | tf_op jit(solution)/shard_map/ff_back_1/pallas_call | solution.py:326
  130.1 6.3 %wgrad_down.2 = (bf16[1,16,96,768]{3,2,1,0:T(8,128)(2,1)S(1)}, bf16[1,16,96,768]{3,2,1,0:T(8,128)(2,1)}) custom-call(s32[5]{0:T(128)S(1)} %stack.48.place_ref.bits, bf16[768,3072]{1,0:T(8,128)(2,1)S(1)} %bitcast.53, bf16[768,768]{1,0:T(8,128)(2,1)S(1)} %bitcast.68), custom_call_target="tpu_custom_call" | custom-call | flops 88763809792 | bytes 1 | tf_op jit(solution)/shard_map/wgrad_down/pallas_call | solution.py:527
  136.5 12.9 %attention_back_1.2 = (bf16[3,256,768]{2,1,0:T(8,128)(2,1)S(1)}, bf16[3,2,256,768]{3,2,1,0:T(8,128)(2,1)S(1)}, bf16[2,2,256,768]{3,2,1,0:T(8,128)(2,1)S(1)}, f32[8,768]{1,0:T(8,128)S(1)}) custom-call(s32[7]{0:T(128)S(1)} %copy-done.9, bf16[3,256,768]{2,1,0:T(8,128)(2,1)S(1)} %copy-done.37, bf16[3,512,768]{2,1,0:T(8,128)(2,1)S(1)} %copy-done.31, ...), custom_call_target="tpu_custom_call" | custom-call | flops 184000004096 | bytes 1 | tf_op jit(solution)/shard_map/attention_back_1/pallas_call | solution.py:413
  149.4 4.2 %exchange_step.11 = (bf16[1,8,96,768]{3,2,1,0:T(8,128)(2,1)S(1)}, bf16[1,8,96,768]{3,2,1,0:T(8,128)(2,1)}) custom-call(s32[5]{0:T(128)S(1)} %stack.48.place_ref.bits, bf16[1,16,96,768]{3,2,1,0:T(8,128)(2,1)S(1)} %get-tuple-element.472.refs_0_, bf16[1,16,96,768]{3,2,1,0:T(8,128)(2,1)} %collective-permute-done.5.refs_1_), custom_call_target="tpu_custom_call" | custom-call | flops 38631903232 | bytes 1 | tf_op jit(solution)/shard_map/exchange_step/pallas_call | solution.py:567
  155.9 6.7 %attention_back_1.3 = (bf16[3,256,768]{2,1,0:T(8,128)(2,1)S(1)}, bf16[3,2,256,768]{3,2,1,0:T(8,128)(2,1)S(1)}, bf16[1,2,256,768]{3,2,1,0:T(8,128)(2,1)S(1)}, f32[8,768]{1,0:T(8,128)S(1)}) custom-call(s32[7]{0:T(128)S(1)} %copy-done.9, bf16[3,256,768]{2,1,0:T(8,128)(2,1)S(1)} %copy-done.37, ...), custom_call_target="tpu_custom_call", output_to_operand_aliasing={{0}: (6, {}), {1}: (7, {})} | custom-call | flops 92000002048 | bytes 1 | tf_op jit(solution)/shard_map/attention_back_1/pallas_call | solution.py:413
  163.3 4.0 %input_back_1.2 = (f32[3,256,768]{2,1,0:T(8,128)S(1)}, bf16[3,2,256,768]{3,2,1,0:T(8,128)(2,1)S(1)}, bf16[2,256,768]{2,1,0:T(8,128)(2,1)}) custom-call(bf16[3,256,768]{2,1,0:T(8,128)(2,1)S(1)} %get-tuple-element.491.dq, bf16[3,2,256,768]{3,2,1,0:T(8,128)(2,1)S(1)} %get-tuple-element.492.near, bf16[2,2,256,768]{3,2,1,0:T(8,128)(2,1)S(1)} %collective-permute-done.6.refs_0_, ...), custom_call_target="tpu_custom_call" | custom-call | flops 92000002048 | bytes 1 | tf_op jit(solution)/shard_map/input_back_1/pallas_call | solution.py:484
  169.0 4.7 %wgrad_up.2 = (bf16[1,16,24,3072]{3,2,1,0:T(8,128)(2,1)S(1)}, bf16[1,16,24,3072]{3,2,1,0:T(8,128)(2,1)S(1)}) custom-call(s32[5]{0:T(128)S(1)} %stack.48.place_ref.bits, bf16[768,768]{1,0:T(8,128)(2,1)S(1)} %bitcast.61, bf16[768,3072]{1,0:T(8,128)(2,1)S(1)} %bitcast.52), custom_call_target="tpu_custom_call" | custom-call | flops 88763809792 | bytes 1 | tf_op jit(solution)/shard_map/wgrad_up/pallas_call | solution.py:527
  174.0 2.1 input_back_1.3
  176.6 5.8 %collective-permute-done.9.refs_3_ = bf16[1,8,96,768]{3,2,1,0:T(8,128)(2,1)} collective-permute-done((bf16[1,8,96,768]{3,2,1,0:T(8,128)(2,1)}, bf16[1,8,96,768]{3,2,1,0:T(8,128)(2,1)}, u32[]{:S(2)}, u32[]{:S(2)}) %collective-permute-start.9) | collective-permute-done | bytes 1179680 | tf_op jit(solution)/shard_map/ppermute | solution.py:19
  182.5 3.8 exchange_step.12
  188.2 6.5 %wgrad_four.1 = (bf16[4,16,24,768]{3,2,1,0:T(8,128)(2,1)S(1)}, bf16[4,16,24,768]{3,2,1,0:T(8,128)(2,1)}) custom-call(s32[5]{0:T(128)S(1)} %stack.48.place_ref.bits, bf16[768,768]{1,0:T(8,128)(2,1)S(1)} %bitcast.60, bf16[768,768]{1,0:T(8,128)(2,1)S(1)} %bitcast.63, bf16[768,768]{1,0:T(8,128)(2,1)S(1)} %bitcast.58, bf16[768,768]{1,0:T(8,128)(2,1)S(1)} %bitcast.59, ...), custom_call_target="tpu_custom_call" | custom-call | flops 88763809792 | bytes 1 | tf_op jit(solution)/shard_map/wgrad_four/pallas_call | solution.py:527
  199.7 17.1 %ff_back_0.1 = (bf16[3,256,768]{2,1,0:T(8,128)(2,1)S(1)}, bf16[3,256,3072]{2,1,0:T(8,128)(2,1)S(1)}, f32[3,256,768]{2,1,0:T(8,128)S(1)}, bf16[3,256,768]{2,1,0:T...) custom-call(f32[3,256,768]{2,1,0:T(8,128)S(1)} %convert_add_fusion.top_grad, ...), custom_call_target="tpu_custom_call" | custom-call | flops 218500005888 | bytes 1 | tf_op jit(solution)/shard_map/ff_back_0/pallas_call | solution.py:326
  216.9 5.6 %exchange_step.13 = (bf16[1,2,96,768]{3,2,1,0:T(8,128)(2,1)S(1)}, bf16[1,2,96,768]{3,2,1,0:T(8,128)(2,1)S(1)}, bf16[4,8,24,768]{3,2,1,0:T(8,128)(2,1)S(1)}, bf16[4,8,24,768]{3,2,1,0:T(8,128)(2,1)}) custom-call(s32[5]{0:T(128)S(1)} %stack.48.place_ref.bits, bf16[1,4,96,768]{3,2,1,0:T(8,128)(2,1)S(1)} %get-tuple-element.516.refs_0_, ...), custom_call_target="tpu_custom_call" | custom-call | flops 45414879232 | bytes 1 | tf_op jit(solution)/shard_map/exchange_step/pallas_call | solution.py:567
  222.5 5.4 %wgrad_down.3 = (bf16[1,16,96,768]{3,2,1,0:T(8,128)(2,1)S(1)}, bf16[1,16,96,768]{3,2,1,0:T(8,128)(2,1)S(1)}) custom-call(s32[5]{0:T(128)S(1)} %stack.48.place_ref.bits, bf16[768,3072]{1,0:T(8,128)(2,1)S(1)} %bitcast.55, bf16[768,768]{1,0:T(8,128)(2,1)S(1)} %bitcast.66), custom_call_target="tpu_custom_call" | custom-call | flops 88763809792 | bytes 1 | tf_op jit(solution)/shard_map/wgrad_down/pallas_call | solution.py:527
  230.1 4.9 %wgrad_up.3 = (bf16[1,16,24,3072]{3,2,1,0:T(8,128)(2,1)S(1)}, bf16[1,16,24,3072]{3,2,1,0:T(8,128)(2,1)S(1)}) custom-call(s32[5]{0:T(128)S(1)} %stack.48.place_ref.bits, bf16[768,768]{1,0:T(8,128)(2,1)S(1)} %bitcast.65, bf16[768,3072]{1,0:T(8,128)(2,1)S(1)} %bitcast.54), custom_call_target="tpu_custom_call" | custom-call | flops 88763809792 | bytes 1 | tf_op jit(solution)/shard_map/wgrad_up/pallas_call | solution.py:527
  235.6 2.3 collective-permute-done.15.refs_1_
  238.6 3.3 exchange_step.14
  242.5 2.6 collective-permute-start.19
  245.1 6.7 %attention_back_0.2 = (bf16[3,256,768]{2,1,0:T(8,128)(2,1)S(1)}, bf16[3,2,256,768]{3,2,1,0:T(8,128)(2,1)S(1)}, bf16[3,2,256,768]{3,2,1,0:T(8,128)(2,1)S(1)}, f32[8,768]{1,0:T(8,128)S(1)}) custom-call(s32[7]{0:T(128)S(1)} %copy-done.9, bf16[3,256,768]{2,1,0:T(8,128)(2,1)S(1)} %copy-done.42, bf16[3,512,768]{2,1,0:T(8,128)(2,1)S(1)} %copy-done.34, ...), custom_call_target="tpu_custom_call" | custom-call | flops 92000002048 | bytes 1 | tf_op jit(solution)/shard_map/attention_back_0/pallas_call | solution.py:413
  251.8 7.1 %collective-permute-done.19.refs_13_ = bf16[1,1,96,768]{3,2,1,0:T(8,128)(2,1)S(1)} collective-permute-done((bf16[1,1,96,768]{3,2,1,0:T(8,128)(2,1)S(1)}, bf16[1,1,96,768]{3,2,1,0:T(8,128)(2,1)S(1)}, u32[]{:S(2)}, u32[]{:S(2)}) %collective-permute-start.19) | collective-permute-done | bytes 147488 | tf_op jit(solution)/shard_map/ppermute | solution.py:19
  260.8 2.5 exchange_lanes.2
  268.4 3.3 collective-permute-start.22
  272.2 13.0 %attention_back_0.3 = (bf16[3,256,768]{2,1,0:T(8,128)(2,1)S(1)}, bf16[3,2,256,768]{3,2,1,0:T(8,128)(2,1)S(1)}, bf16[3,2,256,768]{3,2,1,0:T(8,128)(2,1)S(1)}, f32[8,768]{1,0:T(8,128)S(1)}) custom-call(s32[7]{0:T(128)S(1)} %copy-done.9, bf16[3,256,768]{2,1,0:T(8,128)(2,1)S(1)} %copy-done.42, ...), custom_call_target="tpu_custom_call", output_to_operand_aliasing={{0}: (6, {}), {1}: (7, {}), {2}: (8, {})} | custom-call | flops 184000004096 | bytes 1 | tf_op jit(solution)/shard_map/attention_back_0/pallas_call | solution.py:413
  285.3 6.0 %collective-permute-done.24.refs_9_ = bf16[1,2,24,3072]{3,2,1,0:T(8,128)(2,1)} collective-permute-done((bf16[1,2,24,3072]{3,2,1,0:T(8,128)(2,1)}, bf16[1,2,24,3072]{3,2,1,0:T(8,128)(2,1)}, u32[]{:S(2)}, u32[]{:S(2)}) %collective-permute-start.24) | collective-permute-done | bytes 294944 | tf_op jit(solution)/shard_map/ppermute | solution.py:19
  291.3 3.1 exchange_step.16
  297.0 3.2 collective-permute-start.28
  300.2 3.1 wgrad_rest.1
  305.7 8.0 %collective-permute-done.33.refs_15_ = bf16[1,1,24,3072]{3,2,1,0:T(8,128)(2,1)S(1)} collective-permute-done((bf16[1,1,24,3072]{3,2,1,0:T(8,128)(2,1)S(1)}, bf16[1,1,24,3072]{3,2,1,0:T(8,128)(2,1)S(1)}, u32[]{:S(2)}, u32[]{:S(2)}) %collective-permute-start.33) | collective-permute-done | bytes 147488 | tf_op jit(solution)/shard_map/ppermute | solution.py:19
  313.7 5.1 %collective-permute-done.27.refs_1_ = bf16[1,4,192,256]{3,2,1,0:T(8,128)(2,1)S(1)} collective-permute-done((bf16[1,4,192,256]{3,2,1,0:T(8,128)(2,1)S(1)}, bf16[1,4,192,256]{3,2,1,0:T(8,128)(2,1)S(1)}, u32[]{:S(2)}, u32[]{:S(2)}) %collective-permute-start.27) | collective-permute-done | bytes 393248 | tf_op jit(solution)/shard_map/ppermute | solution.py:19
  320.2 3.4 wgrad_pair.1
  326.3 3.2 collective-permute-start.39
  331.2 4.0 %input_back_0.2.refs_4_ = f32[3,256,768]{2,1,0:T(8,128)} custom-call(bf16[3,256,768]{2,1,0:T(8,128)(2,1)S(1)} %get-tuple-element.631.dq, bf16[3,2,256,768]{3,2,1,0:T(8,128)(2,1)S(1)} %add_convert_fusion.near, f32[3,256,768]{2,1,0:T(8,128)S(1)} %copy-done.30, bf16[2,768,768]{2,1,0:T(8,128)(2,1)S(1)} %copy-done.12, bf16[2,768,768]{2,1,0:T(8,128)(2,1)S(1)} %copy-done.14, ...), custom_call_target="tpu_custom_call" | custom-call | flops 92000002048 | bytes 1 | tf_op jit(solution)/shard_map/input_back_0/pallas_call | solution.py:484
  335.2 4.3 %collective-permute-done.34.refs_1_ = bf16[1,2,192,256]{3,2,1,0:T(8,128)(2,1)S(1)} collective-permute-done((bf16[1,2,192,256]{3,2,1,0:T(8,128)(2,1)S(1)}, bf16[1,2,192,256]{3,2,1,0:T(8,128)(2,1)S(1)}, u32[]{:S(2)}, u32[]{:S(2)}) %collective-permute-start.34) | collective-permute-done | bytes 196640 | tf_op jit(solution)/shard_map/ppermute | solution.py:19
  342.4 2.4 collective-permute-start.44
  347.7 2.1 collective-permute-done.47
  351.6 4.5 %collective-permute-start.46 = (bf16[4,1,24,768]{3,2,1,0:T(8,128)(2,1)S(1)}, bf16[4,1,24,768]{3,2,1,0:T(8,128)(2,1)S(1)}, u32[]{:S(2)}, u32[]{:S(2)}) collective-permute-start(bf16[4,1,24,768]{3,2,1,0:T(8,128)(2,1)S(1)} %get-tuple-element.713), channel_id=1, source_target_pairs={{0,16},{4,20},{8,24},{12,28},{16,0},{20,4},{24,8},{28,12},{1,17},{... | collective-permute-start | bytes 442376 | tf_op jit(solution)/shard_map/ppermute | solution.py:19
  356.2 2.8 input_back_0.3
  358.9 3.6 collective-permute-done.45.refs_5_
  362.5 2.8 collective-permute-done.42.refs_5_
  366.7 2.1 collective-permute-start.50
  370.1 4.4 %collective-permute-done.51 = f32[2,12,768]{2,1,0:T(8,128)S(1)} collective-permute-done((f32[2,12,768]{2,1,0:T(8,128)S(1)}, f32[2,12,768]{2,1,0:T(8,128)S(1)}, u32[]{:S(2)}, u32[]{:S(2)}) %collective-permute-start.51) | collective-permute-done | bytes 73760 | tf_op jit(solution)/shard_map/ppermute | solution.py:19
  384.6 2.2 collective-permute-start.56
  (252 shorter events, 78.1 us)
Async XLA Ops:
  33.5 21.1 %collective-permute-start.2 = (bf16[2,256,768]{2,1,0:T(8,128)(2,1)}, bf16[2,256,768]{2,1,0:T(8,128)(2,1)}, u32[]{:S(2)}, u32[]{:S(2)}) collective-permute-start(bf16[2,256,768]{2,1,0:T(8,128)(2,1)} %get-tuple-element.431), channel_id=1, source_target_pairs={{0,2},{1,3},{2,0},{3,1},{4,6},{5,7},{6,4},{7,5},{8,10},{9,11},{10,... | collective-permute-start | bytes 2359304 | tf_op jit(solution)/shard_map/ppermute | solution.py:19
  54.5 33.2 %collective-permute-start.1 = (bf16[1,256,768]{2,1,0:T(8,128)(2,1)}, bf16[1,256,768]{2,1,0:T(8,128)(2,1)}, u32[]{:S(2)}, u32[]{:S(2)}) collective-permute-start(bf16[1,256,768]{2,1,0:T(8,128)(2,1)} %get-tuple-element.430), channel_id=1, source_target_pairs={{0,2},{1,3},{2,0},{3,1},{4,6},{5,7},{6,4},{7,5},{8,10},{9,11},{10,... | collective-permute-start | bytes 1179656 | tf_op jit(solution)/shard_map/ppermute | solution.py:19
  136.4 13.1 %collective-permute-start.5 = (bf16[1,16,96,768]{3,2,1,0:T(8,128)(2,1)}, bf16[1,16,96,768]{3,2,1,0:T(8,128)(2,1)}, u32[]{:S(2)}, u32[]{:S(2)}) collective-permute-start(bf16[1,16,96,768]{3,2,1,0:T(8,128)(2,1)} %get-tuple-element.478), channel_id=1, source_target_pairs={{0,1},{1,0},{2,3},{3,2},{4,5},{5,4},{6,7},{7,6},{8,9},{9,8},{10,11... | collective-permute-start | bytes 7077896 | tf_op jit(solution)/shard_map/ppermute | solution.py:19
  153.7 9.6 %collective-permute-start.6 = (bf16[2,2,256,768]{3,2,1,0:T(8,128)(2,1)S(1)}, bf16[2,2,256,768]{3,2,1,0:T(8,128)(2,1)S(1)}, u32[]{:S(2)}, u32[]{:S(2)}) collective-permute-start(bf16[2,2,256,768]{3,2,1,0:T(8,128)(2,1)S(1)} %get-tuple-element.489), channel_id=1, source_target_pairs={{0,1},{1,0},{2,3},{3,2},{4,5},{5,4},{6,7},{7,6},{8,9},{9,8},{10,11... | collective-permute-start | bytes 4718600 | tf_op jit(solution)/shard_map/ppermute | solution.py:19
  154.1 28.4 %collective-permute-start.9 = (bf16[1,8,96,768]{3,2,1,0:T(8,128)(2,1)}, bf16[1,8,96,768]{3,2,1,0:T(8,128)(2,1)}, u32[]{:S(2)}, u32[]{:S(2)}) collective-permute-start(bf16[1,8,96,768]{3,2,1,0:T(8,128)(2,1)} %get-tuple-element.512), channel_id=1, source_target_pairs={{0,4},{4,0},{8,12},{12,8},{16,20},{20,16},{24,28},{28,24},{1,5},{5... | collective-permute-start | bytes 3538952 | tf_op jit(solution)/shard_map/ppermute | solution.py:19
  167.4 6.4 %collective-permute-start.7 = (bf16[1,2,256,768]{3,2,1,0:T(8,128)(2,1)S(1)}, bf16[1,2,256,768]{3,2,1,0:T(8,128)(2,1)S(1)}, u32[]{:S(2)}, u32[]{:S(2)}) collective-permute-start(bf16[1,2,256,768]{3,2,1,0:T(8,128)(2,1)S(1)} %get-tuple-element.502), channel_id=1, source_target_pairs={{0,1},{1,0},{2,3},{3,2},{4,5},{5,4},{6,7},{7,6},{8,9},{9,8},{10,11... | collective-permute-start | bytes 2359304 | tf_op jit(solution)/shard_map/ppermute | solution.py:19
  167.4 27.3 %collective-permute-start.10 = (bf16[2,256,768]{2,1,0:T(8,128)(2,1)}, bf16[2,256,768]{2,1,0:T(8,128)(2,1)}, u32[]{:S(2)}, u32[]{:S(2)}) collective-permute-start(bf16[2,256,768]{2,1,0:T(8,128)(2,1)} %get-tuple-element.527), channel_id=1, source_target_pairs={{0,2},{1,3},{2,0},{3,1},{4,6},{5,7},{6,4},{7,5},{8,10},{9,11},{10,... | collective-permute-start | bytes 2359304 | tf_op jit(solution)/shard_map/ppermute | solution.py:19
  173.7 8.8 %collective-permute-start.8 = (bf16[1,16,24,3072]{3,2,1,0:T(8,128)(2,1)S(1)}, bf16[1,16,24,3072]{3,2,1,0:T(8,128)(2,1)S(1)}, u32[]{:S(2)}, u32[]{:S(2)}) collective-permute-start(bf16[1,16,24,3072]{3,2,1,0:T(8,128)(2,1)S(1)} %get-tuple-element.511), channel_id=1, source_target_pairs={{0,1},{1,0},{2,3},{3,2},{4,5},{5,4},{6,7},{7,6},{8,9},{9,8},{10,11... | collective-permute-start | bytes 7077896 | tf_op jit(solution)/shard_map/ppermute | solution.py:19
  176.0 20.0 %collective-permute-start.11 = (bf16[1,256,768]{2,1,0:T(8,128)(2,1)S(1)}, bf16[1,256,768]{2,1,0:T(8,128)(2,1)S(1)}, u32[]{:S(2)}, u32[]{:S(2)}) collective-permute-start(bf16[1,256,768]{2,1,0:T(8,128)(2,1)S(1)} %get-tuple-element.510), channel_id=1, source_target_pairs={{0,2},{1,3},{2,0},{3,1},{4,6},{5,7},{6,4},{7,5},{8,10},{9,11},{10,... | collective-permute-start | bytes 1179656 | tf_op jit(solution)/shard_map/ppermute | solution.py:19
  196.0 20.8 %collective-permute-start.13 = (bf16[4,16,24,768]{3,2,1,0:T(8,128)(2,1)}, bf16[4,16,24,768]{3,2,1,0:T(8,128)(2,1)}, u32[]{:S(2)}, u32[]{:S(2)}) collective-permute-start(bf16[4,16,24,768]{3,2,1,0:T(8,128)(2,1)} %get-tuple-element.542), channel_id=1, source_target_pairs={{0,1},{1,0},{2,3},{3,2},{4,5},{5,4},{6,7},{7,6},{8,9},{9,8},{10,11... | collective-permute-start | bytes 7077896 | tf_op jit(solution)/shard_map/ppermute | solution.py:19
  196.1 20.7 %collective-permute-start.12 = (bf16[1,4,96,768]{3,2,1,0:T(8,128)(2,1)}, bf16[1,4,96,768]{3,2,1,0:T(8,128)(2,1)}, u32[]{:S(2)}, u32[]{:S(2)}) collective-permute-start(bf16[1,4,96,768]{3,2,1,0:T(8,128)(2,1)} %get-tuple-element.541), channel_id=1, source_target_pairs={{0,8},{4,12},{8,0},{12,4},{16,24},{20,28},{24,16},{28,20},{1,9},{5... | collective-permute-start | bytes 1769480 | tf_op jit(solution)/shard_map/ppermute | solution.py:19
  197.8 37.9 %collective-permute-start.16 = (bf16[1,8,24,3072]{3,2,1,0:T(8,128)(2,1)}, bf16[1,8,24,3072]{3,2,1,0:T(8,128)(2,1)}, u32[]{:S(2)}, u32[]{:S(2)}) collective-permute-start(bf16[1,8,24,3072]{3,2,1,0:T(8,128)(2,1)} %get-tuple-element.562), channel_id=1, source_target_pairs={{0,4},{4,0},{8,12},{12,8},{16,20},{20,16},{24,28},{28,24},{1,5},{5... | collective-permute-start | bytes 3538952 | tf_op jit(solution)/shard_map/ppermute | solution.py:19
  227.9 10.0 %collective-permute-start.14 = (bf16[1,16,96,768]{3,2,1,0:T(8,128)(2,1)S(1)}, bf16[1,16,96,768]{3,2,1,0:T(8,128)(2,1)S(1)}, u32[]{:S(2)}, u32[]{:S(2)}) collective-permute-start(bf16[1,16,96,768]{3,2,1,0:T(8,128)(2,1)S(1)} %get-tuple-element.560), channel_id=1, source_target_pairs={{0,1},{1,0},{2,3},{3,2},{4,5},{5,4},{6,7},{7,6},{8,9},{9,8},{10,11... | collective-permute-start | bytes 7077896 | tf_op jit(solution)/shard_map/ppermute | solution.py:19
  228.0 9.9 %collective-permute-start.15 = (bf16[1,2,96,768]{3,2,1,0:T(8,128)(2,1)S(1)}, bf16[1,2,96,768]{3,2,1,0:T(8,128)(2,1)S(1)}, u32[]{:S(2)}, u32[]{:S(2)}) collective-permute-start(bf16[1,2,96,768]{3,2,1,0:T(8,128)(2,1)S(1)} %get-tuple-element.561), channel_id=1, source_target_pairs={{0,2},{1,3},{2,0},{3,1},{4,6},{5,7},{6,4},{7,5},{8,10},{9,11},{10,... | collective-permute-start | bytes 884744 | tf_op jit(solution)/shard_map/ppermute | solution.py:19
  229.6 55.7 %collective-permute-start.23 = (bf16[4,8,24,768]{3,2,1,0:T(8,128)(2,1)}, bf16[4,8,24,768]{3,2,1,0:T(8,128)(2,1)}, u32[]{:S(2)}, u32[]{:S(2)}) collective-permute-start(bf16[4,8,24,768]{3,2,1,0:T(8,128)(2,1)} %get-tuple-element.604), channel_id=1, source_target_pairs={{0,2},{1,3},{2,0},{3,1},{4,6},{5,7},{6,4},{7,5},{8,10},{9,11},{10,... | collective-permute-start | bytes 3538952 | tf_op jit(solution)/shard_map/ppermute | solution.py:19
  241.9 19.0 %collective-permute-start.17 = (bf16[1,16,24,3072]{3,2,1,0:T(8,128)(2,1)S(1)}, bf16[1,16,24,3072]{3,2,1,0:T(8,128)(2,1)S(1)}, u32[]{:S(2)}, u32[]{:S(2)}) collective-permute-start(bf16[1,16,24,3072]{3,2,1,0:T(8,128)(2,1)S(1)} %get-tuple-element.578), channel_id=1, source_target_pairs={{0,1},{1,0},{2,3},{3,2},{4,5},{5,4},{6,7},{7,6},{8,9},{9,8},{10,11... | collective-permute-start | bytes 7077896 | tf_op jit(solution)/shard_map/ppermute | solution.py:19
  241.9 18.9 %collective-permute-start.18 = (bf16[1,4,24,3072]{3,2,1,0:T(8,128)(2,1)S(1)}, bf16[1,4,24,3072]{3,2,1,0:T(8,128)(2,1)S(1)}, u32[]{:S(2)}, u32[]{:S(2)}) collective-permute-start(bf16[1,4,24,3072]{3,2,1,0:T(8,128)(2,1)S(1)} %get-tuple-element.579), channel_id=1, source_target_pairs={{0,8},{4,12},{8,0},{12,4},{16,24},{20,28},{24,16},{28,20},{1,9},{5... | collective-permute-start | bytes 1769480 | tf_op jit(solution)/shard_map/ppermute | solution.py:19
  242.5 16.4 %collective-permute-start.19 = (bf16[1,1,96,768]{3,2,1,0:T(8,128)(2,1)S(1)}, bf16[1,1,96,768]{3,2,1,0:T(8,128)(2,1)S(1)}, u32[]{:S(2)}, u32[]{:S(2)}) collective-permute-start(bf16[1,1,96,768]{3,2,1,0:T(8,128)(2,1)S(1)} %get-tuple-element.580), channel_id=1, source_target_pairs={{0,16},{4,20},{8,24},{12,28},{16,0},{20,4},{24,8},{28,12},{1,17},{... | collective-permute-start | bytes 442376 | tf_op jit(solution)/shard_map/ppermute | solution.py:19
  265.4 25.9 %collective-permute-start.20 = (bf16[1,8,192,256]{3,2,1,0:T(8,128)(2,1)}, bf16[1,8,192,256]{3,2,1,0:T(8,128)(2,1)}, u32[]{:S(2)}, u32[]{:S(2)}) collective-permute-start(bf16[1,8,192,256]{3,2,1,0:T(8,128)(2,1)} %get-tuple-element.601), channel_id=1, source_target_pairs={{0,2},{1,3},{2,0},{3,1},{4,6},{5,7},{6,4},{7,5},{8,10},{9,11},{10,... | collective-permute-start | bytes 2359304 | tf_op jit(solution)/shard_map/ppermute | solution.py:19
  266.9 24.4 %collective-permute-start.21 = (bf16[1,8,192,256]{3,2,1,0:T(8,128)(2,1)}, bf16[1,8,192,256]{3,2,1,0:T(8,128)(2,1)}, u32[]{:S(2)}, u32[]{:S(2)}) collective-permute-start(bf16[1,8,192,256]{3,2,1,0:T(8,128)(2,1)} %get-tuple-element.602), channel_id=1, source_target_pairs={{0,4},{4,0},{8,12},{12,8},{16,20},{20,16},{24,28},{28,24},{1,5},{5... | collective-permute-start | bytes 2359304 | tf_op jit(solution)/shard_map/ppermute | solution.py:19
  268.4 22.8 %collective-permute-start.22 = (bf16[1,8,192,256]{3,2,1,0:T(8,128)(2,1)}, bf16[1,8,192,256]{3,2,1,0:T(8,128)(2,1)}, u32[]{:S(2)}, u32[]{:S(2)}) collective-permute-start(bf16[1,8,192,256]{3,2,1,0:T(8,128)(2,1)} %get-tuple-element.603), channel_id=1, source_target_pairs={{0,8},{4,12},{8,0},{12,4},{16,24},{20,28},{24,16},{28,20},{1,9},{5... | collective-permute-start | bytes 2359304 | tf_op jit(solution)/shard_map/ppermute | solution.py:19
  271.7 19.6 %collective-permute-start.24 = (bf16[1,2,24,3072]{3,2,1,0:T(8,128)(2,1)}, bf16[1,2,24,3072]{3,2,1,0:T(8,128)(2,1)}, u32[]{:S(2)}, u32[]{:S(2)}) collective-permute-start(bf16[1,2,24,3072]{3,2,1,0:T(8,128)(2,1)} %get-tuple-element.605), channel_id=1, source_target_pairs={{0,2},{1,3},{2,0},{3,1},{4,6},{5,7},{6,4},{7,5},{8,10},{9,11},{10,... | collective-permute-start | bytes 884744 | tf_op jit(solution)/shard_map/ppermute | solution.py:19
  294.4 10.5 %collective-permute-start.25 = (bf16[3,2,256,768]{3,2,1,0:T(8,128)(2,1)S(1)}, bf16[3,2,256,768]{3,2,1,0:T(8,128)(2,1)S(1)}, u32[]{:S(2)}, u32[]{:S(2)}) collective-permute-start(bf16[3,2,256,768]{3,2,1,0:T(8,128)(2,1)S(1)} %get-tuple-element.634), channel_id=1, source_target_pairs={{0,1},{1,0},{2,3},{3,2},{4,5},{5,4},{6,7},{7,6},{8,9},{9,8},{10,11... | collective-permute-start | bytes 7077896 | tf_op jit(solution)/shard_map/ppermute | solution.py:19
  294.5 8.8 %collective-permute-start.26 = (f32[2,12,768]{2,1,0:T(8,128)S(1)}, f32[2,12,768]{2,1,0:T(8,128)S(1)}, u32[]{:S(2)}, u32[]{:S(2)}) collective-permute-start(f32[2,12,768]{2,1,0:T(8,128)S(1)} %pad_maximum_fusion), channel_id=1, source_target_pairs={{0,1},{1,0},{2,3},{3,2},{4,5},{5,4},{6,7},{7,6},{8,9},{9,8},{10,11... | collective-permute-start | bytes 221192 | tf_op jit(solution)/shard_map/ppermute | solution.py:19
  295.0 28.7 %collective-permute-start.32 = (bf16[4,4,24,768]{3,2,1,0:T(8,128)(2,1)S(1)}, bf16[4,4,24,768]{3,2,1,0:T(8,128)(2,1)S(1)}, u32[]{:S(2)}, u32[]{:S(2)}) collective-permute-start(bf16[4,4,24,768]{3,2,1,0:T(8,128)(2,1)S(1)} %get-tuple-element.652), channel_id=1, source_target_pairs={{0,4},{4,0},{8,12},{12,8},{16,20},{20,16},{24,28},{28,24},{1,5},{5... | collective-permute-start | bytes 1769480 | tf_op jit(solution)/shard_map/ppermute | solution.py:19
  296.5 22.2 %collective-permute-start.27 = (bf16[1,4,192,256]{3,2,1,0:T(8,128)(2,1)S(1)}, bf16[1,4,192,256]{3,2,1,0:T(8,128)(2,1)S(1)}, u32[]{:S(2)}, u32[]{:S(2)}) collective-permute-start(bf16[1,4,192,256]{3,2,1,0:T(8,128)(2,1)S(1)} %get-tuple-element.647), channel_id=1, source_target_pairs={{0,4},{4,0},{8,12},{12,8},{16,20},{20,16},{24,28},{28,24},{1,5},{5... | collective-permute-start | bytes 1179656 | tf_op jit(solution)/shard_map/ppermute | solution.py:19
  297.0 26.6 %collective-permute-start.28 = (bf16[1,4,192,256]{3,2,1,0:T(8,128)(2,1)S(1)}, bf16[1,4,192,256]{3,2,1,0:T(8,128)(2,1)S(1)}, u32[]{:S(2)}, u32[]{:S(2)}) collective-permute-start(bf16[1,4,192,256]{3,2,1,0:T(8,128)(2,1)S(1)} %get-tuple-element.648), channel_id=1, source_target_pairs={{0,8},{4,12},{8,0},{12,4},{16,24},{20,28},{24,16},{28,20},{1,9},{5... | collective-permute-start | bytes 1179656 | tf_op jit(solution)/shard_map/ppermute | solution.py:19
  303.3 20.3 %collective-permute-start.29 = (bf16[1,4,192,256]{3,2,1,0:T(8,128)(2,1)S(1)}, bf16[1,4,192,256]{3,2,1,0:T(8,128)(2,1)S(1)}, u32[]{:S(2)}, u32[]{:S(2)}) collective-permute-start(bf16[1,4,192,256]{3,2,1,0:T(8,128)(2,1)S(1)} %get-tuple-element.649), channel_id=1, source_target_pairs={{0,2},{1,3},{2,0},{3,1},{4,6},{5,7},{6,4},{7,5},{8,10},{9,11},{10,... | collective-permute-start | bytes 1179656 | tf_op jit(solution)/shard_map/ppermute | solution.py:19
  304.9 8.8 %collective-permute-start.33 = (bf16[1,1,24,3072]{3,2,1,0:T(8,128)(2,1)S(1)}, bf16[1,1,24,3072]{3,2,1,0:T(8,128)(2,1)S(1)}, u32[]{:S(2)}, u32[]{:S(2)}) collective-permute-start(bf16[1,1,24,3072]{3,2,1,0:T(8,128)(2,1)S(1)} %get-tuple-element.653), channel_id=1, source_target_pairs={{0,16},{4,20},{8,24},{12,28},{16,0},{20,4},{24,8},{28,12},{1,17},{... | collective-permute-start | bytes 442376 | tf_op jit(solution)/shard_map/ppermute | solution.py:19
  313.7 10.0 %collective-permute-start.30 = (bf16[2,16,24,768]{3,2,1,0:T(8,128)(2,1)S(1)}, bf16[2,16,24,768]{3,2,1,0:T(8,128)(2,1)S(1)}, u32[]{:S(2)}, u32[]{:S(2)}) collective-permute-start(bf16[2,16,24,768]{3,2,1,0:T(8,128)(2,1)S(1)} %get-tuple-element.650), channel_id=1, source_target_pairs={{0,1},{1,0},{2,3},{3,2},{4,5},{5,4},{6,7},{7,6},{8,9},{9,8},{10,11... | collective-permute-start | bytes 3538952 | tf_op jit(solution)/shard_map/ppermute | solution.py:19
  324.7 6.4 %collective-permute-start.38 = (f32[2,12,768]{2,1,0:T(8,128)S(1)}, f32[2,12,768]{2,1,0:T(8,128)S(1)}, u32[]{:S(2)}, u32[]{:S(2)}) collective-permute-start(f32[2,12,768]{2,1,0:T(8,128)S(1)} %add.41), channel_id=1, source_target_pairs={{0,4},{4,0},{8,12},{12,8},{16,20},{20,16},{24,28},{28,24},{1,5},{5... | collective-permute-start | bytes 221192 | tf_op jit(solution)/shard_map/ppermute | solution.py:19
  326.3 13.2 %collective-permute-start.39 = (bf16[4,2,24,768]{3,2,1,0:T(8,128)(2,1)S(1)}, bf16[4,2,24,768]{3,2,1,0:T(8,128)(2,1)S(1)}, u32[]{:S(2)}, u32[]{:S(2)}) collective-permute-start(bf16[4,2,24,768]{3,2,1,0:T(8,128)(2,1)S(1)} %get-tuple-element.681), channel_id=1, source_target_pairs={{0,8},{4,12},{8,0},{12,4},{16,24},{20,28},{24,16},{28,20},{1,9},{5... | collective-permute-start | bytes 884744 | tf_op jit(solution)/shard_map/ppermute | solution.py:19
  329.5 10.1 %collective-permute-start.34 = (bf16[1,2,192,256]{3,2,1,0:T(8,128)(2,1)S(1)}, bf16[1,2,192,256]{3,2,1,0:T(8,128)(2,1)S(1)}, u32[]{:S(2)}, u32[]{:S(2)}) collective-permute-start(bf16[1,2,192,256]{3,2,1,0:T(8,128)(2,1)S(1)} %get-tuple-element.676), channel_id=1, source_target_pairs={{0,8},{4,12},{8,0},{12,4},{16,24},{20,28},{24,16},{28,20},{1,9},{5... | collective-permute-start | bytes 589832 | tf_op jit(solution)/shard_map/ppermute | solution.py:19
  329.5 10.0 %collective-permute-start.35 = (bf16[1,2,192,256]{3,2,1,0:T(8,128)(2,1)S(1)}, bf16[1,2,192,256]{3,2,1,0:T(8,128)(2,1)S(1)}, u32[]{:S(2)}, u32[]{:S(2)}) collective-permute-start(bf16[1,2,192,256]{3,2,1,0:T(8,128)(2,1)S(1)} %get-tuple-element.677), channel_id=1, source_target_pairs={{0,2},{1,3},{2,0},{3,1},{4,6},{5,7},{6,4},{7,5},{8,10},{9,11},{10,... | collective-permute-start | bytes 589832 | tf_op jit(solution)/shard_map/ppermute | solution.py:19
  330.6 8.9 %collective-permute-start.36 = (bf16[1,2,192,256]{3,2,1,0:T(8,128)(2,1)S(1)}, bf16[1,2,192,256]{3,2,1,0:T(8,128)(2,1)S(1)}, u32[]{:S(2)}, u32[]{:S(2)}) collective-permute-start(bf16[1,2,192,256]{3,2,1,0:T(8,128)(2,1)S(1)} %get-tuple-element.678), channel_id=1, source_target_pairs={{0,4},{4,0},{8,12},{12,8},{16,20},{20,16},{24,28},{28,24},{1,5},{5... | collective-permute-start | bytes 589832 | tf_op jit(solution)/shard_map/ppermute | solution.py:19
  331.2 8.4 %collective-permute-start.37 = (bf16[2,16,24,768]{3,2,1,0:T(8,128)(2,1)S(1)}, bf16[2,16,24,768]{3,2,1,0:T(8,128)(2,1)S(1)}, u32[]{:S(2)}, u32[]{:S(2)}) collective-permute-start(bf16[2,16,24,768]{3,2,1,0:T(8,128)(2,1)S(1)} %get-tuple-element.679), channel_id=1, source_target_pairs={{0,1},{1,0},{2,3},{3,2},{4,5},{5,4},{6,7},{7,6},{8,9},{9,8},{10,11... | collective-permute-start | bytes 3538952 | tf_op jit(solution)/shard_map/ppermute | solution.py:19
  341.9 9.7 %collective-permute-start.43 = (bf16[1,1,192,256]{3,2,1,0:T(8,128)(2,1)S(1)}, bf16[1,1,192,256]{3,2,1,0:T(8,128)(2,1)S(1)}, u32[]{:S(2)}, u32[]{:S(2)}) collective-permute-start(bf16[1,1,192,256]{3,2,1,0:T(8,128)(2,1)S(1)} %get-tuple-element.710), channel_id=1, source_target_pairs={{0,16},{4,20},{8,24},{12,28},{16,0},{20,4},{24,8},{28,12},{1,17},{... | collective-permute-start | bytes 294920 | tf_op jit(solution)/shard_map/ppermute | solution.py:19
  342.4 13.6 %collective-permute-start.44 = (bf16[1,1,192,256]{3,2,1,0:T(8,128)(2,1)S(1)}, bf16[1,1,192,256]{3,2,1,0:T(8,128)(2,1)S(1)}, u32[]{:S(2)}, u32[]{:S(2)}) collective-permute-start(bf16[1,1,192,256]{3,2,1,0:T(8,128)(2,1)S(1)} %get-tuple-element.711), channel_id=1, source_target_pairs={{0,16},{4,20},{8,24},{12,28},{16,0},{20,4},{24,8},{28,12},{1,17},{... | collective-permute-start | bytes 294920 | tf_op jit(solution)/shard_map/ppermute | solution.py:19
  346.7 15.8 %collective-permute-start.40 = (bf16[4,8,24,256]{3,2,1,0:T(8,128)(2,1)S(1)}, bf16[4,8,24,256]{3,2,1,0:T(8,128)(2,1)S(1)}, u32[]{:S(2)}, u32[]{:S(2)}) collective-permute-start(bf16[4,8,24,256]{3,2,1,0:T(8,128)(2,1)S(1)} %get-tuple-element.707), channel_id=1, source_target_pairs={{0,2},{1,3},{2,0},{3,1},{4,6},{5,7},{6,4},{7,5},{8,10},{9,11},{10,... | collective-permute-start | bytes 1179656 | tf_op jit(solution)/shard_map/ppermute | solution.py:19
  347.2 15.3 %collective-permute-start.41 = (bf16[4,8,24,256]{3,2,1,0:T(8,128)(2,1)S(1)}, bf16[4,8,24,256]{3,2,1,0:T(8,128)(2,1)S(1)}, u32[]{:S(2)}, u32[]{:S(2)}) collective-permute-start(bf16[4,8,24,256]{3,2,1,0:T(8,128)(2,1)S(1)} %get-tuple-element.708), channel_id=1, source_target_pairs={{0,4},{4,0},{8,12},{12,8},{16,20},{20,16},{24,28},{28,24},{1,5},{5... | collective-permute-start | bytes 1179656 | tf_op jit(solution)/shard_map/ppermute | solution.py:19
  349.8 15.6 %collective-permute-start.42 = (bf16[4,8,24,256]{3,2,1,0:T(8,128)(2,1)S(1)}, bf16[4,8,24,256]{3,2,1,0:T(8,128)(2,1)S(1)}, u32[]{:S(2)}, u32[]{:S(2)}) collective-permute-start(bf16[4,8,24,256]{3,2,1,0:T(8,128)(2,1)S(1)} %get-tuple-element.709), channel_id=1, source_target_pairs={{0,8},{4,12},{8,0},{12,4},{16,24},{20,28},{24,16},{28,20},{1,9},{5... | collective-permute-start | bytes 1179656 | tf_op jit(solution)/shard_map/ppermute | solution.py:19
  351.6 11.0 %collective-permute-start.46 = (bf16[4,1,24,768]{3,2,1,0:T(8,128)(2,1)S(1)}, bf16[4,1,24,768]{3,2,1,0:T(8,128)(2,1)S(1)}, u32[]{:S(2)}, u32[]{:S(2)}) collective-permute-start(bf16[4,1,24,768]{3,2,1,0:T(8,128)(2,1)S(1)} %get-tuple-element.713), channel_id=1, source_target_pairs={{0,16},{4,20},{8,24},{12,28},{16,0},{20,4},{24,8},{28,12},{1,17},{... | collective-permute-start | bytes 442376 | tf_op jit(solution)/shard_map/ppermute | solution.py:19
  356.1 6.4 %collective-permute-start.45 = (bf16[1,1,192,256]{3,2,1,0:T(8,128)(2,1)S(1)}, bf16[1,1,192,256]{3,2,1,0:T(8,128)(2,1)S(1)}, u32[]{:S(2)}, u32[]{:S(2)}) collective-permute-start(bf16[1,1,192,256]{3,2,1,0:T(8,128)(2,1)S(1)} %get-tuple-element.712), channel_id=1, source_target_pairs={{0,16},{4,20},{8,24},{12,28},{16,0},{20,4},{24,8},{28,12},{1,17},{... | collective-permute-start | bytes 294920 | tf_op jit(solution)/shard_map/ppermute | solution.py:19
  366.2 8.3 %collective-permute-start.48 = (bf16[4,4,24,256]{3,2,1,0:T(8,128)(2,1)S(1)}, bf16[4,4,24,256]{3,2,1,0:T(8,128)(2,1)S(1)}, u32[]{:S(2)}, u32[]{:S(2)}) collective-permute-start(bf16[4,4,24,256]{3,2,1,0:T(8,128)(2,1)S(1)} %get-tuple-element.730), channel_id=1, source_target_pairs={{0,4},{4,0},{8,12},{12,8},{16,20},{20,16},{24,28},{28,24},{1,5},{5... | collective-permute-start | bytes 589832 | tf_op jit(solution)/shard_map/ppermute | solution.py:19
  366.6 8.4 %collective-permute-start.49 = (bf16[4,4,24,256]{3,2,1,0:T(8,128)(2,1)S(1)}, bf16[4,4,24,256]{3,2,1,0:T(8,128)(2,1)S(1)}, u32[]{:S(2)}, u32[]{:S(2)}) collective-permute-start(bf16[4,4,24,256]{3,2,1,0:T(8,128)(2,1)S(1)} %get-tuple-element.731), channel_id=1, source_target_pairs={{0,8},{4,12},{8,0},{12,4},{16,24},{20,28},{24,16},{28,20},{1,9},{5... | collective-permute-start | bytes 589832 | tf_op jit(solution)/shard_map/ppermute | solution.py:19
  366.7 8.4 %collective-permute-start.50 = (bf16[4,4,24,256]{3,2,1,0:T(8,128)(2,1)S(1)}, bf16[4,4,24,256]{3,2,1,0:T(8,128)(2,1)S(1)}, u32[]{:S(2)}, u32[]{:S(2)}) collective-permute-start(bf16[4,4,24,256]{3,2,1,0:T(8,128)(2,1)S(1)} %get-tuple-element.732), channel_id=1, source_target_pairs={{0,2},{1,3},{2,0},{3,1},{4,6},{5,7},{6,4},{7,5},{8,10},{9,11},{10,... | collective-permute-start | bytes 589832 | tf_op jit(solution)/shard_map/ppermute | solution.py:19
  368.8 5.7 %collective-permute-start.51 = (f32[2,12,768]{2,1,0:T(8,128)S(1)}, f32[2,12,768]{2,1,0:T(8,128)S(1)}, u32[]{:S(2)}, u32[]{:S(2)}) collective-permute-start(f32[2,12,768]{2,1,0:T(8,128)S(1)} %add.43), channel_id=1, source_target_pairs={{0,16},{4,20},{8,24},{12,28},{16,0},{20,4},{24,8},{28,12},{1,17},{... | collective-permute-start | bytes 221192 | tf_op jit(solution)/shard_map/ppermute | solution.py:19
  383.8 5.6 %collective-permute-start.55 = (bf16[4,1,24,256]{3,2,1,0:T(8,128)(2,1)S(1)}, bf16[4,1,24,256]{3,2,1,0:T(8,128)(2,1)S(1)}, u32[]{:S(2)}, u32[]{:S(2)}) collective-permute-start(bf16[4,1,24,256]{3,2,1,0:T(8,128)(2,1)S(1)} %get-tuple-element.770), channel_id=1, source_target_pairs={{0,16},{4,20},{8,24},{12,28},{16,0},{20,4},{24,8},{28,12},{1,17},{... | collective-permute-start | bytes 147464 | tf_op jit(solution)/shard_map/ppermute | solution.py:19
  (72 other events, 562.5 us)

commit v5 on v4

--- a/solution.py
+++ b/solution.py
@@ -23,7 +23,7 @@
 TOKENS_MAJOR = (((0,), (0,)), ((), ()))
 ROOT_HALF = 0.7071067811865476
 ROOT_TAU = 0.3989422804014327
-VMEM_MIB = dict(forward=60, ff_back=32, attention_back=16, input_back=18, wgrad=16, step=20, lanes=24, finish=16)
+VMEM_MIB = dict(forward=60, ff_back=28, attention_back=12, input_back=14, wgrad=12, step=16, lanes=20, finish=12)
 FF_PARTS = 4
 FACTS_TAIL = 4
 FAST = jnp.float32

time: 401 us -> 399 us (level)
    unnamed x126 -> x112, local copies, waits for them, and re-layouts: 12.9 us -> 12.9 us
where the time goes in v5:
time: 399 us; the launch traced here: 391 us
  Pallas kernels  241 us (60%)
  waiting for transfers between devices  64.7 us (16%)
  starting transfers between devices  64.1 us (16%)
  local copies, waits for them, and re-layouts  16.5 us (4%)
    pallas_call x4, Pallas kernels, forward_call(): pl.pallas_call(partial(forward_kernel, layer, swapped, start), grid=(coun...  91.3 us
    ppermute x58, waiting for transfers between devices, swapped_2(): lax.ppermute(value, axis, [(i, i ^ 1 << bit) for i in range(lax.axis_size...  64.7 us
    ppermute x58, starting transfers between devices, swapped_2(): lax.ppermute(value, axis, [(i, i ^ 1 << bit) for i in range(lax.axis_size...  64.1 us
    pallas_call x4, Pallas kernels, attention_back_call(): pl.pallas_call(partial(attention_back_kernel, layer, start), grid=(count,...  39.3 us
    pallas_call x7, Pallas kernels, wgrad_call(): pl.pallas_call(partial(wgrad_kernel, count), grid=(steps,), in_specs=[pl....  34.3 us
    pallas_call x2, Pallas kernels, ff_back_call(): pl.pallas_call(partial(ff_back_kernel, layer), grid=(seqs,), in_specs=in_...  31.7 us
    pallas_call x11, Pallas kernels, step_call(): pl.pallas_call(partial(step_kernel, plan), grid=(steps,), in_specs=[pl.Bl...  24.6 us
    pallas_call x4, Pallas kernels, input_back_call(): pl.pallas_call(partial(input_back_kernel, layer, split), grid=(count,), i...  12.9 us
  transfers between devices with their start and end apart: 58, of which 22 were waited for; matrix products, arithmetic and copies ran while one was open for 2% of the time, Pallas kernels for 41%

profile of v5, /device:TPU:0, one launch (start us, length us, event | category | flops | bytes accessed | tf_op | source)
XLA Modules:
  0.0 391.0 jit_solution(5894249325350381470)
XLA Ops:
  4.9 28.5 %layer_forward_0.2 = (bf16[2,256,768]{2,1,0:T(8,128)(2,1)}, f32[3,256,768]{2,1,0:T(8,128)}, bf16[3,256,768]{2,1,0:T(8,128)(2,1)}, bf16[3,256,768]{2,1,0:T(8,128)...) custom-call(s32[7]{0:T(128)} %concatenate.12.facts, ...), custom_call_target="tpu_custom_call" | custom-call | flops 321999994880 | bytes 1 | tf_op jit(solution)/shard_map/layer_forward_0/pallas_call | solution.py:226
  33.5 2.9 collective-permute-start.2
  36.3 16.4 %layer_forward_0.3 = (bf16[1,256,768]{2,1,0:T(8,128)(2,1)}, f32[3,256,768]{2,1,0:T(8,128)}, bf16[3,256,768]{2,1,0:T(8,128)(2,1)}, bf16[3,256,768]{2,1,0:T(8,128)...) custom-call(s32[7]{0:T(128)} %concatenate.12.facts, ...), custom_call_target="tpu_custom_call", output_to_operand_aliasing={{1}: (12, {}), {2}: (13, {}), {3}: (14, {}), {4}: (15, {}),... | custom-call | flops 160999997440 | bytes 1 | tf_op jit(solution)/shard_map/layer_forward_0/pallas_call | solution.py:226
  58.0 29.8 %layer_forward_1.2 = (bf16[2,256,768]{2,1,0:T(8,128)(2,1)}, bf16[3,256,768]{2,1,0:T(8,128)(2,1)}, bf16[3,256,768]{2,1,0:T(8,128)(2,1)}, bf16[3,256,768]{2,1,0:T(...) custom-call(s32[7]{0:T(128)} %concatenate.12.facts, ...), custom_call_target="tpu_custom_call" | custom-call | flops 321999994880 | bytes 1 | tf_op jit(solution)/shard_map/layer_forward_1/pallas_call | solution.py:226
  90.5 16.6 %layer_forward_1.3 = (bf16[1,256,768]{2,1,0:T(8,128)(2,1)}, bf16[3,256,768]{2,1,0:T(8,128)(2,1)}, bf16[3,256,768]{2,1,0:T(8,128)(2,1)}, bf16[3,256,768]{2,1,0:T(...) custom-call(s32[7]{0:T(128)} %concatenate.12.facts, ...), custom_call_target="tpu_custom_call", output_to_operand_aliasing={{1}: (12, {}), {2}: (13, {}), {3}: (14, {}), {4}: (15, {}),... | custom-call | flops 160999997440 | bytes 1 | tf_op jit(solution)/shard_map/layer_forward_1/pallas_call | solution.py:226
  107.2 2.3 copy-done.31
  114.0 16.0 %ff_back_1.1 = (bf16[3,256,768]{2,1,0:T(8,128)(2,1)S(1)}, bf16[3,256,3072]{2,1,0:T(8,128)(2,1)S(1)}, f32[3,256,768]{2,1,0:T(8,128)S(1)}, bf16[3,256,768]{2,1,0:T...) custom-call(bf16[3,256,768]{2,1,0:T(8,128)(2,1)S(1)} %copy-done.17, ...), custom_call_target="tpu_custom_call" | custom-call | flops 218500005888 | bytes 1 | tf_op jit(solution)/shard_map/ff_back_1/pallas_call | solution.py:326
  130.1 6.3 %wgrad_down.2 = (bf16[1,16,96,768]{3,2,1,0:T(8,128)(2,1)S(1)}, bf16[1,16,96,768]{3,2,1,0:T(8,128)(2,1)}) custom-call(s32[5]{0:T(128)S(1)} %stack.48.place_ref.bits, bf16[768,3072]{1,0:T(8,128)(2,1)S(1)} %bitcast.53, bf16[768,768]{1,0:T(8,128)(2,1)S(1)} %bitcast.68), custom_call_target="tpu_custom_call" | custom-call | flops 88763809792 | bytes 1 | tf_op jit(solution)/shard_map/wgrad_down/pallas_call | solution.py:527
  136.6 12.9 %attention_back_1.2 = (bf16[3,256,768]{2,1,0:T(8,128)(2,1)S(1)}, bf16[3,2,256,768]{3,2,1,0:T(8,128)(2,1)S(1)}, bf16[2,2,256,768]{3,2,1,0:T(8,128)(2,1)S(1)}, f32[8,768]{1,0:T(8,128)S(1)}) custom-call(s32[7]{0:T(128)S(1)} %copy-done.9, bf16[3,256,768]{2,1,0:T(8,128)(2,1)S(1)} %copy-done.32, bf16[3,512,768]{2,1,0:T(8,128)(2,1)S(1)} %copy-done.27, ...), custom_call_target="tpu_custom_call" | custom-call | flops 184000004096 | bytes 1 | tf_op jit(solution)/shard_map/attention_back_1/pallas_call | solution.py:413
  149.5 4.0 %exchange_step.11 = (bf16[1,8,96,768]{3,2,1,0:T(8,128)(2,1)S(1)}, bf16[1,8,96,768]{3,2,1,0:T(8,128)(2,1)}) custom-call(s32[5]{0:T(128)S(1)} %stack.48.place_ref.bits, bf16[1,16,96,768]{3,2,1,0:T(8,128)(2,1)S(1)} %get-tuple-element.472.refs_0_, bf16[1,16,96,768]{3,2,1,0:T(8,128)(2,1)} %collective-permute-done.5.refs_1_), custom_call_target="tpu_custom_call" | custom-call | flops 38631903232 | bytes 1 | tf_op jit(solution)/shard_map/exchange_step/pallas_call | solution.py:567
  155.7 6.7 %attention_back_1.3 = (bf16[3,256,768]{2,1,0:T(8,128)(2,1)S(1)}, bf16[3,2,256,768]{3,2,1,0:T(8,128)(2,1)S(1)}, bf16[1,2,256,768]{3,2,1,0:T(8,128)(2,1)S(1)}, f32[8,768]{1,0:T(8,128)S(1)}) custom-call(s32[7]{0:T(128)S(1)} %copy-done.9, bf16[3,256,768]{2,1,0:T(8,128)(2,1)S(1)} %copy-done.32, ...), custom_call_target="tpu_custom_call", output_to_operand_aliasing={{0}: (6, {}), {1}: (7, {})} | custom-call | flops 92000002048 | bytes 1 | tf_op jit(solution)/shard_map/attention_back_1/pallas_call | solution.py:413
  163.1 4.1 %input_back_1.2 = (f32[3,256,768]{2,1,0:T(8,128)S(1)}, bf16[3,2,256,768]{3,2,1,0:T(8,128)(2,1)S(1)}, bf16[2,256,768]{2,1,0:T(8,128)(2,1)}) custom-call(bf16[3,256,768]{2,1,0:T(8,128)(2,1)S(1)} %get-tuple-element.491.dq, bf16[3,2,256,768]{3,2,1,0:T(8,128)(2,1)S(1)} %get-tuple-element.492.near, bf16[2,2,256,768]{3,2,1,0:T(8,128)(2,1)S(1)} %collective-permute-done.6.refs_0_, ...), custom_call_target="tpu_custom_call" | custom-call | flops 92000002048 | bytes 1 | tf_op jit(solution)/shard_map/input_back_1/pallas_call | solution.py:484
  168.8 4.7 %wgrad_up.2 = (bf16[1,16,24,3072]{3,2,1,0:T(8,128)(2,1)S(1)}, bf16[1,16,24,3072]{3,2,1,0:T(8,128)(2,1)S(1)}) custom-call(s32[5]{0:T(128)S(1)} %stack.48.place_ref.bits, bf16[768,768]{1,0:T(8,128)(2,1)S(1)} %bitcast.61, bf16[768,3072]{1,0:T(8,128)(2,1)S(1)} %bitcast.52), custom_call_target="tpu_custom_call" | custom-call | flops 88763809792 | bytes 1 | tf_op jit(solution)/shard_map/wgrad_up/pallas_call | solution.py:527
  173.8 2.1 input_back_1.3
  176.4 5.9 %collective-permute-done.9.refs_3_ = bf16[1,8,96,768]{3,2,1,0:T(8,128)(2,1)} collective-permute-done((bf16[1,8,96,768]{3,2,1,0:T(8,128)(2,1)}, bf16[1,8,96,768]{3,2,1,0:T(8,128)(2,1)}, u32[]{:S(2)}, u32[]{:S(2)}) %collective-permute-start.9) | collective-permute-done | bytes 1179680 | tf_op jit(solution)/shard_map/ppermute | solution.py:19
  182.3 3.9 %exchange_step.12 = (bf16[1,8,24,3072]{3,2,1,0:T(8,128)(2,1)S(1)}, bf16[1,8,24,3072]{3,2,1,0:T(8,128)(2,1)}, bf16[1,4,96,768]{3,2,1,0:T(8,128)(2,1)S(1)}, bf16[1,4,96,768]{3,2,1,0:T(8,128)(2,1)}) custom-call(s32[5]{0:T(128)S(1)} %stack.48.place_ref.bits, bf16[1,16,24,3072]{3,2,1,0:T(8,128)(2,1)S(1)} %get-tuple-element.503.refs_0_, ...), custom_call_target="tpu_custom_call" | custom-call | flops 52197855232 | bytes 1 | tf_op jit(solution)/shard_map/exchange_step/pallas_call | solution.py:567
  188.2 6.5 %wgrad_four.1 = (bf16[4,16,24,768]{3,2,1,0:T(8,128)(2,1)S(1)}, bf16[4,16,24,768]{3,2,1,0:T(8,128)(2,1)}) custom-call(s32[5]{0:T(128)S(1)} %stack.48.place_ref.bits, bf16[768,768]{1,0:T(8,128)(2,1)S(1)} %bitcast.60, bf16[768,768]{1,0:T(8,128)(2,1)S(1)} %bitcast.63, bf16[768,768]{1,0:T(8,128)(2,1)S(1)} %bitcast.58, bf16[768,768]{1,0:T(8,128)(2,1)S(1)} %bitcast.59, ...), custom_call_target="tpu_custom_call" | custom-call | flops 88763809792 | bytes 1 | tf_op jit(solution)/shard_map/wgrad_four/pallas_call | solution.py:527
  199.6 15.7 %ff_back_0.1 = (bf16[3,256,768]{2,1,0:T(8,128)(2,1)S(1)}, bf16[3,256,3072]{2,1,0:T(8,128)(2,1)S(1)}, f32[3,256,768]{2,1,0:T(8,128)S(1)}, bf16[3,256,768]{2,1,0:T...) custom-call(f32[3,256,768]{2,1,0:T(8,128)S(1)} %convert_add_fusion.top_grad, ...), custom_call_target="tpu_custom_call" | custom-call | flops 218500005888 | bytes 1 | tf_op jit(solution)/shard_map/ff_back_0/pallas_call | solution.py:326
  215.4 4.6 %exchange_step.13 = (bf16[1,2,96,768]{3,2,1,0:T(8,128)(2,1)S(1)}, bf16[1,2,96,768]{3,2,1,0:T(8,128)(2,1)S(1)}, bf16[4,8,24,768]{3,2,1,0:T(8,128)(2,1)S(1)}, bf16[4,8,24,768]{3,2,1,0:T(8,128)(2,1)}) custom-call(s32[5]{0:T(128)S(1)} %stack.48.place_ref.bits, bf16[1,4,96,768]{3,2,1,0:T(8,128)(2,1)S(1)} %get-tuple-element.516.refs_0_, ...), custom_call_target="tpu_custom_call" | custom-call | flops 45414879232 | bytes 1 | tf_op jit(solution)/shard_map/exchange_step/pallas_call | solution.py:567
  219.9 5.4 %wgrad_down.3 = (bf16[1,16,96,768]{3,2,1,0:T(8,128)(2,1)S(1)}, bf16[1,16,96,768]{3,2,1,0:T(8,128)(2,1)S(1)}) custom-call(s32[5]{0:T(128)S(1)} %stack.48.place_ref.bits, bf16[768,3072]{1,0:T(8,128)(2,1)S(1)} %bitcast.55, bf16[768,768]{1,0:T(8,128)(2,1)S(1)} %bitcast.66), custom_call_target="tpu_custom_call" | custom-call | flops 88763809792 | bytes 1 | tf_op jit(solution)/shard_map/wgrad_down/pallas_call | solution.py:527
  227.6 4.9 %wgrad_up.3 = (bf16[1,16,24,3072]{3,2,1,0:T(8,128)(2,1)S(1)}, bf16[1,16,24,3072]{3,2,1,0:T(8,128)(2,1)S(1)}) custom-call(s32[5]{0:T(128)S(1)} %stack.48.place_ref.bits, bf16[768,768]{1,0:T(8,128)(2,1)S(1)} %bitcast.65, bf16[768,3072]{1,0:T(8,128)(2,1)S(1)} %bitcast.54), custom_call_target="tpu_custom_call" | custom-call | flops 88763809792 | bytes 1 | tf_op jit(solution)/shard_map/wgrad_up/pallas_call | solution.py:527
  233.1 2.3 collective-permute-done.15.refs_1_
  236.0 3.2 exchange_step.14
  239.8 2.6 collective-permute-start.19
  242.4 6.7 %attention_back_0.2 = (bf16[3,256,768]{2,1,0:T(8,128)(2,1)S(1)}, bf16[3,2,256,768]{3,2,1,0:T(8,128)(2,1)S(1)}, bf16[3,2,256,768]{3,2,1,0:T(8,128)(2,1)S(1)}, f32[8,768]{1,0:T(8,128)S(1)}) custom-call(s32[7]{0:T(128)S(1)} %copy-done.9, bf16[3,256,768]{2,1,0:T(8,128)(2,1)S(1)} %copy-done.33, bf16[3,512,768]{2,1,0:T(8,128)(2,1)S(1)} %copy-done.29, ...), custom_call_target="tpu_custom_call" | custom-call | flops 92000002048 | bytes 1 | tf_op jit(solution)/shard_map/attention_back_0/pallas_call | solution.py:413
  249.1 7.1 %collective-permute-done.19.refs_13_ = bf16[1,1,96,768]{3,2,1,0:T(8,128)(2,1)S(1)} collective-permute-done((bf16[1,1,96,768]{3,2,1,0:T(8,128)(2,1)S(1)}, bf16[1,1,96,768]{3,2,1,0:T(8,128)(2,1)S(1)}, u32[]{:S(2)}, u32[]{:S(2)}) %collective-permute-start.19) | collective-permute-done | bytes 147488 | tf_op jit(solution)/shard_map/ppermute | solution.py:19
  258.2 2.6 exchange_lanes.2
  260.8 2.0 exchange_step.15
  265.6 3.3 collective-permute-start.22
  269.4 13.1 %attention_back_0.3 = (bf16[3,256,768]{2,1,0:T(8,128)(2,1)S(1)}, bf16[3,2,256,768]{3,2,1,0:T(8,128)(2,1)S(1)}, bf16[3,2,256,768]{3,2,1,0:T(8,128)(2,1)S(1)}, f32[8,768]{1,0:T(8,128)S(1)}) custom-call(s32[7]{0:T(128)S(1)} %copy-done.9, bf16[3,256,768]{2,1,0:T(8,128)(2,1)S(1)} %copy-done.33, ...), custom_call_target="tpu_custom_call", output_to_operand_aliasing={{0}: (6, {}), {1}: (7, {}), {2}: (8, {})} | custom-call | flops 184000004096 | bytes 1 | tf_op jit(solution)/shard_map/attention_back_0/pallas_call | solution.py:413
  282.5 6.1 %collective-permute-done.24.refs_9_ = bf16[1,2,24,3072]{3,2,1,0:T(8,128)(2,1)} collective-permute-done((bf16[1,2,24,3072]{3,2,1,0:T(8,128)(2,1)}, bf16[1,2,24,3072]{3,2,1,0:T(8,128)(2,1)}, u32[]{:S(2)}, u32[]{:S(2)}) %collective-permute-start.24) | collective-permute-done | bytes 294944 | tf_op jit(solution)/shard_map/ppermute | solution.py:19
  288.7 3.1 exchange_step.16
  294.4 3.2 collective-permute-start.28
  297.6 3.1 wgrad_rest.1
  303.1 7.9 %collective-permute-done.33.refs_15_ = bf16[1,1,24,3072]{3,2,1,0:T(8,128)(2,1)S(1)} collective-permute-done((bf16[1,1,24,3072]{3,2,1,0:T(8,128)(2,1)S(1)}, bf16[1,1,24,3072]{3,2,1,0:T(8,128)(2,1)S(1)}, u32[]{:S(2)}, u32[]{:S(2)}) %collective-permute-start.33) | collective-permute-done | bytes 147488 | tf_op jit(solution)/shard_map/ppermute | solution.py:19
  311.0 5.1 %collective-permute-done.27.refs_1_ = bf16[1,4,192,256]{3,2,1,0:T(8,128)(2,1)S(1)} collective-permute-done((bf16[1,4,192,256]{3,2,1,0:T(8,128)(2,1)S(1)}, bf16[1,4,192,256]{3,2,1,0:T(8,128)(2,1)S(1)}, u32[]{:S(2)}, u32[]{:S(2)}) %collective-permute-start.27) | collective-permute-done | bytes 393248 | tf_op jit(solution)/shard_map/ppermute | solution.py:19
  317.6 3.4 wgrad_pair.1
  323.6 3.2 collective-permute-start.39
  328.6 4.0 %input_back_0.2.refs_4_ = f32[3,256,768]{2,1,0:T(8,128)} custom-call(bf16[3,256,768]{2,1,0:T(8,128)(2,1)S(1)} %get-tuple-element.631.dq, bf16[3,2,256,768]{3,2,1,0:T(8,128)(2,1)S(1)} %add_convert_fusion.near, f32[3,256,768]{2,1,0:T(8,128)S(1)} %get-tuple-element.705.refs_0_, bf16[2,768,768]{2,1,0:T(8,128)(2,1)S(1)} %copy-done.12, ...), custom_call_target="tpu_custom_call" | custom-call | flops 92000002048 | bytes 1 | tf_op jit(solution)/shard_map/input_back_0/pallas_call | solution.py:484
  332.6 4.2 %collective-permute-done.34.refs_1_ = bf16[1,2,192,256]{3,2,1,0:T(8,128)(2,1)S(1)} collective-permute-done((bf16[1,2,192,256]{3,2,1,0:T(8,128)(2,1)S(1)}, bf16[1,2,192,256]{3,2,1,0:T(8,128)(2,1)S(1)}, u32[]{:S(2)}, u32[]{:S(2)}) %collective-permute-start.34) | collective-permute-done | bytes 196640 | tf_op jit(solution)/shard_map/ppermute | solution.py:19
  339.7 2.4 collective-permute-start.44
  345.1 1.9 collective-permute-done.47
  348.8 4.5 %collective-permute-start.46 = (bf16[4,1,24,768]{3,2,1,0:T(8,128)(2,1)S(1)}, bf16[4,1,24,768]{3,2,1,0:T(8,128)(2,1)S(1)}, u32[]{:S(2)}, u32[]{:S(2)}) collective-permute-start(bf16[4,1,24,768]{3,2,1,0:T(8,128)(2,1)S(1)} %get-tuple-element.713), channel_id=1, source_target_pairs={{0,16},{4,20},{8,24},{12,28},{16,0},{20,4},{24,8},{28,12},{1,17},{... | collective-permute-start | bytes 442376 | tf_op jit(solution)/shard_map/ppermute | solution.py:19
  353.4 2.8 input_back_0.3
  356.2 3.6 collective-permute-done.45.refs_5_
  359.8 2.8 collective-permute-done.42.refs_5_
  364.2 2.1 collective-permute-start.50
  367.3 4.6 %collective-permute-done.51 = f32[2,12,768]{2,1,0:T(8,128)S(1)} collective-permute-done((f32[2,12,768]{2,1,0:T(8,128)S(1)}, f32[2,12,768]{2,1,0:T(8,128)S(1)}, u32[]{:S(2)}, u32[]{:S(2)}) %collective-permute-start.51) | collective-permute-done | bytes 73760 | tf_op jit(solution)/shard_map/ppermute | solution.py:19
  (239 shorter events, 78.3 us)
Async XLA Ops:
  33.5 21.1 %collective-permute-start.2 = (bf16[2,256,768]{2,1,0:T(8,128)(2,1)}, bf16[2,256,768]{2,1,0:T(8,128)(2,1)}, u32[]{:S(2)}, u32[]{:S(2)}) collective-permute-start(bf16[2,256,768]{2,1,0:T(8,128)(2,1)} %get-tuple-element.431), channel_id=1, source_target_pairs={{0,2},{1,3},{2,0},{3,1},{4,6},{5,7},{6,4},{7,5},{8,10},{9,11},{10,... | collective-permute-start | bytes 2359304 | tf_op jit(solution)/shard_map/ppermute | solution.py:19
  54.6 33.2 %collective-permute-start.1 = (bf16[1,256,768]{2,1,0:T(8,128)(2,1)}, bf16[1,256,768]{2,1,0:T(8,128)(2,1)}, u32[]{:S(2)}, u32[]{:S(2)}) collective-permute-start(bf16[1,256,768]{2,1,0:T(8,128)(2,1)} %get-tuple-element.430), channel_id=1, source_target_pairs={{0,2},{1,3},{2,0},{3,1},{4,6},{5,7},{6,4},{7,5},{8,10},{9,11},{10,... | collective-permute-start | bytes 1179656 | tf_op jit(solution)/shard_map/ppermute | solution.py:19
  136.4 13.1 %collective-permute-start.5 = (bf16[1,16,96,768]{3,2,1,0:T(8,128)(2,1)}, bf16[1,16,96,768]{3,2,1,0:T(8,128)(2,1)}, u32[]{:S(2)}, u32[]{:S(2)}) collective-permute-start(bf16[1,16,96,768]{3,2,1,0:T(8,128)(2,1)} %get-tuple-element.478), channel_id=1, source_target_pairs={{0,1},{1,0},{2,3},{3,2},{4,5},{5,4},{6,7},{7,6},{8,9},{9,8},{10,11... | collective-permute-start | bytes 7077896 | tf_op jit(solution)/shard_map/ppermute | solution.py:19
  153.5 9.5 %collective-permute-start.6 = (bf16[2,2,256,768]{3,2,1,0:T(8,128)(2,1)S(1)}, bf16[2,2,256,768]{3,2,1,0:T(8,128)(2,1)S(1)}, u32[]{:S(2)}, u32[]{:S(2)}) collective-permute-start(bf16[2,2,256,768]{3,2,1,0:T(8,128)(2,1)S(1)} %get-tuple-element.489), channel_id=1, source_target_pairs={{0,1},{1,0},{2,3},{3,2},{4,5},{5,4},{6,7},{7,6},{8,9},{9,8},{10,11... | collective-permute-start | bytes 4718600 | tf_op jit(solution)/shard_map/ppermute | solution.py:19
  154.0 28.4 %collective-permute-start.9 = (bf16[1,8,96,768]{3,2,1,0:T(8,128)(2,1)}, bf16[1,8,96,768]{3,2,1,0:T(8,128)(2,1)}, u32[]{:S(2)}, u32[]{:S(2)}) collective-permute-start(bf16[1,8,96,768]{3,2,1,0:T(8,128)(2,1)} %get-tuple-element.512), channel_id=1, source_target_pairs={{0,4},{4,0},{8,12},{12,8},{16,20},{20,16},{24,28},{28,24},{1,5},{5... | collective-permute-start | bytes 3538952 | tf_op jit(solution)/shard_map/ppermute | solution.py:19
  167.2 6.4 %collective-permute-start.7 = (bf16[1,2,256,768]{3,2,1,0:T(8,128)(2,1)S(1)}, bf16[1,2,256,768]{3,2,1,0:T(8,128)(2,1)S(1)}, u32[]{:S(2)}, u32[]{:S(2)}) collective-permute-start(bf16[1,2,256,768]{3,2,1,0:T(8,128)(2,1)S(1)} %get-tuple-element.502), channel_id=1, source_target_pairs={{0,1},{1,0},{2,3},{3,2},{4,5},{5,4},{6,7},{7,6},{8,9},{9,8},{10,11... | collective-permute-start | bytes 2359304 | tf_op jit(solution)/shard_map/ppermute | solution.py:19
  167.2 27.5 %collective-permute-start.10 = (bf16[2,256,768]{2,1,0:T(8,128)(2,1)}, bf16[2,256,768]{2,1,0:T(8,128)(2,1)}, u32[]{:S(2)}, u32[]{:S(2)}) collective-permute-start(bf16[2,256,768]{2,1,0:T(8,128)(2,1)} %get-tuple-element.527), channel_id=1, source_target_pairs={{0,2},{1,3},{2,0},{3,1},{4,6},{5,7},{6,4},{7,5},{8,10},{9,11},{10,... | collective-permute-start | bytes 2359304 | tf_op jit(solution)/shard_map/ppermute | solution.py:19
  173.5 8.8 %collective-permute-start.8 = (bf16[1,16,24,3072]{3,2,1,0:T(8,128)(2,1)S(1)}, bf16[1,16,24,3072]{3,2,1,0:T(8,128)(2,1)S(1)}, u32[]{:S(2)}, u32[]{:S(2)}) collective-permute-start(bf16[1,16,24,3072]{3,2,1,0:T(8,128)(2,1)S(1)} %get-tuple-element.511), channel_id=1, source_target_pairs={{0,1},{1,0},{2,3},{3,2},{4,5},{5,4},{6,7},{7,6},{8,9},{9,8},{10,11... | collective-permute-start | bytes 7077896 | tf_op jit(solution)/shard_map/ppermute | solution.py:19
  175.8 20.0 %collective-permute-start.11 = (bf16[1,256,768]{2,1,0:T(8,128)(2,1)S(1)}, bf16[1,256,768]{2,1,0:T(8,128)(2,1)S(1)}, u32[]{:S(2)}, u32[]{:S(2)}) collective-permute-start(bf16[1,256,768]{2,1,0:T(8,128)(2,1)S(1)} %get-tuple-element.510), channel_id=1, source_target_pairs={{0,2},{1,3},{2,0},{3,1},{4,6},{5,7},{6,4},{7,5},{8,10},{9,11},{10,... | collective-permute-start | bytes 1179656 | tf_op jit(solution)/shard_map/ppermute | solution.py:19
  195.8 19.5 %collective-permute-start.13 = (bf16[4,16,24,768]{3,2,1,0:T(8,128)(2,1)}, bf16[4,16,24,768]{3,2,1,0:T(8,128)(2,1)}, u32[]{:S(2)}, u32[]{:S(2)}) collective-permute-start(bf16[4,16,24,768]{3,2,1,0:T(8,128)(2,1)} %get-tuple-element.542), channel_id=1, source_target_pairs={{0,1},{1,0},{2,3},{3,2},{4,5},{5,4},{6,7},{7,6},{8,9},{9,8},{10,11... | collective-permute-start | bytes 7077896 | tf_op jit(solution)/shard_map/ppermute | solution.py:19
  195.9 19.4 %collective-permute-start.12 = (bf16[1,4,96,768]{3,2,1,0:T(8,128)(2,1)}, bf16[1,4,96,768]{3,2,1,0:T(8,128)(2,1)}, u32[]{:S(2)}, u32[]{:S(2)}) collective-permute-start(bf16[1,4,96,768]{3,2,1,0:T(8,128)(2,1)} %get-tuple-element.541), channel_id=1, source_target_pairs={{0,8},{4,12},{8,0},{12,4},{16,24},{20,28},{24,16},{28,20},{1,9},{5... | collective-permute-start | bytes 1769480 | tf_op jit(solution)/shard_map/ppermute | solution.py:19
  197.6 35.5 %collective-permute-start.16 = (bf16[1,8,24,3072]{3,2,1,0:T(8,128)(2,1)}, bf16[1,8,24,3072]{3,2,1,0:T(8,128)(2,1)}, u32[]{:S(2)}, u32[]{:S(2)}) collective-permute-start(bf16[1,8,24,3072]{3,2,1,0:T(8,128)(2,1)} %get-tuple-element.562), channel_id=1, source_target_pairs={{0,4},{4,0},{8,12},{12,8},{16,20},{20,16},{24,28},{28,24},{1,5},{5... | collective-permute-start | bytes 3538952 | tf_op jit(solution)/shard_map/ppermute | solution.py:19
  225.4 10.0 %collective-permute-start.14 = (bf16[1,16,96,768]{3,2,1,0:T(8,128)(2,1)S(1)}, bf16[1,16,96,768]{3,2,1,0:T(8,128)(2,1)S(1)}, u32[]{:S(2)}, u32[]{:S(2)}) collective-permute-start(bf16[1,16,96,768]{3,2,1,0:T(8,128)(2,1)S(1)} %get-tuple-element.560), channel_id=1, source_target_pairs={{0,1},{1,0},{2,3},{3,2},{4,5},{5,4},{6,7},{7,6},{8,9},{9,8},{10,11... | collective-permute-start | bytes 7077896 | tf_op jit(solution)/shard_map/ppermute | solution.py:19
  225.5 9.9 %collective-permute-start.15 = (bf16[1,2,96,768]{3,2,1,0:T(8,128)(2,1)S(1)}, bf16[1,2,96,768]{3,2,1,0:T(8,128)(2,1)S(1)}, u32[]{:S(2)}, u32[]{:S(2)}) collective-permute-start(bf16[1,2,96,768]{3,2,1,0:T(8,128)(2,1)S(1)} %get-tuple-element.561), channel_id=1, source_target_pairs={{0,2},{1,3},{2,0},{3,1},{4,6},{5,7},{6,4},{7,5},{8,10},{9,11},{10,... | collective-permute-start | bytes 884744 | tf_op jit(solution)/shard_map/ppermute | solution.py:19
  227.0 55.5 %collective-permute-start.23 = (bf16[4,8,24,768]{3,2,1,0:T(8,128)(2,1)}, bf16[4,8,24,768]{3,2,1,0:T(8,128)(2,1)}, u32[]{:S(2)}, u32[]{:S(2)}) collective-permute-start(bf16[4,8,24,768]{3,2,1,0:T(8,128)(2,1)} %get-tuple-element.604), channel_id=1, source_target_pairs={{0,2},{1,3},{2,0},{3,1},{4,6},{5,7},{6,4},{7,5},{8,10},{9,11},{10,... | collective-permute-start | bytes 3538952 | tf_op jit(solution)/shard_map/ppermute | solution.py:19
  239.2 19.0 %collective-permute-start.17 = (bf16[1,16,24,3072]{3,2,1,0:T(8,128)(2,1)S(1)}, bf16[1,16,24,3072]{3,2,1,0:T(8,128)(2,1)S(1)}, u32[]{:S(2)}, u32[]{:S(2)}) collective-permute-start(bf16[1,16,24,3072]{3,2,1,0:T(8,128)(2,1)S(1)} %get-tuple-element.578), channel_id=1, source_target_pairs={{0,1},{1,0},{2,3},{3,2},{4,5},{5,4},{6,7},{7,6},{8,9},{9,8},{10,11... | collective-permute-start | bytes 7077896 | tf_op jit(solution)/shard_map/ppermute | solution.py:19
  239.3 18.9 %collective-permute-start.18 = (bf16[1,4,24,3072]{3,2,1,0:T(8,128)(2,1)S(1)}, bf16[1,4,24,3072]{3,2,1,0:T(8,128)(2,1)S(1)}, u32[]{:S(2)}, u32[]{:S(2)}) collective-permute-start(bf16[1,4,24,3072]{3,2,1,0:T(8,128)(2,1)S(1)} %get-tuple-element.579), channel_id=1, source_target_pairs={{0,8},{4,12},{8,0},{12,4},{16,24},{20,28},{24,16},{28,20},{1,9},{5... | collective-permute-start | bytes 1769480 | tf_op jit(solution)/shard_map/ppermute | solution.py:19
  239.8 16.4 %collective-permute-start.19 = (bf16[1,1,96,768]{3,2,1,0:T(8,128)(2,1)S(1)}, bf16[1,1,96,768]{3,2,1,0:T(8,128)(2,1)S(1)}, u32[]{:S(2)}, u32[]{:S(2)}) collective-permute-start(bf16[1,1,96,768]{3,2,1,0:T(8,128)(2,1)S(1)} %get-tuple-element.580), channel_id=1, source_target_pairs={{0,16},{4,20},{8,24},{12,28},{16,0},{20,4},{24,8},{28,12},{1,17},{... | collective-permute-start | bytes 442376 | tf_op jit(solution)/shard_map/ppermute | solution.py:19
  262.8 25.9 %collective-permute-start.20 = (bf16[1,8,192,256]{3,2,1,0:T(8,128)(2,1)}, bf16[1,8,192,256]{3,2,1,0:T(8,128)(2,1)}, u32[]{:S(2)}, u32[]{:S(2)}) collective-permute-start(bf16[1,8,192,256]{3,2,1,0:T(8,128)(2,1)} %get-tuple-element.601), channel_id=1, source_target_pairs={{0,2},{1,3},{2,0},{3,1},{4,6},{5,7},{6,4},{7,5},{8,10},{9,11},{10,... | collective-permute-start | bytes 2359304 | tf_op jit(solution)/shard_map/ppermute | solution.py:19
  264.2 24.4 %collective-permute-start.21 = (bf16[1,8,192,256]{3,2,1,0:T(8,128)(2,1)}, bf16[1,8,192,256]{3,2,1,0:T(8,128)(2,1)}, u32[]{:S(2)}, u32[]{:S(2)}) collective-permute-start(bf16[1,8,192,256]{3,2,1,0:T(8,128)(2,1)} %get-tuple-element.602), channel_id=1, source_target_pairs={{0,4},{4,0},{8,12},{12,8},{16,20},{20,16},{24,28},{28,24},{1,5},{5... | collective-permute-start | bytes 2359304 | tf_op jit(solution)/shard_map/ppermute | solution.py:19
  265.6 23.0 %collective-permute-start.22 = (bf16[1,8,192,256]{3,2,1,0:T(8,128)(2,1)}, bf16[1,8,192,256]{3,2,1,0:T(8,128)(2,1)}, u32[]{:S(2)}, u32[]{:S(2)}) collective-permute-start(bf16[1,8,192,256]{3,2,1,0:T(8,128)(2,1)} %get-tuple-element.603), channel_id=1, source_target_pairs={{0,8},{4,12},{8,0},{12,4},{16,24},{20,28},{24,16},{28,20},{1,9},{5... | collective-permute-start | bytes 2359304 | tf_op jit(solution)/shard_map/ppermute | solution.py:19
  268.9 19.7 %collective-permute-start.24 = (bf16[1,2,24,3072]{3,2,1,0:T(8,128)(2,1)}, bf16[1,2,24,3072]{3,2,1,0:T(8,128)(2,1)}, u32[]{:S(2)}, u32[]{:S(2)}) collective-permute-start(bf16[1,2,24,3072]{3,2,1,0:T(8,128)(2,1)} %get-tuple-element.605), channel_id=1, source_target_pairs={{0,2},{1,3},{2,0},{3,1},{4,6},{5,7},{6,4},{7,5},{8,10},{9,11},{10,... | collective-permute-start | bytes 884744 | tf_op jit(solution)/shard_map/ppermute | solution.py:19
  291.8 10.5 %collective-permute-start.25 = (bf16[3,2,256,768]{3,2,1,0:T(8,128)(2,1)S(1)}, bf16[3,2,256,768]{3,2,1,0:T(8,128)(2,1)S(1)}, u32[]{:S(2)}, u32[]{:S(2)}) collective-permute-start(bf16[3,2,256,768]{3,2,1,0:T(8,128)(2,1)S(1)} %get-tuple-element.634), channel_id=1, source_target_pairs={{0,1},{1,0},{2,3},{3,2},{4,5},{5,4},{6,7},{7,6},{8,9},{9,8},{10,11... | collective-permute-start | bytes 7077896 | tf_op jit(solution)/shard_map/ppermute | solution.py:19
  291.9 8.8 %collective-permute-start.26 = (f32[2,12,768]{2,1,0:T(8,128)S(1)}, f32[2,12,768]{2,1,0:T(8,128)S(1)}, u32[]{:S(2)}, u32[]{:S(2)}) collective-permute-start(f32[2,12,768]{2,1,0:T(8,128)S(1)} %pad_maximum_fusion), channel_id=1, source_target_pairs={{0,1},{1,0},{2,3},{3,2},{4,5},{5,4},{6,7},{7,6},{8,9},{9,8},{10,11... | collective-permute-start | bytes 221192 | tf_op jit(solution)/shard_map/ppermute | solution.py:19
  292.4 28.7 %collective-permute-start.32 = (bf16[4,4,24,768]{3,2,1,0:T(8,128)(2,1)S(1)}, bf16[4,4,24,768]{3,2,1,0:T(8,128)(2,1)S(1)}, u32[]{:S(2)}, u32[]{:S(2)}) collective-permute-start(bf16[4,4,24,768]{3,2,1,0:T(8,128)(2,1)S(1)} %get-tuple-element.652), channel_id=1, source_target_pairs={{0,4},{4,0},{8,12},{12,8},{16,20},{20,16},{24,28},{28,24},{1,5},{5... | collective-permute-start | bytes 1769480 | tf_op jit(solution)/shard_map/ppermute | solution.py:19
  293.8 22.4 %collective-permute-start.27 = (bf16[1,4,192,256]{3,2,1,0:T(8,128)(2,1)S(1)}, bf16[1,4,192,256]{3,2,1,0:T(8,128)(2,1)S(1)}, u32[]{:S(2)}, u32[]{:S(2)}) collective-permute-start(bf16[1,4,192,256]{3,2,1,0:T(8,128)(2,1)S(1)} %get-tuple-element.647), channel_id=1, source_target_pairs={{0,4},{4,0},{8,12},{12,8},{16,20},{20,16},{24,28},{28,24},{1,5},{5... | collective-permute-start | bytes 1179656 | tf_op jit(solution)/shard_map/ppermute | solution.py:19
  294.4 26.7 %collective-permute-start.28 = (bf16[1,4,192,256]{3,2,1,0:T(8,128)(2,1)S(1)}, bf16[1,4,192,256]{3,2,1,0:T(8,128)(2,1)S(1)}, u32[]{:S(2)}, u32[]{:S(2)}) collective-permute-start(bf16[1,4,192,256]{3,2,1,0:T(8,128)(2,1)S(1)} %get-tuple-element.648), channel_id=1, source_target_pairs={{0,8},{4,12},{8,0},{12,4},{16,24},{20,28},{24,16},{28,20},{1,9},{5... | collective-permute-start | bytes 1179656 | tf_op jit(solution)/shard_map/ppermute | solution.py:19
  300.7 20.4 %collective-permute-start.29 = (bf16[1,4,192,256]{3,2,1,0:T(8,128)(2,1)S(1)}, bf16[1,4,192,256]{3,2,1,0:T(8,128)(2,1)S(1)}, u32[]{:S(2)}, u32[]{:S(2)}) collective-permute-start(bf16[1,4,192,256]{3,2,1,0:T(8,128)(2,1)S(1)} %get-tuple-element.649), channel_id=1, source_target_pairs={{0,2},{1,3},{2,0},{3,1},{4,6},{5,7},{6,4},{7,5},{8,10},{9,11},{10,... | collective-permute-start | bytes 1179656 | tf_op jit(solution)/shard_map/ppermute | solution.py:19
  302.3 8.8 %collective-permute-start.33 = (bf16[1,1,24,3072]{3,2,1,0:T(8,128)(2,1)S(1)}, bf16[1,1,24,3072]{3,2,1,0:T(8,128)(2,1)S(1)}, u32[]{:S(2)}, u32[]{:S(2)}) collective-permute-start(bf16[1,1,24,3072]{3,2,1,0:T(8,128)(2,1)S(1)} %get-tuple-element.653), channel_id=1, source_target_pairs={{0,16},{4,20},{8,24},{12,28},{16,0},{20,4},{24,8},{28,12},{1,17},{... | collective-permute-start | bytes 442376 | tf_op jit(solution)/shard_map/ppermute | solution.py:19
  311.0 10.1 %collective-permute-start.30 = (bf16[2,16,24,768]{3,2,1,0:T(8,128)(2,1)S(1)}, bf16[2,16,24,768]{3,2,1,0:T(8,128)(2,1)S(1)}, u32[]{:S(2)}, u32[]{:S(2)}) collective-permute-start(bf16[2,16,24,768]{3,2,1,0:T(8,128)(2,1)S(1)} %get-tuple-element.650), channel_id=1, source_target_pairs={{0,1},{1,0},{2,3},{3,2},{4,5},{5,4},{6,7},{7,6},{8,9},{9,8},{10,11... | collective-permute-start | bytes 3538952 | tf_op jit(solution)/shard_map/ppermute | solution.py:19
  322.1 6.4 %collective-permute-start.38 = (f32[2,12,768]{2,1,0:T(8,128)S(1)}, f32[2,12,768]{2,1,0:T(8,128)S(1)}, u32[]{:S(2)}, u32[]{:S(2)}) collective-permute-start(f32[2,12,768]{2,1,0:T(8,128)S(1)} %add.41), channel_id=1, source_target_pairs={{0,4},{4,0},{8,12},{12,8},{16,20},{20,16},{24,28},{28,24},{1,5},{5... | collective-permute-start | bytes 221192 | tf_op jit(solution)/shard_map/ppermute | solution.py:19
  323.6 13.2 %collective-permute-start.39 = (bf16[4,2,24,768]{3,2,1,0:T(8,128)(2,1)S(1)}, bf16[4,2,24,768]{3,2,1,0:T(8,128)(2,1)S(1)}, u32[]{:S(2)}, u32[]{:S(2)}) collective-permute-start(bf16[4,2,24,768]{3,2,1,0:T(8,128)(2,1)S(1)} %get-tuple-element.681), channel_id=1, source_target_pairs={{0,8},{4,12},{8,0},{12,4},{16,24},{20,28},{24,16},{28,20},{1,9},{5... | collective-permute-start | bytes 884744 | tf_op jit(solution)/shard_map/ppermute | solution.py:19
  326.7 10.1 %collective-permute-start.34 = (bf16[1,2,192,256]{3,2,1,0:T(8,128)(2,1)S(1)}, bf16[1,2,192,256]{3,2,1,0:T(8,128)(2,1)S(1)}, u32[]{:S(2)}, u32[]{:S(2)}) collective-permute-start(bf16[1,2,192,256]{3,2,1,0:T(8,128)(2,1)S(1)} %get-tuple-element.676), channel_id=1, source_target_pairs={{0,8},{4,12},{8,0},{12,4},{16,24},{20,28},{24,16},{28,20},{1,9},{5... | collective-permute-start | bytes 589832 | tf_op jit(solution)/shard_map/ppermute | solution.py:19
  326.8 10.0 %collective-permute-start.35 = (bf16[1,2,192,256]{3,2,1,0:T(8,128)(2,1)S(1)}, bf16[1,2,192,256]{3,2,1,0:T(8,128)(2,1)S(1)}, u32[]{:S(2)}, u32[]{:S(2)}) collective-permute-start(bf16[1,2,192,256]{3,2,1,0:T(8,128)(2,1)S(1)} %get-tuple-element.677), channel_id=1, source_target_pairs={{0,2},{1,3},{2,0},{3,1},{4,6},{5,7},{6,4},{7,5},{8,10},{9,11},{10,... | collective-permute-start | bytes 589832 | tf_op jit(solution)/shard_map/ppermute | solution.py:19
  327.9 8.9 %collective-permute-start.36 = (bf16[1,2,192,256]{3,2,1,0:T(8,128)(2,1)S(1)}, bf16[1,2,192,256]{3,2,1,0:T(8,128)(2,1)S(1)}, u32[]{:S(2)}, u32[]{:S(2)}) collective-permute-start(bf16[1,2,192,256]{3,2,1,0:T(8,128)(2,1)S(1)} %get-tuple-element.678), channel_id=1, source_target_pairs={{0,4},{4,0},{8,12},{12,8},{16,20},{20,16},{24,28},{28,24},{1,5},{5... | collective-permute-start | bytes 589832 | tf_op jit(solution)/shard_map/ppermute | solution.py:19
  328.5 8.3 %collective-permute-start.37 = (bf16[2,16,24,768]{3,2,1,0:T(8,128)(2,1)S(1)}, bf16[2,16,24,768]{3,2,1,0:T(8,128)(2,1)S(1)}, u32[]{:S(2)}, u32[]{:S(2)}) collective-permute-start(bf16[2,16,24,768]{3,2,1,0:T(8,128)(2,1)S(1)} %get-tuple-element.679), channel_id=1, source_target_pairs={{0,1},{1,0},{2,3},{3,2},{4,5},{5,4},{6,7},{7,6},{8,9},{9,8},{10,11... | collective-permute-start | bytes 3538952 | tf_op jit(solution)/shard_map/ppermute | solution.py:19
  339.1 9.7 %collective-permute-start.43 = (bf16[1,1,192,256]{3,2,1,0:T(8,128)(2,1)S(1)}, bf16[1,1,192,256]{3,2,1,0:T(8,128)(2,1)S(1)}, u32[]{:S(2)}, u32[]{:S(2)}) collective-permute-start(bf16[1,1,192,256]{3,2,1,0:T(8,128)(2,1)S(1)} %get-tuple-element.710), channel_id=1, source_target_pairs={{0,16},{4,20},{8,24},{12,28},{16,0},{20,4},{24,8},{28,12},{1,17},{... | collective-permute-start | bytes 294920 | tf_op jit(solution)/shard_map/ppermute | solution.py:19
  339.7 13.6 %collective-permute-start.44 = (bf16[1,1,192,256]{3,2,1,0:T(8,128)(2,1)S(1)}, bf16[1,1,192,256]{3,2,1,0:T(8,128)(2,1)S(1)}, u32[]{:S(2)}, u32[]{:S(2)}) collective-permute-start(bf16[1,1,192,256]{3,2,1,0:T(8,128)(2,1)S(1)} %get-tuple-element.711), channel_id=1, source_target_pairs={{0,16},{4,20},{8,24},{12,28},{16,0},{20,4},{24,8},{28,12},{1,17},{... | collective-permute-start | bytes 294920 | tf_op jit(solution)/shard_map/ppermute | solution.py:19
  343.9 15.8 %collective-permute-start.40 = (bf16[4,8,24,256]{3,2,1,0:T(8,128)(2,1)S(1)}, bf16[4,8,24,256]{3,2,1,0:T(8,128)(2,1)S(1)}, u32[]{:S(2)}, u32[]{:S(2)}) collective-permute-start(bf16[4,8,24,256]{3,2,1,0:T(8,128)(2,1)S(1)} %get-tuple-element.707), channel_id=1, source_target_pairs={{0,2},{1,3},{2,0},{3,1},{4,6},{5,7},{6,4},{7,5},{8,10},{9,11},{10,... | collective-permute-start | bytes 1179656 | tf_op jit(solution)/shard_map/ppermute | solution.py:19
  344.5 15.3 %collective-permute-start.41 = (bf16[4,8,24,256]{3,2,1,0:T(8,128)(2,1)S(1)}, bf16[4,8,24,256]{3,2,1,0:T(8,128)(2,1)S(1)}, u32[]{:S(2)}, u32[]{:S(2)}) collective-permute-start(bf16[4,8,24,256]{3,2,1,0:T(8,128)(2,1)S(1)} %get-tuple-element.708), channel_id=1, source_target_pairs={{0,4},{4,0},{8,12},{12,8},{16,20},{20,16},{24,28},{28,24},{1,5},{5... | collective-permute-start | bytes 1179656 | tf_op jit(solution)/shard_map/ppermute | solution.py:19
  347.1 15.5 %collective-permute-start.42 = (bf16[4,8,24,256]{3,2,1,0:T(8,128)(2,1)S(1)}, bf16[4,8,24,256]{3,2,1,0:T(8,128)(2,1)S(1)}, u32[]{:S(2)}, u32[]{:S(2)}) collective-permute-start(bf16[4,8,24,256]{3,2,1,0:T(8,128)(2,1)S(1)} %get-tuple-element.709), channel_id=1, source_target_pairs={{0,8},{4,12},{8,0},{12,4},{16,24},{20,28},{24,16},{28,20},{1,9},{5... | collective-permute-start | bytes 1179656 | tf_op jit(solution)/shard_map/ppermute | solution.py:19
  348.8 11.0 %collective-permute-start.46 = (bf16[4,1,24,768]{3,2,1,0:T(8,128)(2,1)S(1)}, bf16[4,1,24,768]{3,2,1,0:T(8,128)(2,1)S(1)}, u32[]{:S(2)}, u32[]{:S(2)}) collective-permute-start(bf16[4,1,24,768]{3,2,1,0:T(8,128)(2,1)S(1)} %get-tuple-element.713), channel_id=1, source_target_pairs={{0,16},{4,20},{8,24},{12,28},{16,0},{20,4},{24,8},{28,12},{1,17},{... | collective-permute-start | bytes 442376 | tf_op jit(solution)/shard_map/ppermute | solution.py:19
  353.3 6.4 %collective-permute-start.45 = (bf16[1,1,192,256]{3,2,1,0:T(8,128)(2,1)S(1)}, bf16[1,1,192,256]{3,2,1,0:T(8,128)(2,1)S(1)}, u32[]{:S(2)}, u32[]{:S(2)}) collective-permute-start(bf16[1,1,192,256]{3,2,1,0:T(8,128)(2,1)S(1)} %get-tuple-element.712), channel_id=1, source_target_pairs={{0,16},{4,20},{8,24},{12,28},{16,0},{20,4},{24,8},{28,12},{1,17},{... | collective-permute-start | bytes 294920 | tf_op jit(solution)/shard_map/ppermute | solution.py:19
  363.4 8.5 %collective-permute-start.48 = (bf16[4,4,24,256]{3,2,1,0:T(8,128)(2,1)S(1)}, bf16[4,4,24,256]{3,2,1,0:T(8,128)(2,1)S(1)}, u32[]{:S(2)}, u32[]{:S(2)}) collective-permute-start(bf16[4,4,24,256]{3,2,1,0:T(8,128)(2,1)S(1)} %get-tuple-element.730), channel_id=1, source_target_pairs={{0,4},{4,0},{8,12},{12,8},{16,20},{20,16},{24,28},{28,24},{1,5},{5... | collective-permute-start | bytes 589832 | tf_op jit(solution)/shard_map/ppermute | solution.py:19
  364.2 8.4 %collective-permute-start.49 = (bf16[4,4,24,256]{3,2,1,0:T(8,128)(2,1)S(1)}, bf16[4,4,24,256]{3,2,1,0:T(8,128)(2,1)S(1)}, u32[]{:S(2)}, u32[]{:S(2)}) collective-permute-start(bf16[4,4,24,256]{3,2,1,0:T(8,128)(2,1)S(1)} %get-tuple-element.731), channel_id=1, source_target_pairs={{0,8},{4,12},{8,0},{12,4},{16,24},{20,28},{24,16},{28,20},{1,9},{5... | collective-permute-start | bytes 589832 | tf_op jit(solution)/shard_map/ppermute | solution.py:19
  364.2 8.4 %collective-permute-start.50 = (bf16[4,4,24,256]{3,2,1,0:T(8,128)(2,1)S(1)}, bf16[4,4,24,256]{3,2,1,0:T(8,128)(2,1)S(1)}, u32[]{:S(2)}, u32[]{:S(2)}) collective-permute-start(bf16[4,4,24,256]{3,2,1,0:T(8,128)(2,1)S(1)} %get-tuple-element.732), channel_id=1, source_target_pairs={{0,2},{1,3},{2,0},{3,1},{4,6},{5,7},{6,4},{7,5},{8,10},{9,11},{10,... | collective-permute-start | bytes 589832 | tf_op jit(solution)/shard_map/ppermute | solution.py:19
  366.3 5.7 %collective-permute-start.51 = (f32[2,12,768]{2,1,0:T(8,128)S(1)}, f32[2,12,768]{2,1,0:T(8,128)S(1)}, u32[]{:S(2)}, u32[]{:S(2)}) collective-permute-start(f32[2,12,768]{2,1,0:T(8,128)S(1)} %add.43), channel_id=1, source_target_pairs={{0,16},{4,20},{8,24},{12,28},{16,0},{20,4},{24,8},{28,12},{1,17},{... | collective-permute-start | bytes 221192 | tf_op jit(solution)/shard_map/ppermute | solution.py:19
  380.9 6.0 %collective-permute-start.55 = (bf16[4,1,24,256]{3,2,1,0:T(8,128)(2,1)S(1)}, bf16[4,1,24,256]{3,2,1,0:T(8,128)(2,1)S(1)}, u32[]{:S(2)}, u32[]{:S(2)}) collective-permute-start(bf16[4,1,24,256]{3,2,1,0:T(8,128)(2,1)S(1)} %get-tuple-element.770), channel_id=1, source_target_pairs={{0,16},{4,20},{8,24},{12,28},{16,0},{20,4},{24,8},{28,12},{1,17},{... | collective-permute-start | bytes 147464 | tf_op jit(solution)/shard_map/ppermute | solution.py:19
  (65 other events, 534.2 us)

commit v6 on v5

--- a/solution.py
+++ b/solution.py
@@ -190,6 +190,10 @@
 KEPT = ("extra", "low", "q", "k", "v", "lse", "ctx", "n1", "r1", "hid", "act", "slope", "n2", "r2")
 
 
+def first_forward_kernel(layer, swapped, start, facts, own, far, vecs, *refs):
+    forward_kernel(layer, swapped, start, facts, own, own, far, own, vecs, *refs)
+
+
 def forward_call(layer, swapped, start, count, facts, own, near, far, top, vecs, weights, kept, sizes):
     seqs, rows, wide, hidden = sizes
 
@@ -217,6 +221,11 @@
         pl.BlockSpec(memory_space=pltpu.SMEM), taken(own), taken(near), taken(far), taken(top),
         pl.BlockSpec(vecs.shape, lambda i: (0, 0, 0)),
     ] + [any_spec] * 6
+    kernel = forward_kernel
+    if own[0] is near[0] and own[0] is top[0]:
+        kernel = first_forward_kernel
+        for place in (4, 2):
+            del ins[place], in_specs[place]
     aliases = {}
     if kept is not None:
         for place, name in enumerate(KEPT):
@@ -224,7 +233,7 @@
         ins += [kept[name] for name in KEPT]
         in_specs += [any_spec] * len(KEPT)
     got = pl.pallas_call(
-        partial(forward_kernel, layer, swapped, start),
+        partial(kernel, layer, swapped, start),
         grid=(count,),
         in_specs=in_specs,
         out_specs=out_specs,

time: 399 us -> 398 us (level)
  no operation moved by 1% of the time
where the time goes in v6:
time: 398 us; the launch traced here: 390 us
  Pallas kernels  240 us (60%)
  waiting for transfers between devices  65 us (16%)
  starting transfers between devices  64.1 us (16%)
  local copies, waits for them, and re-layouts  16.5 us (4%)
    pallas_call x4, Pallas kernels, forward_call(): pl.pallas_call(partial(kernel, layer, swapped, start), grid=(count,), in_...  90.3 us
    ppermute x58, waiting for transfers between devices, swapped_2(): lax.ppermute(value, axis, [(i, i ^ 1 << bit) for i in range(lax.axis_size...  65 us
    ppermute x58, starting transfers between devices, swapped_2(): lax.ppermute(value, axis, [(i, i ^ 1 << bit) for i in range(lax.axis_size...  64.1 us
    pallas_call x4, Pallas kernels, attention_back_call(): pl.pallas_call(partial(attention_back_kernel, layer, start), grid=(count,...  39.3 us
    pallas_call x7, Pallas kernels, wgrad_call(): pl.pallas_call(partial(wgrad_kernel, count), grid=(steps,), in_specs=[pl....  34.3 us
    pallas_call x2, Pallas kernels, ff_back_call(): pl.pallas_call(partial(ff_back_kernel, layer), grid=(seqs,), in_specs=in_...  31.7 us
    pallas_call x11, Pallas kernels, step_call(): pl.pallas_call(partial(step_kernel, plan), grid=(steps,), in_specs=[pl.Bl...  24.6 us
    pallas_call x4, Pallas kernels, input_back_call(): pl.pallas_call(partial(input_back_kernel, layer, split), grid=(count,), i...  12.9 us
  transfers between devices with their start and end apart: 58, of which 22 were waited for; matrix products, arithmetic and copies ran while one was open for 2% of the time, Pallas kernels for 41%

profile of v6, /device:TPU:0, one launch (start us, length us, event | category | flops | bytes accessed | tf_op | source)
XLA Modules:
  0.0 390.3 jit_solution(7637370548244695227)
XLA Ops:
  4.9 27.8 %layer_forward_0.2 = (bf16[2,256,768]{2,1,0:T(8,128)(2,1)}, f32[3,256,768]{2,1,0:T(8,128)}, bf16[3,256,768]{2,1,0:T(8,128)(2,1)}, bf16[3,256,768]{2,1,0:T(8,128)...) custom-call(s32[7]{0:T(128)} %concatenate.12.facts, ...), custom_call_target="tpu_custom_call" | custom-call | flops 321999994880 | bytes 1 | tf_op jit(solution)/shard_map/layer_forward_0/pallas_call | solution.py:235
  32.7 2.9 collective-permute-start.2
  35.6 16.1 %layer_forward_0.3 = (bf16[1,256,768]{2,1,0:T(8,128)(2,1)}, f32[3,256,768]{2,1,0:T(8,128)}, bf16[3,256,768]{2,1,0:T(8,128)(2,1)}, bf16[3,256,768]{2,1,0:T(8,128)...) custom-call(s32[7]{0:T(128)} %concatenate.12.facts, ...), custom_call_target="tpu_custom_call", output_to_operand_aliasing={{1}: (10, {}), {2}: (11, {}), {3}: (12, {}), {4}: (13, {}),... | custom-call | flops 160999997440 | bytes 1 | tf_op jit(solution)/shard_map/layer_forward_0/pallas_call | solution.py:235
  51.7 2.1 collective-permute-done.2.near
  57.2 29.8 %layer_forward_1.2 = (bf16[2,256,768]{2,1,0:T(8,128)(2,1)}, bf16[3,256,768]{2,1,0:T(8,128)(2,1)}, bf16[3,256,768]{2,1,0:T(8,128)(2,1)}, bf16[3,256,768]{2,1,0:T(...) custom-call(s32[7]{0:T(128)} %concatenate.12.facts, ...), custom_call_target="tpu_custom_call" | custom-call | flops 321999994880 | bytes 1 | tf_op jit(solution)/shard_map/layer_forward_1/pallas_call | solution.py:235
  89.8 16.6 %layer_forward_1.3 = (bf16[1,256,768]{2,1,0:T(8,128)(2,1)}, bf16[3,256,768]{2,1,0:T(8,128)(2,1)}, bf16[3,256,768]{2,1,0:T(8,128)(2,1)}, bf16[3,256,768]{2,1,0:T(...) custom-call(s32[7]{0:T(128)} %concatenate.12.facts, ...), custom_call_target="tpu_custom_call", output_to_operand_aliasing={{1}: (12, {}), {2}: (13, {}), {3}: (14, {}), {4}: (15, {}),... | custom-call | flops 160999997440 | bytes 1 | tf_op jit(solution)/shard_map/layer_forward_1/pallas_call | solution.py:235
  106.5 2.3 copy-done.31
  113.3 16.0 %ff_back_1.1 = (bf16[3,256,768]{2,1,0:T(8,128)(2,1)S(1)}, bf16[3,256,3072]{2,1,0:T(8,128)(2,1)S(1)}, f32[3,256,768]{2,1,0:T(8,128)S(1)}, bf16[3,256,768]{2,1,0:T...) custom-call(bf16[3,256,768]{2,1,0:T(8,128)(2,1)S(1)} %copy-done.17, ...), custom_call_target="tpu_custom_call" | custom-call | flops 218500005888 | bytes 1 | tf_op jit(solution)/shard_map/ff_back_1/pallas_call | solution.py:335
  129.4 6.3 %wgrad_down.2 = (bf16[1,16,96,768]{3,2,1,0:T(8,128)(2,1)S(1)}, bf16[1,16,96,768]{3,2,1,0:T(8,128)(2,1)}) custom-call(s32[5]{0:T(128)S(1)} %stack.48.place_ref.bits, bf16[768,3072]{1,0:T(8,128)(2,1)S(1)} %bitcast.53, bf16[768,768]{1,0:T(8,128)(2,1)S(1)} %bitcast.68), custom_call_target="tpu_custom_call" | custom-call | flops 88763809792 | bytes 1 | tf_op jit(solution)/shard_map/wgrad_down/pallas_call | solution.py:536
  135.8 12.9 %attention_back_1.2 = (bf16[3,256,768]{2,1,0:T(8,128)(2,1)S(1)}, bf16[3,2,256,768]{3,2,1,0:T(8,128)(2,1)S(1)}, bf16[2,2,256,768]{3,2,1,0:T(8,128)(2,1)S(1)}, f32[8,768]{1,0:T(8,128)S(1)}) custom-call(s32[7]{0:T(128)S(1)} %copy-done.9, bf16[3,256,768]{2,1,0:T(8,128)(2,1)S(1)} %copy-done.32, bf16[3,512,768]{2,1,0:T(8,128)(2,1)S(1)} %copy-done.27, ...), custom_call_target="tpu_custom_call" | custom-call | flops 184000004096 | bytes 1 | tf_op jit(solution)/shard_map/attention_back_1/pallas_call | solution.py:422
  148.8 4.0 %exchange_step.11 = (bf16[1,8,96,768]{3,2,1,0:T(8,128)(2,1)S(1)}, bf16[1,8,96,768]{3,2,1,0:T(8,128)(2,1)}) custom-call(s32[5]{0:T(128)S(1)} %stack.48.place_ref.bits, bf16[1,16,96,768]{3,2,1,0:T(8,128)(2,1)S(1)} %get-tuple-element.472.refs_0_, bf16[1,16,96,768]{3,2,1,0:T(8,128)(2,1)} %collective-permute-done.5.refs_1_), custom_call_target="tpu_custom_call" | custom-call | flops 38631903232 | bytes 1 | tf_op jit(solution)/shard_map/exchange_step/pallas_call | solution.py:576
  155.0 6.7 %attention_back_1.3 = (bf16[3,256,768]{2,1,0:T(8,128)(2,1)S(1)}, bf16[3,2,256,768]{3,2,1,0:T(8,128)(2,1)S(1)}, bf16[1,2,256,768]{3,2,1,0:T(8,128)(2,1)S(1)}, f32[8,768]{1,0:T(8,128)S(1)}) custom-call(s32[7]{0:T(128)S(1)} %copy-done.9, bf16[3,256,768]{2,1,0:T(8,128)(2,1)S(1)} %copy-done.32, ...), custom_call_target="tpu_custom_call", output_to_operand_aliasing={{0}: (6, {}), {1}: (7, {})} | custom-call | flops 92000002048 | bytes 1 | tf_op jit(solution)/shard_map/attention_back_1/pallas_call | solution.py:422
  162.4 4.1 %input_back_1.2 = (f32[3,256,768]{2,1,0:T(8,128)S(1)}, bf16[3,2,256,768]{3,2,1,0:T(8,128)(2,1)S(1)}, bf16[2,256,768]{2,1,0:T(8,128)(2,1)}) custom-call(bf16[3,256,768]{2,1,0:T(8,128)(2,1)S(1)} %get-tuple-element.491.dq, bf16[3,2,256,768]{3,2,1,0:T(8,128)(2,1)S(1)} %get-tuple-element.492.near, bf16[2,2,256,768]{3,2,1,0:T(8,128)(2,1)S(1)} %collective-permute-done.6.refs_0_, ...), custom_call_target="tpu_custom_call" | custom-call | flops 92000002048 | bytes 1 | tf_op jit(solution)/shard_map/input_back_1/pallas_call | solution.py:493
  168.1 4.7 %wgrad_up.2 = (bf16[1,16,24,3072]{3,2,1,0:T(8,128)(2,1)S(1)}, bf16[1,16,24,3072]{3,2,1,0:T(8,128)(2,1)S(1)}) custom-call(s32[5]{0:T(128)S(1)} %stack.48.place_ref.bits, bf16[768,768]{1,0:T(8,128)(2,1)S(1)} %bitcast.61, bf16[768,3072]{1,0:T(8,128)(2,1)S(1)} %bitcast.52), custom_call_target="tpu_custom_call" | custom-call | flops 88763809792 | bytes 1 | tf_op jit(solution)/shard_map/wgrad_up/pallas_call | solution.py:536
  173.1 2.1 input_back_1.3
  175.7 5.9 %collective-permute-done.9.refs_3_ = bf16[1,8,96,768]{3,2,1,0:T(8,128)(2,1)} collective-permute-done((bf16[1,8,96,768]{3,2,1,0:T(8,128)(2,1)}, bf16[1,8,96,768]{3,2,1,0:T(8,128)(2,1)}, u32[]{:S(2)}, u32[]{:S(2)}) %collective-permute-start.9) | collective-permute-done | bytes 1179680 | tf_op jit(solution)/shard_map/ppermute | solution.py:19
  181.6 3.9 %exchange_step.12 = (bf16[1,8,24,3072]{3,2,1,0:T(8,128)(2,1)S(1)}, bf16[1,8,24,3072]{3,2,1,0:T(8,128)(2,1)}, bf16[1,4,96,768]{3,2,1,0:T(8,128)(2,1)S(1)}, bf16[1,4,96,768]{3,2,1,0:T(8,128)(2,1)}) custom-call(s32[5]{0:T(128)S(1)} %stack.48.place_ref.bits, bf16[1,16,24,3072]{3,2,1,0:T(8,128)(2,1)S(1)} %get-tuple-element.503.refs_0_, ...), custom_call_target="tpu_custom_call" | custom-call | flops 52197855232 | bytes 1 | tf_op jit(solution)/shard_map/exchange_step/pallas_call | solution.py:576
  187.5 6.5 %wgrad_four.1 = (bf16[4,16,24,768]{3,2,1,0:T(8,128)(2,1)S(1)}, bf16[4,16,24,768]{3,2,1,0:T(8,128)(2,1)}) custom-call(s32[5]{0:T(128)S(1)} %stack.48.place_ref.bits, bf16[768,768]{1,0:T(8,128)(2,1)S(1)} %bitcast.60, bf16[768,768]{1,0:T(8,128)(2,1)S(1)} %bitcast.63, bf16[768,768]{1,0:T(8,128)(2,1)S(1)} %bitcast.58, bf16[768,768]{1,0:T(8,128)(2,1)S(1)} %bitcast.59, ...), custom_call_target="tpu_custom_call" | custom-call | flops 88763809792 | bytes 1 | tf_op jit(solution)/shard_map/wgrad_four/pallas_call | solution.py:536
  198.9 15.7 %ff_back_0.1 = (bf16[3,256,768]{2,1,0:T(8,128)(2,1)S(1)}, bf16[3,256,3072]{2,1,0:T(8,128)(2,1)S(1)}, f32[3,256,768]{2,1,0:T(8,128)S(1)}, bf16[3,256,768]{2,1,0:T...) custom-call(f32[3,256,768]{2,1,0:T(8,128)S(1)} %convert_add_fusion.top_grad, ...), custom_call_target="tpu_custom_call" | custom-call | flops 218500005888 | bytes 1 | tf_op jit(solution)/shard_map/ff_back_0/pallas_call | solution.py:335
  214.7 4.6 %exchange_step.13 = (bf16[1,2,96,768]{3,2,1,0:T(8,128)(2,1)S(1)}, bf16[1,2,96,768]{3,2,1,0:T(8,128)(2,1)S(1)}, bf16[4,8,24,768]{3,2,1,0:T(8,128)(2,1)S(1)}, bf16[4,8,24,768]{3,2,1,0:T(8,128)(2,1)}) custom-call(s32[5]{0:T(128)S(1)} %stack.48.place_ref.bits, bf16[1,4,96,768]{3,2,1,0:T(8,128)(2,1)S(1)} %get-tuple-element.516.refs_0_, ...), custom_call_target="tpu_custom_call" | custom-call | flops 45414879232 | bytes 1 | tf_op jit(solution)/shard_map/exchange_step/pallas_call | solution.py:576
  219.2 5.4 %wgrad_down.3 = (bf16[1,16,96,768]{3,2,1,0:T(8,128)(2,1)S(1)}, bf16[1,16,96,768]{3,2,1,0:T(8,128)(2,1)S(1)}) custom-call(s32[5]{0:T(128)S(1)} %stack.48.place_ref.bits, bf16[768,3072]{1,0:T(8,128)(2,1)S(1)} %bitcast.55, bf16[768,768]{1,0:T(8,128)(2,1)S(1)} %bitcast.66), custom_call_target="tpu_custom_call" | custom-call | flops 88763809792 | bytes 1 | tf_op jit(solution)/shard_map/wgrad_down/pallas_call | solution.py:536
  226.9 4.9 %wgrad_up.3 = (bf16[1,16,24,3072]{3,2,1,0:T(8,128)(2,1)S(1)}, bf16[1,16,24,3072]{3,2,1,0:T(8,128)(2,1)S(1)}) custom-call(s32[5]{0:T(128)S(1)} %stack.48.place_ref.bits, bf16[768,768]{1,0:T(8,128)(2,1)S(1)} %bitcast.65, bf16[768,3072]{1,0:T(8,128)(2,1)S(1)} %bitcast.54), custom_call_target="tpu_custom_call" | custom-call | flops 88763809792 | bytes 1 | tf_op jit(solution)/shard_map/wgrad_up/pallas_call | solution.py:536
  232.4 2.3 collective-permute-done.15.refs_1_
  235.3 3.2 exchange_step.14
  239.1 2.6 collective-permute-start.19
  241.7 6.7 %attention_back_0.2 = (bf16[3,256,768]{2,1,0:T(8,128)(2,1)S(1)}, bf16[3,2,256,768]{3,2,1,0:T(8,128)(2,1)S(1)}, bf16[3,2,256,768]{3,2,1,0:T(8,128)(2,1)S(1)}, f32[8,768]{1,0:T(8,128)S(1)}) custom-call(s32[7]{0:T(128)S(1)} %copy-done.9, bf16[3,256,768]{2,1,0:T(8,128)(2,1)S(1)} %copy-done.33, bf16[3,512,768]{2,1,0:T(8,128)(2,1)S(1)} %copy-done.29, ...), custom_call_target="tpu_custom_call" | custom-call | flops 92000002048 | bytes 1 | tf_op jit(solution)/shard_map/attention_back_0/pallas_call | solution.py:422
  248.4 7.1 %collective-permute-done.19.refs_13_ = bf16[1,1,96,768]{3,2,1,0:T(8,128)(2,1)S(1)} collective-permute-done((bf16[1,1,96,768]{3,2,1,0:T(8,128)(2,1)S(1)}, bf16[1,1,96,768]{3,2,1,0:T(8,128)(2,1)S(1)}, u32[]{:S(2)}, u32[]{:S(2)}) %collective-permute-start.19) | collective-permute-done | bytes 147488 | tf_op jit(solution)/shard_map/ppermute | solution.py:19
  257.5 2.6 exchange_lanes.2
  260.1 2.0 exchange_step.15
  264.9 3.3 collective-permute-start.22
  268.7 13.1 %attention_back_0.3 = (bf16[3,256,768]{2,1,0:T(8,128)(2,1)S(1)}, bf16[3,2,256,768]{3,2,1,0:T(8,128)(2,1)S(1)}, bf16[3,2,256,768]{3,2,1,0:T(8,128)(2,1)S(1)}, f32[8,768]{1,0:T(8,128)S(1)}) custom-call(s32[7]{0:T(128)S(1)} %copy-done.9, bf16[3,256,768]{2,1,0:T(8,128)(2,1)S(1)} %copy-done.33, ...), custom_call_target="tpu_custom_call", output_to_operand_aliasing={{0}: (6, {}), {1}: (7, {}), {2}: (8, {})} | custom-call | flops 184000004096 | bytes 1 | tf_op jit(solution)/shard_map/attention_back_0/pallas_call | solution.py:422
  281.8 6.1 %collective-permute-done.24.refs_9_ = bf16[1,2,24,3072]{3,2,1,0:T(8,128)(2,1)} collective-permute-done((bf16[1,2,24,3072]{3,2,1,0:T(8,128)(2,1)}, bf16[1,2,24,3072]{3,2,1,0:T(8,128)(2,1)}, u32[]{:S(2)}, u32[]{:S(2)}) %collective-permute-start.24) | collective-permute-done | bytes 294944 | tf_op jit(solution)/shard_map/ppermute | solution.py:19
  287.9 3.1 exchange_step.16
  293.7 3.2 collective-permute-start.28
  296.9 3.1 wgrad_rest.1
  302.4 7.9 %collective-permute-done.33.refs_15_ = bf16[1,1,24,3072]{3,2,1,0:T(8,128)(2,1)S(1)} collective-permute-done((bf16[1,1,24,3072]{3,2,1,0:T(8,128)(2,1)S(1)}, bf16[1,1,24,3072]{3,2,1,0:T(8,128)(2,1)S(1)}, u32[]{:S(2)}, u32[]{:S(2)}) %collective-permute-start.33) | collective-permute-done | bytes 147488 | tf_op jit(solution)/shard_map/ppermute | solution.py:19
  310.3 5.1 %collective-permute-done.27.refs_1_ = bf16[1,4,192,256]{3,2,1,0:T(8,128)(2,1)S(1)} collective-permute-done((bf16[1,4,192,256]{3,2,1,0:T(8,128)(2,1)S(1)}, bf16[1,4,192,256]{3,2,1,0:T(8,128)(2,1)S(1)}, u32[]{:S(2)}, u32[]{:S(2)}) %collective-permute-start.27) | collective-permute-done | bytes 393248 | tf_op jit(solution)/shard_map/ppermute | solution.py:19
  316.9 3.4 wgrad_pair.1
  322.9 3.2 collective-permute-start.39
  327.9 4.0 %input_back_0.2.refs_4_ = f32[3,256,768]{2,1,0:T(8,128)} custom-call(bf16[3,256,768]{2,1,0:T(8,128)(2,1)S(1)} %get-tuple-element.631.dq, bf16[3,2,256,768]{3,2,1,0:T(8,128)(2,1)S(1)} %add_convert_fusion.near, f32[3,256,768]{2,1,0:T(8,128)S(1)} %get-tuple-element.705.refs_0_, bf16[2,768,768]{2,1,0:T(8,128)(2,1)S(1)} %copy-done.12, ...), custom_call_target="tpu_custom_call" | custom-call | flops 92000002048 | bytes 1 | tf_op jit(solution)/shard_map/input_back_0/pallas_call | solution.py:493
  331.9 4.2 %collective-permute-done.34.refs_1_ = bf16[1,2,192,256]{3,2,1,0:T(8,128)(2,1)S(1)} collective-permute-done((bf16[1,2,192,256]{3,2,1,0:T(8,128)(2,1)S(1)}, bf16[1,2,192,256]{3,2,1,0:T(8,128)(2,1)S(1)}, u32[]{:S(2)}, u32[]{:S(2)}) %collective-permute-start.34) | collective-permute-done | bytes 196640 | tf_op jit(solution)/shard_map/ppermute | solution.py:19
  339.0 2.4 collective-permute-start.44
  348.1 4.5 %collective-permute-start.46 = (bf16[4,1,24,768]{3,2,1,0:T(8,128)(2,1)S(1)}, bf16[4,1,24,768]{3,2,1,0:T(8,128)(2,1)S(1)}, u32[]{:S(2)}, u32[]{:S(2)}) collective-permute-start(bf16[4,1,24,768]{3,2,1,0:T(8,128)(2,1)S(1)} %get-tuple-element.713), channel_id=1, source_target_pairs={{0,16},{4,20},{8,24},{12,28},{16,0},{20,4},{24,8},{28,12},{1,17},{... | collective-permute-start | bytes 442376 | tf_op jit(solution)/shard_map/ppermute | solution.py:19
  352.7 2.8 input_back_0.3
  355.5 3.6 collective-permute-done.45.refs_5_
  359.1 2.8 collective-permute-done.42.refs_5_
  363.5 2.0 collective-permute-start.50
  366.6 4.6 %collective-permute-done.51 = f32[2,12,768]{2,1,0:T(8,128)S(1)} collective-permute-done((f32[2,12,768]{2,1,0:T(8,128)S(1)}, f32[2,12,768]{2,1,0:T(8,128)S(1)}, u32[]{:S(2)}, u32[]{:S(2)}) %collective-permute-start.51) | collective-permute-done | bytes 73760 | tf_op jit(solution)/shard_map/ppermute | solution.py:19
  (239 shorter events, 78.5 us)
Async XLA Ops:
  32.7 21.1 %collective-permute-start.2 = (bf16[2,256,768]{2,1,0:T(8,128)(2,1)}, bf16[2,256,768]{2,1,0:T(8,128)(2,1)}, u32[]{:S(2)}, u32[]{:S(2)}) collective-permute-start(bf16[2,256,768]{2,1,0:T(8,128)(2,1)} %get-tuple-element.431), channel_id=1, source_target_pairs={{0,2},{1,3},{2,0},{3,1},{4,6},{5,7},{6,4},{7,5},{8,10},{9,11},{10,... | collective-permute-start | bytes 2359304 | tf_op jit(solution)/shard_map/ppermute | solution.py:19
  53.8 33.2 %collective-permute-start.1 = (bf16[1,256,768]{2,1,0:T(8,128)(2,1)}, bf16[1,256,768]{2,1,0:T(8,128)(2,1)}, u32[]{:S(2)}, u32[]{:S(2)}) collective-permute-start(bf16[1,256,768]{2,1,0:T(8,128)(2,1)} %get-tuple-element.430), channel_id=1, source_target_pairs={{0,2},{1,3},{2,0},{3,1},{4,6},{5,7},{6,4},{7,5},{8,10},{9,11},{10,... | collective-permute-start | bytes 1179656 | tf_op jit(solution)/shard_map/ppermute | solution.py:19
  135.7 13.1 %collective-permute-start.5 = (bf16[1,16,96,768]{3,2,1,0:T(8,128)(2,1)}, bf16[1,16,96,768]{3,2,1,0:T(8,128)(2,1)}, u32[]{:S(2)}, u32[]{:S(2)}) collective-permute-start(bf16[1,16,96,768]{3,2,1,0:T(8,128)(2,1)} %get-tuple-element.478), channel_id=1, source_target_pairs={{0,1},{1,0},{2,3},{3,2},{4,5},{5,4},{6,7},{7,6},{8,9},{9,8},{10,11... | collective-permute-start | bytes 7077896 | tf_op jit(solution)/shard_map/ppermute | solution.py:19
  152.8 9.5 %collective-permute-start.6 = (bf16[2,2,256,768]{3,2,1,0:T(8,128)(2,1)S(1)}, bf16[2,2,256,768]{3,2,1,0:T(8,128)(2,1)S(1)}, u32[]{:S(2)}, u32[]{:S(2)}) collective-permute-start(bf16[2,2,256,768]{3,2,1,0:T(8,128)(2,1)S(1)} %get-tuple-element.489), channel_id=1, source_target_pairs={{0,1},{1,0},{2,3},{3,2},{4,5},{5,4},{6,7},{7,6},{8,9},{9,8},{10,11... | collective-permute-start | bytes 4718600 | tf_op jit(solution)/shard_map/ppermute | solution.py:19
  153.2 28.4 %collective-permute-start.9 = (bf16[1,8,96,768]{3,2,1,0:T(8,128)(2,1)}, bf16[1,8,96,768]{3,2,1,0:T(8,128)(2,1)}, u32[]{:S(2)}, u32[]{:S(2)}) collective-permute-start(bf16[1,8,96,768]{3,2,1,0:T(8,128)(2,1)} %get-tuple-element.512), channel_id=1, source_target_pairs={{0,4},{4,0},{8,12},{12,8},{16,20},{20,16},{24,28},{28,24},{1,5},{5... | collective-permute-start | bytes 3538952 | tf_op jit(solution)/shard_map/ppermute | solution.py:19
  166.4 6.4 %collective-permute-start.7 = (bf16[1,2,256,768]{3,2,1,0:T(8,128)(2,1)S(1)}, bf16[1,2,256,768]{3,2,1,0:T(8,128)(2,1)S(1)}, u32[]{:S(2)}, u32[]{:S(2)}) collective-permute-start(bf16[1,2,256,768]{3,2,1,0:T(8,128)(2,1)S(1)} %get-tuple-element.502), channel_id=1, source_target_pairs={{0,1},{1,0},{2,3},{3,2},{4,5},{5,4},{6,7},{7,6},{8,9},{9,8},{10,11... | collective-permute-start | bytes 2359304 | tf_op jit(solution)/shard_map/ppermute | solution.py:19
  166.5 27.5 %collective-permute-start.10 = (bf16[2,256,768]{2,1,0:T(8,128)(2,1)}, bf16[2,256,768]{2,1,0:T(8,128)(2,1)}, u32[]{:S(2)}, u32[]{:S(2)}) collective-permute-start(bf16[2,256,768]{2,1,0:T(8,128)(2,1)} %get-tuple-element.527), channel_id=1, source_target_pairs={{0,2},{1,3},{2,0},{3,1},{4,6},{5,7},{6,4},{7,5},{8,10},{9,11},{10,... | collective-permute-start | bytes 2359304 | tf_op jit(solution)/shard_map/ppermute | solution.py:19
  172.8 8.8 %collective-permute-start.8 = (bf16[1,16,24,3072]{3,2,1,0:T(8,128)(2,1)S(1)}, bf16[1,16,24,3072]{3,2,1,0:T(8,128)(2,1)S(1)}, u32[]{:S(2)}, u32[]{:S(2)}) collective-permute-start(bf16[1,16,24,3072]{3,2,1,0:T(8,128)(2,1)S(1)} %get-tuple-element.511), channel_id=1, source_target_pairs={{0,1},{1,0},{2,3},{3,2},{4,5},{5,4},{6,7},{7,6},{8,9},{9,8},{10,11... | collective-permute-start | bytes 7077896 | tf_op jit(solution)/shard_map/ppermute | solution.py:19
  175.1 20.0 %collective-permute-start.11 = (bf16[1,256,768]{2,1,0:T(8,128)(2,1)S(1)}, bf16[1,256,768]{2,1,0:T(8,128)(2,1)S(1)}, u32[]{:S(2)}, u32[]{:S(2)}) collective-permute-start(bf16[1,256,768]{2,1,0:T(8,128)(2,1)S(1)} %get-tuple-element.510), channel_id=1, source_target_pairs={{0,2},{1,3},{2,0},{3,1},{4,6},{5,7},{6,4},{7,5},{8,10},{9,11},{10,... | collective-permute-start | bytes 1179656 | tf_op jit(solution)/shard_map/ppermute | solution.py:19
  195.1 19.5 %collective-permute-start.13 = (bf16[4,16,24,768]{3,2,1,0:T(8,128)(2,1)}, bf16[4,16,24,768]{3,2,1,0:T(8,128)(2,1)}, u32[]{:S(2)}, u32[]{:S(2)}) collective-permute-start(bf16[4,16,24,768]{3,2,1,0:T(8,128)(2,1)} %get-tuple-element.542), channel_id=1, source_target_pairs={{0,1},{1,0},{2,3},{3,2},{4,5},{5,4},{6,7},{7,6},{8,9},{9,8},{10,11... | collective-permute-start | bytes 7077896 | tf_op jit(solution)/shard_map/ppermute | solution.py:19
  195.2 19.4 %collective-permute-start.12 = (bf16[1,4,96,768]{3,2,1,0:T(8,128)(2,1)}, bf16[1,4,96,768]{3,2,1,0:T(8,128)(2,1)}, u32[]{:S(2)}, u32[]{:S(2)}) collective-permute-start(bf16[1,4,96,768]{3,2,1,0:T(8,128)(2,1)} %get-tuple-element.541), channel_id=1, source_target_pairs={{0,8},{4,12},{8,0},{12,4},{16,24},{20,28},{24,16},{28,20},{1,9},{5... | collective-permute-start | bytes 1769480 | tf_op jit(solution)/shard_map/ppermute | solution.py:19
  196.8 35.5 %collective-permute-start.16 = (bf16[1,8,24,3072]{3,2,1,0:T(8,128)(2,1)}, bf16[1,8,24,3072]{3,2,1,0:T(8,128)(2,1)}, u32[]{:S(2)}, u32[]{:S(2)}) collective-permute-start(bf16[1,8,24,3072]{3,2,1,0:T(8,128)(2,1)} %get-tuple-element.562), channel_id=1, source_target_pairs={{0,4},{4,0},{8,12},{12,8},{16,20},{20,16},{24,28},{28,24},{1,5},{5... | collective-permute-start | bytes 3538952 | tf_op jit(solution)/shard_map/ppermute | solution.py:19
  224.7 10.0 %collective-permute-start.14 = (bf16[1,16,96,768]{3,2,1,0:T(8,128)(2,1)S(1)}, bf16[1,16,96,768]{3,2,1,0:T(8,128)(2,1)S(1)}, u32[]{:S(2)}, u32[]{:S(2)}) collective-permute-start(bf16[1,16,96,768]{3,2,1,0:T(8,128)(2,1)S(1)} %get-tuple-element.560), channel_id=1, source_target_pairs={{0,1},{1,0},{2,3},{3,2},{4,5},{5,4},{6,7},{7,6},{8,9},{9,8},{10,11... | collective-permute-start | bytes 7077896 | tf_op jit(solution)/shard_map/ppermute | solution.py:19
  224.8 9.9 %collective-permute-start.15 = (bf16[1,2,96,768]{3,2,1,0:T(8,128)(2,1)S(1)}, bf16[1,2,96,768]{3,2,1,0:T(8,128)(2,1)S(1)}, u32[]{:S(2)}, u32[]{:S(2)}) collective-permute-start(bf16[1,2,96,768]{3,2,1,0:T(8,128)(2,1)S(1)} %get-tuple-element.561), channel_id=1, source_target_pairs={{0,2},{1,3},{2,0},{3,1},{4,6},{5,7},{6,4},{7,5},{8,10},{9,11},{10,... | collective-permute-start | bytes 884744 | tf_op jit(solution)/shard_map/ppermute | solution.py:19
  226.3 55.5 %collective-permute-start.23 = (bf16[4,8,24,768]{3,2,1,0:T(8,128)(2,1)}, bf16[4,8,24,768]{3,2,1,0:T(8,128)(2,1)}, u32[]{:S(2)}, u32[]{:S(2)}) collective-permute-start(bf16[4,8,24,768]{3,2,1,0:T(8,128)(2,1)} %get-tuple-element.604), channel_id=1, source_target_pairs={{0,2},{1,3},{2,0},{3,1},{4,6},{5,7},{6,4},{7,5},{8,10},{9,11},{10,... | collective-permute-start | bytes 3538952 | tf_op jit(solution)/shard_map/ppermute | solution.py:19
  238.5 19.0 %collective-permute-start.17 = (bf16[1,16,24,3072]{3,2,1,0:T(8,128)(2,1)S(1)}, bf16[1,16,24,3072]{3,2,1,0:T(8,128)(2,1)S(1)}, u32[]{:S(2)}, u32[]{:S(2)}) collective-permute-start(bf16[1,16,24,3072]{3,2,1,0:T(8,128)(2,1)S(1)} %get-tuple-element.578), channel_id=1, source_target_pairs={{0,1},{1,0},{2,3},{3,2},{4,5},{5,4},{6,7},{7,6},{8,9},{9,8},{10,11... | collective-permute-start | bytes 7077896 | tf_op jit(solution)/shard_map/ppermute | solution.py:19
  238.6 18.9 %collective-permute-start.18 = (bf16[1,4,24,3072]{3,2,1,0:T(8,128)(2,1)S(1)}, bf16[1,4,24,3072]{3,2,1,0:T(8,128)(2,1)S(1)}, u32[]{:S(2)}, u32[]{:S(2)}) collective-permute-start(bf16[1,4,24,3072]{3,2,1,0:T(8,128)(2,1)S(1)} %get-tuple-element.579), channel_id=1, source_target_pairs={{0,8},{4,12},{8,0},{12,4},{16,24},{20,28},{24,16},{28,20},{1,9},{5... | collective-permute-start | bytes 1769480 | tf_op jit(solution)/shard_map/ppermute | solution.py:19
  239.1 16.4 %collective-permute-start.19 = (bf16[1,1,96,768]{3,2,1,0:T(8,128)(2,1)S(1)}, bf16[1,1,96,768]{3,2,1,0:T(8,128)(2,1)S(1)}, u32[]{:S(2)}, u32[]{:S(2)}) collective-permute-start(bf16[1,1,96,768]{3,2,1,0:T(8,128)(2,1)S(1)} %get-tuple-element.580), channel_id=1, source_target_pairs={{0,16},{4,20},{8,24},{12,28},{16,0},{20,4},{24,8},{28,12},{1,17},{... | collective-permute-start | bytes 442376 | tf_op jit(solution)/shard_map/ppermute | solution.py:19
  262.0 25.9 %collective-permute-start.20 = (bf16[1,8,192,256]{3,2,1,0:T(8,128)(2,1)}, bf16[1,8,192,256]{3,2,1,0:T(8,128)(2,1)}, u32[]{:S(2)}, u32[]{:S(2)}) collective-permute-start(bf16[1,8,192,256]{3,2,1,0:T(8,128)(2,1)} %get-tuple-element.601), channel_id=1, source_target_pairs={{0,2},{1,3},{2,0},{3,1},{4,6},{5,7},{6,4},{7,5},{8,10},{9,11},{10,... | collective-permute-start | bytes 2359304 | tf_op jit(solution)/shard_map/ppermute | solution.py:19
  263.5 24.4 %collective-permute-start.21 = (bf16[1,8,192,256]{3,2,1,0:T(8,128)(2,1)}, bf16[1,8,192,256]{3,2,1,0:T(8,128)(2,1)}, u32[]{:S(2)}, u32[]{:S(2)}) collective-permute-start(bf16[1,8,192,256]{3,2,1,0:T(8,128)(2,1)} %get-tuple-element.602), channel_id=1, source_target_pairs={{0,4},{4,0},{8,12},{12,8},{16,20},{20,16},{24,28},{28,24},{1,5},{5... | collective-permute-start | bytes 2359304 | tf_op jit(solution)/shard_map/ppermute | solution.py:19
  264.9 23.0 %collective-permute-start.22 = (bf16[1,8,192,256]{3,2,1,0:T(8,128)(2,1)}, bf16[1,8,192,256]{3,2,1,0:T(8,128)(2,1)}, u32[]{:S(2)}, u32[]{:S(2)}) collective-permute-start(bf16[1,8,192,256]{3,2,1,0:T(8,128)(2,1)} %get-tuple-element.603), channel_id=1, source_target_pairs={{0,8},{4,12},{8,0},{12,4},{16,24},{20,28},{24,16},{28,20},{1,9},{5... | collective-permute-start | bytes 2359304 | tf_op jit(solution)/shard_map/ppermute | solution.py:19
  268.2 19.7 %collective-permute-start.24 = (bf16[1,2,24,3072]{3,2,1,0:T(8,128)(2,1)}, bf16[1,2,24,3072]{3,2,1,0:T(8,128)(2,1)}, u32[]{:S(2)}, u32[]{:S(2)}) collective-permute-start(bf16[1,2,24,3072]{3,2,1,0:T(8,128)(2,1)} %get-tuple-element.605), channel_id=1, source_target_pairs={{0,2},{1,3},{2,0},{3,1},{4,6},{5,7},{6,4},{7,5},{8,10},{9,11},{10,... | collective-permute-start | bytes 884744 | tf_op jit(solution)/shard_map/ppermute | solution.py:19
  291.1 10.5 %collective-permute-start.25 = (bf16[3,2,256,768]{3,2,1,0:T(8,128)(2,1)S(1)}, bf16[3,2,256,768]{3,2,1,0:T(8,128)(2,1)S(1)}, u32[]{:S(2)}, u32[]{:S(2)}) collective-permute-start(bf16[3,2,256,768]{3,2,1,0:T(8,128)(2,1)S(1)} %get-tuple-element.634), channel_id=1, source_target_pairs={{0,1},{1,0},{2,3},{3,2},{4,5},{5,4},{6,7},{7,6},{8,9},{9,8},{10,11... | collective-permute-start | bytes 7077896 | tf_op jit(solution)/shard_map/ppermute | solution.py:19
  291.2 8.8 %collective-permute-start.26 = (f32[2,12,768]{2,1,0:T(8,128)S(1)}, f32[2,12,768]{2,1,0:T(8,128)S(1)}, u32[]{:S(2)}, u32[]{:S(2)}) collective-permute-start(f32[2,12,768]{2,1,0:T(8,128)S(1)} %pad_maximum_fusion), channel_id=1, source_target_pairs={{0,1},{1,0},{2,3},{3,2},{4,5},{5,4},{6,7},{7,6},{8,9},{9,8},{10,11... | collective-permute-start | bytes 221192 | tf_op jit(solution)/shard_map/ppermute | solution.py:19
  291.7 28.7 %collective-permute-start.32 = (bf16[4,4,24,768]{3,2,1,0:T(8,128)(2,1)S(1)}, bf16[4,4,24,768]{3,2,1,0:T(8,128)(2,1)S(1)}, u32[]{:S(2)}, u32[]{:S(2)}) collective-permute-start(bf16[4,4,24,768]{3,2,1,0:T(8,128)(2,1)S(1)} %get-tuple-element.652), channel_id=1, source_target_pairs={{0,4},{4,0},{8,12},{12,8},{16,20},{20,16},{24,28},{28,24},{1,5},{5... | collective-permute-start | bytes 1769480 | tf_op jit(solution)/shard_map/ppermute | solution.py:19
  293.0 22.4 %collective-permute-start.27 = (bf16[1,4,192,256]{3,2,1,0:T(8,128)(2,1)S(1)}, bf16[1,4,192,256]{3,2,1,0:T(8,128)(2,1)S(1)}, u32[]{:S(2)}, u32[]{:S(2)}) collective-permute-start(bf16[1,4,192,256]{3,2,1,0:T(8,128)(2,1)S(1)} %get-tuple-element.647), channel_id=1, source_target_pairs={{0,4},{4,0},{8,12},{12,8},{16,20},{20,16},{24,28},{28,24},{1,5},{5... | collective-permute-start | bytes 1179656 | tf_op jit(solution)/shard_map/ppermute | solution.py:19
  293.7 26.7 %collective-permute-start.28 = (bf16[1,4,192,256]{3,2,1,0:T(8,128)(2,1)S(1)}, bf16[1,4,192,256]{3,2,1,0:T(8,128)(2,1)S(1)}, u32[]{:S(2)}, u32[]{:S(2)}) collective-permute-start(bf16[1,4,192,256]{3,2,1,0:T(8,128)(2,1)S(1)} %get-tuple-element.648), channel_id=1, source_target_pairs={{0,8},{4,12},{8,0},{12,4},{16,24},{20,28},{24,16},{28,20},{1,9},{5... | collective-permute-start | bytes 1179656 | tf_op jit(solution)/shard_map/ppermute | solution.py:19
  300.0 20.4 %collective-permute-start.29 = (bf16[1,4,192,256]{3,2,1,0:T(8,128)(2,1)S(1)}, bf16[1,4,192,256]{3,2,1,0:T(8,128)(2,1)S(1)}, u32[]{:S(2)}, u32[]{:S(2)}) collective-permute-start(bf16[1,4,192,256]{3,2,1,0:T(8,128)(2,1)S(1)} %get-tuple-element.649), channel_id=1, source_target_pairs={{0,2},{1,3},{2,0},{3,1},{4,6},{5,7},{6,4},{7,5},{8,10},{9,11},{10,... | collective-permute-start | bytes 1179656 | tf_op jit(solution)/shard_map/ppermute | solution.py:19
  301.5 8.8 %collective-permute-start.33 = (bf16[1,1,24,3072]{3,2,1,0:T(8,128)(2,1)S(1)}, bf16[1,1,24,3072]{3,2,1,0:T(8,128)(2,1)S(1)}, u32[]{:S(2)}, u32[]{:S(2)}) collective-permute-start(bf16[1,1,24,3072]{3,2,1,0:T(8,128)(2,1)S(1)} %get-tuple-element.653), channel_id=1, source_target_pairs={{0,16},{4,20},{8,24},{12,28},{16,0},{20,4},{24,8},{28,12},{1,17},{... | collective-permute-start | bytes 442376 | tf_op jit(solution)/shard_map/ppermute | solution.py:19
  310.3 10.1 %collective-permute-start.30 = (bf16[2,16,24,768]{3,2,1,0:T(8,128)(2,1)S(1)}, bf16[2,16,24,768]{3,2,1,0:T(8,128)(2,1)S(1)}, u32[]{:S(2)}, u32[]{:S(2)}) collective-permute-start(bf16[2,16,24,768]{3,2,1,0:T(8,128)(2,1)S(1)} %get-tuple-element.650), channel_id=1, source_target_pairs={{0,1},{1,0},{2,3},{3,2},{4,5},{5,4},{6,7},{7,6},{8,9},{9,8},{10,11... | collective-permute-start | bytes 3538952 | tf_op jit(solution)/shard_map/ppermute | solution.py:19
  321.4 6.4 %collective-permute-start.38 = (f32[2,12,768]{2,1,0:T(8,128)S(1)}, f32[2,12,768]{2,1,0:T(8,128)S(1)}, u32[]{:S(2)}, u32[]{:S(2)}) collective-permute-start(f32[2,12,768]{2,1,0:T(8,128)S(1)} %add.41), channel_id=1, source_target_pairs={{0,4},{4,0},{8,12},{12,8},{16,20},{20,16},{24,28},{28,24},{1,5},{5... | collective-permute-start | bytes 221192 | tf_op jit(solution)/shard_map/ppermute | solution.py:19
  322.9 13.2 %collective-permute-start.39 = (bf16[4,2,24,768]{3,2,1,0:T(8,128)(2,1)S(1)}, bf16[4,2,24,768]{3,2,1,0:T(8,128)(2,1)S(1)}, u32[]{:S(2)}, u32[]{:S(2)}) collective-permute-start(bf16[4,2,24,768]{3,2,1,0:T(8,128)(2,1)S(1)} %get-tuple-element.681), channel_id=1, source_target_pairs={{0,8},{4,12},{8,0},{12,4},{16,24},{20,28},{24,16},{28,20},{1,9},{5... | collective-permute-start | bytes 884744 | tf_op jit(solution)/shard_map/ppermute | solution.py:19
  326.0 10.1 %collective-permute-start.34 = (bf16[1,2,192,256]{3,2,1,0:T(8,128)(2,1)S(1)}, bf16[1,2,192,256]{3,2,1,0:T(8,128)(2,1)S(1)}, u32[]{:S(2)}, u32[]{:S(2)}) collective-permute-start(bf16[1,2,192,256]{3,2,1,0:T(8,128)(2,1)S(1)} %get-tuple-element.676), channel_id=1, source_target_pairs={{0,8},{4,12},{8,0},{12,4},{16,24},{20,28},{24,16},{28,20},{1,9},{5... | collective-permute-start | bytes 589832 | tf_op jit(solution)/shard_map/ppermute | solution.py:19
  326.1 10.0 %collective-permute-start.35 = (bf16[1,2,192,256]{3,2,1,0:T(8,128)(2,1)S(1)}, bf16[1,2,192,256]{3,2,1,0:T(8,128)(2,1)S(1)}, u32[]{:S(2)}, u32[]{:S(2)}) collective-permute-start(bf16[1,2,192,256]{3,2,1,0:T(8,128)(2,1)S(1)} %get-tuple-element.677), channel_id=1, source_target_pairs={{0,2},{1,3},{2,0},{3,1},{4,6},{5,7},{6,4},{7,5},{8,10},{9,11},{10,... | collective-permute-start | bytes 589832 | tf_op jit(solution)/shard_map/ppermute | solution.py:19
  327.2 8.9 %collective-permute-start.36 = (bf16[1,2,192,256]{3,2,1,0:T(8,128)(2,1)S(1)}, bf16[1,2,192,256]{3,2,1,0:T(8,128)(2,1)S(1)}, u32[]{:S(2)}, u32[]{:S(2)}) collective-permute-start(bf16[1,2,192,256]{3,2,1,0:T(8,128)(2,1)S(1)} %get-tuple-element.678), channel_id=1, source_target_pairs={{0,4},{4,0},{8,12},{12,8},{16,20},{20,16},{24,28},{28,24},{1,5},{5... | collective-permute-start | bytes 589832 | tf_op jit(solution)/shard_map/ppermute | solution.py:19
  327.8 8.3 %collective-permute-start.37 = (bf16[2,16,24,768]{3,2,1,0:T(8,128)(2,1)S(1)}, bf16[2,16,24,768]{3,2,1,0:T(8,128)(2,1)S(1)}, u32[]{:S(2)}, u32[]{:S(2)}) collective-permute-start(bf16[2,16,24,768]{3,2,1,0:T(8,128)(2,1)S(1)} %get-tuple-element.679), channel_id=1, source_target_pairs={{0,1},{1,0},{2,3},{3,2},{4,5},{5,4},{6,7},{7,6},{8,9},{9,8},{10,11... | collective-permute-start | bytes 3538952 | tf_op jit(solution)/shard_map/ppermute | solution.py:19
  338.4 9.7 %collective-permute-start.43 = (bf16[1,1,192,256]{3,2,1,0:T(8,128)(2,1)S(1)}, bf16[1,1,192,256]{3,2,1,0:T(8,128)(2,1)S(1)}, u32[]{:S(2)}, u32[]{:S(2)}) collective-permute-start(bf16[1,1,192,256]{3,2,1,0:T(8,128)(2,1)S(1)} %get-tuple-element.710), channel_id=1, source_target_pairs={{0,16},{4,20},{8,24},{12,28},{16,0},{20,4},{24,8},{28,12},{1,17},{... | collective-permute-start | bytes 294920 | tf_op jit(solution)/shard_map/ppermute | solution.py:19
  339.0 13.6 %collective-permute-start.44 = (bf16[1,1,192,256]{3,2,1,0:T(8,128)(2,1)S(1)}, bf16[1,1,192,256]{3,2,1,0:T(8,128)(2,1)S(1)}, u32[]{:S(2)}, u32[]{:S(2)}) collective-permute-start(bf16[1,1,192,256]{3,2,1,0:T(8,128)(2,1)S(1)} %get-tuple-element.711), channel_id=1, source_target_pairs={{0,16},{4,20},{8,24},{12,28},{16,0},{20,4},{24,8},{28,12},{1,17},{... | collective-permute-start | bytes 294920 | tf_op jit(solution)/shard_map/ppermute | solution.py:19
  343.2 15.8 %collective-permute-start.40 = (bf16[4,8,24,256]{3,2,1,0:T(8,128)(2,1)S(1)}, bf16[4,8,24,256]{3,2,1,0:T(8,128)(2,1)S(1)}, u32[]{:S(2)}, u32[]{:S(2)}) collective-permute-start(bf16[4,8,24,256]{3,2,1,0:T(8,128)(2,1)S(1)} %get-tuple-element.707), channel_id=1, source_target_pairs={{0,2},{1,3},{2,0},{3,1},{4,6},{5,7},{6,4},{7,5},{8,10},{9,11},{10,... | collective-permute-start | bytes 1179656 | tf_op jit(solution)/shard_map/ppermute | solution.py:19
  343.8 15.3 %collective-permute-start.41 = (bf16[4,8,24,256]{3,2,1,0:T(8,128)(2,1)S(1)}, bf16[4,8,24,256]{3,2,1,0:T(8,128)(2,1)S(1)}, u32[]{:S(2)}, u32[]{:S(2)}) collective-permute-start(bf16[4,8,24,256]{3,2,1,0:T(8,128)(2,1)S(1)} %get-tuple-element.708), channel_id=1, source_target_pairs={{0,4},{4,0},{8,12},{12,8},{16,20},{20,16},{24,28},{28,24},{1,5},{5... | collective-permute-start | bytes 1179656 | tf_op jit(solution)/shard_map/ppermute | solution.py:19
  346.4 15.5 %collective-permute-start.42 = (bf16[4,8,24,256]{3,2,1,0:T(8,128)(2,1)S(1)}, bf16[4,8,24,256]{3,2,1,0:T(8,128)(2,1)S(1)}, u32[]{:S(2)}, u32[]{:S(2)}) collective-permute-start(bf16[4,8,24,256]{3,2,1,0:T(8,128)(2,1)S(1)} %get-tuple-element.709), channel_id=1, source_target_pairs={{0,8},{4,12},{8,0},{12,4},{16,24},{20,28},{24,16},{28,20},{1,9},{5... | collective-permute-start | bytes 1179656 | tf_op jit(solution)/shard_map/ppermute | solution.py:19
  348.1 11.0 %collective-permute-start.46 = (bf16[4,1,24,768]{3,2,1,0:T(8,128)(2,1)S(1)}, bf16[4,1,24,768]{3,2,1,0:T(8,128)(2,1)S(1)}, u32[]{:S(2)}, u32[]{:S(2)}) collective-permute-start(bf16[4,1,24,768]{3,2,1,0:T(8,128)(2,1)S(1)} %get-tuple-element.713), channel_id=1, source_target_pairs={{0,16},{4,20},{8,24},{12,28},{16,0},{20,4},{24,8},{28,12},{1,17},{... | collective-permute-start | bytes 442376 | tf_op jit(solution)/shard_map/ppermute | solution.py:19
  352.6 6.4 %collective-permute-start.45 = (bf16[1,1,192,256]{3,2,1,0:T(8,128)(2,1)S(1)}, bf16[1,1,192,256]{3,2,1,0:T(8,128)(2,1)S(1)}, u32[]{:S(2)}, u32[]{:S(2)}) collective-permute-start(bf16[1,1,192,256]{3,2,1,0:T(8,128)(2,1)S(1)} %get-tuple-element.712), channel_id=1, source_target_pairs={{0,16},{4,20},{8,24},{12,28},{16,0},{20,4},{24,8},{28,12},{1,17},{... | collective-permute-start | bytes 294920 | tf_op jit(solution)/shard_map/ppermute | solution.py:19
  362.7 8.5 %collective-permute-start.48 = (bf16[4,4,24,256]{3,2,1,0:T(8,128)(2,1)S(1)}, bf16[4,4,24,256]{3,2,1,0:T(8,128)(2,1)S(1)}, u32[]{:S(2)}, u32[]{:S(2)}) collective-permute-start(bf16[4,4,24,256]{3,2,1,0:T(8,128)(2,1)S(1)} %get-tuple-element.730), channel_id=1, source_target_pairs={{0,4},{4,0},{8,12},{12,8},{16,20},{20,16},{24,28},{28,24},{1,5},{5... | collective-permute-start | bytes 589832 | tf_op jit(solution)/shard_map/ppermute | solution.py:19
  363.5 8.4 %collective-permute-start.49 = (bf16[4,4,24,256]{3,2,1,0:T(8,128)(2,1)S(1)}, bf16[4,4,24,256]{3,2,1,0:T(8,128)(2,1)S(1)}, u32[]{:S(2)}, u32[]{:S(2)}) collective-permute-start(bf16[4,4,24,256]{3,2,1,0:T(8,128)(2,1)S(1)} %get-tuple-element.731), channel_id=1, source_target_pairs={{0,8},{4,12},{8,0},{12,4},{16,24},{20,28},{24,16},{28,20},{1,9},{5... | collective-permute-start | bytes 589832 | tf_op jit(solution)/shard_map/ppermute | solution.py:19
  363.5 8.4 %collective-permute-start.50 = (bf16[4,4,24,256]{3,2,1,0:T(8,128)(2,1)S(1)}, bf16[4,4,24,256]{3,2,1,0:T(8,128)(2,1)S(1)}, u32[]{:S(2)}, u32[]{:S(2)}) collective-permute-start(bf16[4,4,24,256]{3,2,1,0:T(8,128)(2,1)S(1)} %get-tuple-element.732), channel_id=1, source_target_pairs={{0,2},{1,3},{2,0},{3,1},{4,6},{5,7},{6,4},{7,5},{8,10},{9,11},{10,... | collective-permute-start | bytes 589832 | tf_op jit(solution)/shard_map/ppermute | solution.py:19
  365.5 5.7 %collective-permute-start.51 = (f32[2,12,768]{2,1,0:T(8,128)S(1)}, f32[2,12,768]{2,1,0:T(8,128)S(1)}, u32[]{:S(2)}, u32[]{:S(2)}) collective-permute-start(f32[2,12,768]{2,1,0:T(8,128)S(1)} %add.43), channel_id=1, source_target_pairs={{0,16},{4,20},{8,24},{12,28},{16,0},{20,4},{24,8},{28,12},{1,17},{... | collective-permute-start | bytes 221192 | tf_op jit(solution)/shard_map/ppermute | solution.py:19
  380.2 6.0 %collective-permute-start.55 = (bf16[4,1,24,256]{3,2,1,0:T(8,128)(2,1)S(1)}, bf16[4,1,24,256]{3,2,1,0:T(8,128)(2,1)S(1)}, u32[]{:S(2)}, u32[]{:S(2)}) collective-permute-start(bf16[4,1,24,256]{3,2,1,0:T(8,128)(2,1)S(1)} %get-tuple-element.770), channel_id=1, source_target_pairs={{0,16},{4,20},{8,24},{12,28},{16,0},{20,4},{24,8},{28,12},{1,17},{... | collective-permute-start | bytes 147464 | tf_op jit(solution)/shard_map/ppermute | solution.py:19
  (65 other events, 534.2 us)
